TPU v7x, 128 devices: a whole 4x4x4 slice. The times are simulated.
128 devices in a mesh: dp: 2 (over core), wide: 16 (over x, y), narrow: 4 (over z).
Axes of the slice: x: 4, y: 4, z: 4, core: 2. Of those that a mesh axis runs over, the one named last changes fastest.
Arguments:
- hidden_in: bfloat16 [6, 2048, 768], P('dp', 'wide'), may hold values from -6 to 6
- segments: int32 [6, 2048], P('dp', 'wide'), may hold values from 0 to 4, as said below
- weight_query: bfloat16 [768, 768], P(None, 'narrow'), may hold values from -0.21875 to 0.21875
- bias_query: float32 [768], P('narrow'), may hold values from -3 to 3
- weight_key: bfloat16 [768, 768], P(None, 'narrow'), may hold values from -0.21875 to 0.21875
- bias_key: float32 [768], P('narrow'), may hold values from -3 to 3
- weight_value: bfloat16 [768, 768], P(None, 'narrow'), may hold values from -0.21875 to 0.21875
- bias_value: float32 [768], P('narrow'), may hold values from -1.2 to 1.2
- weight_out: bfloat16 [768, 768], P('narrow'), may hold values from -1 to 1
- bias_out: float32 [768], replicated, may hold values from -3 to 3
- gain_one: float32 [768], replicated, may hold values from 0.5 to 1.5
- shift_one: float32 [768], replicated, may hold values from -3 to 3
- weight_up: bfloat16 [768, 3072], P('wide', 'narrow'), may hold values from -0.21875 to 0.21875
- bias_up: float32 [3072], P('narrow'), may hold values from -3 to 3
- weight_down: bfloat16 [3072, 768], P('narrow', 'wide'), may hold values from -0.109375 to 0.109375
- bias_down: float32 [768], replicated, may hold values from -3 to 3
- gain_two: float32 [768], replicated, may hold values from 0.5 to 1.5
- shift_two: float32 [768], replicated, may hold values from -3 to 3
- cotangent: bfloat16 [6, 2048, 768], P('dp', 'wide'), may hold values from -6 to 6
Outputs:
- layer_out: float32 [6, 2048, 768], P('dp', 'wide')
- grad_input: float32 [6, 2048, 768], P('dp', 'wide')
- grad_weight_query: float32 [768, 768], P(('dp', 'wide'), 'narrow')
- grad_bias_query: float32 [768], P('narrow')
- grad_weight_key: float32 [768, 768], P(('dp', 'wide'), 'narrow')
- grad_bias_key: float32 [768], P('narrow')
- grad_weight_value: float32 [768, 768], P(('dp', 'wide'), 'narrow')
- grad_bias_value: float32 [768], P('narrow')
- grad_weight_out: float32 [768, 768], P('narrow', ('dp', 'wide'))
- grad_bias_out: float32 [768], replicated
- grad_gain_one: float32 [768], replicated
- grad_shift_one: float32 [768], replicated
- grad_weight_up: float32 [768, 3072], P(('dp', 'wide'), 'narrow')
- grad_bias_up: float32 [3072], P('narrow')
- grad_weight_down: float32 [3072, 768], P('narrow', ('dp', 'wide'))
- grad_bias_down: float32 [768], replicated
- grad_gain_two: float32 [768], replicated
- grad_shift_two: float32 [768], replicated
Inputs may be any that keep to these rules, and one draw needn't show every extreme that they name: `segments`: along each row the ids start at 0, never fall and rise by at most 1 from one token to the next; a document is a run of equal ids, and every row holds exactly five documents.
All inputs are finite; a program needn't handle non-finite values.
Results may differ from a plain program's by a relative error of at most 0.023.
Values may be sent and summed in bfloat16 or wider, within the bound.
No kernel may reach another device: no remote copies, remote signals or barrier semaphores. Data moves between devices by JAX's collectives and lax.ppermute only.
A program may use at most 128 MiB of HBM per device.

v0:
```python
import math

import jax
import jax.numpy as jnp
import numpy as np
from jax import lax
from jax.sharding import PartitionSpec as P

HD = 64


EPSILON = 1e-12
NEG_LARGE = -1e30


def laid_out(parts, dim):
    parts = jnp.moveaxis(parts, 0, dim)
    shape = parts.shape
    return parts.reshape(*shape[:dim], shape[dim] * shape[dim + 1], *shape[dim + 2 :])


def copy_for_each(x, axis):
    peers = lax.axis_size(axis)
    return lax.all_to_all(jnp.broadcast_to(x[None], (peers, *x.shape)), axis, 0, 0, tiled=True)


def collect(x, axis, dim):
    return laid_out(copy_for_each(x, axis), dim)


def gather_together(arrays, axis, dims):
    vector = jnp.concatenate([a.reshape(-1) for a in arrays])
    lines, at, done = (lax.all_gather(vector, axis), 0, [])
    for a, dim in zip(arrays, dims):
        parts = lines[:, at : at + a.size].reshape(-1, *a.shape)
        done.append(laid_out(parts, dim))
        at += a.size
    return tuple(done)


def taken_together(x, axis):
    return copy_for_each(x, axis).sum(axis=0)


def sent_together(arrays, axis, dim, along):
    ends, at = ([], 0)
    for a in arrays[:-1]:
        at += a.shape[along]
        ends.append(at)
    both = jnp.concatenate(arrays, axis=along)
    return tuple(jnp.split(lax.all_gather(both, axis, axis=dim, tiled=True), ends, axis=along))


def taken_together_2(x, axis):
    everything = copy_for_each(x, axis)
    return jnp.sum(everything.astype(jnp.float32), axis=0)


def sent_together_2(arrays, axis, dim, along):
    widths = [a.shape[along] for a in arrays]
    both = jnp.concatenate(arrays, axis=along)
    whole = lax.psum_scatter(both, axis, scatter_dimension=dim, tiled=True)
    return tuple(jnp.split(whole, [sum(widths[:k]) for k in range(1, len(widths))], axis=along))


def in_one(arrays, axis):
    vector, at, done = (jnp.concatenate([a.reshape(-1) for a in arrays]), 0, [])
    subtotal = taken_together(vector, axis)
    for a in arrays:
        done.append(subtotal[at : at + a.size].reshape(a.shape))
        at += a.size
    return tuple(done)


def layer_norm(residual, gain_vec, shift_vec):
    center = residual - jnp.mean(residual, axis=-1, keepdims=True)
    spread = jnp.mean(center * center, axis=-1, keepdims=True)
    return center * lax.rsqrt(spread + EPSILON) * gain_vec + shift_vec


def gelu_exact(pre_act):
    return jax.nn.gelu(pre_act, approximate=False)


def rotary_tables(positions):
    inverse = jnp.asarray(np.power(10000.0, -np.arange(0, HD, 2) / HD), dtype=jnp.float32)
    angles = positions[..., None] * jnp.repeat(inverse, 2)
    return (jnp.cos(angles), jnp.sin(angles))


def pair_swap(tensor):
    paired = tensor.reshape(tensor.shape[:-1] + (tensor.shape[-1] // 2, 2))
    return jnp.stack([-paired[..., 1], paired[..., 0]], axis=-1).reshape(tensor.shape)


def widen(freq_table, tensor):
    repeats = tensor.shape[-1] // freq_table.shape[-1]
    return jnp.tile(freq_table, (1,) * (freq_table.ndim - 1) + (repeats,))


def rotate(tensor, cosine_tab, sine_tab):
    return tensor * widen(cosine_tab, tensor) + pair_swap(tensor) * widen(sine_tab, tensor)


def rotate_back(tensor, cosine_tab, sine_tab):
    return tensor * widen(cosine_tab, tensor) - pair_swap(tensor) * widen(sine_tab, tensor)


def contract_rows(left, right):
    return lax.dot_general(
        left, right, (((0,), (0,)), ((), ())), preferred_element_type=jnp.float32
    )


def contract_cols(left, right):
    return lax.dot_general(
        left, right, (((1,), (1,)), ((), ())), preferred_element_type=jnp.float32
    )


def column_sum(tensor):
    return jnp.sum(tensor.astype(jnp.float32), axis=0)


def block_slices(query_heads, key_all, value_all, seg_query, seg_keys, first_key, block_len):
    heads_local, head_size = (query_heads.shape[1], query_heads.shape[2])
    key_block = lax.dynamic_slice_in_dim(key_all, first_key, block_len, 0).reshape(
        block_len, heads_local, head_size
    )
    value_block = lax.dynamic_slice_in_dim(value_all, first_key, block_len, 0).reshape(
        block_len, heads_local, head_size
    )
    seg_block = lax.dynamic_slice_in_dim(seg_keys, first_key, block_len, 0)
    scores = jnp.einsum("qhd,khd->hqk", query_heads, key_block, preferred_element_type=jnp.float32)
    allowed = (seg_query[:, None] == seg_block[None, :])[None, :, :]
    return (scores, allowed, key_block, value_block)


def attend_row(query_heads, key_all, value_all, seg_query, seg_keys, block_len):
    row_width, heads_local, head_size = query_heads.shape
    block_count = key_all.shape[0] // block_len

    def statistic(state_pair, block_idx):
        run_max, run_sum = state_pair
        scores, allowed, key_block, value_block = block_slices(
            query_heads, key_all, value_all, seg_query, seg_keys, block_idx * block_len, block_len
        )
        new_max = jnp.maximum(run_max, jnp.max(jnp.where(allowed, scores, NEG_LARGE), axis=-1))
        weights = jnp.where(allowed, jnp.exp(scores - new_max[..., None]), 0.0)
        run_sum = run_sum * jnp.exp(run_max - new_max) + jnp.sum(weights, axis=-1)
        return ((new_max, run_sum), None)

    start_max = jnp.full((heads_local, row_width), NEG_LARGE, jnp.float32)
    (run_max, run_sum), _ = lax.scan(
        statistic, (start_max, jnp.zeros_like(start_max)), jnp.arange(block_count)
    )
    log_total = run_max + jnp.log(run_sum)

    def accumulate(accum_sum, block_idx):
        scores, allowed, key_block, value_block = block_slices(
            query_heads, key_all, value_all, seg_query, seg_keys, block_idx * block_len, block_len
        )
        prob_low = jnp.where(allowed, jnp.exp(scores - log_total[..., None]), 0.0).astype(
            jnp.bfloat16
        )
        return (
            accum_sum
            + jnp.einsum("hqk,khd->qhd", prob_low, value_block, preferred_element_type=jnp.float32),
            None,
        )

    accum_sum, _ = lax.scan(
        accumulate,
        jnp.zeros((row_width, heads_local, head_size), jnp.float32),
        jnp.arange(block_count),
    )
    return (accum_sum.reshape(row_width, heads_local * head_size).astype(jnp.bfloat16), log_total)


def attend_row_back(
    query_heads, key_all, value_all, grad_heads, seg_query, seg_keys, log_total, block_len
):
    row_width, heads_local, head_size = query_heads.shape
    block_count = key_all.shape[0] // block_len
    local_dim = heads_local * head_size

    def prob_and_grad(block_idx):
        scores, allowed, key_block, value_block = block_slices(
            query_heads, key_all, value_all, seg_query, seg_keys, block_idx * block_len, block_len
        )
        prob_full = jnp.where(allowed, jnp.exp(scores - log_total[..., None]), 0.0)
        grad_prob = jnp.einsum(
            "qhd,khd->hqk", grad_heads, value_block, preferred_element_type=jnp.float32
        )
        return (prob_full, grad_prob, key_block)

    def gather_delta(accum_sum, block_idx):
        prob_full, grad_prob, key_block = prob_and_grad(block_idx)
        return (accum_sum + jnp.sum(prob_full * grad_prob, axis=-1), None)

    row_delta, _ = lax.scan(
        gather_delta, jnp.zeros((heads_local, row_width), jnp.float32), jnp.arange(block_count)
    )
    start_query = jnp.zeros((row_width, heads_local, head_size), jnp.float32)

    def query_block(grad_query, block_idx):
        prob_full, grad_prob, key_block = prob_and_grad(block_idx)
        grad_score = (prob_full * (grad_prob - row_delta[..., None])).astype(jnp.bfloat16)
        return (
            grad_query
            + jnp.einsum("hqk,khd->qhd", grad_score, key_block, preferred_element_type=jnp.float32),
            None,
        )

    grad_query, _ = lax.scan(query_block, start_query, jnp.arange(block_count))
    return (grad_query.reshape(row_width, local_dim), None, None, row_delta)


def key_side_back(
    query_all,
    grad_all,
    log_all,
    delta_all,
    key_heads,
    value_heads,
    seg_all_row,
    seg_local,
    block_len,
):
    row_width, heads_local, head_size = key_heads.shape
    block_count = query_all.shape[0] // block_len

    def key_block(carry_pair, block_idx):
        grad_key, grad_value = carry_pair
        first_query = block_idx * block_len
        query_block_heads = lax.dynamic_slice_in_dim(query_all, first_query, block_len, 0).reshape(
            block_len, heads_local, head_size
        )
        grad_block_heads = lax.dynamic_slice_in_dim(grad_all, first_query, block_len, 0).reshape(
            block_len, heads_local, head_size
        )
        log_block = lax.dynamic_slice_in_dim(log_all, first_query, block_len, 1)
        delta_block = lax.dynamic_slice_in_dim(delta_all, first_query, block_len, 1)
        seg_block = lax.dynamic_slice_in_dim(seg_all_row, first_query, block_len, 0)
        scores = jnp.einsum(
            "qhd,khd->hqk", query_block_heads, key_heads, preferred_element_type=jnp.float32
        )
        allowed = (seg_block[:, None] == seg_local[None, :])[None, :, :]
        prob_full = jnp.where(allowed, jnp.exp(scores - log_block[..., None]), 0.0)
        grad_prob = jnp.einsum(
            "qhd,khd->hqk", grad_block_heads, value_heads, preferred_element_type=jnp.float32
        )
        grad_score = (prob_full * (grad_prob - delta_block[..., None])).astype(jnp.bfloat16)
        grad_key = grad_key + jnp.einsum(
            "hqk,qhd->khd", grad_score, query_block_heads, preferred_element_type=jnp.float32
        )
        grad_value = grad_value + jnp.einsum(
            "hqk,qhd->khd",
            prob_full.astype(jnp.bfloat16),
            grad_block_heads,
            preferred_element_type=jnp.float32,
        )
        return ((grad_key, grad_value), None)

    start_zero = jnp.zeros((row_width, heads_local, head_size), jnp.float32)
    (grad_key, grad_value), _ = lax.scan(
        key_block, (start_zero, start_zero), jnp.arange(block_count)
    )
    local_dim = heads_local * head_size
    return (grad_key.reshape(row_width, local_dim), grad_value.reshape(row_width, local_dim))


def body(
    hidden_in,
    segments,
    weight_query,
    bias_query,
    weight_key,
    bias_key,
    weight_value,
    bias_value,
    weight_out,
    bias_out,
    gain_one,
    shift_one,
    weight_up,
    bias_up,
    weight_down,
    bias_down,
    gain_two,
    shift_two,
    cotangent,
):
    row_count, row_width, model_dim = hidden_in.shape
    local_dim = weight_query.shape[1]
    tokens = row_count * row_width
    row_length = row_width * lax.axis_size("wide")
    block_len = math.gcd(row_length, 512)
    score_scale = HD ** (-0.5)
    heads_shape = (row_width, local_dim // HD, HD)
    seg_all = collect(segments, "wide", 1)
    places = jnp.arange(row_length, dtype=jnp.int32)[None, :]
    opening = jnp.concatenate(
        [jnp.ones((row_count, 1), jnp.bool_), seg_all[:, 1:] != seg_all[:, :-1]], axis=1
    )
    pos_all = places - lax.cummax(jnp.where(opening, places, 0), axis=1)
    positions = lax.dynamic_slice_in_dim(
        pos_all, lax.axis_index("wide") * row_width, row_width, 1
    ).astype(jnp.float32)
    cosine_tab, sine_tab = rotary_tables(positions)
    flat_in = hidden_in.reshape(tokens, model_dim)

    def project(weight_mat, bias_vec):
        return (
            jnp.dot(flat_in, weight_mat, preferred_element_type=jnp.float32) + bias_vec
        ).reshape(row_count, row_width, local_dim)

    query_rot = (
        rotate(project(weight_query, bias_query), cosine_tab, sine_tab) * score_scale
    ).astype(jnp.bfloat16)
    key_rot = rotate(project(weight_key, bias_key), cosine_tab, sine_tab).astype(jnp.bfloat16)
    value_low = project(weight_value, bias_value).astype(jnp.bfloat16)
    key_all, value_all = gather_together((key_rot, value_low), "wide", (1, 1))
    attn_rows = []
    log_rows = []
    for row_idx in range(row_count):
        attn_row, log_row = attend_row(
            query_rot[row_idx].reshape(heads_shape),
            key_all[row_idx],
            value_all[row_idx],
            segments[row_idx],
            seg_all[row_idx],
            block_len,
        )
        attn_rows.append(attn_row)
        log_rows.append(log_row)
    attn_low = jnp.stack(attn_rows).reshape(tokens, local_dim)
    attn_out = (
        taken_together(jnp.dot(attn_low, weight_out, preferred_element_type=jnp.float32), "narrow")
        + bias_out
    )
    resid_one = flat_in.astype(jnp.float32) + attn_out
    normed_one, norm_one_back = jax.vjp(layer_norm, resid_one, gain_one, shift_one)
    normed_low = normed_one.astype(jnp.bfloat16)
    up_full = collect(weight_up, "wide", 0)
    down_full = collect(weight_down, "wide", 1)
    pre_act = jnp.dot(normed_low, up_full, preferred_element_type=jnp.float32) + bias_up
    hidden_act, gelu_back = jax.vjp(gelu_exact, pre_act)
    hidden_low = hidden_act.astype(jnp.bfloat16)
    ffn_out = (
        taken_together(jnp.dot(hidden_low, down_full, preferred_element_type=jnp.float32), "narrow")
        + bias_down
    )
    layer_out, norm_two_back = jax.vjp(layer_norm, normed_one + ffn_out, gain_two, shift_two)
    grad_two, grad_gain_two, grad_shift_two = norm_two_back(
        cotangent.reshape(tokens, model_dim).astype(jnp.float32)
    )
    grad_ffn = grad_two.astype(jnp.bfloat16)
    grad_bias_down = column_sum(grad_ffn)
    grad_weight_down = contract_rows(hidden_low, grad_ffn)
    (grad_pre,) = gelu_back(contract_cols(grad_ffn, down_full))
    grad_pre_low = grad_pre.astype(jnp.bfloat16)
    grad_bias_up = column_sum(grad_pre_low)
    grad_weight_up = contract_rows(normed_low, grad_pre_low)
    grad_normed = grad_two + taken_together(contract_cols(grad_pre_low, up_full), "narrow")
    grad_one, grad_gain_one, grad_shift_one = norm_one_back(grad_normed)
    grad_attn_out = grad_one.astype(jnp.bfloat16)
    grad_bias_out = column_sum(grad_attn_out)
    grad_weight_out = contract_rows(attn_low, grad_attn_out)
    grad_attn = (
        contract_cols(grad_attn_out, weight_out)
        .astype(jnp.bfloat16)
        .reshape(row_count, row_width, local_dim)
    )
    key_back, value_back = (key_all, value_all)
    query_grads = []
    key_grads = []
    value_grads = []
    delta_rows = []
    for row_idx in range(row_count):
        grad_qrow, unused_key, unused_value, delta_row = attend_row_back(
            query_rot[row_idx].reshape(heads_shape),
            key_back[row_idx],
            value_back[row_idx],
            grad_attn[row_idx].reshape(heads_shape),
            segments[row_idx],
            seg_all[row_idx],
            log_rows[row_idx],
            block_len,
        )
        query_grads.append(grad_qrow)
        delta_rows.append(delta_row)
    query_all, grad_all = gather_together((query_rot, grad_attn), "wide", (1, 1))
    log_all, delta_all = sent_together((jnp.stack(log_rows), jnp.stack(delta_rows)), "wide", 2, 0)
    for row_idx in range(row_count):
        key_share, value_share = key_side_back(
            query_all[row_idx],
            grad_all[row_idx],
            log_all[row_idx],
            delta_all[row_idx],
            key_rot[row_idx].reshape(heads_shape),
            value_low[row_idx].reshape(heads_shape),
            seg_all[row_idx],
            segments[row_idx],
            block_len,
        )
        key_grads.append(key_share)
        value_grads.append(value_share)
    grad_query = (
        rotate_back(jnp.stack(query_grads) * score_scale, cosine_tab, sine_tab)
        .astype(jnp.bfloat16)
        .reshape(tokens, local_dim)
    )
    grad_key = (
        rotate_back(jnp.stack(key_grads), cosine_tab, sine_tab)
        .astype(jnp.bfloat16)
        .reshape(tokens, local_dim)
    )
    grad_value = jnp.stack(value_grads).astype(jnp.bfloat16).reshape(tokens, local_dim)
    input_part = (
        contract_cols(grad_query, weight_query)
        + contract_cols(grad_key, weight_key)
        + contract_cols(grad_value, weight_value)
    )
    grad_input = grad_one + taken_together_2(input_part.astype(jnp.bfloat16), "narrow").astype(
        jnp.float32
    )
    row_grads = tuple(
        (
            part.astype(jnp.float32)
            for part in sent_together_2(
                (
                    contract_rows(flat_in, grad_query).astype(jnp.bfloat16),
                    contract_rows(flat_in, grad_key).astype(jnp.bfloat16),
                    contract_rows(flat_in, grad_value).astype(jnp.bfloat16),
                    grad_weight_up.astype(jnp.bfloat16),
                ),
                ("dp", "wide"),
                0,
                1,
            )
        )
    )
    col_grads = tuple(
        (
            part.astype(jnp.float32)
            for part in sent_together_2(
                (grad_weight_out.astype(jnp.bfloat16), grad_weight_down.astype(jnp.bfloat16)),
                ("dp", "wide"),
                1,
                0,
            )
        )
    )
    vector_grads = in_one(
        (
            column_sum(grad_query),
            column_sum(grad_key),
            column_sum(grad_value),
            grad_bias_up,
            grad_bias_out,
            grad_bias_down,
            grad_gain_one,
            grad_shift_one,
            grad_gain_two,
            grad_shift_two,
        ),
        ("dp", "wide"),
    )
    out_shape = (row_count, row_width, model_dim)
    return (
        layer_out.reshape(out_shape),
        grad_input.reshape(out_shape),
        row_grads[0],
        vector_grads[0],
        row_grads[1],
        vector_grads[1],
        row_grads[2],
        vector_grads[2],
        col_grads[0],
        vector_grads[4],
        vector_grads[6],
        vector_grads[7],
        row_grads[3],
        vector_grads[3],
        col_grads[1],
        vector_grads[5],
        vector_grads[8],
        vector_grads[9],
    )


def solution(mesh):
    in_specs = (
        P("dp", "wide", None),
        P("dp", "wide"),
        P(None, "narrow"),
        P("narrow"),
        P(None, "narrow"),
        P("narrow"),
        P(None, "narrow"),
        P("narrow"),
        P("narrow", None),
        P(),
        P(),
        P(),
        P("wide", "narrow"),
        P("narrow"),
        P("narrow", "wide"),
        P(),
        P(),
        P(),
        P("dp", "wide", None),
    )
    out_specs = (
        P("dp", "wide", None),
        P("dp", "wide", None),
        P(("dp", "wide"), "narrow"),
        P("narrow"),
        P(("dp", "wide"), "narrow"),
        P("narrow"),
        P(("dp", "wide"), "narrow"),
        P("narrow"),
        P("narrow", ("dp", "wide")),
        P(),
        P(),
        P(),
        P(("dp", "wide"), "narrow"),
        P("narrow"),
        P("narrow", ("dp", "wide")),
        P(),
        P(),
        P(),
    )
    return jax.shard_map(body, mesh=mesh, in_specs=in_specs, out_specs=out_specs, check_vma=False)
```

profile of v0, /device:TPU:0, one launch (start us, length us, event | category | flops | bytes accessed | tf_op | source)
XLA Modules:
  0.0 933.6 jit_solution(7076348448328632454)
XLA Ops:
  8.6 7.2 all-to-all-start
  20.7 11.7 %copy.378 = f32[3,128,96,2]{3,2,1,0:T(8,128)} copy(f32[3,128,96,2]{1,0,3,2:T(4,128)S(1)} %pad_maximum_fusion.3) | data formatting | bytes 589824 | tf_op jit(solution)/shard_map/stack | solution.py:93
  32.4 14.6 %reshape.1844 = f32[73728]{0:T(1024)} reshape(f32[3,128,96,2]{3,2,1,0:T(8,128)} %copy.378) | data formatting | bytes 589824 | tf_op jit(solution)/shard_map/reshape | solution.py:93
  47.4 11.5 %copy.346 = f32[3,128,96,2]{3,2,1,0:T(8,128)} copy(f32[3,128,96,2]{1,0,3,2:T(4,128)S(1)} %pad_maximum_fusion.2) | data formatting | bytes 589824 | tf_op jit(solution)/shard_map/stack | solution.py:93
  58.9 14.5 %reshape.1834 = f32[73728]{0:T(1024)} reshape(f32[3,128,96,2]{3,2,1,0:T(8,128)} %copy.346) | data formatting | bytes 589824 | tf_op jit(solution)/shard_map/reshape | solution.py:93
  83.7 2.1 multiply_convert_fusion.1
  92.9 50.2 %all-gather.5.cloned.1.call-done = bf16[2359296]{0:T(1024)(128)(2,1)} async-done(((bf16[147456]{0:T(1024)(128)(2,1)}), bf16[2359296]{0:T(1024)(128)(2,1)}) %all-gather.5.cloned.1.call-update) | async-done | bytes 4718608 | tf_op jit(solution)/shard_map/all_gather | solution.py:33
  143.1 5.1 reshape.1853
  148.2 4.2 fusion.183
  152.4 6.0 reshape.1835
  158.4 3.6 fusion.186
  162.0 2.2 copy.359
  164.2 5.1 reshape.1836
  169.3 3.6 fusion.187
  176.4 17.7 %while.177 = (s32[]{:T(128)}, f32[3,128]{1,0:T(4,128)S(1)}, f32[3,128]{1,0:T(4,128)}, s32[1,128]{1,0:T(1,128)}, s32[4]{0:T(128)}, /*index=5*/s32[2048]{0:T(1024)...) while((s32[]{:T(128)}, f32[3,128]{1,0:T(4,128)S(1)}, ...), condition=%wide.region_5.6_spmd.clone, body=%wide.region_2.5_spmd.clone.sunk | while | flops 26216324 | bytes 2435274 | solution.py:154
  194.1 2.2 copy.357
  196.9 14.5 %while.179 = (s32[]{:T(128)}, f32[3,128]{1,0:T(4,128)S(1)}, f32[3,128]{1,0:T(4,128)S(1)}, s32[1,128]{1,0:T(1,128)S(1)}, s32[4]{0:T(128)}, /*index=5*/s32[2048]{0...) while((s32[]{:T(128)}, f32[3,128]{1,0:T(4,128)S(1)}, ...), condition=%wide.region_11.12_spmd.clone, body=%wide.region_8.11_spmd.clone.sunk | while | flops 26216324 | bytes 2435274 | solution.py:154
  211.9 19.4 %while.181 = (s32[]{:T(128)}, f32[3,128]{1,0:T(4,128)S(1)}, f32[3,128]{1,0:T(4,128)S(1)}, s32[1,128]{1,0:T(1,128)}, s32[4]{0:T(128)}, /*index=5*/s32[2048]{0:T(1...) while((s32[]{:T(128)}, f32[3,128]{1,0:T(4,128)S(1)}, ...), condition=%wide.region_17.18_spmd.clone, body=%wide.region_14.17_spmd.clone.sunk | while | flops 26216324 | bytes 2435274 | solution.py:154
  233.2 23.3 %while.182 = (s32[]{:T(128)}, f32[128,3,64]{0,2,1:T(8,128)}, s32[4]{0:T(128)S(1)}, bf16[2048,192]{0,1:T(8,128)(2,1)}, s32[1,128]{1,0:T(1,128)}, /*index=5*/s32[2...) while((s32[]{:T(128)}, f32[128,3,64]{0,2,1:T(8,128)}, ...), condition=%wide.region_19.20_spmd.clone, body=%wide.region_18.19_spmd.clone.sunk | while | flops 51036168 | bytes 1564881 | solution.py:172
  242.7 2.1 fusion.396
  248.6 2.1 fusion.396
  254.4 2.1 fusion.396
  257.6 2.2 copy.356
  259.8 12.3 %while.180 = (s32[]{:T(128)}, f32[128,3,64]{0,2,1:T(8,128)S(1)}, s32[4]{0:T(128)S(1)}, bf16[2048,192]{0,1:T(8,128)(2,1)}, s32[1,128]{1,0:T(1,128)S(1)}, /*index=...) while((s32[]{:T(128)}, f32[128,3,64]{0,2,1:T(8,128)S(1)}, ...), condition=%wide.region_13.14_spmd.clone, body=%wide.region_12.13_spmd.clone.sunk | while | flops 51036168 | bytes 1564881 | solution.py:172
  273.6 10.8 %while.178 = (s32[]{:T(128)}, f32[128,3,64]{0,2,1:T(8,128)S(1)}, s32[4]{0:T(128)S(1)}, bf16[2048,192]{0,1:T(8,128)(2,1)S(1)}, s32[1,128]{1,0:T(1,128)}, /*index=...) while((s32[]{:T(128)}, f32[128,3,64]{0,2,1:T(8,128)S(1)}, ...), condition=%wide.region_7.8_spmd.clone, body=%wide.region_6.7_spmd.clone.sunk | while | flops 51036168 | bytes 1564881 | solution.py:172
  285.6 58.9 %all_to_all.41 = f32[4,384,768]{2,1,0:T(8,128)} all-to-all(f32[4,384,768]{2,1,0:T(8,128)S(1)} %broadcast_in_dim.297), channel_id=1, replica_groups=mesh['dp'=2,'wide'=16,'narrow'=4] {'narrow'}, dimensions={0} | all-to-all | bytes 9437184 | tf_op jit(solution)/shard_map/all_to_all | solution.py:24
  345.5 5.3 all-to-all-start.2
  350.8 2.8 reduce_sum.309
  355.5 12.9 %all-to-all-done.2 = bf16[16,48,768]{2,1,0:T(8,128)(2,1)} async-done(((bf16[16,48,768]{2,1,0:T(8,128)(2,1)}), bf16[16,48,768]{2,1,0:T(8,128)(2,1)}, u32[]{:S(2)}, u32[]{:S(2)}) %all-to-all-start.2) | async-done | bytes 1179680 | tf_op jit(solution)/shard_map/all_to_all | solution.py:24
  369.6 3.8 all-to-all-start.3
  374.1 5.4 multiply_convert_fusion
  379.5 10.7 %all-to-all-done.3 = bf16[16,768,48]{1,2,0:T(8,128)(2,1)S(1)} async-done(((bf16[16,768,48]{1,2,0:T(8,128)(2,1)}), bf16[16,768,48]{1,2,0:T(8,128)(2,1)S(1)}, u32[]{:S(2)}, u32[]{:S(2)}) %all-to-all-start.3) | async-done | bytes 1179680 | tf_op jit(solution)/shard_map/all_to_all | solution.py:24
  390.2 2.1 fusion.196
  392.7 55.3 %all_to_all.42 = f32[4,384,768]{2,1,0:T(8,128)} all-to-all(f32[4,384,768]{2,1,0:T(8,128)S(1)} %broadcast_in_dim.300), channel_id=1, replica_groups=mesh['dp'=2,'wide'=16,'narrow'=4] {'narrow'}, dimensions={0} | all-to-all | bytes 9437184 | tf_op jit(solution)/shard_map/all_to_all | solution.py:24
  448.0 3.9 reduce_sum.313
  462.2 2.6 broadcast_in_dim.303
  464.9 5.1 all-to-all-start.5
  477.0 43.7 %all-to-all-done.5 = f32[4,384,768]{2,1,0:T(8,128)} async-done(((f32[4,384,768]{2,1,0:T(8,128)}), f32[4,384,768]{2,1,0:T(8,128)}, u32[]{:S(2)}, u32[]{:S(2)}) %all-to-all-start.5) | async-done | bytes 4718624 | tf_op jit(solution)/shard_map/all_to_all | solution.py:24
  520.7 3.8 reduce_sum.319
  524.5 4.0 multiply_reduce_fusion.1
  534.5 24.9 %while.187 = (s32[]{:T(128)}, f32[3,128]{1,0:T(4,128)}, s32[1,128]{1,0:T(1,128)}, s32[4]{0:T(128)S(1)}, s32[2048]{0:T(1024)}, /*index=5*/bf16[2048,192]{0,1:T(8,...) while((s32[]{:T(128)}, f32[3,128]{1,0:T(4,128)}, ...), condition=%wide.region_43.44_spmd.clone, body=%wide.region_41.43_spmd.clone.sunk | while | flops 51184004 | bytes 2996441 | solution.py:201
  559.3 24.1 %while.188 = (s32[]{:T(128)}, f32[128,3,64]{0,2,1:T(8,128)}, s32[4]{0:T(128)S(1)}, bf16[2048,192]{0,1:T(8,128)(2,1)S(1)}, s32[1,128]{1,0:T(1,128)}, /*index=5*/s...) while((s32[]{:T(128)}, f32[128,3,64]{0,2,1:T(8,128)}, ...), condition=%wide.region_45.46_spmd.clone, body=%wide.region_44.45_spmd.clone.sunk | while | flops 76595200 | bytes 3385057 | solution.py:215
  583.6 13.1 %while.185 = (s32[]{:T(128)}, f32[3,128]{1,0:T(4,128)S(1)}, s32[1,128]{1,0:T(1,128)S(1)}, s32[4]{0:T(128)S(1)}, s32[2048]{0:T(1024)S(1)}, /*index=5*/bf16[2048,1...) while((s32[]{:T(128)}, f32[3,128]{1,0:T(4,128)S(1)}, ...), condition=%wide.region_38.39_spmd.clone, body=%wide.region_36.38_spmd.clone.sunk | while | flops 51184004 | bytes 3193077 | solution.py:201
  597.2 11.5 %while.183 = (s32[]{:T(128)}, f32[3,128]{1,0:T(4,128)S(1)}, s32[1,128]{1,0:T(1,128)}, s32[4]{0:T(128)S(1)}, s32[2048]{0:T(1024)S(1)}, /*index=5*/bf16[2048,192]{...) while((s32[]{:T(128)}, f32[3,128]{1,0:T(4,128)S(1)}, ...), condition=%wide.region_33.34_spmd.clone, body=%wide.region_31.33_spmd.clone.sunk | while | flops 51184004 | bytes 2996441 | solution.py:201
  611.6 2.1 convolution_convert_fusion
  614.9 2.6 copy.410
  618.3 26.6 %all_gather.19 = f32[6,3,2048]{2,1,0:T(4,128)} all-gather(f32[6,3,128]{2,1,0:T(4,128)S(1)} %constant_dynamic-update-slice_fusion), channel_id=1, replica_groups=mesh['dp'=2,'wide'=16,'narrow'=4] {'wide'}, dimensions={2}, use_global_device_ids=true | all-gather | bytes 156672 | tf_op jit(solution)/shard_map/all_gather | solution.py:51
  644.9 19.9 %while.186 = (s32[]{:T(128)}, f32[128,3,64]{0,2,1:T(8,128)}, s32[4]{0:T(128)S(1)}, bf16[2048,192]{0,1:T(8,128)(2,1)}, s32[1,128]{1,0:T(1,128)S(1)}, /*index=5*/s...) while((s32[]{:T(128)}, f32[128,3,64]{0,2,1:T(8,128)}, ...), condition=%wide.region_40.41_spmd.clone, body=%wide.region_39.40_spmd.clone.sunk | while | flops 76595200 | bytes 3385057 | solution.py:215
  665.3 17.3 %while.184 = (s32[]{:T(128)}, f32[128,3,64]{0,2,1:T(8,128)}, s32[4]{0:T(128)S(1)}, bf16[2048,192]{0,1:T(8,128)(2,1)S(1)}, s32[1,128]{1,0:T(1,128)}, /*index=5*/s...) while((s32[]{:T(128)}, f32[128,3,64]{0,2,1:T(8,128)}, ...), condition=%wide.region_35.36_spmd.clone, body=%wide.region_34.35_spmd.clone.sunk | while | flops 76595200 | bytes 3581693 | solution.py:215
  687.9 5.1 reshape.1854
  693.0 4.3 fusion.182
  697.2 6.0 reshape.1845
  703.2 3.7 fusion.185
  706.9 2.2 copy.384
  709.1 4.7 reshape.1848
  713.8 3.5 fusion.184
  718.3 22.8 %while.191 = (s32[]{:T(128)}, f32[128,3,64]{0,2,1:T(8,128)S(1)}, f32[128,3,64]{0,2,1:T(8,128)S(1)}, s32[4]{0:T(128)S(1)}, bf16[2048,192]{0,1:T(8,128)(2,1)}, /*i...) while((s32[]{:T(128)}, f32[128,3,64]{0,2,1:T(8,128)S(1)}, ...), condition=%wide.region_51.52_spmd.clone, body=%wide.region_50.51_spmd.clone.sunk | while | flops 102006784 | bytes 4598510 | solution.py:266
  744.1 17.5 %while.190 = (s32[]{:T(128)}, f32[128,3,64]{0,2,1:T(8,128)S(1)}, f32[128,3,64]{0,2,1:T(8,128)S(1)}, s32[4]{0:T(128)S(1)}, bf16[2048,192]{0,1:T(8,128)(2,1)S(1)},...) while((s32[]{:T(128)}, f32[128,3,64]{0,2,1:T(8,128)S(1)}, ...), condition=%wide.region_49.50_spmd.clone, body=%wide.region_48.49_spmd.clone.sunk | while | flops 102006784 | bytes 4598510 | solution.py:266
  764.5 23.6 %while.189 = (s32[]{:T(128)}, f32[128,3,64]{0,2,1:T(8,128)S(1)}, f32[128,3,64]{0,2,1:T(8,128)S(1)}, s32[4]{0:T(128)S(1)}, bf16[2048,192]{0,1:T(8,128)(2,1)S(1)},...) while((s32[]{:T(128)}, f32[128,3,64]{0,2,1:T(8,128)S(1)}, ...), condition=%wide.region_47.48_spmd.clone, body=%wide.region_46.47_spmd.clone.sunk | while | flops 102006784 | bytes 4795146 | solution.py:266
  795.7 4.6 all-to-all-start.6
  806.6 15.8 %all-to-all-done.6 = bf16[4,384,768]{2,1,0:T(8,128)(2,1)} async-done(((bf16[4,384,768]{2,1,0:T(8,128)(2,1)}), bf16[4,384,768]{2,1,0:T(8,128)(2,1)}, u32[]{:S(2)}, u32[]{:S(2)}) %all-to-all-start.6) | async-done | bytes 2359328 | tf_op jit(solution)/shard_map/all_to_all | solution.py:24
  822.4 2.2 convert_reduce_fusion
  827.3 5.5 all-to-all-start.7
  837.4 82.3 %all-reduce.4.cloned.1.call-done = bf16[768,1344]{0,1:T(8,128)(2,1)} async-done(((bf16[768,1344]{0,1:T(8,128)(2,1)}), bf16[768,1344]{0,1:T(8,128)(2,1)}) %all-reduce.4.cloned.1.call-update) | async-done | bytes 2064400
  (889 shorter events, 330.8 us)
Async XLA Ops:
  7.2 277.3 %copy-start = (bf16[192,768]{1,0:T(8,128)(2,1)S(1)}, bf16[192,768]{1,0:T(8,128)(2,1)}, u32[]{:S(2)}) copy-start(bf16[192,768]{1,0:T(8,128)(2,1)} %param.58) | copy-start | bytes 884740
  8.6 65.8 %all-to-all-start = ((s32[16,3,128]{2,1,0:T(4,128)}), s32[16,3,128]{2,1,0:T(4,128)}, u32[]{:S(2)}, u32[]{:S(2)}) async-start(s32[16,3,128]{2,1,0:T(4,128)} %broadcast_in_dim.294), calls=%async_computation | async-start | bytes 65536 | tf_op jit(solution)/shard_map/all_to_all | solution.py:24
  15.7 127.4 %all-gather.5.cloned.1.call-start = ((), (), s32[]{:S(2)}) async-start(), calls=%async_computation.9 | async-start | bytes 5013504 | tf_op jit(solution)/shard_map/all_gather | solution.py:33
  32.4 14.6 %copy-start.125 = (f32[32]{0:T(128)S(1)}, f32[32]{0:T(128)}, u32[]{:S(2)}) copy-start(f32[32]{0:T(128)} %constant.309.clone) | copy-start | bytes 388
  77.9 10.2 %copy-start.38 = (f32[3,128,64]{1,2,0:T(8,128)}, f32[3,128,64]{1,2,0:T(8,128)S(1)}, u32[]{:S(2)}) copy-start(f32[3,128,64]{1,2,0:T(8,128)S(1)} %get-tuple-element.2769) | copy-start | bytes 294916
  77.9 10.3 %copy-start.51 = (f32[3,128,64]{1,2,0:T(8,128)}, f32[3,128,64]{1,2,0:T(8,128)S(1)}, u32[]{:S(2)}) copy-start(f32[3,128,64]{1,2,0:T(8,128)S(1)} %get-tuple-element.2770) | copy-start | bytes 294916
  88.3 2.5 copy-start.44
  256.5 3.3 copy-start.5
  256.5 3.3 copy-start.96
  257.6 26.9 %copy-start.69 = (bf16[128,3,64]{0,2,1:T(8,128)(2,1)}, bf16[128,3,64]{0,2,1:T(8,128)(2,1)S(1)}, u32[]{:S(2)}) copy-start(bf16[128,3,64]{0,2,1:T(8,128)(2,1)S(1)} %convert_element_type.301) | copy-start | bytes 147460
  272.1 12.4 %copy-start.71 = (bf16[128,3,64]{0,2,1:T(8,128)(2,1)}, bf16[128,3,64]{0,2,1:T(8,128)(2,1)S(1)}, u32[]{:S(2)}) copy-start(bf16[128,3,64]{0,2,1:T(8,128)(2,1)S(1)} %convert_element_type.299) | copy-start | bytes 147460
  285.6 58.9 %copy-start.97 = (bf16[48,768]{1,0:T(8,128)(2,1)S(1)}, bf16[48,768]{1,0:T(8,128)(2,1)}, u32[]{:S(2)}) copy-start(bf16[48,768]{1,0:T(8,128)(2,1)} %param.62) | copy-start | bytes 221188
  345.5 22.8 %all-to-all-start.2 = ((bf16[16,48,768]{2,1,0:T(8,128)(2,1)}), bf16[16,48,768]{2,1,0:T(8,128)(2,1)}, u32[]{:S(2)}, u32[]{:S(2)}) async-start(bf16[16,48,768]{2,1,0:T(8,128)(2,1)} %broadcast_in_dim.298), calls=%async_computation.2 | async-start | bytes 2359296 | tf_op jit(solution)/shard_map/all_to_all | solution.py:24
  350.8 2.8 copy-start.113
  354.6 13.7 %copy-start.98 = (bf16[768,48]{0,1:T(8,128)(2,1)S(1)}, bf16[768,48]{0,1:T(8,128)(2,1)}, u32[]{:S(2)}) copy-start(bf16[768,48]{0,1:T(8,128)(2,1)} %param.64) | copy-start | bytes 221188
  369.6 3.8 copy-start.91
  369.6 3.9 copy-start.99
  369.6 20.6 %all-to-all-start.3 = ((bf16[16,768,48]{1,2,0:T(8,128)(2,1)}), bf16[16,768,48]{1,2,0:T(8,128)(2,1)S(1)}, u32[]{:S(2)}, u32[]{:S(2)}) async-start(bf16[16,768,48]{1,2,0:T(8,128)(2,1)} %broadcast_in_dim.299), calls=%async_computation.3 | async-start | bytes 2359296 | tf_op jit(solution)/shard_map/all_to_all | solution.py:24
  448.0 3.9 copy-start.115
  454.6 2.8 copy-start.129
  464.9 5.3 copy-start.56
  464.9 55.9 %all-to-all-start.5 = ((f32[4,384,768]{2,1,0:T(8,128)}), f32[4,384,768]{2,1,0:T(8,128)}, u32[]{:S(2)}, u32[]{:S(2)}) async-start(f32[4,384,768]{2,1,0:T(8,128)} %broadcast_in_dim.303), calls=%async_computation.5 | async-start | bytes 9437184 | tf_op jit(solution)/shard_map/all_to_all | solution.py:24
  470.0 217.9 %all-gather.7.cloned.1.call-start = ((), (), s32[]{:S(2)}) async-start(), calls=%async_computation.10 | async-start | bytes 5013504 | tf_op jit(solution)/shard_map/all_gather | solution.py:33
  477.0 47.5 %copy-start.121 = (f32[768]{0:T(1024)S(1)}, f32[768]{0:T(1024)}, u32[]{:S(2)}) copy-start(f32[768]{0:T(1024)} %param.67) | copy-start | bytes 9220
  528.5 3.1 copy-start.103
  559.3 24.2 %copy-start.75 = (s32[1,128]{1,0:T(1,128)S(1)}, s32[1,128]{1,0:T(1,128)}, u32[]{:S(2)}) copy-start(s32[1,128]{1,0:T(1,128)} %copy-done.74) | copy-start | bytes 1540
  559.3 24.2 %copy-start.83 = (f32[3,128]{1,0:T(4,128)S(1)}, f32[3,128]{1,0:T(4,128)}, u32[]{:S(2)}) copy-start(f32[3,128]{1,0:T(4,128)} %copy-done.82) | copy-start | bytes 4612
  559.3 24.2 %copy-start.88 = (f32[3,128]{1,0:T(4,128)S(1)}, f32[3,128]{1,0:T(4,128)}, u32[]{:S(2)}) copy-start(f32[3,128]{1,0:T(4,128)} %custom-call.11) | copy-start | bytes 4612
  583.5 13.2 %copy-start.4 = (bf16[2048,192]{0,1:T(8,128)(2,1)S(1)}, bf16[2048,192]{0,1:T(8,128)(2,1)}, u32[]{:S(2)}) copy-start(bf16[2048,192]{0,1:T(8,128)(2,1)} %copy-done.3) | copy-start | bytes 2359300
  583.5 13.2 %copy-start.9 = (bf16[2048,192]{0,1:T(8,128)(2,1)S(1)}, bf16[2048,192]{0,1:T(8,128)(2,1)}, u32[]{:S(2)}) copy-start(bf16[2048,192]{0,1:T(8,128)(2,1)} %copy-done.8) | copy-start | bytes 2359300
  583.5 13.2 %copy-start.26 = (bf16[128,192]{0,1:T(8,128)(2,1)S(1)}, bf16[128,192]{0,1:T(8,128)(2,1)}, u32[]{:S(2)}) copy-start(bf16[128,192]{0,1:T(8,128)(2,1)} %get-tuple-element.2752) | copy-start | bytes 147460
  583.5 13.2 %copy-start.80 = (f32[3,128]{1,0:T(4,128)S(1)}, f32[3,128]{1,0:T(4,128)}, u32[]{:S(2)}) copy-start(f32[3,128]{1,0:T(4,128)} %copy-done.79) | copy-start | bytes 4612
  583.5 13.2 %copy-start.85 = (f32[3,128]{1,0:T(4,128)S(1)}, f32[3,128]{1,0:T(4,128)}, u32[]{:S(2)}) copy-start(f32[3,128]{1,0:T(4,128)} %custom-call.9) | copy-start | bytes 4612
  583.6 2.9 copy-start.28
  586.8 2.9 copy-start.28
  590.1 2.9 copy-start.28
  593.4 2.9 copy-start.28
  596.7 12.0 %copy-start.63 = (bf16[384,192]{1,0:T(8,128)(2,1)S(1)}, bf16[384,192]{1,0:T(8,128)(2,1)}, u32[]{:S(2)}) copy-start(bf16[384,192]{1,0:T(8,128)(2,1)} %copy.379) | copy-start | bytes 442372
  596.7 12.3 %copy-start.66 = (bf16[73728]{0:T(1024)(128)(2,1)S(1)}, bf16[73728]{0:T(1024)(128)(2,1)}, u32[]{:S(2)}) copy-start(bf16[73728]{0:T(1024)(128)(2,1)} %get-tuple-element.2717) | copy-start | bytes 442372
  609.1 2.5 copy-start.43
  609.8 224.3 %reduce-scatter.5.cloned.1.call-start = ((), (), s32[]{:S(2)}) async-start(), calls=%async_computation.11 | async-start | bytes 1622016
  614.9 2.6 copy-start.87
  614.9 2.6 copy-start.107
  614.9 2.6 copy-start.90
  614.9 30.0 %copy-start.76 = (s32[1,128]{1,0:T(1,128)S(1)}, s32[1,128]{1,0:T(1,128)}, u32[]{:S(2)}) copy-start(s32[1,128]{1,0:T(1,128)} %copy-done.74) | copy-start | bytes 1540
  614.9 30.0 %copy-start.84 = (f32[3,128]{1,0:T(4,128)S(1)}, f32[3,128]{1,0:T(4,128)}, u32[]{:S(2)}) copy-start(f32[3,128]{1,0:T(4,128)} %copy-done.82) | copy-start | bytes 4612
  644.9 19.9 %copy-start.81 = (f32[3,128]{1,0:T(4,128)S(1)}, f32[3,128]{1,0:T(4,128)}, u32[]{:S(2)}) copy-start(f32[3,128]{1,0:T(4,128)} %copy-done.79) | copy-start | bytes 4612
  764.8 5.0 copy-start.48
  770.6 5.0 copy-start.48
  776.4 5.0 copy-start.48
  782.3 5.0 copy-start.48
  795.7 4.7 copy-start.94
  795.7 4.9 copy-start.13
  795.7 4.9 copy-start.42
  795.7 4.9 copy-start.93
  795.7 4.9 copy-start.100
  795.7 4.9 copy-start.104
  795.7 26.7 %all-to-all-start.6 = ((bf16[4,384,768]{2,1,0:T(8,128)(2,1)}), bf16[4,384,768]{2,1,0:T(8,128)(2,1)}, u32[]{:S(2)}, u32[]{:S(2)}) async-start(bf16[4,384,768]{2,1,0:T(8,128)(2,1)} %broadcast_in_dim.310), calls=%async_computation.6 | async-start | bytes 4718592 | tf_op jit(solution)/shard_map/all_to_all | solution.py:24
  800.3 119.4 %all-reduce.4.cloned.1.call-start = ((), (), s32[]{:S(2)}) async-start(), calls=%async_computation.12 | async-start | bytes 4128768
  806.5 18.0 %copy-start.19 = (f32[3,128,768]{2,1,0:T(8,128)S(1)}, f32[3,128,768]{2,1,0:T(8,128)}, u32[]{:S(2)}) copy-start(f32[3,128,768]{2,1,0:T(8,128)} %get-tuple-element.2649) | copy-start | bytes 3538948
  806.5 18.0 %copy-start.105 = (f32[3,128]{1,0:T(4,128)S(1)}, f32[3,128]{1,0:T(4,128)}, u32[]{:S(2)}) copy-start(f32[3,128]{1,0:T(4,128)} %get-tuple-element.2771) | copy-start | bytes 4612
  826.0 6.8 copy-start.127
  827.3 97.6 %all-to-all-start.7 = ((f32[32,1,5952]{2,1,0:T(1,128)}), f32[32,1,5952]{2,1,0:T(1,128)S(1)}, u32[]{:S(2)}, u32[]{:S(2)}) async-start(f32[32,1,5952]{2,1,0:T(1,128)} %broadcast_in_dim.311), calls=%async_computation.7 | async-start | bytes 1540096 | tf_op jit(solution)/shard_map/all_to_all | solution.py:24
  919.7 6.9 copy-start.1
  (85 other events, 121.2 us)
Sparse Core Ops, SparseCore 0:
  86.7 56.3 all-gather.4
  610.0 54.1 all-gather.6
  684.9 75.4 reduce-scatter.4
  806.7 113.0 all-reduce.3
where the time goes:
time: 945 us; the launch traced here: 934 us
  local copies, waits for them, and re-layouts  287 us (30%)
  waiting for transfers between devices  216 us (23%)
  blocking collectives  141 us (15%)
  matrix products  104 us (11%)
  other arithmetic  94.9 us (10%)
  loops' own time  42.3 us (4%)
  starting transfers between devices  31.7 us (3%)
  between operations  16.8 us (2%)
    all_to_all x2, blocking collectives, copy_for_each(): lax.all_to_all(jnp.broadcast_to(x[None], (peers, *x.shape)), axis, 0, 0,...  114 us
    all_to_all x6, waiting for transfers between devices, copy_for_each(): lax.all_to_all(jnp.broadcast_to(x[None], (peers, *x.shape)), axis, 0, 0,...  83.1 us
    unnamed x6, waiting for transfers between devices  82.4 us
    all_gather x2, waiting for transfers between devices, gather_together(): lines, at, done = (lax.all_gather(vector, axis), 0, [])  50.2 us
    unnamed x290, local copies, waits for them, and re-layouts  45.2 us
    dynamic_slice x60, local copies, waits for them, and re-layouts, attend_row(): lax.scan(statistic, (start_max, jnp.zeros_like(start_max)), jnp.arange(bl...  42.9 us
    all_to_all x6, starting transfers between devices, copy_for_each(): lax.all_to_all(jnp.broadcast_to(x[None], (peers, *x.shape)), axis, 0, 0,...  31.6 us
    reshape x2, local copies, waits for them, and re-layouts, pair_swap(): jnp.stack([-paired[..., 1], paired[..., 0]], axis=-1).reshape(tensor.shape)  29.1 us
  transfers between devices with their start and end apart: 10, of which 6 were waited for; matrix products, arithmetic and copies ran while one was open for 26% of the time, Pallas kernels for 0%

commit v1 on v0

v1 whole, which is shorter than its diff:
```python
import functools
import math

import jax
import jax.numpy as jnp
import numpy as np
from jax import lax
from jax.experimental import pallas as pl
from jax.experimental.pallas import tpu as pltpu
from jax.sharding import PartitionSpec as P

D = 768
HD = 64
R = 3
T = 128
NH = 3
E = NH * HD
F = 768
NW = 16
NN = 4
TOK = R * T
L = NW * T
C = T // NN
CH = R * C
PAIRS = R * NH
G = D // (2 * NW)
SLOT = 3 * HD + 16
AUG = HD + 16
NWG = 1792
EPSILON = 1e-12
BIG = 1e30
LOG2E = math.log2(math.e)
LN2 = math.log(2.0)
f32, bf16 = jnp.float32, jnp.bfloat16


def dot(a, b, dims):
    return lax.dot_general(a, b, (dims, ((), ())), preferred_element_type=f32)


NORMAL, BOTH_LAST, BOTH_FIRST = ((1,), (0,)), ((1,), (1,)), ((0,), (0,))


def call(name, kernel, outs, args, scratch=(), flops=0, any_space=()):
    return pl.pallas_call(
        kernel,
        out_shape=[jax.ShapeDtypeStruct(s, t) for s, t in outs],
        in_specs=[pl.BlockSpec(memory_space=pltpu.VMEM) for _ in args],
        out_specs=[pl.BlockSpec(memory_space=pltpu.VMEM) for _ in outs],
        scratch_shapes=list(scratch),
        compiler_params=pltpu.CompilerParams(vmem_limit_bytes=48 * 1024 * 1024),
        cost_estimate=pl.CostEstimate(flops=flops, bytes_accessed=4 * 1024 * 1024, transcendentals=0),
        name=name,
    )(*args)


def row_of(ref):
    return ref[...].reshape(1, ref.shape[-1])


def split3(v):
    hi = v.astype(bf16).astype(f32)
    rest = v - hi
    mid = rest.astype(bf16).astype(f32)
    return hi, mid, rest - mid


def sine_cosine(angle):
    turns = jnp.floor(angle * (2.0 / math.pi) + 0.5)
    r = ((angle - turns * 1.5703125) - turns * 4.837512969970703125e-4) - turns * 7.54978995489188e-8
    z = r * r
    sine = r + r * z * (-1.6666654611e-1 + z * (8.3321608736e-3 + z * -1.9515295891e-4))
    cosine = 1.0 - 0.5 * z + z * z * (4.166664568298827e-2 + z * (-1.388731625493765e-3 + z * 2.443315711809948e-5))
    quarter = turns - 4.0 * jnp.floor(turns * 0.25)
    odd = (quarter == 1.0) | (quarter == 3.0)
    sin_abs = jnp.where(odd, cosine, sine)
    cos_abs = jnp.where(odd, sine, cosine)
    return jnp.where(quarter >= 2.0, -sin_abs, sin_abs), jnp.where((quarter == 1.0) | (quarter == 2.0), -cos_abs, cos_abs)


def swap_pairs(t):
    rows = lax.broadcasted_iota(jnp.int32, t.shape, 0)
    return jnp.where(rows % 2 == 0, pltpu.roll(t, HD - 1, 0), pltpu.roll(t, 1, 0))


def project_kernel(x, seg, wq, bq, wk, bk, wv, bv, slots):
    flat = x[...].reshape(TOK, D)
    for j, (w, b) in enumerate(((wq, bq), (wk, bk), (wv, bv))):
        y = dot(flat, w[...], NORMAL) + row_of(b)
        yt = y.T.astype(bf16)
        for r in range(R):
            for h in range(NH):
                slots[r * NH + h, j * HD : (j + 1) * HD, :] = yt[h * HD : (h + 1) * HD, r * T : (r + 1) * T]
    for r in range(R):
        ids = jnp.broadcast_to(seg[r : r + 1, :].astype(f32), (16, T)).astype(bf16)
        for h in range(NH):
            slots[r * NH + h, 3 * HD :, :] = ids


def attend_kernel(got, freq, out, q_t, k_t, v_t, o_t, cos_t, sin_t, k_nat):
    @pl.when(lax.axis_index("wide") < PAIRS)
    def _():
        ids = [got[w, 3 * HD :, :].astype(f32)[0:1, :] for w in range(NW)]
        starts = []
        for d in range(1, 5):
            below = jnp.zeros((1, T), f32)
            for w in range(NW):
                below = below + jnp.where(ids[w] < d, 1.0, 0.0)
            starts.append(jnp.sum(below, axis=1, keepdims=True))
        odd = lax.broadcasted_iota(jnp.int32, (HD, T), 0) % 2 == 1
        ext = lax.broadcasted_iota(jnp.int32, (16, T), 0)
        lane = lax.broadcasted_iota(jnp.int32, (1, T), 1).astype(f32)
        for w in range(NW):
            at = slice(w * T, (w + 1) * T)
            start = jnp.zeros((1, T), f32)
            for d in range(1, 5):
                start = jnp.where(ids[w] == d, starts[d - 1], start)
            sine, cosine = sine_cosine(freq[...] * (lane + (w * T) - start))
            sine = jnp.where(odd, sine, -sine)
            cos_t[:, at] = cosine
            sin_t[:, at] = sine
            query = got[w, 0:HD, :].astype(f32)
            key = got[w, HD : 2 * HD, :].astype(f32)
            query = (query * cosine + swap_pairs(query) * sine) * (HD**-0.5 * LOG2E)
            key = key * cosine + swap_pairs(key) * sine
            same = ids[w] == ext.astype(f32)
            doc = ext < 5
            key_ext = jnp.where(doc, jnp.where(same, 1.0, 0.0), jnp.where(ext < 8, 1.0, 0.0))
            q_t[0:HD, at] = query.astype(bf16)
            q_t[HD:AUG, at] = jnp.where(doc, jnp.where(same, 0.0, -BIG), 0.0).astype(bf16)
            k_t[0:HD, at] = key.astype(bf16)
            k_t[HD:AUG, at] = key_ext.astype(bf16)
            k_nat[at, :] = jnp.concatenate([key, key_ext], axis=0).T.astype(bf16)
            v_t[0:HD, at] = got[w, 2 * HD : 3 * HD, :]
            v_t[HD:AUG, at] = jnp.where(ext < 3, 1.0, 0.0).astype(bf16)

        def tile(i, carry):
            at = pl.ds(pl.multiple_of(i * 256, 256), 256)
            s = dot(k_nat[...], q_t[:, at], NORMAL)
            top = jnp.max(s, axis=0, keepdims=True)
            p = jnp.exp2(s - top).astype(bf16)
            o = dot(v_t[...], p, NORMAL)
            total = o[HD : HD + 1, :]
            o = o[0:HD, :] / total
            o_t[:, at] = o
            low = o.astype(bf16)
            out[2 * i] = low[:, 0:T]
            out[2 * i + 1] = low[:, T:]
            hi, mid, lo = split3(-(top + jnp.log(total) * LOG2E))
            rows = lax.broadcasted_iota(jnp.int32, (16, 256), 0)
            more = jnp.where(rows == 5, hi, jnp.where(rows == 6, mid, jnp.where(rows == 7, lo, 0.0)))
            q_t[HD:AUG, at] = (q_t[HD:AUG, at].astype(f32) + more).astype(bf16)
            return carry

        lax.fori_loop(0, L // 256, tile, 0)


def attend_back_kernel(got, q_t, k_t, v_t, o_t, cos_t, sin_t, out, do_t, do_nat, q_nat, k_nat, v_nat, dq_t):
    @pl.when(lax.axis_index("wide") < PAIRS)
    def _():
        ext = lax.broadcasted_iota(jnp.int32, (16, T), 0)
        for w in range(NW):
            at = slice(w * T, (w + 1) * T)
            low = got[w]
            grad = low.astype(f32)
            delta = -jnp.sum(grad * o_t[:, at], axis=0, keepdims=True)
            hi, mid, lo = split3(delta)
            do_t[0:HD, at] = low
            do_t[HD:AUG, at] = jnp.where(
                ext == 0, hi, jnp.where(ext == 1, mid, jnp.where(ext == 2, lo, 0.0))
            ).astype(bf16)
            do_nat[at, :] = grad.T.astype(bf16)
            q_nat[at, :] = q_t[0:HD, at].astype(f32).T.astype(bf16)
            k_nat[at, :] = k_t[:, at].astype(f32).T.astype(bf16)
            v_nat[at, :] = v_t[:, at].astype(f32).T.astype(bf16)
        dq_t[...] = jnp.zeros((HD, L), f32)

        def folded(t):
            total = t[:, 0:T]
            for k in range(1, t.shape[1] // T):
                total = total + t[:, k * T : (k + 1) * T]
            return total

        def tile(j, carry):
            sum_key, sum_value = carry
            at = pl.ds(pl.multiple_of(j * 256, 256), 256)
            p = jnp.exp2(dot(k_nat[at, :], q_t[...], NORMAL))
            dp = dot(v_nat[at, :], do_t[...], NORMAL)
            ds = (p * dp).astype(bf16)
            dv = dot(p.astype(bf16), do_nat[...], NORMAL).T.astype(bf16)
            dk = dot(ds, q_nat[...], NORMAL).T * LN2
            dk = (dk * cos_t[:, at] - swap_pairs(dk) * sin_t[:, at]).astype(bf16)
            dq_t[...] += dot(k_t[0:HD, at], ds, NORMAL)
            for k in range(2):
                out[2 * j + k, HD : 2 * HD, :] = dk[:, k * T : (k + 1) * T]
                out[2 * j + k, 2 * HD : 3 * HD, :] = dv[:, k * T : (k + 1) * T]
            return sum_key + folded(dk.astype(f32)), sum_value + folded(dv.astype(f32))

        zero = jnp.zeros((HD, T), f32)
        sum_key, sum_value = lax.fori_loop(0, L // 256, tile, (zero, zero))
        sum_query = zero
        for w in range(NW):
            at = slice(w * T, (w + 1) * T)
            dq = dq_t[:, at] * (HD**-0.5)
            dq = (dq * cos_t[:, at] - swap_pairs(dq) * sin_t[:, at]).astype(bf16)
            out[w, 0:HD, :] = dq
            sum_query = sum_query + dq.astype(f32)
        rows = [jnp.sum(t.T, axis=0, keepdims=True) for t in (sum_query, sum_key, sum_value)]
        first = jnp.concatenate([rows[0], rows[1]], axis=1)
        second = jnp.concatenate([rows[2], rows[2]], axis=1)
        first_hi, second_hi = first.astype(bf16).astype(f32), second.astype(bf16).astype(f32)
        block = jnp.where(
            ext == 0,
            first_hi,
            jnp.where(ext == 1, second_hi, jnp.where(ext == 2, first - first_hi, second - second_hi)),
        )
        block = jnp.where(ext < 4, block, 0.0).astype(bf16)
        for w in range(NW):
            out[w, 3 * HD :, :] = block


def chunk_rows(c, r):
    return pl.ds(pl.multiple_of(r * T + c * C, C), C)


def forward_kernel(
    o0, o1, o2, o3, w0, w1, w2, w3, x, b_out, g_one, s_one, up_down, b_up,
    normed_low, hidden_low, slope, xhat_own, rstd_own, part0, part1, part2, part3,
    resid, xhat, rstd, wide_part,
):
    n = lax.axis_index("narrow")
    for r in range(R):
        at = slice(r * T, (r + 1) * T)
        heads = jnp.concatenate([o[r * NH : (r + 1) * NH].reshape(E, T) for o in (o0, o1, o2, o3)], axis=0)
        weight = jnp.concatenate([w[...] for w in (w0, w1, w2, w3)], axis=0)
        resid[at, :] = x[r].astype(f32) + (dot(heads, weight, BOTH_FIRST) + row_of(b_out))
    residual = resid[...]
    center = residual - jnp.mean(residual, axis=-1, keepdims=True)
    inverse = lax.rsqrt(jnp.mean(center * center, axis=-1, keepdims=True) + EPSILON)
    unit = center * inverse
    xhat[...] = unit
    rstd[...] = jnp.broadcast_to(inverse, (TOK, T))
    low = (unit * row_of(g_one) + row_of(s_one)).astype(bf16)
    normed_low[...] = low
    up = up_down[:, 0 : D // NW, :].reshape(D, F)
    down = up_down[:, D // NW :, :].reshape(D, F)
    pre = dot(low, up, NORMAL) + row_of(b_up)
    half = 0.5 * (1.0 + lax.erf(pre * (2.0**-0.5)))
    slope[...] = half + pre * jnp.exp(-0.5 * pre * pre) * (1.0 / math.sqrt(2.0 * math.pi))
    hidden = (pre * half).astype(bf16)
    hidden_low[...] = hidden
    wide_part[...] = dot(hidden, down, BOTH_LAST)
    for r in range(R):
        to = slice(r * C, (r + 1) * C)
        xhat_own[to, :] = xhat[chunk_rows(n, r), :]
        rstd_own[to, :] = rstd[chunk_rows(n, r), :]
        part0[to, :] = wide_part[chunk_rows(n, r), :]
        for s, part in ((1, part1), (2, part2), (3, part3)):
            part[to, :] = wide_part[chunk_rows((n + s) % NN, r), :].astype(bf16)


def norm_two_kernel(
    part0, part1, part2, part3, xhat_own, cot, g_one, s_one, b_down, g_two, s_two,
    layer_low, grad_ffn, grad_two, sums,
):
    n = lax.axis_index("narrow")
    total = part0[...] + part1[...].astype(f32) + part2[...].astype(f32) + part3[...].astype(f32)
    normed = xhat_own[...] * row_of(g_one) + row_of(s_one)
    residual = normed + (total + row_of(b_down))
    center = residual - jnp.mean(residual, axis=-1, keepdims=True)
    inverse = lax.rsqrt(jnp.mean(center * center, axis=-1, keepdims=True) + EPSILON)
    unit = center * inverse
    layer_low[...] = (unit * row_of(g_two) + row_of(s_two)).astype(bf16)
    ct = jnp.concatenate([cot[r, pl.ds(pl.multiple_of(n * C, C), C), :] for r in range(R)], axis=0).astype(f32)
    scaled = ct * row_of(g_two)
    grad = inverse * (
        scaled
        - jnp.mean(scaled, axis=-1, keepdims=True)
        - unit * jnp.mean(scaled * unit, axis=-1, keepdims=True)
    )
    grad_two[...] = grad
    low = grad.astype(bf16)
    grad_ffn[...] = low
    sums[...] = jnp.concatenate(
        [
            jnp.sum(ct * unit, axis=0, keepdims=True),
            jnp.sum(ct, axis=0, keepdims=True),
            jnp.sum(low.astype(f32), axis=0, keepdims=True),
            jnp.zeros((5, D), f32),
        ],
        axis=0,
    )


def assemble(n, parts, whole):
    for s, part in enumerate(parts):
        c = (n + NN - s) % NN
        for r in range(R):
            whole[chunk_rows(c, r), :] = part[r * C : (r + 1) * C, :].astype(whole.dtype)


def ffn_back_kernel(g0, g1, g2, g3, up_down, slope, grad_all, grad_pre, part0, part1, part2, part3, wide_part):
    n = lax.axis_index("narrow")
    assemble(n, (g0, g1, g2, g3), grad_all)
    up = up_down[:, 0 : D // NW, :].reshape(D, F)
    down = up_down[:, D // NW :, :].reshape(D, F)
    low = (slope[...] * dot(grad_all[...], down, NORMAL)).astype(bf16)
    grad_pre[...] = low
    wide_part[...] = dot(low, up, BOTH_LAST)
    for r in range(R):
        to = slice(r * C, (r + 1) * C)
        part0[to, :] = wide_part[chunk_rows(n, r), :]
        for s, part in ((1, part1), (2, part2), (3, part3)):
            part[to, :] = wide_part[chunk_rows((n + s) % NN, r), :].astype(bf16)


def norm_one_back_kernel(
    part0, part1, part2, part3, grad_two, xhat_own, rstd_own, g_one, sums_two, grad_one, grad_low, sums
):
    total = part0[...] + part1[...].astype(f32) + part2[...].astype(f32) + part3[...].astype(f32)
    grad = grad_two[...] + total
    unit = xhat_own[...]
    scaled = grad * row_of(g_one)
    one = rstd_own[:, 0:1] * (
        scaled
        - jnp.mean(scaled, axis=-1, keepdims=True)
        - unit * jnp.mean(scaled * unit, axis=-1, keepdims=True)
    )
    grad_one[...] = one
    low = one.astype(bf16)
    grad_low[...] = low
    sums[...] = jnp.concatenate(
        [
            sums_two[0:3, :],
            jnp.sum(grad * unit, axis=0, keepdims=True),
            jnp.sum(grad, axis=0, keepdims=True),
            jnp.sum(low.astype(f32), axis=0, keepdims=True),
            jnp.zeros((2, D), f32),
        ],
        axis=0,
    )


def grad_attn_kernel(g0, g1, g2, g3, w_out, grad_all, slots):
    n = lax.axis_index("narrow")
    assemble(n, (g0, g1, g2, g3), grad_all)
    grad = dot(w_out[...], grad_all[...], BOTH_LAST).astype(bf16)
    for r in range(R):
        for h in range(NH):
            slots[r * NH + h] = grad[h * HD : (h + 1) * HD, r * T : (r + 1) * T]


def weights_kernel(
    normed_low, grad_pre, grad_ffn, hidden_low, grad_out, attn, v0, v1, v2, v3, send, keep, sums, whole, vectors
):
    n, c = lax.axis_index("narrow"), lax.axis_index("dp")
    whole[:, 0:F] = dot(normed_low[...], grad_pre[...], BOTH_FIRST)
    whole[:, F : 2 * F] = dot(grad_ffn[...], hidden_low[...], BOTH_FIRST)
    heads = jnp.concatenate([attn[r * NH : (r + 1) * NH].reshape(E, T) for r in range(R)], axis=1)
    whole[:, 2 * F : 2 * F + E] = dot(grad_out[...], heads, ((0,), (1,)))
    half = D // 2
    send[:, 0 : 2 * F + E] = whole[pl.ds(pl.multiple_of((1 - c) * half, half), half), :].astype(bf16)
    keep[:, 0 : 2 * F + E] = whole[pl.ds(pl.multiple_of(c * half, half), half), :]
    for s, v in enumerate((v0, v1, v2, v3)):
        vectors[(n + NN - s) % NN] = v[...]
    total = vectors[0] + vectors[1] + vectors[2] + vectors[3]
    bias = jnp.sum(grad_pre[...].astype(f32), axis=0, keepdims=True)
    row = lax.broadcasted_iota(jnp.int32, (8, D), 0)
    sums[...] = jnp.where(row == 6, bias, total)


def weights_add_kernel(keep, got, sums, sums_got, slots):
    both = (keep[...] + got[...].astype(f32)).astype(bf16)
    total = sums[...] + sums_got[...]
    vec = jnp.concatenate([total[:, 256 * k : 256 * (k + 1)] for k in range(3)], axis=0).astype(bf16)
    for w in range(NW):
        slots[w, :, 0:NWG] = both[w * G : (w + 1) * G, :]
        slots[w, :, NWG:] = vec


def weights_sum_kernel(got, up, down, out, g_two, s_two, b_down, g_one, s_one, b_out, b_up):
    total = got[0].astype(f32)
    for w in range(1, NW):
        total = total + got[w].astype(f32)
    up[...] = total[:, 0:F]
    down[...] = total[:, F : 2 * F].T
    out[...] = total[:, 2 * F : 2 * F + E].T
    vec = jnp.concatenate([total[8 * k : 8 * (k + 1), NWG:] for k in range(3)], axis=1)
    for k, ref in enumerate((g_two, s_two, b_down, g_one, s_one, b_out, b_up)):
        ref[...] = vec[k : k + 1, :].reshape(D)


def input_back_kernel(got, x, wq, wk, wv, part0, part1, part2, part3, send, keep, sums, whole, wide_part):
    n, c = lax.axis_index("narrow"), lax.axis_index("dp")
    flat = x[...].reshape(TOK, D)
    total = None
    for j, w in enumerate((wq, wk, wv)):
        grad_t = jnp.concatenate(
            [
                jnp.concatenate([got[r * NH + h, j * HD : (j + 1) * HD, :] for h in range(NH)], axis=0)
                for r in range(R)
            ],
            axis=1,
        )
        grad = grad_t.astype(f32).T.astype(bf16)
        term = dot(grad, w[...], BOTH_LAST)
        total = term if total is None else total + term
        whole[:, j * E : (j + 1) * E] = dot(flat, grad, BOTH_FIRST)
    wide_part[...] = total
    for r in range(R):
        to = slice(r * C, (r + 1) * C)
        part0[to, :] = wide_part[chunk_rows(n, r), :]
        for s, part in ((1, part1), (2, part2), (3, part3)):
            part[to, :] = wide_part[chunk_rows((n + s) % NN, r), :].astype(bf16)
    half = D // 2
    send[...] = whole[pl.ds(pl.multiple_of((1 - c) * half, half), half), :].astype(bf16)
    keep[...] = whole[pl.ds(pl.multiple_of(c * half, half), half), :]
    heads = []
    for h in range(NH):
        block = got[h, 3 * HD :, :].astype(f32)
        for r in range(1, R):
            block = block + got[r * NH + h, 3 * HD :, :].astype(f32)
        heads.append(block)
    first = jnp.concatenate([b[0:1, 0:HD] + b[2:3, 0:HD] for b in heads], axis=1)
    second = jnp.concatenate([b[0:1, HD:] + b[2:3, HD:] for b in heads], axis=1)
    third = jnp.concatenate([b[1:2, 0:HD] + b[3:4, 0:HD] for b in heads], axis=1)
    sums[...] = jnp.concatenate([first, second, third, jnp.zeros((5, E), f32)], axis=0)


def input_add_kernel(keep, got, sums, sums_got, slots, b_q, b_k, b_v):
    both = (keep[...] + got[...].astype(f32)).astype(bf16)
    for w in range(NW):
        slots[w] = both[w * G : (w + 1) * G, :]
    total = sums[...] + sums_got[...]
    for k, ref in enumerate((b_q, b_k, b_v)):
        ref[...] = total[k : k + 1, :].reshape(E)


def input_sum_kernel(got, g_q, g_k, g_v):
    total = got[0].astype(f32)
    for w in range(1, NW):
        total = total + got[w].astype(f32)
    for k, ref in enumerate((g_q, g_k, g_v)):
        ref[...] = total[:, k * E : (k + 1) * E]


def input_chunk_kernel(part0, part1, part2, part3, grad_one, low):
    total = part0[...] + part1[...].astype(f32) + part2[...].astype(f32) + part3[...].astype(f32)
    low[...] = (grad_one[...] + total).astype(bf16)


def spread_kernel(g0, g1, g2, g3, out):
    n = lax.axis_index("narrow")
    for s, part in enumerate((g0, g1, g2, g3)):
        at = pl.ds(pl.multiple_of((n + NN - s) % NN * C, C), C)
        for r in range(R):
            out[r, at, :] = part[r * C : (r + 1) * C, :].astype(f32)


def shifted(x, s):
    return lax.ppermute(x, "narrow", [(i, (i + s) % NN) for i in range(NN)])


def gather_narrow(x):
    return (x, shifted(x, 1), shifted(x, 2), shifted(x, 3))


def scatter_narrow(parts):
    return (parts[0], shifted(parts[1], 1), shifted(parts[2], 2), shifted(parts[3], 3))


def other_core(x):
    return lax.ppermute(x, "dp", [(0, 1), (1, 0)])


def exchange(slots):
    return lax.all_to_all(slots, "wide", 0, 0, tiled=True)


def body(
    hidden_in, segments, weight_query, bias_query, weight_key, bias_key, weight_value, bias_value,
    weight_out, bias_out, gain_one, shift_one, weight_up, bias_up, weight_down, bias_down,
    gain_two, shift_two, cotangent,
):
    frequency = np.repeat(np.power(10000.0, -np.arange(0, HD, 2) / HD), 2).astype(np.float32)
    frequency = jnp.asarray(np.broadcast_to(frequency[:, None], (HD, T)))
    up_down = jnp.concatenate([weight_up, weight_down.T], axis=0)
    up_down = lax.all_gather(up_down, "wide", axis=0, tiled=False)
    weights_out = gather_narrow(weight_out)

    (slots,) = call(
        "project",
        project_kernel,
        [((NW, SLOT, T), bf16)],
        (hidden_in, segments, weight_query, bias_query, weight_key, bias_key, weight_value, bias_value),
        flops=2 * TOK * D * 3 * E,
    )
    got = exchange(slots)
    out_slots, q_t, k_t, v_t, o_t, cos_t, sin_t = call(
        "attend",
        attend_kernel,
        [
            ((NW, HD, T), bf16),
            ((AUG, L), bf16),
            ((AUG, L), bf16),
            ((AUG, L), bf16),
            ((HD, L), f32),
            ((HD, L), f32),
            ((HD, L), f32),
        ],
        (got, frequency),
        scratch=[pltpu.VMEM((L, AUG), bf16)],
        flops=16 * L * L * HD,
    )
    attn = exchange(out_slots)[0:PAIRS]
    heads = gather_narrow(attn)
    chunk_f32, chunk_low = ((CH, D), f32), ((CH, D), bf16)
    tok_low = ((TOK, D), bf16)
    parts4 = [chunk_f32, chunk_low, chunk_low, chunk_low]
    normed_low, hidden_low, slope, xhat_own, rstd_own, *parts = call(
        "forward",
        forward_kernel,
        [tok_low, tok_low, ((TOK, F), f32), chunk_f32, ((CH, T), f32), *parts4],
        (*heads, *weights_out, hidden_in, bias_out, gain_one, shift_one, up_down, bias_up),
        scratch=[
            pltpu.VMEM((TOK, D), f32),
            pltpu.VMEM((TOK, D), f32),
            pltpu.VMEM((TOK, T), f32),
            pltpu.VMEM((TOK, D), f32),
        ],
        flops=3 * 2 * TOK * D * F,
    )
    parts = scatter_narrow(parts)
    layer_low, grad_ffn, grad_two, sums_two = call(
        "norm_two",
        norm_two_kernel,
        [chunk_low, chunk_low, chunk_f32, ((8, D), f32)],
        (*parts, xhat_own, cotangent, gain_one, shift_one, bias_down, gain_two, shift_two),
    )
    grads = gather_narrow(grad_ffn)
    grad_ffn_all, grad_pre, *parts = call(
        "ffn_back",
        ffn_back_kernel,
        [tok_low, ((TOK, F), bf16), *parts4],
        (*grads, up_down, slope),
        scratch=[pltpu.VMEM((TOK, D), f32)],
        flops=2 * 2 * TOK * D * F,
    )
    parts = scatter_narrow(parts)
    grad_one, grad_low, sums_one = call(
        "norm_one_back",
        norm_one_back_kernel,
        [chunk_f32, chunk_low, ((8, D), f32)],
        (*parts, grad_two, xhat_own, rstd_own, gain_one, sums_two),
    )
    grads = gather_narrow(grad_low)
    grad_out_all, slots = call(
        "grad_attn",
        grad_attn_kernel,
        [tok_low, ((NW, HD, T), bf16)],
        (*grads, weight_out),
        flops=2 * TOK * D * E,
    )
    got = exchange(slots)
    (slots,) = call(
        "attend_back",
        attend_back_kernel,
        [((NW, SLOT, T), bf16)],
        (got, q_t, k_t, v_t, o_t, cos_t, sin_t),
        scratch=[
            pltpu.VMEM((AUG, L), bf16),
            pltpu.VMEM((L, HD), bf16),
            pltpu.VMEM((L, HD), bf16),
            pltpu.VMEM((L, AUG), bf16),
            pltpu.VMEM((L, AUG), bf16),
            pltpu.VMEM((HD, L), f32),
        ],
        flops=40 * L * L * HD,
    )
    vectors = gather_narrow(sums_one)
    send, keep, sums = call(
        "weights",
        weights_kernel,
        [((D // 2, NWG), bf16), ((D // 2, NWG), f32), ((8, D), f32)],
        (normed_low, grad_pre, grad_ffn_all, hidden_low, grad_out_all, attn, *vectors),
        scratch=[pltpu.VMEM((D, 2 * F + E), f32), pltpu.VMEM((NN, 8, D), f32)],
        flops=2 * TOK * D * (2 * F + E),
    )
    (weight_slots,) = call(
        "weights_add",
        weights_add_kernel,
        [((NW, G, NWG + 256), bf16)],
        (keep, other_core(send), sums, other_core(sums)),
    )
    vec = ((D,), f32)
    grad_up, grad_down, grad_out, g_two, s_two, b_down, g_one, s_one, b_out, b_up = call(
        "weights_sum",
        weights_sum_kernel,
        [((G, F), f32), ((F, G), f32), ((E, G), f32), vec, vec, vec, vec, vec, vec, vec],
        (exchange(weight_slots),),
    )
    whole_out = ((R, T, D), f32)
    (layer_out,) = call("layer_out", spread_kernel, [whole_out], gather_narrow(layer_low))

    got = exchange(slots)
    *parts, send, keep, sums = call(
        "input_back",
        input_back_kernel,
        [*parts4, ((D // 2, 3 * E), bf16), ((D // 2, 3 * E), f32), ((8, E), f32)],
        (got, hidden_in, weight_query, weight_key, weight_value),
        scratch=[pltpu.VMEM((D, 3 * E), f32), pltpu.VMEM((TOK, D), f32)],
        flops=2 * 2 * TOK * D * 3 * E,
    )
    parts = scatter_narrow(parts)
    slots, b_query, b_key, b_value = call(
        "input_add",
        input_add_kernel,
        [((NW, G, 3 * E), bf16), ((E,), f32), ((E,), f32), ((E,), f32)],
        (keep, other_core(send), sums, other_core(sums)),
    )
    (input_low,) = call("input_chunk", input_chunk_kernel, [chunk_low], (*parts, grad_one))
    (grad_input,) = call("grad_input", spread_kernel, [whole_out], gather_narrow(input_low))
    g_query, g_key, g_value = call(
        "input_sum", input_sum_kernel, [((G, E), f32)] * 3, (exchange(slots),)
    )
    return (
        layer_out, grad_input, g_query, b_query, g_key, b_key, g_value, b_value, grad_out, b_out,
        g_one, s_one, grad_up, b_up, grad_down, b_down, g_two, s_two,
    )


def solution(mesh):
    tokens, whole = P("dp", "wide", None), P()
    column, vector = P(None, "narrow"), P("narrow")
    rows_split, columns_split = P(("dp", "wide"), "narrow"), P("narrow", ("dp", "wide"))
    in_specs = (
        tokens, P("dp", "wide"), column, vector, column, vector, column, vector, P("narrow", None), whole,
        whole, whole, P("wide", "narrow"), vector, P("narrow", "wide"), whole, whole, whole, tokens,
    )
    out_specs = (
        tokens, tokens, rows_split, vector, rows_split, vector, rows_split, vector, columns_split, whole,
        whole, whole, rows_split, vector, columns_split, whole, whole, whole,
    )
    return jax.shard_map(body, mesh=mesh, in_specs=in_specs, out_specs=out_specs, check_vma=False)
```

time: 945 us -> 241 us (0.26)
  local copies, waits for them, and re-layouts: 287 us -> 20.2 us
  waiting for transfers between devices: 216 us -> 71.7 us
  blocking collectives: 141 us -> 13.5 us
  matrix products: 104 us -> 0 us
  other arithmetic: 94.9 us -> 1.64 us
  Pallas kernels: 0 us -> 46.8 us
  loops' own time: 42.3 us -> 0 us
  starting transfers between devices: 31.7 us -> 70.5 us
    dot_general x126 -> x0, matrix products: 104 us -> none  [the longest x12 23.5 us: query_block(): jnp.einsum('hqk,khd->qhd', grad_score, key_block, preferred_element_type=...]
    dynamic_slice x192 -> x0, local copies, waits for them, and re-layouts: 103 us -> none  [the longest x60 42.9 us: attend_row(): lax.scan(statistic, (start_max, jnp.zeros_like(start_max)), jnp.arange(bl...]
    all_to_all x2 -> x1, blocking collectives: 114 us -> 13.5 us  [exchange(): return lax.all_to_all(slots, 'wide', 0, 0, tiled=True)]
    unnamed x6 -> x1, waiting for transfers between devices: 82.4 us -> 0.02 us
    all_to_all x6 -> x5, waiting for transfers between devices: 83.1 us -> 25.1 us  [exchange(): return lax.all_to_all(slots, 'wide', 0, 0, tiled=True)]
    reshape x10 -> x0, local copies, waits for them, and re-layouts: 53.1 us -> none  [the longest x2 29.1 us: pair_swap(): jnp.stack([-paired[..., 1], paired[..., 0]], axis=-1).reshape(tensor.shape)]
    all_gather x2 -> x1, waiting for transfers between devices: 50.2 us -> 0.01 us  [body(): up_down = lax.all_gather(up_down, 'wide', axis=0, tiled=False)]
    pallas_call x0 -> x17, Pallas kernels: none -> 46.8 us  [call(): pl.pallas_call(kernel, out_shape=[jax.ShapeDtypeStruct(s, t) for s, t in...]
  transfers between devices with their start and end apart: 10 -> 40, of which waited for: 6 -> 23; matrix products, arithmetic and copies ran while one was open for 26% -> 1% of each run, Pallas kernels for 0% -> 11%
where the time goes in v1:
time: 241 us; the launch traced here: 239 us
  waiting for transfers between devices  71.7 us (30%)
  starting transfers between devices  70.5 us (29%)
  Pallas kernels  46.8 us (19%)
  local copies, waits for them, and re-layouts  20.2 us (8%)
  between operations  14.6 us (6%)
  blocking collectives  13.5 us (6%)
    pallas_call x17, Pallas kernels, call(): pl.pallas_call(kernel, out_shape=[jax.ShapeDtypeStruct(s, t) for s, t in...  46.8 us
    ppermute x30, starting transfers between devices, shifted(): return lax.ppermute(x, 'narrow', [(i, (i + s) % NN) for i in range(NN)])  44.6 us
    ppermute x30, waiting for transfers between devices, shifted(): return lax.ppermute(x, 'narrow', [(i, (i + s) % NN) for i in range(NN)])  44 us
    all_to_all x5, starting transfers between devices, exchange(): return lax.all_to_all(slots, 'wide', 0, 0, tiled=True)  25.2 us
    all_to_all x5, waiting for transfers between devices, exchange(): return lax.all_to_all(slots, 'wide', 0, 0, tiled=True)  25.1 us
    unnamed x101, local copies, waits for them, and re-layouts  20.2 us
    all_to_all x1, blocking collectives, exchange(): return lax.all_to_all(slots, 'wide', 0, 0, tiled=True)  13.5 us
  transfers between devices with their start and end apart: 40, of which 23 were waited for; matrix products, arithmetic and copies ran while one was open for 1% of the time, Pallas kernels for 11%

profile of v1, /device:TPU:0, one launch (start us, length us, event | category | flops | bytes accessed | tf_op | source)
XLA Modules:
  0.0 238.9 jit_solution(9089517466425457314)
XLA Ops:
  7.3 1.6 pad_maximum_fusion
  9.0 1.1 copy.38.wq
  10.1 1.1 copy.39.wk
  11.5 1.6 project.1
  13.1 7.3 %all-to-all-start = ((bf16[16,208,128]{2,1,0:T(8,128)(2,1)}), bf16[16,208,128]{2,1,0:T(8,128)(2,1)S(1)}, u32[]{:S(2)}, u32[]{:S(2)}) async-start(bf16[16,208,128]{2,1,0:T(8,128)(2,1)} %project.1), calls=%async_computation | async-start | bytes 1703936 | tf_op jit(solution)/shard_map/all_to_all | solution.py:477
  20.4 2.0 collective-permute-start.3
  22.4 14.9 %all-to-all-done.got = bf16[16,208,128]{2,1,0:T(8,128)(2,1)S(1)} async-done(((bf16[16,208,128]{2,1,0:T(8,128)(2,1)}), bf16[16,208,128]{2,1,0:T(8,128)(2,1)S(1)}, u32[]{:S(2)}, u32[]{:S(2)}) %all-to-all-start) | async-done | bytes 852000 | tf_op jit(solution)/shard_map/all_to_all | solution.py:477
  37.4 11.8 %attend.1 = (bf16[16,64,128]{2,1,0:T(8,128)(2,1)}, bf16[80,2048]{1,0:T(8,128)(2,1)S(1)}, bf16[80,2048]{1,0:T(8,128)(2,1)S(1)}, bf16[80,2048]{1,0:T(8,128)(2,1)S(...) custom-call(bf16[16,208,128]{2,1,0:T(8,128)(2,1)S(1)} %all-to-all-done.got, ...), custom_call_target="tpu_custom_call" | custom-call | flops 4294967296 | bytes 4194304 | tf_op jit(solution)/shard_map/attend/pallas_call | solution.py:45
  53.8 3.5 %all-to-all-start.1 = ((bf16[16,64,128]{2,1,0:T(8,128)(2,1)}), bf16[16,64,128]{2,1,0:T(8,128)(2,1)S(1)}, u32[]{:S(2)}, u32[]{:S(2)}) async-start(bf16[16,64,128]{2,1,0:T(8,128)(2,1)} %get-tuple-element.76), calls=%async_computation.1 | async-start | bytes 524288 | tf_op jit(solution)/shard_map/all_to_all | solution.py:477
  57.4 3.5 %collective-permute-start.4 = (bf16[192,768]{1,0:T(8,128)(2,1)S(1)}, bf16[192,768]{1,0:T(8,128)(2,1)S(1)}, u32[]{:S(2)}, u32[]{:S(2)}) collective-permute-start(bf16[192,768]{1,0:T(8,128)(2,1)S(1)} %copy-done.4), channel_id=1, source_target_pairs={{0,2},{1,3},{2,0},{3,1},{4,6},{5,7},{6,4},{7,5},{8,10},{9,11},{10,... | collective-permute-start | bytes 884744 | tf_op jit(solution)/shard_map/ppermute | solution.py:461
  60.9 1.0 collective-permute-start.5
  61.8 4.3 %all-to-all-done.1 = bf16[16,64,128]{2,1,0:T(8,128)(2,1)S(1)} async-done(((bf16[16,64,128]{2,1,0:T(8,128)(2,1)}), bf16[16,64,128]{2,1,0:T(8,128)(2,1)S(1)}, u32[]{:S(2)}, u32[]{:S(2)}) %all-to-all-start.1) | async-done | bytes 262176 | tf_op jit(solution)/shard_map/all_to_all | solution.py:477
  66.1 1.9 collective-permute-start
  68.0 3.0 %collective-permute-start.1 = (bf16[9,64,128]{2,1,0:T(8,128)(2,1)S(1)}, bf16[9,64,128]{2,1,0:T(8,128)(2,1)S(1)}, u32[]{:S(2)}, u32[]{:S(2)}) collective-permute-start(bf16[9,64,128]{2,1,0:T(8,128)(2,1)S(1)} %slice.4.o0.attn), channel_id=1, source_target_pairs={{0,2},{1,3},{2,0},{3,1},{4,6},{5,7},{6,4},{7,5},{8,10},{9,11},{10,... | collective-permute-start | bytes 442376 | tf_op jit(solution)/shard_map/ppermute | solution.py:461
  71.0 1.4 collective-permute-start.2
  72.4 3.8 %collective-permute-done.5.w3 = bf16[192,768]{1,0:T(8,128)(2,1)S(1)} collective-permute-done((bf16[192,768]{1,0:T(8,128)(2,1)S(1)}, bf16[192,768]{1,0:T(8,128)(2,1)S(1)}, u32[]{:S(2)}, u32[]{:S(2)}) %collective-permute-start.5) | collective-permute-done | bytes 294944 | tf_op jit(solution)/shard_map/ppermute | solution.py:461
  76.8 2.8 %collective-permute-done.2.o3 = bf16[9,64,128]{2,1,0:T(8,128)(2,1)S(1)} collective-permute-done((bf16[9,64,128]{2,1,0:T(8,128)(2,1)S(1)}, bf16[9,64,128]{2,1,0:T(8,128)(2,1)S(1)}, u32[]{:S(2)}, u32[]{:S(2)}) %collective-permute-start.2) | collective-permute-done | bytes 147488 | tf_op jit(solution)/shard_map/ppermute | solution.py:461
  79.6 1.0 copy-done.21
  80.6 4.2 %forward.1 = (bf16[384,768]{1,0:T(8,128)(2,1)S(1)}, bf16[384,768]{1,0:T(8,128)(2,1)S(1)}, f32[384,768]{1,0:T(8,128)S(1)}, f32[96,768]{1,0:T(8,128)S(1)}, f32[96,...) custom-call(bf16[9,64,128]{2,1,0:T(8,128)(2,1)S(1)} %slice.4.o0.attn, ...), custom_call_target="tpu_custom_call" | custom-call | flops 1358954496 | bytes 4194304 | tf_op jit(solution)/shard_map/forward/pallas_call | solution.py:45
  85.2 3.6 %collective-permute-start.7 = (bf16[96,768]{1,0:T(8,128)(2,1)S(1)}, bf16[96,768]{1,0:T(8,128)(2,1)S(1)}, u32[]{:S(2)}, u32[]{:S(2)}) collective-permute-start(bf16[96,768]{1,0:T(8,128)(2,1)S(1)} %get-tuple-element.79), channel_id=1, source_target_pairs={{0,2},{1,3},{2,0},{3,1},{4,6},{5,7},{6,4},{7,5},{8,10},{9,11},{10,... | collective-permute-start | bytes 442376 | tf_op jit(solution)/shard_map/ppermute | solution.py:461
  88.8 2.6 %collective-permute-done.6.part1 = bf16[96,768]{1,0:T(8,128)(2,1)S(1)} collective-permute-done((bf16[96,768]{1,0:T(8,128)(2,1)S(1)}, bf16[96,768]{1,0:T(8,128)(2,1)S(1)}, u32[]{:S(2)}, u32[]{:S(2)}) %collective-permute-start.6) | collective-permute-done | bytes 147488 | tf_op jit(solution)/shard_map/ppermute | solution.py:461
  91.4 4.1 %collective-permute-done.7.part2 = bf16[96,768]{1,0:T(8,128)(2,1)S(1)} collective-permute-done((bf16[96,768]{1,0:T(8,128)(2,1)S(1)}, bf16[96,768]{1,0:T(8,128)(2,1)S(1)}, u32[]{:S(2)}, u32[]{:S(2)}) %collective-permute-start.7) | collective-permute-done | bytes 147488 | tf_op jit(solution)/shard_map/ppermute | solution.py:461
  96.0 3.6 %collective-permute-start.13 = (bf16[96,768]{1,0:T(8,128)(2,1)S(1)}, bf16[96,768]{1,0:T(8,128)(2,1)S(1)}, u32[]{:S(2)}, u32[]{:S(2)}) collective-permute-start(bf16[96,768]{1,0:T(8,128)(2,1)S(1)} %get-tuple-element.83.g0), channel_id=1, source_target_pairs={{0,2},{1,3},{2,0},{3,1},{4,6},{5,7},{6,4},{7,5},{8,10},{9,11},{10,... | collective-permute-start | bytes 442376 | tf_op jit(solution)/shard_map/ppermute | solution.py:461
  99.6 3.6 %collective-permute-done.12.g1 = bf16[96,768]{1,0:T(8,128)(2,1)S(1)} collective-permute-done((bf16[96,768]{1,0:T(8,128)(2,1)S(1)}, bf16[96,768]{1,0:T(8,128)(2,1)S(1)}, u32[]{:S(2)}, u32[]{:S(2)}) %collective-permute-start.12) | collective-permute-done | bytes 147488 | tf_op jit(solution)/shard_map/ppermute | solution.py:461
  103.2 2.9 %collective-permute-done.13.g2 = bf16[96,768]{1,0:T(8,128)(2,1)S(1)} collective-permute-done((bf16[96,768]{1,0:T(8,128)(2,1)S(1)}, bf16[96,768]{1,0:T(8,128)(2,1)S(1)}, u32[]{:S(2)}, u32[]{:S(2)}) %collective-permute-start.13) | collective-permute-done | bytes 147488 | tf_op jit(solution)/shard_map/ppermute | solution.py:461
  106.1 1.3 ffn_back.1
  107.5 3.7 %collective-permute-start.16 = (bf16[96,768]{1,0:T(8,128)(2,1)S(1)}, bf16[96,768]{1,0:T(8,128)(2,1)S(1)}, u32[]{:S(2)}, u32[]{:S(2)}) collective-permute-start(bf16[96,768]{1,0:T(8,128)(2,1)S(1)} %get-tuple-element.87), channel_id=1, source_target_pairs={{0,2},{1,3},{2,0},{3,1},{4,6},{5,7},{6,4},{7,5},{8,10},{9,11},{10,... | collective-permute-start | bytes 442376 | tf_op jit(solution)/shard_map/ppermute | solution.py:461
  111.2 4.1 %collective-permute-done.15.part1 = bf16[96,768]{1,0:T(8,128)(2,1)S(1)} collective-permute-done((bf16[96,768]{1,0:T(8,128)(2,1)S(1)}, bf16[96,768]{1,0:T(8,128)(2,1)S(1)}, u32[]{:S(2)}, u32[]{:S(2)}) %collective-permute-start.15) | collective-permute-done | bytes 147488 | tf_op jit(solution)/shard_map/ppermute | solution.py:461
  115.2 2.1 collective-permute-done.16.part2
  117.8 3.6 %collective-permute-start.19 = (bf16[96,768]{1,0:T(8,128)(2,1)S(1)}, bf16[96,768]{1,0:T(8,128)(2,1)S(1)}, u32[]{:S(2)}, u32[]{:S(2)}) collective-permute-start(bf16[96,768]{1,0:T(8,128)(2,1)S(1)} %get-tuple-element.92.g0), channel_id=1, source_target_pairs={{0,2},{1,3},{2,0},{3,1},{4,6},{5,7},{6,4},{7,5},{8,10},{9,11},{10,... | collective-permute-start | bytes 442376 | tf_op jit(solution)/shard_map/ppermute | solution.py:461
  121.4 4.3 %collective-permute-done.18.g1 = bf16[96,768]{1,0:T(8,128)(2,1)S(1)} collective-permute-done((bf16[96,768]{1,0:T(8,128)(2,1)S(1)}, bf16[96,768]{1,0:T(8,128)(2,1)S(1)}, u32[]{:S(2)}, u32[]{:S(2)}) %collective-permute-start.18) | collective-permute-done | bytes 147488 | tf_op jit(solution)/shard_map/ppermute | solution.py:461
  125.7 1.6 collective-permute-done.19.g2
  128.6 13.5 %all_to_all.30.got = bf16[16,64,128]{2,1,0:T(8,128)(2,1)S(1)} all-to-all(bf16[16,64,128]{2,1,0:T(8,128)(2,1)S(1)} %get-tuple-element.93), channel_id=1, replica_groups=mesh['dp'=2,'wide'=16,'narrow'=4] {'wide'}, dimensions={0} | all-to-all | bytes 524288 | tf_op jit(solution)/shard_map/all_to_all | solution.py:477
  142.1 12.9 %attend_back.1 = bf16[16,208,128]{2,1,0:T(8,128)(2,1)} custom-call(bf16[16,64,128]{2,1,0:T(8,128)(2,1)S(1)} %all_to_all.30.got, bf16[80,2048]{1,0:T(8,128)(2,1)S(1)} %copy-done.41, bf16[80,2048]{1,0:T(8,128)(2,1)S(1)} %copy-done.43, bf16[80,2048]{1,0:T(8,128)(2,1)S(1)} %copy-done.45, f32[64,2048]{1,0:T(8,128)S(1)} %copy-done.35, f32[64,2048]{1,0:T(8,128)S(1)} %copy-done.37, ...), custom_call_target="tpu_custom_call" | custom-call | flops 10737418240 | bytes 4194304 | tf_op jit(solution)/shard_map/attend_back/pallas_call | solution.py:45
  155.0 3.6 %all-to-all-start.3 = ((bf16[16,208,128]{2,1,0:T(8,128)(2,1)}), bf16[16,208,128]{2,1,0:T(8,128)(2,1)S(1)}, u32[]{:S(2)}, u32[]{:S(2)}) async-start(bf16[16,208,128]{2,1,0:T(8,128)(2,1)} %attend_back.1), calls=%async_computation.3 | async-start | bytes 1703936 | tf_op jit(solution)/shard_map/all_to_all | solution.py:477
  159.2 3.7 %collective-permute-start.30 = (f32[8,768]{1,0:T(8,128)S(1)}, f32[8,768]{1,0:T(8,128)S(1)}, u32[]{:S(2)}, u32[]{:S(2)}) collective-permute-start(f32[8,768]{1,0:T(8,128)S(1)} %get-tuple-element.120.v0), channel_id=1, source_target_pairs={{0,2},{1,3},{2,0},{3,1},{4,6},{5,7},{6,4},{7,5},{8,10},{9,11},{10,... | collective-permute-start | bytes 73736 | tf_op jit(solution)/shard_map/ppermute | solution.py:461
  163.8 1.2 collective-permute-done.30.v2
  164.9 1.8 collective-permute-done.31.v3
  166.7 1.1 copy-done.15
  167.8 1.1 copy-done.17
  168.8 1.1 copy-done.19
  169.9 1.1 copy-done.31
  171.0 1.1 copy-done.33
  172.0 4.5 %weights.1 = (bf16[384,1792]{1,0:T(8,128)(2,1)}, f32[384,1792]{1,0:T(8,128)}, f32[8,768]{1,0:T(8,128)S(1)}) custom-call(bf16[384,768]{1,0:T(8,128)(2,1)S(1)} %copy-done.31, bf16[384,768]{1,0:T(8,128)(2,1)S(1)} %copy-done.17, bf16[384,768]{1,0:T(8,128)(2,1)S(1)} %copy-done.15, bf16[384,768]{1,0:T(8,128)(2,1)S(1)} %copy-done.33, ...), custom_call_target="tpu_custom_call" | custom-call | flops 1019215872 | bytes 4194304 | tf_op jit(solution)/shard_map/weights/pallas_call | solution.py:45
  176.5 1.7 input_back.1
  180.8 1.5 collective-permute-done.28.sums_got
  183.1 7.1 %all-to-all-start.4 = ((bf16[16,24,576]{2,1,0:T(8,128)(2,1)}), bf16[16,24,576]{2,1,0:T(8,128)(2,1)S(1)}, u32[]{:S(2)}, u32[]{:S(2)}) async-start(bf16[16,24,576]{2,1,0:T(8,128)(2,1)} %get-tuple-element.108), calls=%async_computation.4 | async-start | bytes 983040 | tf_op jit(solution)/shard_map/all_to_all | solution.py:477
  190.4 1.1 collective-permute-done.33.sums_got
  191.5 1.8 copy-done
  193.3 2.7 %weights_add.1 = bf16[16,24,2048]{2,1,0:T(8,128)(2,1)} custom-call(f32[384,1792]{1,0:T(8,128)S(1)} %copy-done, bf16[384,1792]{1,0:T(8,128)(2,1)} %collective-permute-done.32.got, f32[8,768]{1,0:T(8,128)S(1)} %get-tuple-element.123.sums, f32[8,768]{1,0:T(8,128)S(1)} %collective-permute-done.33.sums_got), custom_call_target="tpu_custom_call" | custom-call | bytes 4194304 | tf_op jit(solution)/shard_map/weights_add/pallas_call | solution.py:45
  196.0 5.9 %all-to-all-done.4.got = bf16[16,24,576]{2,1,0:T(8,128)(2,1)S(1)} async-done(((bf16[16,24,576]{2,1,0:T(8,128)(2,1)}), bf16[16,24,576]{2,1,0:T(8,128)(2,1)S(1)}, u32[]{:S(2)}, u32[]{:S(2)}) %all-to-all-start.4) | async-done | bytes 442400 | tf_op jit(solution)/shard_map/all_to_all | solution.py:477
  201.9 3.7 %all-to-all-start.5 = ((bf16[16,24,2048]{2,1,0:T(8,128)(2,1)}), bf16[16,24,2048]{2,1,0:T(8,128)(2,1)S(1)}, u32[]{:S(2)}, u32[]{:S(2)}) async-start(bf16[16,24,2048]{2,1,0:T(8,128)(2,1)} %weights_add.1), calls=%async_computation.5 | async-start | bytes 3145728 | tf_op jit(solution)/shard_map/all_to_all | solution.py:477
  205.7 2.7 %collective-permute-start.22 = (bf16[96,768]{1,0:T(8,128)(2,1)S(1)}, bf16[96,768]{1,0:T(8,128)(2,1)S(1)}, u32[]{:S(2)}, u32[]{:S(2)}) collective-permute-start(bf16[96,768]{1,0:T(8,128)(2,1)S(1)} %copy-done.25), channel_id=1, source_target_pairs={{0,2},{1,3},{2,0},{3,1},{4,6},{5,7},{6,4},{7,5},{8,10},{9,11},{10,... | collective-permute-start | bytes 442376 | tf_op jit(solution)/shard_map/ppermute | solution.py:461
  208.4 1.5 collective-permute-start.23
  209.9 2.0 collective-permute-start.10
  211.9 1.2 collective-permute-start.11
  213.1 3.6 %collective-permute-done.21.part1 = bf16[96,768]{1,0:T(8,128)(2,1)S(1)} collective-permute-done((bf16[96,768]{1,0:T(8,128)(2,1)S(1)}, bf16[96,768]{1,0:T(8,128)(2,1)S(1)}, u32[]{:S(2)}, u32[]{:S(2)}) %collective-permute-start.21) | collective-permute-done | bytes 147488 | tf_op jit(solution)/shard_map/ppermute | solution.py:461
  216.7 1.0 collective-permute-done.23.part3
  217.8 2.0 collective-permute-start.24
  219.8 2.9 %collective-permute-start.25 = (bf16[96,768]{1,0:T(8,128)(2,1)S(1)}, bf16[96,768]{1,0:T(8,128)(2,1)S(1)}, u32[]{:S(2)}, u32[]{:S(2)}) collective-permute-start(bf16[96,768]{1,0:T(8,128)(2,1)S(1)} %input_chunk.1.g0), channel_id=1, source_target_pairs={{0,2},{1,3},{2,0},{3,1},{4,6},{5,7},{6,4},{7,5},{8,10},{9,11},{10,... | collective-permute-start | bytes 442376 | tf_op jit(solution)/shard_map/ppermute | solution.py:461
  223.5 1.1 collective-permute-done.9.g1
  224.6 1.1 layer_out.1
  225.7 2.1 collective-permute-done.24.g1
  227.8 1.1 grad_input.1
  (139 shorter events, 17.3 us)
Async XLA Ops:
  7.3 72.4 %all-gather.3.cloned.1.call-start = ((), (), s32[]{:S(2)}) async-start(), calls=%async_computation.6 | async-start | bytes 2506752 | tf_op jit(solution)/shard_map/all_gather | solution.py:488
  13.1 7.3 %copy-start.4 = (bf16[192,768]{1,0:T(8,128)(2,1)S(1)}, bf16[192,768]{1,0:T(8,128)(2,1)}, u32[]{:S(2)}) copy-start(bf16[192,768]{1,0:T(8,128)(2,1)} %w_out.1) | copy-start | bytes 884740
  13.1 24.2 %copy-start.47 = (f32[64]{0:T(128)S(1)}, f32[64]{0:T(128)}, u32[]{:S(2)}) copy-start(f32[64]{0:T(128)} %constant.2.clone) | copy-start | bytes 772
  13.1 24.2 %all-to-all-start = ((bf16[16,208,128]{2,1,0:T(8,128)(2,1)}), bf16[16,208,128]{2,1,0:T(8,128)(2,1)S(1)}, u32[]{:S(2)}, u32[]{:S(2)}) async-start(bf16[16,208,128]{2,1,0:T(8,128)(2,1)} %project.1), calls=%async_computation | async-start | bytes 1703936 | tf_op jit(solution)/shard_map/all_to_all | solution.py:477
  20.4 50.6 %collective-permute-start.3 = (bf16[192,768]{1,0:T(8,128)(2,1)S(1)}, bf16[192,768]{1,0:T(8,128)(2,1)}, u32[]{:S(2)}, u32[]{:S(2)}) collective-permute-start(bf16[192,768]{1,0:T(8,128)(2,1)S(1)} %copy-done.4), channel_id=1, source_target_pairs={{0,1},{1,2},{2,3},{3,0},{4,5},{5,6},{6,7},{7,4},{8,9},{9,10},{10,1... | collective-permute-start | bytes 884744 | tf_op jit(solution)/shard_map/ppermute | solution.py:461
  37.4 42.2 %copy-start.5 = (f32[768]{0:T(1024)S(1)}, f32[768]{0:T(1024)}, u32[]{:S(2)}) copy-start(f32[768]{0:T(1024)} %g_one.5) | copy-start | bytes 9220
  37.4 42.2 %copy-start.6 = (f32[768]{0:T(1024)S(1)}, f32[768]{0:T(1024)}, u32[]{:S(2)}) copy-start(f32[768]{0:T(1024)} %s_one.3) | copy-start | bytes 9220
  37.4 42.2 %copy-start.28 = (f32[768]{0:T(1024)S(1)}, f32[768]{0:T(1024)}, u32[]{:S(2)}) copy-start(f32[768]{0:T(1024)} %b_out.1) | copy-start | bytes 9220
  37.4 42.2 %copy-start.29 = (f32[768]{0:T(1024)S(1)}, f32[768]{0:T(1024)}, u32[]{:S(2)}) copy-start(f32[768]{0:T(1024)} %b_up.1) | copy-start | bytes 9220
  53.8 12.3 %all-to-all-start.1 = ((bf16[16,64,128]{2,1,0:T(8,128)(2,1)}), bf16[16,64,128]{2,1,0:T(8,128)(2,1)S(1)}, u32[]{:S(2)}, u32[]{:S(2)}) async-start(bf16[16,64,128]{2,1,0:T(8,128)(2,1)} %get-tuple-element.76), calls=%async_computation.1 | async-start | bytes 524288 | tf_op jit(solution)/shard_map/all_to_all | solution.py:477
  57.4 15.0 %collective-permute-start.4 = (bf16[192,768]{1,0:T(8,128)(2,1)S(1)}, bf16[192,768]{1,0:T(8,128)(2,1)S(1)}, u32[]{:S(2)}, u32[]{:S(2)}) collective-permute-start(bf16[192,768]{1,0:T(8,128)(2,1)S(1)} %copy-done.4), channel_id=1, source_target_pairs={{0,2},{1,3},{2,0},{3,1},{4,6},{5,7},{6,4},{7,5},{8,10},{9,11},{10,... | collective-permute-start | bytes 884744 | tf_op jit(solution)/shard_map/ppermute | solution.py:461
  60.9 15.3 %collective-permute-start.5 = (bf16[192,768]{1,0:T(8,128)(2,1)S(1)}, bf16[192,768]{1,0:T(8,128)(2,1)S(1)}, u32[]{:S(2)}, u32[]{:S(2)}) collective-permute-start(bf16[192,768]{1,0:T(8,128)(2,1)S(1)} %copy-done.4), channel_id=1, source_target_pairs={{0,3},{1,0},{2,1},{3,2},{4,7},{5,4},{6,5},{7,6},{8,11},{9,8},{10,9... | collective-permute-start | bytes 884744 | tf_op jit(solution)/shard_map/ppermute | solution.py:461
  66.1 10.7 %collective-permute-start = (bf16[9,64,128]{2,1,0:T(8,128)(2,1)S(1)}, bf16[9,64,128]{2,1,0:T(8,128)(2,1)S(1)}, u32[]{:S(2)}, u32[]{:S(2)}) collective-permute-start(bf16[9,64,128]{2,1,0:T(8,128)(2,1)S(1)} %slice.4.o0.attn), channel_id=1, source_target_pairs={{0,1},{1,2},{2,3},{3,0},{4,5},{5,6},{6,7},{7,4},{8,9},{9,10},{10,1... | collective-permute-start | bytes 442376 | tf_op jit(solution)/shard_map/ppermute | solution.py:461
  68.0 8.9 %collective-permute-start.1 = (bf16[9,64,128]{2,1,0:T(8,128)(2,1)S(1)}, bf16[9,64,128]{2,1,0:T(8,128)(2,1)S(1)}, u32[]{:S(2)}, u32[]{:S(2)}) collective-permute-start(bf16[9,64,128]{2,1,0:T(8,128)(2,1)S(1)} %slice.4.o0.attn), channel_id=1, source_target_pairs={{0,2},{1,3},{2,0},{3,1},{4,6},{5,7},{6,4},{7,5},{8,10},{9,11},{10,... | collective-permute-start | bytes 442376 | tf_op jit(solution)/shard_map/ppermute | solution.py:461
  71.0 8.6 %collective-permute-start.2 = (bf16[9,64,128]{2,1,0:T(8,128)(2,1)S(1)}, bf16[9,64,128]{2,1,0:T(8,128)(2,1)S(1)}, u32[]{:S(2)}, u32[]{:S(2)}) collective-permute-start(bf16[9,64,128]{2,1,0:T(8,128)(2,1)S(1)} %slice.4.o0.attn), channel_id=1, source_target_pairs={{0,3},{1,0},{2,1},{3,2},{4,7},{5,4},{6,5},{7,6},{8,11},{9,8},{10,9... | collective-permute-start | bytes 442376 | tf_op jit(solution)/shard_map/ppermute | solution.py:461
  80.6 14.9 %copy-start.3 = (bf16[3,128,768]{2,1,0:T(8,128)(2,1)S(1)}, bf16[3,128,768]{2,1,0:T(8,128)(2,1)}, u32[]{:S(2)}) copy-start(bf16[3,128,768]{2,1,0:T(8,128)(2,1)} %cot.1) | copy-start | bytes 1769476
  80.6 14.9 %copy-start.7 = (f32[768]{0:T(1024)S(1)}, f32[768]{0:T(1024)}, u32[]{:S(2)}) copy-start(f32[768]{0:T(1024)} %b_down.1) | copy-start | bytes 9220
  80.6 14.9 %copy-start.8 = (f32[768]{0:T(1024)S(1)}, f32[768]{0:T(1024)}, u32[]{:S(2)}) copy-start(f32[768]{0:T(1024)} %g_two.1) | copy-start | bytes 9220
  80.6 14.9 %copy-start.9 = (f32[768]{0:T(1024)S(1)}, f32[768]{0:T(1024)}, u32[]{:S(2)}) copy-start(f32[768]{0:T(1024)} %s_two.1) | copy-start | bytes 9220
  80.6 25.5 %copy-start.2 = (bf16[1536,768]{1,0:T(8,128)(2,1)S(1)}, bf16[1536,768]{1,0:T(8,128)(2,1)}, u32[]{:S(2)}) copy-start(bf16[1536,768]{1,0:T(8,128)(2,1)} %all-gather.3.cloned.1.call-done) | copy-start | bytes 7077892
  84.8 21.2 %copy-start.30 = (bf16[384,768]{1,0:T(8,128)(2,1)}, bf16[384,768]{1,0:T(8,128)(2,1)S(1)}, u32[]{:S(2)}) copy-start(bf16[384,768]{1,0:T(8,128)(2,1)S(1)} %get-tuple-element.115.normed_low) | copy-start | bytes 1769476
  84.8 22.6 %copy-start.32 = (bf16[384,768]{1,0:T(8,128)(2,1)}, bf16[384,768]{1,0:T(8,128)(2,1)S(1)}, u32[]{:S(2)}) copy-start(bf16[384,768]{1,0:T(8,128)(2,1)S(1)} %get-tuple-element.118.hidden_low) | copy-start | bytes 1769476
  84.8 6.6 %collective-permute-start.6 = (bf16[96,768]{1,0:T(8,128)(2,1)S(1)}, bf16[96,768]{1,0:T(8,128)(2,1)S(1)}, u32[]{:S(2)}, u32[]{:S(2)}) collective-permute-start(bf16[96,768]{1,0:T(8,128)(2,1)S(1)} %get-tuple-element.78), channel_id=1, source_target_pairs={{0,1},{1,2},{2,3},{3,0},{4,5},{5,6},{6,7},{7,4},{8,9},{9,10},{10,1... | collective-permute-start | bytes 442376 | tf_op jit(solution)/shard_map/ppermute | solution.py:461
  85.2 10.3 %collective-permute-start.7 = (bf16[96,768]{1,0:T(8,128)(2,1)S(1)}, bf16[96,768]{1,0:T(8,128)(2,1)S(1)}, u32[]{:S(2)}, u32[]{:S(2)}) collective-permute-start(bf16[96,768]{1,0:T(8,128)(2,1)S(1)} %get-tuple-element.79), channel_id=1, source_target_pairs={{0,2},{1,3},{2,0},{3,1},{4,6},{5,7},{6,4},{7,5},{8,10},{9,11},{10,... | collective-permute-start | bytes 442376 | tf_op jit(solution)/shard_map/ppermute | solution.py:461
  88.8 6.7 %collective-permute-start.8 = (bf16[96,768]{1,0:T(8,128)(2,1)S(1)}, bf16[96,768]{1,0:T(8,128)(2,1)S(1)}, u32[]{:S(2)}, u32[]{:S(2)}) collective-permute-start(bf16[96,768]{1,0:T(8,128)(2,1)S(1)} %get-tuple-element.80), channel_id=1, source_target_pairs={{0,3},{1,0},{2,1},{3,2},{4,7},{5,4},{6,5},{7,6},{8,11},{9,8},{10,9... | collective-permute-start | bytes 442376 | tf_op jit(solution)/shard_map/ppermute | solution.py:461
  95.9 7.3 %collective-permute-start.12 = (bf16[96,768]{1,0:T(8,128)(2,1)S(1)}, bf16[96,768]{1,0:T(8,128)(2,1)S(1)}, u32[]{:S(2)}, u32[]{:S(2)}) collective-permute-start(bf16[96,768]{1,0:T(8,128)(2,1)S(1)} %get-tuple-element.83.g0), channel_id=1, source_target_pairs={{0,1},{1,2},{2,3},{3,0},{4,5},{5,6},{6,7},{7,4},{8,9},{9,10},{10,1... | collective-permute-start | bytes 442376 | tf_op jit(solution)/shard_map/ppermute | solution.py:461
  96.0 10.1 %collective-permute-start.13 = (bf16[96,768]{1,0:T(8,128)(2,1)S(1)}, bf16[96,768]{1,0:T(8,128)(2,1)S(1)}, u32[]{:S(2)}, u32[]{:S(2)}) collective-permute-start(bf16[96,768]{1,0:T(8,128)(2,1)S(1)} %get-tuple-element.83.g0), channel_id=1, source_target_pairs={{0,2},{1,3},{2,0},{3,1},{4,6},{5,7},{6,4},{7,5},{8,10},{9,11},{10,... | collective-permute-start | bytes 442376 | tf_op jit(solution)/shard_map/ppermute | solution.py:461
  99.6 6.5 %collective-permute-start.14 = (bf16[96,768]{1,0:T(8,128)(2,1)S(1)}, bf16[96,768]{1,0:T(8,128)(2,1)S(1)}, u32[]{:S(2)}, u32[]{:S(2)}) collective-permute-start(bf16[96,768]{1,0:T(8,128)(2,1)S(1)} %get-tuple-element.83.g0), channel_id=1, source_target_pairs={{0,3},{1,0},{2,1},{3,2},{4,7},{5,4},{6,5},{7,6},{8,11},{9,8},{10,9... | collective-permute-start | bytes 442376 | tf_op jit(solution)/shard_map/ppermute | solution.py:461
  107.4 10.4 %copy-start.14 = (bf16[384,768]{1,0:T(8,128)(2,1)}, bf16[384,768]{1,0:T(8,128)(2,1)S(1)}, u32[]{:S(2)}) copy-start(bf16[384,768]{1,0:T(8,128)(2,1)S(1)} %get-tuple-element.117.grad_ffn) | copy-start | bytes 1769476
  107.4 20.3 %copy-start.16 = (bf16[384,768]{1,0:T(8,128)(2,1)}, bf16[384,768]{1,0:T(8,128)(2,1)S(1)}, u32[]{:S(2)}) copy-start(bf16[384,768]{1,0:T(8,128)(2,1)S(1)} %get-tuple-element.116.grad_pre) | copy-start | bytes 1769476
  107.4 7.8 %collective-permute-start.15 = (bf16[96,768]{1,0:T(8,128)(2,1)S(1)}, bf16[96,768]{1,0:T(8,128)(2,1)S(1)}, u32[]{:S(2)}, u32[]{:S(2)}) collective-permute-start(bf16[96,768]{1,0:T(8,128)(2,1)S(1)} %get-tuple-element.86), channel_id=1, source_target_pairs={{0,1},{1,2},{2,3},{3,0},{4,5},{5,6},{6,7},{7,4},{8,9},{9,10},{10,1... | collective-permute-start | bytes 442376 | tf_op jit(solution)/shard_map/ppermute | solution.py:461
  107.5 9.8 %collective-permute-start.16 = (bf16[96,768]{1,0:T(8,128)(2,1)S(1)}, bf16[96,768]{1,0:T(8,128)(2,1)S(1)}, u32[]{:S(2)}, u32[]{:S(2)}) collective-permute-start(bf16[96,768]{1,0:T(8,128)(2,1)S(1)} %get-tuple-element.87), channel_id=1, source_target_pairs={{0,2},{1,3},{2,0},{3,1},{4,6},{5,7},{6,4},{7,5},{8,10},{9,11},{10,... | collective-permute-start | bytes 442376 | tf_op jit(solution)/shard_map/ppermute | solution.py:461
  111.2 6.2 %collective-permute-start.17 = (bf16[96,768]{1,0:T(8,128)(2,1)S(1)}, bf16[96,768]{1,0:T(8,128)(2,1)S(1)}, u32[]{:S(2)}, u32[]{:S(2)}) collective-permute-start(bf16[96,768]{1,0:T(8,128)(2,1)S(1)} %get-tuple-element.88), channel_id=1, source_target_pairs={{0,3},{1,0},{2,1},{3,2},{4,7},{5,4},{6,5},{7,6},{8,11},{9,8},{10,9... | collective-permute-start | bytes 442376 | tf_op jit(solution)/shard_map/ppermute | solution.py:461
  117.3 24.7 %copy-start.35 = (f32[64,2048]{1,0:T(8,128)S(1)}, f32[64,2048]{1,0:T(8,128)}, u32[]{:S(2)}) copy-start(f32[64,2048]{1,0:T(8,128)} %copy-done.34) | copy-start | bytes 1572868
  117.3 24.7 %copy-start.37 = (f32[64,2048]{1,0:T(8,128)S(1)}, f32[64,2048]{1,0:T(8,128)}, u32[]{:S(2)}) copy-start(f32[64,2048]{1,0:T(8,128)} %copy-done.36) | copy-start | bytes 1572868
  117.3 24.7 %copy-start.39 = (f32[64,2048]{1,0:T(8,128)S(1)}, f32[64,2048]{1,0:T(8,128)}, u32[]{:S(2)}) copy-start(f32[64,2048]{1,0:T(8,128)} %copy-done.38) | copy-start | bytes 1572868
  117.3 24.7 %copy-start.41 = (bf16[80,2048]{1,0:T(8,128)(2,1)S(1)}, bf16[80,2048]{1,0:T(8,128)(2,1)}, u32[]{:S(2)}) copy-start(bf16[80,2048]{1,0:T(8,128)(2,1)} %copy-done.40) | copy-start | bytes 983044
  117.4 24.7 %copy-start.43 = (bf16[80,2048]{1,0:T(8,128)(2,1)S(1)}, bf16[80,2048]{1,0:T(8,128)(2,1)}, u32[]{:S(2)}) copy-start(bf16[80,2048]{1,0:T(8,128)(2,1)} %copy-done.42) | copy-start | bytes 983044
  117.4 24.7 %copy-start.45 = (bf16[80,2048]{1,0:T(8,128)(2,1)S(1)}, bf16[80,2048]{1,0:T(8,128)(2,1)}, u32[]{:S(2)}) copy-start(bf16[80,2048]{1,0:T(8,128)(2,1)} %copy-done.44) | copy-start | bytes 983044
  117.7 8.0 %collective-permute-start.18 = (bf16[96,768]{1,0:T(8,128)(2,1)S(1)}, bf16[96,768]{1,0:T(8,128)(2,1)S(1)}, u32[]{:S(2)}, u32[]{:S(2)}) collective-permute-start(bf16[96,768]{1,0:T(8,128)(2,1)S(1)} %get-tuple-element.92.g0), channel_id=1, source_target_pairs={{0,1},{1,2},{2,3},{3,0},{4,5},{5,6},{6,7},{7,4},{8,9},{9,10},{10,1... | collective-permute-start | bytes 442376 | tf_op jit(solution)/shard_map/ppermute | solution.py:461
  117.8 9.5 %collective-permute-start.19 = (bf16[96,768]{1,0:T(8,128)(2,1)S(1)}, bf16[96,768]{1,0:T(8,128)(2,1)S(1)}, u32[]{:S(2)}, u32[]{:S(2)}) collective-permute-start(bf16[96,768]{1,0:T(8,128)(2,1)S(1)} %get-tuple-element.92.g0), channel_id=1, source_target_pairs={{0,2},{1,3},{2,0},{3,1},{4,6},{5,7},{6,4},{7,5},{8,10},{9,11},{10,... | collective-permute-start | bytes 442376 | tf_op jit(solution)/shard_map/ppermute | solution.py:461
  121.4 5.9 %collective-permute-start.20 = (bf16[96,768]{1,0:T(8,128)(2,1)S(1)}, bf16[96,768]{1,0:T(8,128)(2,1)S(1)}, u32[]{:S(2)}, u32[]{:S(2)}) collective-permute-start(bf16[96,768]{1,0:T(8,128)(2,1)S(1)} %get-tuple-element.92.g0), channel_id=1, source_target_pairs={{0,3},{1,0},{2,1},{3,2},{4,7},{5,4},{6,5},{7,6},{8,11},{9,8},{10,9... | collective-permute-start | bytes 442376 | tf_op jit(solution)/shard_map/ppermute | solution.py:461
  155.0 21.5 %all-to-all-start.3 = ((bf16[16,208,128]{2,1,0:T(8,128)(2,1)}), bf16[16,208,128]{2,1,0:T(8,128)(2,1)S(1)}, u32[]{:S(2)}, u32[]{:S(2)}) async-start(bf16[16,208,128]{2,1,0:T(8,128)(2,1)} %attend_back.1), calls=%async_computation.3 | async-start | bytes 1703936 | tf_op jit(solution)/shard_map/all_to_all | solution.py:477
  158.7 5.1 %collective-permute-start.29 = (f32[8,768]{1,0:T(8,128)S(1)}, f32[8,768]{1,0:T(8,128)S(1)}, u32[]{:S(2)}, u32[]{:S(2)}) collective-permute-start(f32[8,768]{1,0:T(8,128)S(1)} %get-tuple-element.120.v0), channel_id=1, source_target_pairs={{0,1},{1,2},{2,3},{3,0},{4,5},{5,6},{6,7},{7,4},{8,9},{9,10},{10,1... | collective-permute-start | bytes 73736 | tf_op jit(solution)/shard_map/ppermute | solution.py:461
  159.2 5.8 %collective-permute-start.30 = (f32[8,768]{1,0:T(8,128)S(1)}, f32[8,768]{1,0:T(8,128)S(1)}, u32[]{:S(2)}, u32[]{:S(2)}) collective-permute-start(f32[8,768]{1,0:T(8,128)S(1)} %get-tuple-element.120.v0), channel_id=1, source_target_pairs={{0,2},{1,3},{2,0},{3,1},{4,6},{5,7},{6,4},{7,5},{8,10},{9,11},{10,... | collective-permute-start | bytes 73736 | tf_op jit(solution)/shard_map/ppermute | solution.py:461
  162.9 3.8 %collective-permute-start.31 = (f32[8,768]{1,0:T(8,128)S(1)}, f32[8,768]{1,0:T(8,128)S(1)}, u32[]{:S(2)}, u32[]{:S(2)}) collective-permute-start(f32[8,768]{1,0:T(8,128)S(1)} %get-tuple-element.120.v0), channel_id=1, source_target_pairs={{0,3},{1,0},{2,1},{3,2},{4,7},{5,4},{6,5},{7,6},{8,11},{9,8},{10,9... | collective-permute-start | bytes 73736 | tf_op jit(solution)/shard_map/ppermute | solution.py:461
  176.5 15.0 %collective-permute-start.32 = (bf16[384,1792]{1,0:T(8,128)(2,1)}, bf16[384,1792]{1,0:T(8,128)(2,1)}, u32[]{:S(2)}, u32[]{:S(2)}) collective-permute-start(bf16[384,1792]{1,0:T(8,128)(2,1)} %get-tuple-element.122), channel_id=1, source_target_pairs={{0,64},{64,0},{1,65},{65,1},{2,66},{66,2},{3,67},{67,3},{4,68},{68... | collective-permute-start | bytes 4128776 | tf_op jit(solution)/shard_map/ppermute | solution.py:473
  180.3 2.0 collective-permute-start.27
  180.8 1.5 collective-permute-start.28
  183.1 18.8 %all-to-all-start.4 = ((bf16[16,24,576]{2,1,0:T(8,128)(2,1)}), bf16[16,24,576]{2,1,0:T(8,128)(2,1)S(1)}, u32[]{:S(2)}, u32[]{:S(2)}) async-start(bf16[16,24,576]{2,1,0:T(8,128)(2,1)} %get-tuple-element.108), calls=%async_computation.4 | async-start | bytes 983040 | tf_op jit(solution)/shard_map/all_to_all | solution.py:477
  190.2 1.3 collective-permute-start.33
  196.0 9.6 %copy-start.27 = (bf16[96,768]{1,0:T(8,128)(2,1)S(1)}, bf16[96,768]{1,0:T(8,128)(2,1)}, u32[]{:S(2)}) copy-start(bf16[96,768]{1,0:T(8,128)(2,1)} %copy-done.26) | copy-start | bytes 442372
  196.0 9.7 %copy-start.25 = (bf16[96,768]{1,0:T(8,128)(2,1)S(1)}, bf16[96,768]{1,0:T(8,128)(2,1)}, u32[]{:S(2)}) copy-start(bf16[96,768]{1,0:T(8,128)(2,1)} %copy-done.24) | copy-start | bytes 442372
  196.0 12.4 %copy-start.23 = (bf16[96,768]{1,0:T(8,128)(2,1)S(1)}, bf16[96,768]{1,0:T(8,128)(2,1)}, u32[]{:S(2)}) copy-start(bf16[96,768]{1,0:T(8,128)(2,1)} %copy-done.22) | copy-start | bytes 442372
  201.9 27.8 %all-to-all-start.5 = ((bf16[16,24,2048]{2,1,0:T(8,128)(2,1)}), bf16[16,24,2048]{2,1,0:T(8,128)(2,1)S(1)}, u32[]{:S(2)}, u32[]{:S(2)}) async-start(bf16[16,24,2048]{2,1,0:T(8,128)(2,1)} %weights_add.1), calls=%async_computation.5 | async-start | bytes 3145728 | tf_op jit(solution)/shard_map/all_to_all | solution.py:477
  205.6 11.0 %collective-permute-start.21 = (bf16[96,768]{1,0:T(8,128)(2,1)S(1)}, bf16[96,768]{1,0:T(8,128)(2,1)S(1)}, u32[]{:S(2)}, u32[]{:S(2)}) collective-permute-start(bf16[96,768]{1,0:T(8,128)(2,1)S(1)} %copy-done.27), channel_id=1, source_target_pairs={{0,1},{1,2},{2,3},{3,0},{4,5},{5,6},{6,7},{7,4},{8,9},{9,10},{10,1... | collective-permute-start | bytes 442376 | tf_op jit(solution)/shard_map/ppermute | solution.py:461
  205.7 11.0 %collective-permute-start.22 = (bf16[96,768]{1,0:T(8,128)(2,1)S(1)}, bf16[96,768]{1,0:T(8,128)(2,1)S(1)}, u32[]{:S(2)}, u32[]{:S(2)}) collective-permute-start(bf16[96,768]{1,0:T(8,128)(2,1)S(1)} %copy-done.25), channel_id=1, source_target_pairs={{0,2},{1,3},{2,0},{3,1},{4,6},{5,7},{6,4},{7,5},{8,10},{9,11},{10,... | collective-permute-start | bytes 442376 | tf_op jit(solution)/shard_map/ppermute | solution.py:461
  208.4 9.3 %collective-permute-start.23 = (bf16[96,768]{1,0:T(8,128)(2,1)S(1)}, bf16[96,768]{1,0:T(8,128)(2,1)S(1)}, u32[]{:S(2)}, u32[]{:S(2)}) collective-permute-start(bf16[96,768]{1,0:T(8,128)(2,1)S(1)} %copy-done.23), channel_id=1, source_target_pairs={{0,3},{1,0},{2,1},{3,2},{4,7},{5,4},{6,5},{7,6},{8,11},{9,8},{10,9... | collective-permute-start | bytes 442376 | tf_op jit(solution)/shard_map/ppermute | solution.py:461
  209.9 12.8 %collective-permute-start.10 = (bf16[96,768]{1,0:T(8,128)(2,1)S(1)}, bf16[96,768]{1,0:T(8,128)(2,1)S(1)}, u32[]{:S(2)}, u32[]{:S(2)}) collective-permute-start(bf16[96,768]{1,0:T(8,128)(2,1)S(1)} %get-tuple-element.82.g0), channel_id=1, source_target_pairs={{0,2},{1,3},{2,0},{3,1},{4,6},{5,7},{6,4},{7,5},{8,10},{9,11},{10,... | collective-permute-start | bytes 442376 | tf_op jit(solution)/shard_map/ppermute | solution.py:461
  211.9 11.6 %collective-permute-start.11 = (bf16[96,768]{1,0:T(8,128)(2,1)S(1)}, bf16[96,768]{1,0:T(8,128)(2,1)S(1)}, u32[]{:S(2)}, u32[]{:S(2)}) collective-permute-start(bf16[96,768]{1,0:T(8,128)(2,1)S(1)} %get-tuple-element.82.g0), channel_id=1, source_target_pairs={{0,3},{1,0},{2,1},{3,2},{4,7},{5,4},{6,5},{7,6},{8,11},{9,8},{10,9... | collective-permute-start | bytes 442376 | tf_op jit(solution)/shard_map/ppermute | solution.py:461
  216.7 7.9 %collective-permute-start.9 = (bf16[96,768]{1,0:T(8,128)(2,1)S(1)}, bf16[96,768]{1,0:T(8,128)(2,1)S(1)}, u32[]{:S(2)}, u32[]{:S(2)}) collective-permute-start(bf16[96,768]{1,0:T(8,128)(2,1)S(1)} %get-tuple-element.82.g0), channel_id=1, source_target_pairs={{0,1},{1,2},{2,3},{3,0},{4,5},{5,6},{6,7},{7,4},{8,9},{9,10},{10,1... | collective-permute-start | bytes 442376 | tf_op jit(solution)/shard_map/ppermute | solution.py:461
  217.8 10.0 %collective-permute-start.24 = (bf16[96,768]{1,0:T(8,128)(2,1)S(1)}, bf16[96,768]{1,0:T(8,128)(2,1)S(1)}, u32[]{:S(2)}, u32[]{:S(2)}) collective-permute-start(bf16[96,768]{1,0:T(8,128)(2,1)S(1)} %input_chunk.1.g0), channel_id=1, source_target_pairs={{0,1},{1,2},{2,3},{3,0},{4,5},{5,6},{6,7},{7,4},{8,9},{9,10},{10,1... | collective-permute-start | bytes 442376 | tf_op jit(solution)/shard_map/ppermute | solution.py:461
  219.8 7.9 %collective-permute-start.25 = (bf16[96,768]{1,0:T(8,128)(2,1)S(1)}, bf16[96,768]{1,0:T(8,128)(2,1)S(1)}, u32[]{:S(2)}, u32[]{:S(2)}) collective-permute-start(bf16[96,768]{1,0:T(8,128)(2,1)S(1)} %input_chunk.1.g0), channel_id=1, source_target_pairs={{0,2},{1,3},{2,0},{3,1},{4,6},{5,7},{6,4},{7,5},{8,10},{9,11},{10,... | collective-permute-start | bytes 442376 | tf_op jit(solution)/shard_map/ppermute | solution.py:461
  222.7 5.1 %collective-permute-start.26 = (bf16[96,768]{1,0:T(8,128)(2,1)S(1)}, bf16[96,768]{1,0:T(8,128)(2,1)S(1)}, u32[]{:S(2)}, u32[]{:S(2)}) collective-permute-start(bf16[96,768]{1,0:T(8,128)(2,1)S(1)} %input_chunk.1.g0), channel_id=1, source_target_pairs={{0,3},{1,0},{2,1},{3,2},{4,7},{5,4},{6,5},{7,6},{8,11},{9,8},{10,9... | collective-permute-start | bytes 442376 | tf_op jit(solution)/shard_map/ppermute | solution.py:461
  (24 other events, 41.3 us)
Sparse Core Ops, SparseCore 0:
  10.3 54.5 all-gather.2

commit v2 on v1

v2 whole, which is shorter than its diff:
```python
import functools
import math

import jax
import jax.numpy as jnp
import numpy as np
from jax import lax
from jax.experimental import pallas as pl
from jax.experimental.pallas import tpu as pltpu
from jax.sharding import PartitionSpec as P

D = 768
HD = 64
R = 3
T = 128
NH = 3
E = NH * HD
F = 768
NW = 16
NN = 4
TOK = R * T
L = NW * T
C = T // NN
CH = R * C
PAIRS = R * NH
G = D // (2 * NW)
SLOT = 3 * HD + 16
AUG = HD + 16
EPSILON = 1e-12
BIG = 1e30
LOG2E = math.log2(math.e)
LN2 = math.log(2.0)
COST = 10**11
f32, bf16 = jnp.float32, jnp.bfloat16


def dot(a, b, dims):
    return lax.dot_general(a, b, (dims, ((), ())), preferred_element_type=f32)


NORMAL, BOTH_LAST, BOTH_FIRST = ((1,), (0,)), ((1,), (1,)), ((0,), (0,))


def call(
    name, kernel, outs, args, scratch=(), cost=1024, mib=16, after=(), far_in=(), any_in=(), near=(), far=(), aliases={},
    token=False,
):
    if token:
        outs = [*outs, ((8, 128), f32)]

    def run(*refs):
        end = len(args) + len(after)
        if token:
            at = end + len(outs) - 1
            refs[at][...] = jnp.zeros((8, 128), f32)
            refs = refs[:at] + refs[at + 1 :]
        kernel(*refs[: len(args)], *refs[end:])

    def shape(k, s, t):
        return pltpu.VMEM(s, t) if k in near else pltpu.HBM(s, t) if k in far else jax.ShapeDtypeStruct(s, t)

    args = [pltpu.with_memory_space_constraint(a, pltpu.HBM) if k in far_in else a for k, a in enumerate(args)]
    return pl.pallas_call(
        run,
        out_shape=[shape(k, s, t) for k, (s, t) in enumerate(outs)],
        in_specs=[
            pl.BlockSpec(memory_space=pltpu.HBM if k in far_in else pl.ANY if k in any_in else pltpu.VMEM)
            for k in range(len(args))
        ]
        + [pl.BlockSpec(memory_space=pl.ANY) for _ in after],
        out_specs=[pl.BlockSpec(memory_space=pltpu.HBM if k in far else pltpu.VMEM) for k in range(len(outs))],
        scratch_shapes=list(scratch),
        input_output_aliases=aliases,
        compiler_params=pltpu.CompilerParams(vmem_limit_bytes=mib * 1024 * 1024),
        cost_estimate=pl.CostEstimate(flops=cost, bytes_accessed=1024, transcendentals=0),
        name=name,
    )(*args, *after)


def later(x, *after):
    return pl.pallas_call(
        lambda *refs: None,
        out_shape=jax.ShapeDtypeStruct(x.shape, x.dtype),
        in_specs=[pl.BlockSpec(memory_space=pltpu.HBM)] + [pl.BlockSpec(memory_space=pl.ANY) for _ in after],
        out_specs=pl.BlockSpec(memory_space=pltpu.HBM),
        input_output_aliases={0: 0},
        cost_estimate=pl.CostEstimate(flops=1024, bytes_accessed=1024, transcendentals=0),
        name="later",
    )(x, *after)


def copies(pairs, sems):
    made = [pltpu.make_async_copy(a, b, sems.at[k]) for k, (a, b) in enumerate(pairs)]
    for copy in made:
        copy.start()
    return made


def row_of(ref):
    return ref[...].reshape(1, ref.shape[-1])


def split3(v):
    hi = v.astype(bf16).astype(f32)
    rest = v - hi
    mid = rest.astype(bf16).astype(f32)
    return hi, mid, (rest - mid).astype(bf16).astype(f32)


def sine_cosine(angle):
    turns = jnp.floor(angle * (2.0 / math.pi) + 0.5)
    r = ((angle - turns * 1.5703125) - turns * 4.837512969970703125e-4) - turns * 7.54978995489188e-8
    z = r * r
    sine = r + r * z * (-1.6666654611e-1 + z * (8.3321608736e-3 + z * -1.9515295891e-4))
    cosine = 1.0 - 0.5 * z + z * z * (4.166664568298827e-2 + z * (-1.388731625493765e-3 + z * 2.443315711809948e-5))
    quarter = turns - 4.0 * jnp.floor(turns * 0.25)
    odd = (quarter == 1.0) | (quarter == 3.0)
    sin_abs = jnp.where(odd, cosine, sine)
    cos_abs = jnp.where(odd, sine, cosine)
    return jnp.where(quarter >= 2.0, -sin_abs, sin_abs), jnp.where((quarter == 1.0) | (quarter == 2.0), -cos_abs, cos_abs)


def swap_pairs(t):
    rows = lax.broadcasted_iota(jnp.int32, t.shape, 0)
    return jnp.where(rows % 2 == 0, pltpu.roll(t, HD - 1, 0), pltpu.roll(t, 1, 0))


def project_kernel(x_far, seg, wq, bq, wk, bk, wv, bv, slots, x, near, bias0, bias1, bias2, ids, sems):
    pairs = [(x_far, x), (wq, near.at[0]), (bq, bias0), (wk, near.at[1]), (bk, bias1)]
    pairs += [(wv, near.at[2]), (bv, bias2), (seg, ids)]
    loads = copies(pairs, sems)
    for load in loads:
        load.wait()
    flat = x[...].reshape(TOK, D)
    for j, b in enumerate((bias0, bias1, bias2)):
        w = near.at[j]
        bias = jnp.broadcast_to(row_of(b), (T, E)).T
        yt = (dot(w[...], flat, BOTH_LAST) + jnp.concatenate([bias] * R, axis=1)).astype(bf16)
        for r in range(R):
            for h in range(NH):
                slots[r * NH + h, j * HD : (j + 1) * HD, :] = yt[h * HD : (h + 1) * HD, r * T : (r + 1) * T]
    for r in range(R):
        block = jnp.broadcast_to(ids[r : r + 1, :].astype(f32), (16, T)).astype(bf16)
        for h in range(NH):
            slots[r * NH + h, 3 * HD :, :] = block


def stack_kernel(a, b, c, d, out, sems):
    for copy in copies([(part, out.at[s]) for s, part in enumerate((a, b, c, d))], sems):
        copy.wait()


def attend_kernel(
    got, freq, out_far, q_far, k_far, v_far, o_far, cos_far, sin_far,
    out, q_t, k_t, v_t, o_t, cos_t, sin_t, k_nat, sems,
):
    @pl.when(lax.axis_index("wide") < PAIRS)
    def _():
        ids = [got[w, 3 * HD :, :].astype(f32)[0:1, :] for w in range(NW)]
        starts = []
        for d in range(1, 5):
            below = jnp.zeros((1, T), f32)
            for w in range(NW):
                below = below + jnp.where(ids[w] < d, 1.0, 0.0)
            starts.append(jnp.sum(below, axis=1, keepdims=True))
        odd = lax.broadcasted_iota(jnp.int32, (HD, T), 0) % 2 == 1
        ext = lax.broadcasted_iota(jnp.int32, (16, T), 0)
        lane = lax.broadcasted_iota(jnp.int32, (1, T), 1).astype(f32)
        for w in range(NW):
            at = slice(w * T, (w + 1) * T)
            start = jnp.zeros((1, T), f32)
            for d in range(1, 5):
                start = jnp.where(ids[w] == d, starts[d - 1], start)
            sine, cosine = sine_cosine(freq[...] * (lane + (w * T) - start))
            sine = jnp.where(odd, sine, -sine)
            cos_t[:, at] = cosine
            sin_t[:, at] = sine
            query = got[w, 0:HD, :].astype(f32)
            key = got[w, HD : 2 * HD, :].astype(f32)
            query = (query * cosine + swap_pairs(query) * sine) * (HD**-0.5 * LOG2E)
            key = key * cosine + swap_pairs(key) * sine
            same = ids[w] == ext.astype(f32)
            doc = ext < 5
            key_ext = jnp.where(doc, jnp.where(same, 1.0, 0.0), jnp.where(ext < 8, 1.0, 0.0))
            q_t[0:HD, at] = query.astype(bf16)
            q_t[HD:AUG, at] = jnp.where(doc, jnp.where(same, 0.0, -BIG), 0.0).astype(bf16)
            k_t[0:HD, at] = key.astype(bf16)
            k_t[HD:AUG, at] = key_ext.astype(bf16)
            k_nat[at, :] = jnp.concatenate([key, key_ext], axis=0).T.astype(bf16)
            v_t[0:HD, at] = got[w, 2 * HD : 3 * HD, :]
            v_t[HD:AUG, at] = jnp.where(ext < 3, 1.0, 0.0).astype(bf16)

        stores = copies([(k_t, k_far), (v_t, v_far), (cos_t, cos_far), (sin_t, sin_far)], sems)

        def tile(i, carry):
            at = pl.ds(pl.multiple_of(i * 256, 256), 256)
            s = dot(k_nat[...], q_t[:, at], NORMAL)
            top = jnp.max(s, axis=0, keepdims=True)
            p = jnp.exp2(s - top).astype(bf16)
            o = dot(v_t[...], p, NORMAL)
            total = o[HD : HD + 1, :]
            o = o[0:HD, :] / total
            o_t[:, at] = o
            natural = o.T
            for j in range(2 * NN):
                block = natural[j * C : (j + 1) * C, :]
                out[2 * NN * i + j] = jnp.concatenate([block[0 : C // 2], block[C // 2 :]], axis=1).astype(bf16)
            hi, mid, lo = split3(-(top + jnp.log(total) * LOG2E))
            rows = lax.broadcasted_iota(jnp.int32, (16, 256), 0)
            more = jnp.where(rows == 5, hi, jnp.where(rows == 6, mid, jnp.where(rows == 7, lo, 0.0)))
            q_t[HD:AUG, at] = (q_t[HD:AUG, at].astype(f32) + more).astype(bf16)
            return carry

        lax.fori_loop(0, L // 256, tile, 0)
        last = [(out, out_far, 4), (q_t, q_far, 5), (o_t, o_far, 6)]
        last = [pltpu.make_async_copy(a, b, sems.at[k]) for a, b, k in last]
        for store in last:
            store.start()
        for store in stores + last:
            store.wait()


def attend_back_kernel(
    got_far, o_far, q_far, k_far, v_far, cos_far, sin_far, out_far,
    out, got, o_t, q_t, k_t, v_t, cos_t, sin_t, do_t, do_nat, q_nat, k_nat, v_nat, dq_t, sems,
):
    @pl.when(lax.axis_index("wide") < PAIRS)
    def _():
        pairs = [(q_far, q_t), (k_far, k_t), (v_far, v_t), (got_far, got), (o_far, o_t), (cos_far, cos_t), (sin_far, sin_t)]
        loads = copies(pairs, sems)
        for load in loads[:3]:
            load.wait()
        ext = lax.broadcasted_iota(jnp.int32, (16, T), 0)
        for w in range(NW):
            at = slice(w * T, (w + 1) * T)
            q_nat[at, :] = q_t[0:HD, at].astype(f32).T.astype(bf16)
            k_nat[at, :] = k_t[:, at].astype(f32).T.astype(bf16)
            v_nat[at, :] = v_t[:, at].astype(f32).T.astype(bf16)
        for load in loads[3:]:
            load.wait()
        for w in range(NW):
            at = slice(w * T, (w + 1) * T)
            pieces = []
            for n in range(NN):
                piece = got[w * NN + n].astype(f32)
                pieces += [piece[:, 0:HD], piece[:, HD:]]
            natural = jnp.concatenate(pieces, axis=0)
            do_nat[at, :] = natural.astype(bf16)
            grad = natural.T
            delta = -jnp.sum(grad * o_t[:, at], axis=0, keepdims=True)
            hi, mid, lo = split3(delta)
            do_t[0:HD, at] = grad.astype(bf16)
            do_t[HD:AUG, at] = jnp.where(
                ext == 0, hi, jnp.where(ext == 1, mid, jnp.where(ext == 2, lo, 0.0))
            ).astype(bf16)
        dq_t[...] = jnp.zeros((HD, L), f32)

        def folded(t):
            total = t[:, 0:T]
            for k in range(1, t.shape[1] // T):
                total = total + t[:, k * T : (k + 1) * T]
            return total

        def tile(j, carry):
            sum_key, sum_value = carry
            at = pl.ds(pl.multiple_of(j * 256, 256), 256)
            p = jnp.exp2(dot(k_nat[at, :], q_t[...], NORMAL))
            dp = dot(v_nat[at, :], do_t[...], NORMAL)
            ds = (p * dp).astype(bf16)
            dv = dot(p.astype(bf16), do_nat[...], NORMAL).T.astype(bf16)
            dk = dot(ds, q_nat[...], NORMAL).T * LN2
            dk = (dk * cos_t[:, at] - swap_pairs(dk) * sin_t[:, at]).astype(bf16)
            dq_t[...] += dot(k_t[0:HD, at], ds, NORMAL)
            for k in range(2):
                out[2 * j + k, HD : 2 * HD, :] = dk[:, k * T : (k + 1) * T]
                out[2 * j + k, 2 * HD : 3 * HD, :] = dv[:, k * T : (k + 1) * T]
            return sum_key + folded(dk.astype(f32)), sum_value + folded(dv.astype(f32))

        zero = jnp.zeros((HD, T), f32)
        sum_key, sum_value = lax.fori_loop(0, L // 256, tile, (zero, zero))
        sum_query = zero
        stores = []
        for w in range(NW):
            at = slice(w * T, (w + 1) * T)
            dq = dq_t[:, at] * (HD**-0.5)
            dq = (dq * cos_t[:, at] - swap_pairs(dq) * sin_t[:, at]).astype(bf16)
            out[w, 0:HD, :] = dq
            stores += copies([(out.at[w, 0 : 3 * HD, :], out_far.at[w, 0 : 3 * HD, :])], sems.at[w:])
            sum_query = sum_query + dq.astype(f32)
        rows = [jnp.sum(t.T, axis=0, keepdims=True) for t in (sum_query, sum_key, sum_value)]
        first = jnp.concatenate([rows[0], rows[1]], axis=1)
        second = jnp.concatenate([rows[2], rows[2]], axis=1)
        first_hi, second_hi = first.astype(bf16).astype(f32), second.astype(bf16).astype(f32)
        block = jnp.where(
            ext == 0,
            first_hi,
            jnp.where(ext == 1, second_hi, jnp.where(ext == 2, first - first_hi, second - second_hi)),
        )
        block = jnp.where(ext < 4, block, 0.0).astype(bf16)
        for w in range(NW):
            out[w, 3 * HD :, :] = block
        for store in stores:
            store.wait()
        stores = copies([(out.at[:, 3 * HD :, :], out_far.at[:, 3 * HD :, :])], sems)
        stores[0].wait()


def chunk_rows(c, r):
    return pl.ds(pl.multiple_of(r * T + c * C, C), C)


def row_mean(t):
    return jnp.mean(t, axis=-1, keepdims=True)


def column_sum(t):
    return jnp.sum(t, axis=0, keepdims=True)


def gelu_and_slope(pre):
    half = 0.5 * (1.0 + lax.erf(pre * (2.0**-0.5)))
    return (pre * half).astype(bf16), half + pre * jnp.exp(-0.5 * pre * pre) * (1.0 / math.sqrt(2.0 * math.pi))


ATTN, NORMED, FIRST = 0, 32, 128
FFN, OUT, SUMS, LAST = 0, 96, 192, 208


def first_kernel(
    w0, m1, m2, m3, u1, u2, u3, x, attn, b_out, g_one, s_one, w_out_far, state_far, pack0, pack1, pack2, pack3,
    w_out, state, heads, packs, sems,
):
    n, c = lax.axis_index("narrow"), lax.axis_index("dp")
    pairs = [(w0, w_out.at[0:E, :])]
    for s, (mine, other) in enumerate(((m1, u1), (m2, u2), (m3, u3)), 1):
        for source, core in ((mine, c), (other, 1 - c)):
            pairs.append((source, w_out.at[pl.ds(pl.multiple_of(s * E + core * (E // 2), E // 2), E // 2), :]))
    loads = copies(pairs, sems)
    for s in range(NN):
        for r in range(R):
            for h in range(NH):
                block = attn[(r * NH + h) * NN + (n + NN - s) % NN]
                at = s * E + h * HD
                heads[r * C : r * C + C // 2, at : at + HD] = block[:, 0:HD]
                heads[r * C + C // 2 : (r + 1) * C, at : at + HD] = block[:, HD:]
    mine = pl.ds(pl.multiple_of(n * C, C), C)
    tokens = jnp.concatenate([x[r, mine, :] for r in range(R)], axis=0).astype(f32)
    for load in loads:
        load.wait()
    stores = copies([(w_out, w_out_far)], sems.at[5:])
    residual = tokens + (dot(heads[...], w_out[...], NORMAL) + row_of(b_out))
    center = residual - row_mean(residual)
    rstd = lax.rsqrt(row_mean(center * center) + EPSILON)
    unit = center * rstd
    state[:, 0:D] = unit
    state[:, D:] = jnp.broadcast_to(rstd, (CH, T))
    stores += copies([(state, state_far)], sems.at[4:])
    low = (unit * row_of(g_one) + row_of(s_one)).astype(bf16)
    for s, pack in enumerate((pack0, pack1, pack2, pack3)):
        packs[s, NORMED:FIRST, :] = low
        for r in range(R):
            packs[s, ATTN:NORMED, 256 * r : 256 * r + E] = heads[r * C : (r + 1) * C, s * E : (s + 1) * E]
        stores.append(pltpu.make_async_copy(packs.at[s], pack, sems.at[s]))
        stores[-1].start()
    for store in stores:
        store.wait()


def middle_kernel(
    every_far, state_far, cot_far, w_out_far, g_one, s_one, b0, b1, b2, b3, b_down, g_two, s_two,
    slots_far, one_far, pack_far, layer_far,
    state, cot, w_out, weights, slope, grad_one, slots, pack, layer, sems,
):
    n = lax.axis_index("narrow")
    first = copies([(state_far, state), (cot_far, cot), (w_out_far, w_out)], sems.at[8:])
    pairs = [(every_far.at[which, :, s], weights.at[which, s]) for which in range(2) for s in range(NN)]
    loads = copies(pairs, sems)
    for load in first:
        load.wait()
    mine = pl.ds(pl.multiple_of(n * C, C), C)
    ct = jnp.concatenate([cot[r, mine, :] for r in range(R)], axis=0).astype(f32)
    unit, rstd = state[:, 0:D], state[:, D : D + 1]
    normed = unit * row_of(g_one) + row_of(s_one)
    low = normed.astype(bf16)

    def weight(which, s):
        return weights[which, s].reshape(D, F)

    total = None
    for s, b in enumerate((b0, b1, b2, b3)):
        loads[s].wait()
        hidden, slope[s] = gelu_and_slope(dot(low, weight(0, s), NORMAL) + row_of(b))
        loads[NN + s].wait()
        term = dot(hidden, weight(1, s), BOTH_LAST)
        total = term if s == 0 else total + term
    residual = normed + (total + row_of(b_down))
    center = residual - row_mean(residual)
    rstd_two = lax.rsqrt(row_mean(center * center) + EPSILON)
    unit_two = center * rstd_two
    layer[...] = (unit_two * row_of(g_two) + row_of(s_two)).astype(bf16)
    scaled = ct * row_of(g_two)
    grad_two = rstd_two * (scaled - row_mean(scaled) - unit_two * row_mean(scaled * unit_two))
    low_two = grad_two.astype(bf16)
    pack[FFN:OUT, :] = low_two
    total = None
    for s in range(NN):
        pre = (slope[s] * dot(low_two, weight(1, s), NORMAL)).astype(bf16)
        term = dot(pre, weight(0, s), BOTH_LAST)
        total = term if s == 0 else total + term
    grad = grad_two + total
    scaled = grad * row_of(g_one)
    one = rstd * (scaled - row_mean(scaled) - unit * row_mean(scaled * unit))
    grad_one[...] = one
    low_one = one.astype(bf16)
    every = dot(low_one, w_out[...], BOTH_LAST)
    for s in range(NN):
        for r in range(R):
            for h in range(NH):
                block = every[r * C : (r + 1) * C, s * E + h * HD : s * E + (h + 1) * HD]
                slot = jnp.concatenate([block[0 : C // 2], block[C // 2 :]], axis=1).astype(bf16)
                slots[(r * NH + h) * NN + (n + NN - s) % NN] = slot
    stores = copies([(slots, slots_far), (grad_one, one_far), (layer, layer_far)], sems)
    pack[OUT:SUMS, :] = low_one
    sums = [ct * unit_two, ct, low_two.astype(f32), grad * unit, grad, low_one.astype(f32)]
    pack[SUMS:LAST, :] = jnp.concatenate([column_sum(t) for t in sums] + [jnp.zeros((10, D), f32)], axis=0).astype(bf16)
    stores += copies([(pack, pack_far)], sems.at[3:])
    for store in stores:
        store.wait()


def halves(whole, send, send_far, keep_far, sems):
    c = lax.axis_index("dp")
    half = D // 2
    send[0:half, :] = whole[pl.ds(pl.multiple_of((1 - c) * half, half), half), :].astype(bf16)
    return copies([(send, send_far), (whole.at[pl.ds(pl.multiple_of(c * half, half), half), :], keep_far)], sems)


def hidden_kernel(a0, a1, a2, a3, every_far, b_up, hidden_far, slope_far, firsts, weights, hidden, slope, sems):
    pairs = [(p, firsts.at[s]) for s, p in enumerate((a0, a1, a2, a3))] + [(every_far.at[0, :, 0], weights)]
    for load in copies(pairs, sems):
        load.wait()
    normed = firsts[:, NORMED:FIRST, :].reshape(TOK, D)
    act, slant = gelu_and_slope(dot(normed, weights[...].reshape(D, F), NORMAL) + row_of(b_up))
    hidden[...] = act
    slope[...] = slant
    for store in copies([(hidden, hidden_far), (slope, slope_far)], sems):
        store.wait()


def weights_kernel(
    a0, a1, a2, a3, p0, p1, p2, p3, every_far, hidden_far, slope_far,
    send0_far, send1_far, send2_far, send3_far, keep_far, out_whole, sums,
    firsts, packs, weights, hidden, slope, whole, send, vectors, sems,
):
    n, c = lax.axis_index("narrow"), lax.axis_index("dp")
    pairs = [(every_far.at[1, :, 0], weights), (slope_far, slope)]
    pairs += [(p, packs.at[s]) for s, p in enumerate((p0, p1, p2, p3))]
    pairs += [(p, firsts.at[s]) for s, p in enumerate((a0, a1, a2, a3))] + [(hidden_far, hidden)]
    loads = copies(pairs, sems)
    for load in loads[:6]:
        load.wait()
    grad_ffn = packs[:, FFN:OUT, :].reshape(TOK, D)
    pre = (slope[...] * dot(grad_ffn, weights[...].reshape(D, F), NORMAL)).astype(bf16)
    for load in loads[6:]:
        load.wait()
    whole[:, 0:F] = dot(firsts[:, NORMED:FIRST, :].reshape(TOK, D), pre, BOTH_FIRST)
    whole[:, F:] = dot(grad_ffn, hidden[...], BOTH_FIRST)
    half = D // 2
    send[...] = whole[pl.ds(pl.multiple_of((1 - c) * half, half), half), :].astype(bf16)
    pairs = [(send.at[96 * k : 96 * (k + 1), :], far) for k, far in enumerate((send0_far, send1_far, send2_far, send3_far))]
    stores = copies([*pairs, (whole.at[pl.ds(pl.multiple_of(c * half, half), half), :], keep_far)], sems)
    heads = [firsts[s, ATTN:NORMED, 256 * r : 256 * r + E] for s in range(NN) for r in range(R)]
    out_whole[...] = dot(packs[:, OUT:SUMS, :].reshape(TOK, D), jnp.concatenate(heads, axis=0), BOTH_FIRST)
    for s in range(NN):
        vectors[(n + NN - s) % NN] = packs[s, SUMS:LAST, :].astype(f32)[0:8, :]
    total = vectors[0] + vectors[1] + vectors[2] + vectors[3]
    row = lax.broadcasted_iota(jnp.int32, (8, D), 0)
    sums[...] = jnp.where(row == 6, column_sum(pre.astype(f32)), total)
    for store in stores:
        store.wait()


def weights_add_kernel(keep_far, got0, got1, got2, got3, slots_far, keep, got, slots, sems):
    pairs = [(far, got.at[96 * k : 96 * (k + 1), :]) for k, far in enumerate((got0, got1, got2, got3))]
    for load in copies([(keep_far, keep), *pairs], sems):
        load.wait()
    both = (keep[...] + got[...].astype(f32)).astype(bf16)
    stores = []
    for w in range(NW):
        slots[w] = both[w * G : (w + 1) * G, :]
        stores.append(pltpu.make_async_copy(slots.at[w], slots_far.at[w, :, 0 : 2 * F], sems.at[w]))
        stores[w].start()
    for store in stores:
        store.wait()


def input_back_kernel(
    x_far, wq, wk, wv, got, out_whole, vec, part0_far, part1_far, part2_far, part3_far, send_far, keep_far, sums,
    part0, part1, part2, part3, whole, send, wide_part, x, near, sems,
):
    n = lax.axis_index("narrow")
    loads = copies([(x_far, x), (wq, near.at[0]), (wk, near.at[1]), (wv, near.at[2])], sems)
    grads = []
    for j in range(3):
        grad_t = jnp.concatenate(
            [
                jnp.concatenate([got[r * NH + h, j * HD : (j + 1) * HD, :] for h in range(NH)], axis=0)
                for r in range(R)
            ],
            axis=1,
        )
        grads.append(grad_t.astype(f32).T.astype(bf16))
    grad = jnp.concatenate(grads, axis=1)
    whole[:, 3 * E :] = out_whole[...]
    loads[0].wait()
    whole[:, 0 : 3 * E] = dot(x[...].reshape(TOK, D), grad, BOTH_FIRST)
    for load in loads[1:]:
        load.wait()
    wide_part[...] = dot(grad, near[...].reshape(3 * E, D), NORMAL)
    for r in range(R):
        to = slice(r * C, (r + 1) * C)
        part0[to, :] = wide_part[chunk_rows(n, r), :]
        for s, part in ((1, part1), (2, part2), (3, part3)):
            part[to, :] = wide_part[chunk_rows((n + s) % NN, r), :].astype(bf16)
    pairs = [(part0, part0_far), (part1, part1_far), (part2, part2_far), (part3, part3_far)]
    stores = copies(pairs, sems)
    heads = []
    for h in range(NH):
        block = got[h, 3 * HD :, :].astype(f32)
        for r in range(1, R):
            block = block + got[r * NH + h, 3 * HD :, :].astype(f32)
        heads.append(block)
    first = jnp.concatenate([b[0:1, 0:HD] + b[2:3, 0:HD] for b in heads], axis=1)
    second = jnp.concatenate([b[0:1, HD:] + b[2:3, HD:] for b in heads], axis=1)
    third = jnp.concatenate([b[1:2, 0:HD] + b[3:4, 0:HD] for b in heads], axis=1)
    row = jnp.concatenate([first, second, third], axis=1)
    sums[...] = row
    hi, mid, lo = split3(jnp.concatenate([row, jnp.zeros((1, E), f32)], axis=1))
    send[D // 2 :, :] = jnp.concatenate([vec[...], hi, mid, lo, jnp.zeros((5, D), f32)], axis=0).astype(bf16)
    for store in stores + halves(whole, send, send_far, keep_far, sems.at[4:]):
        store.wait()


def input_add_kernel(keep_far, got_far, slots_in, sums, vec, slots_far, b_q, b_k, b_v, keep, got, slots, sems):
    for load in copies([(keep_far, keep), (got_far, got)], sems):
        load.wait()
    both = (keep[...] + got[0 : D // 2, :].astype(f32)).astype(bf16)
    more = got[D // 2 :, :].astype(f32)
    rows = vec[...].astype(bf16).astype(f32) + more[0:8, :]
    lanes = D // 3
    rows = jnp.concatenate([rows[:, lanes * k : lanes * (k + 1)] for k in range(3)], axis=0).astype(bf16)
    stores = []
    for w in range(NW):
        slots[w] = jnp.concatenate([both[w * G : (w + 1) * G, :], rows], axis=1)
        stores.append(pltpu.make_async_copy(slots.at[w], slots_far.at[w, :, 2 * F :], sems.at[w]))
        stores[w].start()
    hi, mid, lo = split3(sums[...])
    bias = more[:, 0 : 3 * E]
    total = (hi + bias[8:9, :]) + ((mid + bias[9:10, :]) + (lo + bias[10:11, :]))
    for k, ref in enumerate((b_q, b_k, b_v)):
        ref[...] = total[:, k * E : (k + 1) * E].reshape(E)
    for store in stores:
        store.wait()


def input_sum_kernel(got, g_up, g_down, g_q, g_k, g_v, g_out, g_two, s_two, b_down, g_one, s_one, b_out, b_up):
    total = got[0].astype(f32)
    for w in range(1, NW):
        total = total + got[w].astype(f32)
    g_up[...] = total[:, 0:F]
    g_down[...] = total[:, F : 2 * F]
    for k, ref in enumerate((g_q, g_k, g_v, g_out)):
        ref[...] = total[:, 2 * F + k * E : 2 * F + (k + 1) * E]
    vec = jnp.concatenate([total[8 * k : 8 * (k + 1), 2 * F + D :] for k in range(3)], axis=1)
    for k, ref in enumerate((g_two, s_two, b_down, g_one, s_one, b_out, b_up)):
        ref[...] = vec[k : k + 1, :].reshape(D)


def input_chunk_kernel(part_far, one_far, part1, part2, part3, low, part0, grad_one, sems):
    for load in copies([(part_far, part0), (one_far, grad_one)], sems):
        load.wait()
    total = part0[...] + part1[...].astype(f32) + part2[...].astype(f32) + part3[...].astype(f32)
    low[...] = (grad_one[...] + total).astype(bf16)


def spread_kernel(g0, g1, g2, g3, out):
    n = lax.axis_index("narrow")
    for s, part in enumerate((g0, g1, g2, g3)):
        at = pl.ds(pl.multiple_of((n + NN - s) % NN * C, C), C)
        for r in range(R):
            out[r, at, :] = part[r * C : (r + 1) * C, :].astype(f32)


def shifted(x, s):
    return lax.ppermute(x, "narrow", [(i, (i + s) % NN) for i in range(NN)])


def gather_narrow(x):
    return (x, shifted(x, 1), shifted(x, 2), shifted(x, 3))


def scatter_narrow(parts):
    return (parts[0], shifted(parts[1], 1), shifted(parts[2], 2), shifted(parts[3], 3))


def other_core(x):
    return lax.ppermute(x, "dp", [(0, 1), (1, 0)])


def exchange(slots):
    return lax.all_to_all(slots, "wide", 0, 0, tiled=True)


def exchange_all(slots):
    return lax.all_to_all(slots, ("wide", "narrow"), 0, 0, tiled=True)


def body(
    hidden_in, segments, weight_query, bias_query, weight_key, bias_key, weight_value, bias_value,
    weight_out, bias_out, gain_one, shift_one, weight_up, bias_up, weight_down, bias_down,
    gain_two, shift_two, cotangent,
):
    frequency = np.repeat(np.power(10000.0, -np.arange(0, HD, 2) / HD), 2).astype(np.float32)
    frequency = jnp.asarray(np.broadcast_to(frequency[:, None], (HD, T)))
    shard = jnp.where(lax.axis_index("dp") == 0, weight_up, weight_down.T)
    shards = gather_narrow(shard)
    mine = lax.dynamic_slice_in_dim(weight_out, lax.axis_index("dp") * (E // 2), E // 2, 0)
    weights_got = gather_narrow(mine)[1:]
    weights_out = (weight_out, *weights_got, *(other_core(w) for w in weights_got))
    biases_up = gather_narrow(bias_up)
    query_t, key_t, value_t = weight_query.T, weight_key.T, weight_value.T

    slots, token = call(
        "project",
        project_kernel,
        [((NW, SLOT, T), bf16)],
        (hidden_in, segments, query_t, bias_query, key_t, bias_key, value_t, bias_value),
        scratch=[
            pltpu.VMEM((R, T, D), bf16),
            pltpu.VMEM((3, E, D), bf16),
            pltpu.VMEM((E,), f32),
            pltpu.VMEM((E,), f32),
            pltpu.VMEM((E,), f32),
            pltpu.VMEM((R, T), jnp.int32),
            pltpu.SemaphoreType.DMA((8,)),
        ],
        far_in=range(8),
        token=True,
    )
    (shards,) = call(
        "stack",
        stack_kernel,
        [((NN, D // NW, F), bf16)],
        shards,
        scratch=[pltpu.SemaphoreType.DMA((NN,))],
        any_in=range(NN),
        far=(0,),
        after=(token,),
    )
    every = lax.all_gather(shards, ("dp", "wide")).reshape(2, NW, NN, D // NW, F)
    got = exchange(slots)
    out_slots, q_t, k_t, v_t, o_t, cos_t, sin_t = call(
        "attend",
        attend_kernel,
        [
            ((NW * NN, C // 2, 2 * HD), bf16),
            ((AUG, L), bf16),
            ((AUG, L), bf16),
            ((AUG, L), bf16),
            ((HD, L), f32),
            ((HD, L), f32),
            ((HD, L), f32),
        ],
        (got, frequency),
        scratch=[
            pltpu.VMEM((NW * NN, C // 2, 2 * HD), bf16),
            pltpu.VMEM((AUG, L), bf16),
            pltpu.VMEM((AUG, L), bf16),
            pltpu.VMEM((AUG, L), bf16),
            pltpu.VMEM((HD, L), f32),
            pltpu.VMEM((HD, L), f32),
            pltpu.VMEM((HD, L), f32),
            pltpu.VMEM((L, AUG), bf16),
            pltpu.SemaphoreType.DMA((7,)),
        ],
        after=weights_got,
        far=range(7),
    )
    attn = exchange_all(out_slots)
    chunk_f32, chunk_low = ((CH, D), f32), ((CH, D), bf16)
    parts4 = [chunk_f32, chunk_low, chunk_low, chunk_low]
    slot_shape = (NW * NN, C // 2, 2 * HD)
    w_out, state, *firsts, token = call(
        "first",
        first_kernel,
        [((D, D), bf16), ((CH, D + T), f32)] + [((FIRST, D), bf16)] * NN,
        (*weights_out, hidden_in, attn, bias_out, gain_one, shift_one),
        scratch=[
            pltpu.VMEM((D, D), bf16),
            pltpu.VMEM((CH, D + T), f32),
            pltpu.VMEM((CH, D), bf16),
            pltpu.VMEM((NN, FIRST, D), bf16),
            pltpu.SemaphoreType.DMA((7,)),
        ],
        far_in=range(7),
        far=range(6),
        token=True,
        after=biases_up[1:],
    )
    firsts = (firsts[0], *(shifted(firsts[s], NN - s) for s in range(1, NN)))
    every = later(every, token)
    slots, grad_one, pack, layer = call(
        "middle",
        middle_kernel,
        [(slot_shape, bf16), chunk_f32, ((LAST, D), bf16), chunk_low],
        (every, state, cotangent, w_out, gain_one, shift_one, *biases_up, bias_down, gain_two, shift_two),
        scratch=[
            pltpu.VMEM((CH, D + T), f32),
            pltpu.VMEM((R, T, D), bf16),
            pltpu.VMEM((D, D), bf16),
            pltpu.VMEM((2, NN, NW, D // NW, F), bf16),
            pltpu.VMEM((NN, CH, F), f32),
            pltpu.VMEM((CH, D), f32),
            pltpu.VMEM(slot_shape, bf16),
            pltpu.VMEM((LAST, D), bf16),
            pltpu.VMEM((CH, D), bf16),
            pltpu.SemaphoreType.DMA((11,)),
        ],
        mib=32,
        far_in=range(4),
        far=range(4),
    )
    got = exchange_all(later(slots, *firsts[1:]))
    packs = gather_narrow(pack)
    firsts = (firsts[0], firsts[3], firsts[2], firsts[1])
    hidden, slope, token = call(
        "hidden",
        hidden_kernel,
        [((TOK, F), bf16), ((TOK, F), f32)],
        (*firsts, every, bias_up),
        scratch=[
            pltpu.VMEM((NN, FIRST, D), bf16),
            pltpu.VMEM((NW, D // NW, F), bf16),
            pltpu.VMEM((TOK, F), bf16),
            pltpu.VMEM((TOK, F), f32),
            pltpu.SemaphoreType.DMA((5,)),
        ],
        far_in=range(5),
        far=(0, 1),
        token=True,
    )
    slots, token = call(
        "attend_back",
        attend_back_kernel,
        [((NW, SLOT, T), bf16)],
        (got, o_t, q_t, k_t, v_t, cos_t, sin_t),
        scratch=[
            pltpu.VMEM((NW, SLOT, T), bf16),
            pltpu.VMEM((NW * NN, C // 2, 2 * HD), bf16),
            pltpu.VMEM((HD, L), f32),
            pltpu.VMEM((AUG, L), bf16),
            pltpu.VMEM((AUG, L), bf16),
            pltpu.VMEM((AUG, L), bf16),
            pltpu.VMEM((HD, L), f32),
            pltpu.VMEM((HD, L), f32),
            pltpu.VMEM((AUG, L), bf16),
            pltpu.VMEM((L, HD), bf16),
            pltpu.VMEM((L, HD), bf16),
            pltpu.VMEM((L, AUG), bf16),
            pltpu.VMEM((L, AUG), bf16),
            pltpu.VMEM((HD, L), f32),
            pltpu.SemaphoreType.DMA((NW,)),
        ],
        far_in=range(7),
        far=(0,),
        after=(token, *packs[1:]),
        token=True,
    )
    layers = gather_narrow(later(layer, token))
    whole_out = ((R, T, D), f32)
    *sends, up_keep, out_whole, vec = call(
        "weights",
        weights_kernel,
        [((96, 2 * F), bf16)] * 4 + [((D // 2, 2 * F), f32), ((D, E), f32), ((8, D), f32)],
        (*firsts, *packs, every, hidden, slope),
        scratch=[
            pltpu.VMEM((NN, FIRST, D), bf16),
            pltpu.VMEM((NN, LAST, D), bf16),
            pltpu.VMEM((NW, D // NW, F), bf16),
            pltpu.VMEM((TOK, F), bf16),
            pltpu.VMEM((TOK, F), f32),
            pltpu.VMEM((D, 2 * F), f32),
            pltpu.VMEM((D // 2, 2 * F), bf16),
            pltpu.VMEM((NN, 8, D), f32),
            pltpu.SemaphoreType.DMA((11,)),
        ],
        mib=32,
        far_in=range(11),
        far=range(5),
        after=(token,),
    )
    slots_shape = ((NW, G, 2 * F + D + D // 3), bf16)
    last_slots, added = call(
        "weights_add",
        weights_add_kernel,
        [slots_shape],
        (up_keep, *(other_core(send) for send in sends)),
        scratch=[
            pltpu.VMEM((D // 2, 2 * F), f32),
            pltpu.VMEM((D // 2, 2 * F), bf16),
            pltpu.VMEM((NW, G, 2 * F), bf16),
            pltpu.SemaphoreType.DMA((NW,)),
        ],
        far_in=range(5),
        far=(0,),
        token=True,
    )

    got = exchange(slots)
    *parts, send, keep, sums = call(
        "input_back",
        input_back_kernel,
        [*parts4, ((D // 2 + 16, D), bf16), ((D // 2, D), f32), ((1, 3 * E), f32)],
        (hidden_in, query_t, key_t, value_t, got, out_whole, vec),
        scratch=[
            pltpu.VMEM((CH, D), f32),
            pltpu.VMEM((CH, D), bf16),
            pltpu.VMEM((CH, D), bf16),
            pltpu.VMEM((CH, D), bf16),
            pltpu.VMEM((D, D), f32),
            pltpu.VMEM((D // 2 + 16, D), bf16),
            pltpu.VMEM((TOK, D), f32),
            pltpu.VMEM((R, T, D), bf16),
            pltpu.VMEM((3, E, D), bf16),
            pltpu.SemaphoreType.DMA((6,)),
        ],
        far_in=range(4),
        far=range(6),
        after=(added, *layers[1:]),
    )
    parts = scatter_narrow(parts)
    slots, b_query, b_key, b_value = call(
        "input_add",
        input_add_kernel,
        [slots_shape, ((E,), f32), ((E,), f32), ((E,), f32)],
        (keep, other_core(send), last_slots, sums, vec),
        scratch=[
            pltpu.VMEM((D // 2, D), f32),
            pltpu.VMEM((D // 2 + 16, D), bf16),
            pltpu.VMEM((NW, G, D + D // 3), bf16),
            pltpu.SemaphoreType.DMA((NW,)),
        ],
        any_in=(1,),
        far_in=(0, 2),
        far=(0,),
        aliases={2: 0},
    )
    (input_low,) = call("input_chunk", input_chunk_kernel, [chunk_low], (parts[0], grad_one, *parts[1:]),
        scratch=[pltpu.VMEM((CH, D), f32), pltpu.VMEM((CH, D), f32), pltpu.SemaphoreType.DMA((2,))],
        cost=COST, far_in=(0, 1),
    )
    (layer_out,) = call("layer_out", spread_kernel, [whole_out], layers)
    (grad_input,) = call("grad_input", spread_kernel, [whole_out], gather_narrow(input_low))
    flat = ((D,), f32)
    grad_up, grad_down, g_query, g_key, g_value, g_out, g_two, s_two, b_down, g_one, s_one, b_out, b_up = call(
        "input_sum", input_sum_kernel, [((G, F), f32)] * 2 + [((G, E), f32)] * 4 + [flat] * 7, (exchange(slots),)
    )
    return (
        layer_out, grad_input, g_query, b_query, g_key, b_key, g_value, b_value, g_out.T, b_out,
        g_one, s_one, grad_up, b_up, grad_down.T, b_down, g_two, s_two,
    )


def solution(mesh):
    tokens, whole = P("dp", "wide", None), P()
    column, vector = P(None, "narrow"), P("narrow")
    rows_split, columns_split = P(("dp", "wide"), "narrow"), P("narrow", ("dp", "wide"))
    in_specs = (
        tokens, P("dp", "wide"), column, vector, column, vector, column, vector, P("narrow", None), whole,
        whole, whole, P("wide", "narrow"), vector, P("narrow", "wide"), whole, whole, whole, tokens,
    )
    out_specs = (
        tokens, tokens, rows_split, vector, rows_split, vector, rows_split, vector, columns_split, whole,
        whole, whole, rows_split, vector, columns_split, whole, whole, whole,
    )
    return jax.shard_map(body, mesh=mesh, in_specs=in_specs, out_specs=out_specs, check_vma=False)
```

time: 241 us -> 211 us (0.88)
  Pallas kernels: 46.8 us -> 71.8 us
  waiting for transfers between devices: 71.7 us -> 54.6 us
  local copies, waits for them, and re-layouts: 20.2 us -> 3.16 us
  blocking collectives: 13.5 us -> 0 us
  starting transfers between devices: 70.5 us -> 64.8 us
    pallas_call x17 -> x18, Pallas kernels: 46.8 us -> 71.8 us  [the longest x15 71.8 us: call(): pl.pallas_call(run, out_shape=[shape(k, s, t) for k, (s, t) in enumerate(...]
    ppermute x30 -> x24, waiting for transfers between devices: 44 us -> 23.2 us  [shifted(): return lax.ppermute(x, 'narrow', [(i, (i + s) % NN) for i in range(NN)])]
    unnamed x101 -> x60, local copies, waits for them, and re-layouts: 20.2 us -> 3.07 us
    all_to_all x1 -> x0, blocking collectives: 13.5 us -> none  [exchange(): return lax.all_to_all(slots, 'wide', 0, 0, tiled=True)]
    all_to_all x0 -> x2, starting transfers between devices: none -> 13.5 us  [exchange_all(): return lax.all_to_all(slots, ('wide', 'narrow'), 0, 0, tiled=True)]
    ppermute x30 -> x24, starting transfers between devices: 44.6 us -> 31.3 us  [shifted(): return lax.ppermute(x, 'narrow', [(i, (i + s) % NN) for i in range(NN)])]
    all_to_all x0 -> x2, waiting for transfers between devices: none -> 9.5 us  [exchange_all(): return lax.all_to_all(slots, ('wide', 'narrow'), 0, 0, tiled=True)]
    all_to_all x5 -> x3, starting transfers between devices: 25.2 us -> 18.1 us  [exchange(): return lax.all_to_all(slots, 'wide', 0, 0, tiled=True)]
  transfers between devices with their start and end apart: 40 -> 38, of which waited for: 23 -> 18; matrix products, arithmetic and copies ran while one was open for 1% -> 0% of each run, Pallas kernels for 11% -> 24%
where the time goes in v2:
time: 211 us; the launch traced here: 210 us
  Pallas kernels  71.8 us (34%)
  starting transfers between devices  64.8 us (31%)
  waiting for transfers between devices  54.6 us (26%)
  between operations  14.6 us (7%)
  local copies, waits for them, and re-layouts  3.16 us (1%)
    pallas_call x15, Pallas kernels, call(): pl.pallas_call(run, out_shape=[shape(k, s, t) for k, (s, t) in enumerate(...  71.8 us
    ppermute x24, starting transfers between devices, shifted(): return lax.ppermute(x, 'narrow', [(i, (i + s) % NN) for i in range(NN)])  31.3 us
    ppermute x24, waiting for transfers between devices, shifted(): return lax.ppermute(x, 'narrow', [(i, (i + s) % NN) for i in range(NN)])  23.2 us
    all_to_all x3, waiting for transfers between devices, exchange(): return lax.all_to_all(slots, 'wide', 0, 0, tiled=True)  21.9 us
    all_to_all x3, starting transfers between devices, exchange(): return lax.all_to_all(slots, 'wide', 0, 0, tiled=True)  18.1 us
    all_to_all x2, starting transfers between devices, exchange_all(): return lax.all_to_all(slots, ('wide', 'narrow'), 0, 0, tiled=True)  13.5 us
    all_to_all x2, waiting for transfers between devices, exchange_all(): return lax.all_to_all(slots, ('wide', 'narrow'), 0, 0, tiled=True)  9.5 us
  transfers between devices with their start and end apart: 38, of which 18 were waited for; matrix products, arithmetic and copies ran while one was open for 0% of the time, Pallas kernels for 24%

profile of v2, /device:TPU:0, one launch (start us, length us, event | category | flops | bytes accessed | tf_op | source)
XLA Modules:
  0.0 209.8 jit_solution(10065446473089674985)
XLA Ops:
  7.2 0.9 bitcast_select_fusion.refs_0_
  8.2 4.2 %collective-permute-start.2 = (bf16[48,768]{1,0:T(8,128)(2,1)S(1)}, bf16[48,768]{1,0:T(8,128)(2,1)S(1)}, u32[]{:S(2)}, u32[]{:S(2)}) collective-permute-start(bf16[48,768]{1,0:T(8,128)(2,1)S(1)} %bitcast_select_fusion.refs_0_), channel_id=1, source_target_pairs={{0,3},{1,0},{2,1},{3,2},{4,7},{5,4},{6,5},{7,6},{8,11},{9,8},{10,9... | collective-permute-start | bytes 221192 | tf_op jit(solution)/shard_map/ppermute | solution.py:595
  12.4 1.3 collective-permute-start
  13.6 3.1 %project.1 = (bf16[16,208,128]{2,1,0:T(8,128)(2,1)}, f32[8,128]{1,0:T(8,128)S(1)}) custom-call(bf16[3,128,768]{2,1,0:T(8,128)(2,1)} %refs_0_.5, s32[3,128]{1,0:T(4,128)} %refs_1_.2, bf16[192,768]{1,0:T(8,128)(2,1)} %bitcast.9, f32[192]{0:T(256)} %refs_3_.1, bf16[192,768]{1,0:T(8,128)(2,1)} %bitcast.11, f32[192]{0:T(256)} %refs_5_.3, ...), custom_call_target="tpu_custom_call" | custom-call | flops 1024 | bytes 1024 | tf_op jit(solution)/shard_map/project/pallas_call | solution.py:63
  16.8 1.6 collective-permute-done.1.refs_2_
  18.4 0.4 collective-permute-done.refs_1_
  18.9 0.8 stack.1
  19.7 7.2 %all-to-all-start = ((bf16[16,208,128]{2,1,0:T(8,128)(2,1)}), bf16[16,208,128]{2,1,0:T(8,128)(2,1)S(1)}, u32[]{:S(2)}, u32[]{:S(2)}) async-start(bf16[16,208,128]{2,1,0:T(8,128)(2,1)} %get-tuple-element.77), calls=%async_computation | async-start | bytes 1703936 | tf_op jit(solution)/shard_map/all_to_all | solution.py:611
  27.0 0.9 collective-permute-start.5
  27.9 1.4 collective-permute-start.4
  29.2 0.6 collective-permute-start.3
  29.8 2.8 %collective-permute-done.5.refs_4_.refs_3_ = bf16[96,768]{1,0:T(8,128)(2,1)S(1)} collective-permute-done((bf16[96,768]{1,0:T(8,128)(2,1)S(1)}, bf16[96,768]{1,0:T(8,128)(2,1)S(1)}, u32[]{:S(2)}, u32[]{:S(2)}) %collective-permute-start.5) | collective-permute-done | bytes 147488 | tf_op jit(solution)/shard_map/ppermute | solution.py:595
  32.7 2.2 %collective-permute-done.4.refs_3_.refs_2_ = bf16[96,768]{1,0:T(8,128)(2,1)S(1)} collective-permute-done((bf16[96,768]{1,0:T(8,128)(2,1)S(1)}, bf16[96,768]{1,0:T(8,128)(2,1)S(1)}, u32[]{:S(2)}, u32[]{:S(2)}) %collective-permute-start.4) | collective-permute-done | bytes 147488 | tf_op jit(solution)/shard_map/ppermute | solution.py:595
  34.8 1.5 collective-permute-done.3.refs_2_.refs_1_
  36.3 6.1 %all-to-all-done.refs_0_ = bf16[16,208,128]{2,1,0:T(8,128)(2,1)S(1)} async-done(((bf16[16,208,128]{2,1,0:T(8,128)(2,1)}), bf16[16,208,128]{2,1,0:T(8,128)(2,1)S(1)}, u32[]{:S(2)}, u32[]{:S(2)}) %all-to-all-start) | async-done | bytes 852000 | tf_op jit(solution)/shard_map/all_to_all | solution.py:611
  42.5 13.4 %attend.1 = (bf16[64,16,128]{2,1,0:T(8,128)(2,1)}, bf16[80,2048]{1,0:T(8,128)(2,1)}, bf16[80,2048]{1,0:T(8,128)(2,1)}, bf16[80,2048]{1,0:T(8,128)(2,1)}, f32[64,...) custom-call(bf16[16,208,128]{2,1,0:T(8,128)(2,1)S(1)} %all-to-all-done.refs_0_, ...), custom_call_target="tpu_custom_call" | custom-call | flops 1024 | bytes 1024 | tf_op jit(solution)/shard_map/attend/pallas_call | solution.py:63
  55.9 5.2 %all-to-all-start.1 = ((bf16[64,16,128]{2,1,0:T(8,128)(2,1)}), bf16[64,16,128]{2,1,0:T(8,128)(2,1)S(1)}, u32[]{:S(2)}, u32[]{:S(2)}) async-start(bf16[64,16,128]{2,1,0:T(8,128)(2,1)} %get-tuple-element.78), calls=%async_computation.1 | async-start | bytes 524288 | tf_op jit(solution)/shard_map/all_to_all | solution.py:615
  61.2 0.5 collective-permute-start.7
  61.8 2.8 %collective-permute-start.11 = (f32[768]{0:T(1024)S(1)}, f32[768]{0:T(1024)S(1)}, u32[]{:S(2)}, u32[]{:S(2)}) collective-permute-start(f32[768]{0:T(1024)S(1)} %copy-done.10), channel_id=1, source_target_pairs={{0,3},{1,0},{2,1},{3,2},{4,7},{5,4},{6,5},{7,6},{8,11},{9,8},{10,9... | collective-permute-start | bytes 9224 | tf_op jit(solution)/shard_map/ppermute | solution.py:595
  64.6 0.9 collective-permute-start.10
  65.4 0.5 collective-permute-done.11.refs_14_.refs_9_
  65.9 1.1 collective-permute-start.9
  67.0 2.7 %collective-permute-done.10.refs_13_.refs_8_ = f32[768]{0:T(1024)S(1)} collective-permute-done((f32[768]{0:T(1024)S(1)}, f32[768]{0:T(1024)S(1)}, u32[]{:S(2)}, u32[]{:S(2)}) %collective-permute-start.10) | collective-permute-done | bytes 3104 | tf_op jit(solution)/shard_map/ppermute | solution.py:595
  69.7 1.3 collective-permute-done.9.refs_12_.refs_7_
  71.1 2.9 %all-to-all-done.1.refs_8_ = bf16[64,16,128]{2,1,0:T(8,128)(2,1)S(1)} async-done(((bf16[64,16,128]{2,1,0:T(8,128)(2,1)}), bf16[64,16,128]{2,1,0:T(8,128)(2,1)S(1)}, u32[]{:S(2)}, u32[]{:S(2)}) %all-to-all-start.1) | async-done | bytes 262176 | tf_op jit(solution)/shard_map/all_to_all | solution.py:615
  74.0 3.1 %first.1 = (bf16[768,768]{1,0:T(8,128)(2,1)}, f32[96,896]{1,0:T(8,128)}, bf16[128,768]{1,0:T(8,128)(2,1)}, bf16[128,768]{1,0:T(8,128)(2,1)}, bf16[128,768]{1,0:T...) custom-call(bf16[192,768]{1,0:T(8,128)(2,1)} %refs_0_.4, bf16[96,768]{1,0:T(8,128)(2,1)} %copy-done.7, ...), custom_call_target="tpu_custom_call" | custom-call | flops 1024 | bytes 1024 | tf_op jit(solution)/shard_map/first/pallas_call | solution.py:63
  77.5 2.3 %collective-permute-start.13 = (bf16[128,768]{1,0:T(8,128)(2,1)}, bf16[128,768]{1,0:T(8,128)(2,1)S(1)}, u32[]{:S(2)}, u32[]{:S(2)}) collective-permute-start(bf16[128,768]{1,0:T(8,128)(2,1)} %get-tuple-element.85), channel_id=1, source_target_pairs={{0,2},{1,3},{2,0},{3,1},{4,6},{5,7},{6,4},{7,5},{8,10},{9,11},{10,... | collective-permute-start | bytes 589832 | tf_op jit(solution)/shard_map/ppermute | solution.py:595
  79.7 0.5 collective-permute-start.14
  80.2 0.7 copy-done.13
  80.9 11.0 %middle.1 = (bf16[64,16,128]{2,1,0:T(8,128)(2,1)}, f32[96,768]{1,0:T(8,128)}, bf16[208,768]{1,0:T(8,128)(2,1)}, bf16[96,768]{1,0:T(8,128)(2,1)}) custom-call(bf16[2,16,4,48,768]{4,3,2,1,0:T(8,128)(2,1)} %later.3.refs_0_.refs_4_.refs_8_, f32[96,896]{1,0:T(8,128)} %get-tuple-element.80.refs_1_, bf16[3,128,768]{2,1,0:T(8,128)(2,1)} %refs_2_.1, ...), custom_call_target="tpu_custom_call" | custom-call | flops 1024 | bytes 1024 | tf_op jit(solution)/shard_map/middle/pallas_call | solution.py:63
  91.9 3.0 %collective-permute-start.17 = (bf16[208,768]{1,0:T(8,128)(2,1)}, bf16[208,768]{1,0:T(8,128)(2,1)S(1)}, u32[]{:S(2)}, u32[]{:S(2)}) collective-permute-start(bf16[208,768]{1,0:T(8,128)(2,1)} %get-tuple-element.95.refs_4_), channel_id=1, source_target_pairs={{0,3},{1,0},{2,1},{3,2},{4,7},{5,4},{6,5},{7,6},{8,11},{9,8},{10,9... | collective-permute-start | bytes 958472 | tf_op jit(solution)/shard_map/ppermute | solution.py:595
  94.9 0.7 collective-permute-start.16
  95.6 0.9 collective-permute-start.15
  96.6 0.6 copy-done.18
  97.3 8.3 %all-to-all-start.2 = ((bf16[64,16,128]{2,1,0:T(8,128)(2,1)}), bf16[64,16,128]{2,1,0:T(8,128)(2,1)S(1)}, u32[]{:S(2)}, u32[]{:S(2)}) async-start(bf16[64,16,128]{2,1,0:T(8,128)(2,1)} %later.4), calls=%async_computation.2 | async-start | bytes 524288 | tf_op jit(solution)/shard_map/all_to_all | solution.py:615
  105.6 3.8 %hidden.1 = (bf16[384,768]{1,0:T(8,128)(2,1)}, f32[384,768]{1,0:T(8,128)}, f32[8,128]{1,0:T(8,128)S(1)}) custom-call(bf16[128,768]{1,0:T(8,128)(2,1)} %get-tuple-element.93.refs_0_, bf16[128,768]{1,0:T(8,128)(2,1)} %copy-done.19, bf16[128,768]{1,0:T(8,128)(2,1)} %copy-done.18, bf16[128,768]{1,0:T(8,128)(2,1)} %copy-done.17, ...), custom_call_target="tpu_custom_call" | custom-call | flops 1024 | bytes 1024 | tf_op jit(solution)/shard_map/hidden/pallas_call | solution.py:63
  109.4 6.6 %all-to-all-done.2.refs_0_ = bf16[64,16,128]{2,1,0:T(8,128)(2,1)S(1)} async-done(((bf16[64,16,128]{2,1,0:T(8,128)(2,1)}), bf16[64,16,128]{2,1,0:T(8,128)(2,1)S(1)}, u32[]{:S(2)}, u32[]{:S(2)}) %all-to-all-start.2) | async-done | bytes 262176 | tf_op jit(solution)/shard_map/all_to_all | solution.py:615
  116.1 0.7 copy-done.20
  116.7 15.1 %attend_back.1 = (bf16[16,208,128]{2,1,0:T(8,128)(2,1)}, f32[8,128]{1,0:T(8,128)S(1)}) custom-call(bf16[64,16,128]{2,1,0:T(8,128)(2,1)} %copy-done.20, f32[64,2048]{1,0:T(8,128)} %get-tuple-element.87.refs_1_, bf16[80,2048]{1,0:T(8,128)(2,1)} %get-tuple-element.88.refs_2_, bf16[80,2048]{1,0:T(8,128)(2,1)} %get-tuple-element.89.refs_3_, ...), custom_call_target="tpu_custom_call" | custom-call | flops 1024 | bytes 1024 | tf_op jit(solution)/shard_map/attend_back/pallas_call | solution.py:63
  131.9 4.0 %all-to-all-start.3 = ((bf16[16,208,128]{2,1,0:T(8,128)(2,1)}), bf16[16,208,128]{2,1,0:T(8,128)(2,1)S(1)}, u32[]{:S(2)}, u32[]{:S(2)}) async-start(bf16[16,208,128]{2,1,0:T(8,128)(2,1)} %get-tuple-element.97), calls=%async_computation.3 | async-start | bytes 1703936 | tf_op jit(solution)/shard_map/all_to_all | solution.py:611
  135.9 6.6 %weights.1 = (bf16[96,1536]{1,0:T(8,128)(2,1)}, bf16[96,1536]{1,0:T(8,128)(2,1)}, bf16[96,1536]{1,0:T(8,128)(2,1)}, bf16[96,1536]{1,0:T(8,128)(2,1)}, f32[384,15...) custom-call(bf16[128,768]{1,0:T(8,128)(2,1)} %get-tuple-element.93.refs_0_, bf16[128,768]{1,0:T(8,128)(2,1)} %copy-done.19, ...), custom_call_target="tpu_custom_call" | custom-call | flops 1024 | bytes 1024 | tf_op jit(solution)/shard_map/weights/pallas_call | solution.py:63
  142.6 0.5 collective-permute-start.22
  143.7 0.9 collective-permute-start.20
  144.6 1.6 collective-permute-start.19
  146.2 0.7 copy-done.23
  147.1 3.2 %weights_add.1 = (bf16[16,24,2560]{2,1,0:T(8,128)(2,1)}, f32[8,128]{1,0:T(8,128)S(1)}) custom-call(f32[384,1536]{1,0:T(8,128)} %get-tuple-element.102.refs_0_, bf16[96,1536]{1,0:T(8,128)(2,1)} %copy-done.22, bf16[96,1536]{1,0:T(8,128)(2,1)} %copy-done.23, bf16[96,1536]{1,0:T(8,128)(2,1)} %copy-done.24, bf16[96,1536]{1,0:T(8,128)(2,1)} %copy-done.25), custom_call_target="tpu_custom_call" | custom-call | flops 1024 | bytes 1024 | tf_op jit(solution)/shard_map/weights_add/pallas_call | solution.py:63
  150.6 2.4 %collective-permute-done.19.refs_2_.refs_9_ = bf16[96,768]{1,0:T(8,128)(2,1)S(1)} collective-permute-done((bf16[96,768]{1,0:T(8,128)(2,1)}, bf16[96,768]{1,0:T(8,128)(2,1)S(1)}, u32[]{:S(2)}, u32[]{:S(2)}) %collective-permute-start.19) | collective-permute-done | bytes 147488 | tf_op jit(solution)/shard_map/ppermute | solution.py:595
  153.0 2.2 %collective-permute-done.18.refs_1_.refs_8_ = bf16[96,768]{1,0:T(8,128)(2,1)S(1)} collective-permute-done((bf16[96,768]{1,0:T(8,128)(2,1)}, bf16[96,768]{1,0:T(8,128)(2,1)S(1)}, u32[]{:S(2)}, u32[]{:S(2)}) %collective-permute-start.18) | collective-permute-done | bytes 147488 | tf_op jit(solution)/shard_map/ppermute | solution.py:595
  155.2 4.3 %input_back.1 = (f32[96,768]{1,0:T(8,128)}, bf16[96,768]{1,0:T(8,128)(2,1)}, bf16[96,768]{1,0:T(8,128)(2,1)}, bf16[96,768]{1,0:T(8,128)(2,1)}, bf16[400,768]{1,0...) custom-call(bf16[3,128,768]{2,1,0:T(8,128)(2,1)} %refs_0_.5, bf16[192,768]{1,0:T(8,128)(2,1)} %bitcast.10, ...), custom_call_target="tpu_custom_call" | custom-call | flops 1024 | bytes 1024 | tf_op jit(solution)/shard_map/input_back/pallas_call | solution.py:63
  159.7 2.0 collective-permute-start.26
  161.7 2.0 collective-permute-start.27
  163.7 3.1 %input_add.1 = (bf16[16,24,2560]{2,1,0:T(8,128)(2,1)}, f32[192]{0:T(256)}, f32[192]{0:T(256)}, f32[192]{0:T(256)}) custom-call(f32[384,768]{1,0:T(8,128)} %get-tuple-element.113.refs_0_, bf16[400,768]{1,0:T(8,128)(2,1)S(1)} %collective-permute-done.31.refs_1_, bf16[16,24,2560]{2,1,0:T(8,128)(2,1)} %get-tuple-element.115.refs_2_, ...), custom_call_target="tpu_custom_call", output_to_operand_aliasing={{0}: (2, {})} | custom-call | flops 1024 | bytes 1024 | tf_op jit(solution)/shard_map/input_add/pallas_call | solution.py:63
  166.8 6.9 %all-to-all-start.4 = ((bf16[16,24,2560]{2,1,0:T(8,128)(2,1)}), bf16[16,24,2560]{2,1,0:T(8,128)(2,1)S(1)}, u32[]{:S(2)}, u32[]{:S(2)}) async-start(bf16[16,24,2560]{2,1,0:T(8,128)(2,1)} %get-tuple-element.117), calls=%async_computation.4 | async-start | bytes 3932160 | tf_op jit(solution)/shard_map/all_to_all | solution.py:611
  173.8 1.2 input_chunk.1.refs_0_
  175.0 0.5 collective-permute-start.30
  175.5 2.1 collective-permute-start.29
  177.6 1.3 collective-permute-start.28
  178.9 1.1 layer_out.1
  180.0 1.7 collective-permute-done.30.refs_3_
  181.8 2.0 collective-permute-done.29.refs_2_
  183.7 1.4 collective-permute-done.28.refs_1_
  185.2 1.1 grad_input.1
  186.3 15.7 %all-to-all-done.4.refs_0_ = bf16[16,24,2560]{2,1,0:T(8,128)(2,1)S(1)} async-done(((bf16[16,24,2560]{2,1,0:T(8,128)(2,1)}), bf16[16,24,2560]{2,1,0:T(8,128)(2,1)S(1)}, u32[]{:S(2)}, u32[]{:S(2)}) %all-to-all-start.4) | async-done | bytes 1966112 | tf_op jit(solution)/shard_map/all_to_all | solution.py:611
  202.0 0.9 input_sum.1
  (94 shorter events, 2.2 us)
Async XLA Ops:
  7.2 73.0 %all-gather.3.cloned.1.call-start = ((), (), s32[]{:S(2)}) async-start(), calls=%async_computation.5 | async-start | bytes 9732096 | tf_op jit(solution)/shard_map/all_gather | solution.py:660
  8.2 8.6 %collective-permute-start.2 = (bf16[48,768]{1,0:T(8,128)(2,1)S(1)}, bf16[48,768]{1,0:T(8,128)(2,1)S(1)}, u32[]{:S(2)}, u32[]{:S(2)}) collective-permute-start(bf16[48,768]{1,0:T(8,128)(2,1)S(1)} %bitcast_select_fusion.refs_0_), channel_id=1, source_target_pairs={{0,3},{1,0},{2,1},{3,2},{4,7},{5,4},{6,5},{7,6},{8,11},{9,8},{10,9... | collective-permute-start | bytes 221192 | tf_op jit(solution)/shard_map/ppermute | solution.py:595
  12.4 6.0 %collective-permute-start.1 = (bf16[48,768]{1,0:T(8,128)(2,1)S(1)}, bf16[48,768]{1,0:T(8,128)(2,1)S(1)}, u32[]{:S(2)}, u32[]{:S(2)}) collective-permute-start(bf16[48,768]{1,0:T(8,128)(2,1)S(1)} %bitcast_select_fusion.refs_0_), channel_id=1, source_target_pairs={{0,2},{1,3},{2,0},{3,1},{4,6},{5,7},{6,4},{7,5},{8,10},{9,11},{10,... | collective-permute-start | bytes 221192 | tf_op jit(solution)/shard_map/ppermute | solution.py:595
  12.4 6.5 %collective-permute-start = (bf16[48,768]{1,0:T(8,128)(2,1)S(1)}, bf16[48,768]{1,0:T(8,128)(2,1)S(1)}, u32[]{:S(2)}, u32[]{:S(2)}) collective-permute-start(bf16[48,768]{1,0:T(8,128)(2,1)S(1)} %bitcast_select_fusion.refs_0_), channel_id=1, source_target_pairs={{0,1},{1,2},{2,3},{3,0},{4,5},{5,6},{6,7},{7,4},{8,9},{9,10},{10,1... | collective-permute-start | bytes 221192 | tf_op jit(solution)/shard_map/ppermute | solution.py:595
  13.6 13.3 %copy-start.21 = (bf16[192,768]{1,0:T(8,128)(2,1)S(1)}, bf16[192,768]{1,0:T(8,128)(2,1)}, u32[]{:S(2)}) copy-start(bf16[192,768]{1,0:T(8,128)(2,1)} %refs_0_.4) | copy-start | bytes 884740
  13.6 28.8 %copy-start.29 = (f32[64]{0:T(128)S(1)}, f32[64]{0:T(128)}, u32[]{:S(2)}) copy-start(f32[64]{0:T(128)} %constant.14.clone) | copy-start | bytes 772
  19.7 42.1 %copy-start.10 = (f32[768]{0:T(1024)S(1)}, f32[768]{0:T(1024)}, u32[]{:S(2)}) copy-start(f32[768]{0:T(1024)} %refs_5_.5) | copy-start | bytes 9220
  19.7 54.3 %copy-start = (bf16[3,128,768]{2,1,0:T(8,128)(2,1)S(1)}, bf16[3,128,768]{2,1,0:T(8,128)(2,1)}, u32[]{:S(2)}) copy-start(bf16[3,128,768]{2,1,0:T(8,128)(2,1)} %refs_0_.5) | copy-start | bytes 1769476
  19.7 54.3 %copy-start.8 = (f32[768]{0:T(1024)S(1)}, f32[768]{0:T(1024)}, u32[]{:S(2)}) copy-start(f32[768]{0:T(1024)} %refs_4_.1) | copy-start | bytes 9220
  19.7 54.3 %copy-start.9 = (f32[768]{0:T(1024)S(1)}, f32[768]{0:T(1024)}, u32[]{:S(2)}) copy-start(f32[768]{0:T(1024)} %refs_5_.4) | copy-start | bytes 9220
  19.7 54.3 %copy-start.12 = (f32[768]{0:T(1024)S(1)}, f32[768]{0:T(1024)}, u32[]{:S(2)}) copy-start(f32[768]{0:T(1024)} %refs_9_.1) | copy-start | bytes 9220
  19.7 22.7 %all-to-all-start = ((bf16[16,208,128]{2,1,0:T(8,128)(2,1)}), bf16[16,208,128]{2,1,0:T(8,128)(2,1)S(1)}, u32[]{:S(2)}, u32[]{:S(2)}) async-start(bf16[16,208,128]{2,1,0:T(8,128)(2,1)} %get-tuple-element.77), calls=%async_computation | async-start | bytes 1703936 | tf_op jit(solution)/shard_map/all_to_all | solution.py:611
  27.0 5.7 %collective-permute-start.5 = (bf16[96,768]{1,0:T(8,128)(2,1)S(1)}, bf16[96,768]{1,0:T(8,128)(2,1)S(1)}, u32[]{:S(2)}, u32[]{:S(2)}) collective-permute-start(bf16[96,768]{1,0:T(8,128)(2,1)S(1)} %constant_dynamic-slice_fusion), channel_id=1, source_target_pairs={{0,3},{1,0},{2,1},{3,2},{4,7},{5,4},{6,5},{7,6},{8,11},{9,8},{10,9... | collective-permute-start | bytes 442376 | tf_op jit(solution)/shard_map/ppermute | solution.py:595
  27.9 7.0 %collective-permute-start.4 = (bf16[96,768]{1,0:T(8,128)(2,1)S(1)}, bf16[96,768]{1,0:T(8,128)(2,1)S(1)}, u32[]{:S(2)}, u32[]{:S(2)}) collective-permute-start(bf16[96,768]{1,0:T(8,128)(2,1)S(1)} %constant_dynamic-slice_fusion), channel_id=1, source_target_pairs={{0,2},{1,3},{2,0},{3,1},{4,6},{5,7},{6,4},{7,5},{8,10},{9,11},{10,... | collective-permute-start | bytes 442376 | tf_op jit(solution)/shard_map/ppermute | solution.py:595
  29.2 7.1 %collective-permute-start.3 = (bf16[96,768]{1,0:T(8,128)(2,1)S(1)}, bf16[96,768]{1,0:T(8,128)(2,1)S(1)}, u32[]{:S(2)}, u32[]{:S(2)}) collective-permute-start(bf16[96,768]{1,0:T(8,128)(2,1)S(1)} %constant_dynamic-slice_fusion), channel_id=1, source_target_pairs={{0,1},{1,2},{2,3},{3,0},{4,5},{5,6},{6,7},{7,4},{8,9},{9,10},{10,1... | collective-permute-start | bytes 442376 | tf_op jit(solution)/shard_map/ppermute | solution.py:595
  32.7 41.3 %copy-start.5 = (bf16[96,768]{1,0:T(8,128)(2,1)}, bf16[96,768]{1,0:T(8,128)(2,1)S(1)}, u32[]{:S(2)}) copy-start(bf16[96,768]{1,0:T(8,128)(2,1)S(1)} %collective-permute-done.5.refs_4_.refs_3_) | copy-start | bytes 442372
  34.8 39.1 %copy-start.6 = (bf16[96,768]{1,0:T(8,128)(2,1)}, bf16[96,768]{1,0:T(8,128)(2,1)S(1)}, u32[]{:S(2)}) copy-start(bf16[96,768]{1,0:T(8,128)(2,1)S(1)} %collective-permute-done.4.refs_3_.refs_2_) | copy-start | bytes 442372
  36.3 37.6 %copy-start.7 = (bf16[96,768]{1,0:T(8,128)(2,1)}, bf16[96,768]{1,0:T(8,128)(2,1)S(1)}, u32[]{:S(2)}) copy-start(bf16[96,768]{1,0:T(8,128)(2,1)S(1)} %collective-permute-done.3.refs_2_.refs_1_) | copy-start | bytes 442372
  55.9 18.0 %all-to-all-start.1 = ((bf16[64,16,128]{2,1,0:T(8,128)(2,1)}), bf16[64,16,128]{2,1,0:T(8,128)(2,1)S(1)}, u32[]{:S(2)}, u32[]{:S(2)}) async-start(bf16[64,16,128]{2,1,0:T(8,128)(2,1)} %get-tuple-element.78), calls=%async_computation.1 | async-start | bytes 524288 | tf_op jit(solution)/shard_map/all_to_all | solution.py:615
  61.1 9.9 %collective-permute-start.8 = (bf16[96,768]{1,0:T(8,128)(2,1)S(1)}, bf16[96,768]{1,0:T(8,128)(2,1)S(1)}, u32[]{:S(2)}, u32[]{:S(2)}) collective-permute-start(bf16[96,768]{1,0:T(8,128)(2,1)S(1)} %collective-permute-done.5.refs_4_.refs_3_), channel_id=1, source_target_pairs={{0,64},{64,0},{1,65},{65,1},{2,66},{66,2},{3,67},{67,3},{4,68},{68... | collective-permute-start | bytes 442376 | tf_op jit(solution)/shard_map/ppermute | solution.py:607
  61.2 9.8 %collective-permute-start.7 = (bf16[96,768]{1,0:T(8,128)(2,1)S(1)}, bf16[96,768]{1,0:T(8,128)(2,1)S(1)}, u32[]{:S(2)}, u32[]{:S(2)}) collective-permute-start(bf16[96,768]{1,0:T(8,128)(2,1)S(1)} %collective-permute-done.4.refs_3_.refs_2_), channel_id=1, source_target_pairs={{0,64},{64,0},{1,65},{65,1},{2,66},{66,2},{3,67},{67,3},{4,68},{68... | collective-permute-start | bytes 442376 | tf_op jit(solution)/shard_map/ppermute | solution.py:607
  61.7 9.4 %collective-permute-start.6 = (bf16[96,768]{1,0:T(8,128)(2,1)S(1)}, bf16[96,768]{1,0:T(8,128)(2,1)S(1)}, u32[]{:S(2)}, u32[]{:S(2)}) collective-permute-start(bf16[96,768]{1,0:T(8,128)(2,1)S(1)} %collective-permute-done.3.refs_2_.refs_1_), channel_id=1, source_target_pairs={{0,64},{64,0},{1,65},{65,1},{2,66},{66,2},{3,67},{67,3},{4,68},{68... | collective-permute-start | bytes 442376 | tf_op jit(solution)/shard_map/ppermute | solution.py:607
  61.8 4.1 %collective-permute-start.11 = (f32[768]{0:T(1024)S(1)}, f32[768]{0:T(1024)S(1)}, u32[]{:S(2)}, u32[]{:S(2)}) collective-permute-start(f32[768]{0:T(1024)S(1)} %copy-done.10), channel_id=1, source_target_pairs={{0,3},{1,0},{2,1},{3,2},{4,7},{5,4},{6,5},{7,6},{8,11},{9,8},{10,9... | collective-permute-start | bytes 9224 | tf_op jit(solution)/shard_map/ppermute | solution.py:595
  64.6 5.1 %collective-permute-start.10 = (f32[768]{0:T(1024)S(1)}, f32[768]{0:T(1024)S(1)}, u32[]{:S(2)}, u32[]{:S(2)}) collective-permute-start(f32[768]{0:T(1024)S(1)} %copy-done.10), channel_id=1, source_target_pairs={{0,2},{1,3},{2,0},{3,1},{4,6},{5,7},{6,4},{7,5},{8,10},{9,11},{10,... | collective-permute-start | bytes 9224 | tf_op jit(solution)/shard_map/ppermute | solution.py:595
  65.9 5.1 %collective-permute-start.9 = (f32[768]{0:T(1024)S(1)}, f32[768]{0:T(1024)S(1)}, u32[]{:S(2)}, u32[]{:S(2)}) collective-permute-start(f32[768]{0:T(1024)S(1)} %copy-done.10), channel_id=1, source_target_pairs={{0,1},{1,2},{2,3},{3,0},{4,5},{5,6},{6,7},{7,4},{8,9},{9,10},{10,1... | collective-permute-start | bytes 9224 | tf_op jit(solution)/shard_map/ppermute | solution.py:595
  71.0 2.9 %copy-start.26 = (bf16[96,768]{1,0:T(8,128)(2,1)}, bf16[96,768]{1,0:T(8,128)(2,1)S(1)}, u32[]{:S(2)}) copy-start(bf16[96,768]{1,0:T(8,128)(2,1)S(1)} %collective-permute-done.8.refs_6_) | copy-start | bytes 442372
  71.0 2.9 %copy-start.27 = (bf16[96,768]{1,0:T(8,128)(2,1)}, bf16[96,768]{1,0:T(8,128)(2,1)S(1)}, u32[]{:S(2)}) copy-start(bf16[96,768]{1,0:T(8,128)(2,1)S(1)} %collective-permute-done.7.refs_5_) | copy-start | bytes 442372
  71.1 2.9 %copy-start.28 = (bf16[96,768]{1,0:T(8,128)(2,1)}, bf16[96,768]{1,0:T(8,128)(2,1)S(1)}, u32[]{:S(2)}) copy-start(bf16[96,768]{1,0:T(8,128)(2,1)S(1)} %collective-permute-done.6.refs_4_) | copy-start | bytes 442372
  77.1 3.1 %copy-start.16 = (f32[8,128]{1,0:T(8,128)}, f32[8,128]{1,0:T(8,128)S(1)}, u32[]{:S(2)}) copy-start(f32[8,128]{1,0:T(8,128)S(1)} %get-tuple-element.79.refs_1_) | copy-start | bytes 12292
  77.1 18.5 %collective-permute-start.12 = (bf16[128,768]{1,0:T(8,128)(2,1)}, bf16[128,768]{1,0:T(8,128)(2,1)S(1)}, u32[]{:S(2)}, u32[]{:S(2)}) collective-permute-start(bf16[128,768]{1,0:T(8,128)(2,1)} %get-tuple-element.84), channel_id=1, source_target_pairs={{0,3},{1,0},{2,1},{3,2},{4,7},{5,4},{6,5},{7,6},{8,11},{9,8},{10,9... | collective-permute-start | bytes 589832 | tf_op jit(solution)/shard_map/ppermute | solution.py:595
  77.5 19.1 %collective-permute-start.13 = (bf16[128,768]{1,0:T(8,128)(2,1)}, bf16[128,768]{1,0:T(8,128)(2,1)S(1)}, u32[]{:S(2)}, u32[]{:S(2)}) collective-permute-start(bf16[128,768]{1,0:T(8,128)(2,1)} %get-tuple-element.85), channel_id=1, source_target_pairs={{0,2},{1,3},{2,0},{3,1},{4,6},{5,7},{6,4},{7,5},{8,10},{9,11},{10,... | collective-permute-start | bytes 589832 | tf_op jit(solution)/shard_map/ppermute | solution.py:595
  79.7 16.8 %collective-permute-start.14 = (bf16[128,768]{1,0:T(8,128)(2,1)}, bf16[128,768]{1,0:T(8,128)(2,1)S(1)}, u32[]{:S(2)}, u32[]{:S(2)}) collective-permute-start(bf16[128,768]{1,0:T(8,128)(2,1)} %get-tuple-element.86), channel_id=1, source_target_pairs={{0,1},{1,2},{2,3},{3,0},{4,5},{5,6},{6,7},{7,4},{8,9},{9,10},{10,1... | collective-permute-start | bytes 589832 | tf_op jit(solution)/shard_map/ppermute | solution.py:595
  80.2 0.7 copy-start.15
  91.9 24.1 %collective-permute-start.17 = (bf16[208,768]{1,0:T(8,128)(2,1)}, bf16[208,768]{1,0:T(8,128)(2,1)S(1)}, u32[]{:S(2)}, u32[]{:S(2)}) collective-permute-start(bf16[208,768]{1,0:T(8,128)(2,1)} %get-tuple-element.95.refs_4_), channel_id=1, source_target_pairs={{0,3},{1,0},{2,1},{3,2},{4,7},{5,4},{6,5},{7,6},{8,11},{9,8},{10,9... | collective-permute-start | bytes 958472 | tf_op jit(solution)/shard_map/ppermute | solution.py:595
  94.9 21.1 %collective-permute-start.16 = (bf16[208,768]{1,0:T(8,128)(2,1)}, bf16[208,768]{1,0:T(8,128)(2,1)S(1)}, u32[]{:S(2)}, u32[]{:S(2)}) collective-permute-start(bf16[208,768]{1,0:T(8,128)(2,1)} %get-tuple-element.95.refs_4_), channel_id=1, source_target_pairs={{0,2},{1,3},{2,0},{3,1},{4,6},{5,7},{6,4},{7,5},{8,10},{9,11},{10,... | collective-permute-start | bytes 958472 | tf_op jit(solution)/shard_map/ppermute | solution.py:595
  95.6 1.0 copy-start.17
  95.6 20.5 %collective-permute-start.15 = (bf16[208,768]{1,0:T(8,128)(2,1)}, bf16[208,768]{1,0:T(8,128)(2,1)S(1)}, u32[]{:S(2)}, u32[]{:S(2)}) collective-permute-start(bf16[208,768]{1,0:T(8,128)(2,1)} %get-tuple-element.95.refs_4_), channel_id=1, source_target_pairs={{0,1},{1,2},{2,3},{3,0},{4,5},{5,6},{6,7},{7,4},{8,9},{9,10},{10,1... | collective-permute-start | bytes 958472 | tf_op jit(solution)/shard_map/ppermute | solution.py:595
  96.6 0.7 copy-start.19
  97.3 18.7 %all-to-all-start.2 = ((bf16[64,16,128]{2,1,0:T(8,128)(2,1)}), bf16[64,16,128]{2,1,0:T(8,128)(2,1)S(1)}, u32[]{:S(2)}, u32[]{:S(2)}) async-start(bf16[64,16,128]{2,1,0:T(8,128)(2,1)} %later.4), calls=%async_computation.2 | async-start | bytes 524288 | tf_op jit(solution)/shard_map/all_to_all | solution.py:615
  116.0 15.9 %copy-start.1 = (bf16[208,768]{1,0:T(8,128)(2,1)}, bf16[208,768]{1,0:T(8,128)(2,1)S(1)}, u32[]{:S(2)}) copy-start(bf16[208,768]{1,0:T(8,128)(2,1)S(1)} %collective-permute-done.17.refs_10_.refs_7_) | copy-start | bytes 958468
  116.0 15.9 %copy-start.2 = (bf16[208,768]{1,0:T(8,128)(2,1)}, bf16[208,768]{1,0:T(8,128)(2,1)S(1)}, u32[]{:S(2)}) copy-start(bf16[208,768]{1,0:T(8,128)(2,1)S(1)} %collective-permute-done.16.refs_9_.refs_6_) | copy-start | bytes 958468
  116.1 15.9 %copy-start.3 = (bf16[208,768]{1,0:T(8,128)(2,1)}, bf16[208,768]{1,0:T(8,128)(2,1)S(1)}, u32[]{:S(2)}) copy-start(bf16[208,768]{1,0:T(8,128)(2,1)S(1)} %collective-permute-done.15.refs_8_.refs_5_) | copy-start | bytes 958468
  131.9 10.7 %copy-start.11 = (f32[8,128]{1,0:T(8,128)}, f32[8,128]{1,0:T(8,128)S(1)}, u32[]{:S(2)}) copy-start(f32[8,128]{1,0:T(8,128)S(1)} %get-tuple-element.96.refs_1_.refs_11_) | copy-start | bytes 12292
  131.9 23.3 %all-to-all-start.3 = ((bf16[16,208,128]{2,1,0:T(8,128)(2,1)}), bf16[16,208,128]{2,1,0:T(8,128)(2,1)S(1)}, u32[]{:S(2)}, u32[]{:S(2)}) async-start(bf16[16,208,128]{2,1,0:T(8,128)(2,1)} %get-tuple-element.97), calls=%async_computation.3 | async-start | bytes 1703936 | tf_op jit(solution)/shard_map/all_to_all | solution.py:611
  142.6 2.0 collective-permute-start.21
  142.6 3.5 %collective-permute-start.22 = (bf16[96,1536]{1,0:T(8,128)(2,1)}, bf16[96,1536]{1,0:T(8,128)(2,1)S(1)}, u32[]{:S(2)}, u32[]{:S(2)}) collective-permute-start(bf16[96,1536]{1,0:T(8,128)(2,1)} %get-tuple-element.104), channel_id=1, source_target_pairs={{0,64},{64,0},{1,65},{65,1},{2,66},{66,2},{3,67},{67,3},{4,68},{68... | collective-permute-start | bytes 884744 | tf_op jit(solution)/shard_map/ppermute | solution.py:607
  143.1 3.1 %collective-permute-start.23 = (bf16[96,1536]{1,0:T(8,128)(2,1)}, bf16[96,1536]{1,0:T(8,128)(2,1)S(1)}, u32[]{:S(2)}, u32[]{:S(2)}) collective-permute-start(bf16[96,1536]{1,0:T(8,128)(2,1)} %get-tuple-element.105), channel_id=1, source_target_pairs={{0,64},{64,0},{1,65},{65,1},{2,66},{66,2},{3,67},{67,3},{4,68},{68... | collective-permute-start | bytes 884744 | tf_op jit(solution)/shard_map/ppermute | solution.py:607
  143.2 3.0 %collective-permute-start.24 = (bf16[96,1536]{1,0:T(8,128)(2,1)}, bf16[96,1536]{1,0:T(8,128)(2,1)S(1)}, u32[]{:S(2)}, u32[]{:S(2)}) collective-permute-start(bf16[96,1536]{1,0:T(8,128)(2,1)} %get-tuple-element.106), channel_id=1, source_target_pairs={{0,64},{64,0},{1,65},{65,1},{2,66},{66,2},{3,67},{67,3},{4,68},{68... | collective-permute-start | bytes 884744 | tf_op jit(solution)/shard_map/ppermute | solution.py:607
  143.7 6.9 %collective-permute-start.20 = (bf16[96,768]{1,0:T(8,128)(2,1)}, bf16[96,768]{1,0:T(8,128)(2,1)S(1)}, u32[]{:S(2)}, u32[]{:S(2)}) collective-permute-start(bf16[96,768]{1,0:T(8,128)(2,1)} %later.5.refs_0_), channel_id=1, source_target_pairs={{0,3},{1,0},{2,1},{3,2},{4,7},{5,4},{6,5},{7,6},{8,11},{9,8},{10,9... | collective-permute-start | bytes 442376 | tf_op jit(solution)/shard_map/ppermute | solution.py:595
  144.6 1.7 copy-start.22
  144.6 8.4 %collective-permute-start.19 = (bf16[96,768]{1,0:T(8,128)(2,1)}, bf16[96,768]{1,0:T(8,128)(2,1)S(1)}, u32[]{:S(2)}, u32[]{:S(2)}) collective-permute-start(bf16[96,768]{1,0:T(8,128)(2,1)} %later.5.refs_0_), channel_id=1, source_target_pairs={{0,2},{1,3},{2,0},{3,1},{4,6},{5,7},{6,4},{7,5},{8,10},{9,11},{10,... | collective-permute-start | bytes 442376 | tf_op jit(solution)/shard_map/ppermute | solution.py:595
  146.2 0.7 copy-start.23
  146.2 9.0 %collective-permute-start.18 = (bf16[96,768]{1,0:T(8,128)(2,1)}, bf16[96,768]{1,0:T(8,128)(2,1)S(1)}, u32[]{:S(2)}, u32[]{:S(2)}) collective-permute-start(bf16[96,768]{1,0:T(8,128)(2,1)} %later.5.refs_0_), channel_id=1, source_target_pairs={{0,1},{1,2},{2,3},{3,0},{4,5},{5,6},{6,7},{7,4},{8,9},{9,10},{10,1... | collective-permute-start | bytes 442376 | tf_op jit(solution)/shard_map/ppermute | solution.py:595
  146.2 0.8 copy-start.24
  146.2 0.9 copy-start.25
  159.5 4.2 %collective-permute-start.31 = (bf16[400,768]{1,0:T(8,128)(2,1)}, bf16[400,768]{1,0:T(8,128)(2,1)S(1)}, u32[]{:S(2)}, u32[]{:S(2)}) collective-permute-start(bf16[400,768]{1,0:T(8,128)(2,1)} %get-tuple-element.114), channel_id=1, source_target_pairs={{0,64},{64,0},{1,65},{65,1},{2,66},{66,2},{3,67},{67,3},{4,68},{68... | collective-permute-start | bytes 1843208 | tf_op jit(solution)/shard_map/ppermute | solution.py:607
  159.6 14.2 %collective-permute-start.25 = (bf16[96,768]{1,0:T(8,128)(2,1)}, bf16[96,768]{1,0:T(8,128)(2,1)S(1)}, u32[]{:S(2)}, u32[]{:S(2)}) collective-permute-start(bf16[96,768]{1,0:T(8,128)(2,1)} %get-tuple-element.110), channel_id=1, source_target_pairs={{0,1},{1,2},{2,3},{3,0},{4,5},{5,6},{6,7},{7,4},{8,9},{9,10},{10,1... | collective-permute-start | bytes 442376 | tf_op jit(solution)/shard_map/ppermute | solution.py:595
  159.7 14.1 %collective-permute-start.26 = (bf16[96,768]{1,0:T(8,128)(2,1)}, bf16[96,768]{1,0:T(8,128)(2,1)S(1)}, u32[]{:S(2)}, u32[]{:S(2)}) collective-permute-start(bf16[96,768]{1,0:T(8,128)(2,1)} %get-tuple-element.111), channel_id=1, source_target_pairs={{0,2},{1,3},{2,0},{3,1},{4,6},{5,7},{6,4},{7,5},{8,10},{9,11},{10,... | collective-permute-start | bytes 442376 | tf_op jit(solution)/shard_map/ppermute | solution.py:595
  161.7 12.1 %collective-permute-start.27 = (bf16[96,768]{1,0:T(8,128)(2,1)}, bf16[96,768]{1,0:T(8,128)(2,1)S(1)}, u32[]{:S(2)}, u32[]{:S(2)}) collective-permute-start(bf16[96,768]{1,0:T(8,128)(2,1)} %get-tuple-element.112), channel_id=1, source_target_pairs={{0,3},{1,0},{2,1},{3,2},{4,7},{5,4},{6,5},{7,6},{8,11},{9,8},{10,9... | collective-permute-start | bytes 442376 | tf_op jit(solution)/shard_map/ppermute | solution.py:595
  166.8 35.2 %all-to-all-start.4 = ((bf16[16,24,2560]{2,1,0:T(8,128)(2,1)}), bf16[16,24,2560]{2,1,0:T(8,128)(2,1)S(1)}, u32[]{:S(2)}, u32[]{:S(2)}) async-start(bf16[16,24,2560]{2,1,0:T(8,128)(2,1)} %get-tuple-element.117), calls=%async_computation.4 | async-start | bytes 3932160 | tf_op jit(solution)/shard_map/all_to_all | solution.py:611
  173.8 5.1 %copy-start.4 = (bf16[96,768]{1,0:T(8,128)(2,1)S(1)}, bf16[96,768]{1,0:T(8,128)(2,1)}, u32[]{:S(2)}) copy-start(bf16[96,768]{1,0:T(8,128)(2,1)} %later.5.refs_0_) | copy-start | bytes 442372
  175.0 6.7 %collective-permute-start.30 = (bf16[96,768]{1,0:T(8,128)(2,1)S(1)}, bf16[96,768]{1,0:T(8,128)(2,1)S(1)}, u32[]{:S(2)}, u32[]{:S(2)}) collective-permute-start(bf16[96,768]{1,0:T(8,128)(2,1)S(1)} %input_chunk.1.refs_0_), channel_id=1, source_target_pairs={{0,3},{1,0},{2,1},{3,2},{4,7},{5,4},{6,5},{7,6},{8,11},{9,8},{10,9... | collective-permute-start | bytes 442376 | tf_op jit(solution)/shard_map/ppermute | solution.py:595
  175.5 8.2 %collective-permute-start.29 = (bf16[96,768]{1,0:T(8,128)(2,1)S(1)}, bf16[96,768]{1,0:T(8,128)(2,1)S(1)}, u32[]{:S(2)}, u32[]{:S(2)}) collective-permute-start(bf16[96,768]{1,0:T(8,128)(2,1)S(1)} %input_chunk.1.refs_0_), channel_id=1, source_target_pairs={{0,2},{1,3},{2,0},{3,1},{4,6},{5,7},{6,4},{7,5},{8,10},{9,11},{10,... | collective-permute-start | bytes 442376 | tf_op jit(solution)/shard_map/ppermute | solution.py:595
  177.6 7.6 %collective-permute-start.28 = (bf16[96,768]{1,0:T(8,128)(2,1)S(1)}, bf16[96,768]{1,0:T(8,128)(2,1)S(1)}, u32[]{:S(2)}, u32[]{:S(2)}) collective-permute-start(bf16[96,768]{1,0:T(8,128)(2,1)S(1)} %input_chunk.1.refs_0_), channel_id=1, source_target_pairs={{0,1},{1,2},{2,3},{3,0},{4,5},{5,6},{6,7},{7,4},{8,9},{9,10},{10,1... | collective-permute-start | bytes 442376 | tf_op jit(solution)/shard_map/ppermute | solution.py:595
  (4 other events, 2.8 us)
Sparse Core Ops, SparseCore 0:
  19.8 60.3 all-gather.2

commit v3 on v2

--- a/solution.py
+++ b/solution.py
@@ -24,6 +24,9 @@
 CH = R * C
 PAIRS = R * NH
 G = D // (2 * NW)
+WG = 1792
+QKV = 640
+FIRST_ROWS, LAST_ROWS = 14 * G, 6 * G
 SLOT = 3 * HD + 16
 AUG = HD + 16
 EPSILON = 1e-12
@@ -41,6 +44,10 @@
 NORMAL, BOTH_LAST, BOTH_FIRST = ((1,), (0,)), ((1,), (1,)), ((0,), (0,))
 
 
+def in_far_memory(arrays):
+    return [pltpu.with_memory_space_constraint(a, pltpu.HBM) if a.size > 1024 else a for a in arrays]
+
+
 def call(
     name, kernel, outs, args, scratch=(), cost=1024, mib=16, after=(), far_in=(), any_in=(), near=(), far=(), aliases={},
     token=False,
@@ -60,6 +67,7 @@
         return pltpu.VMEM(s, t) if k in near else pltpu.HBM(s, t) if k in far else jax.ShapeDtypeStruct(s, t)
 
     args = [pltpu.with_memory_space_constraint(a, pltpu.HBM) if k in far_in else a for k, a in enumerate(args)]
+    after = in_far_memory(after)
     return pl.pallas_call(
         run,
         out_shape=[shape(k, s, t) for k, (s, t) in enumerate(outs)],
@@ -86,7 +94,7 @@
         input_output_aliases={0: 0},
         cost_estimate=pl.CostEstimate(flops=1024, bytes_accessed=1024, transcendentals=0),
         name="later",
-    )(x, *after)
+    )(x, *in_far_memory(after))
 
 
 def copies(pairs, sems):
@@ -277,7 +285,7 @@
             return sum_key + folded(dk.astype(f32)), sum_value + folded(dv.astype(f32))
 
         zero = jnp.zeros((HD, T), f32)
-        sum_key, sum_value = lax.fori_loop(0, L // 256, tile, (zero, zero))
+        sum_key, sum_value = lax.fori_loop(0, L // 256, tile, (zero, zero), unroll=2)
         sum_query = zero
         stores = []
         for w in range(NW):
@@ -367,12 +375,15 @@
 
 
 def middle_kernel(
-    every_far, state_far, cot_far, w_out_far, g_one, s_one, b0, b1, b2, b3, b_down, g_two, s_two,
+    every_far, state_far, cot_far, w_out_far, g_one_far, s_one_far, b0_far, b_down_far, g_two_far, s_two_far, b1, b2, b3,
     slots_far, one_far, pack_far, layer_far,
-    state, cot, w_out, weights, slope, grad_one, slots, pack, layer, sems,
+    state, cot, w_out, g_one, s_one, b0, b_down, g_two, s_two,
+    weights, slope, grad_one, slots, pack, layer, sems,
 ):
     n = lax.axis_index("narrow")
-    first = copies([(state_far, state), (cot_far, cot), (w_out_far, w_out)], sems.at[8:])
+    pairs = [(state_far, state), (cot_far, cot), (w_out_far, w_out), (g_one_far, g_one), (s_one_far, s_one)]
+    pairs += [(b0_far, b0), (b_down_far, b_down), (g_two_far, g_two), (s_two_far, s_two)]
+    first = copies(pairs, sems.at[8:])
     pairs = [(every_far.at[which, :, s], weights.at[which, s]) for which in range(2) for s in range(NN)]
     loads = copies(pairs, sems)
     for load in first:
@@ -428,13 +439,6 @@
         store.wait()
 
 
-def halves(whole, send, send_far, keep_far, sems):
-    c = lax.axis_index("dp")
-    half = D // 2
-    send[0:half, :] = whole[pl.ds(pl.multiple_of((1 - c) * half, half), half), :].astype(bf16)
-    return copies([(send, send_far), (whole.at[pl.ds(pl.multiple_of(c * half, half), half), :], keep_far)], sems)
-
-
 def hidden_kernel(a0, a1, a2, a3, every_far, b_up, hidden_far, slope_far, firsts, weights, hidden, slope, sems):
     pairs = [(p, firsts.at[s]) for s, p in enumerate((a0, a1, a2, a3))] + [(every_far.at[0, :, 0], weights)]
     for load in copies(pairs, sems):
@@ -449,8 +453,8 @@
 
 def weights_kernel(
     a0, a1, a2, a3, p0, p1, p2, p3, every_far, hidden_far, slope_far,
-    send0_far, send1_far, send2_far, send3_far, keep_far, out_whole, sums,
-    firsts, packs, weights, hidden, slope, whole, send, vectors, sems,
+    send0_far, send1_far, send2_far, send3_far, keep_far, sums_far,
+    firsts, packs, weights, hidden, slope, whole, sums, vectors, sems,
 ):
     n, c = lax.axis_index("narrow"), lax.axis_index("dp")
     pairs = [(every_far.at[1, :, 0], weights), (slope_far, slope)]
@@ -463,43 +467,33 @@
     pre = (slope[...] * dot(grad_ffn, weights[...].reshape(D, F), NORMAL)).astype(bf16)
     for load in loads[6:]:
         load.wait()
-    whole[:, 0:F] = dot(firsts[:, NORMED:FIRST, :].reshape(TOK, D), pre, BOTH_FIRST)
-    whole[:, F:] = dot(grad_ffn, hidden[...], BOTH_FIRST)
+    whole[:, 0:F] = dot(firsts[:, NORMED:FIRST, :].reshape(TOK, D), pre, BOTH_FIRST).astype(bf16)
+    whole[:, F : 2 * F] = dot(grad_ffn, hidden[...], BOTH_FIRST).astype(bf16)
+    heads = [firsts[s, ATTN:NORMED, 256 * r : 256 * r + E] for s in range(NN) for r in range(R)]
+    heads = jnp.concatenate(heads, axis=0)
+    whole[:, 2 * F : 2 * F + E] = dot(packs[:, OUT:SUMS, :].reshape(TOK, D), heads, BOTH_FIRST).astype(bf16)
     half = D // 2
-    send[...] = whole[pl.ds(pl.multiple_of((1 - c) * half, half), half), :].astype(bf16)
-    pairs = [(send.at[96 * k : 96 * (k + 1), :], far) for k, far in enumerate((send0_far, send1_far, send2_far, send3_far))]
-    stores = copies([*pairs, (whole.at[pl.ds(pl.multiple_of(c * half, half), half), :], keep_far)], sems)
-    heads = [firsts[s, ATTN:NORMED, 256 * r : 256 * r + E] for s in range(NN) for r in range(R)]
-    out_whole[...] = dot(packs[:, OUT:SUMS, :].reshape(TOK, D), jnp.concatenate(heads, axis=0), BOTH_FIRST)
+    pairs = [(whole.at[pl.ds(pl.multiple_of(c * half, half), half), :], keep_far)]
+    for k, far in enumerate((send0_far, send1_far, send2_far, send3_far)):
+        pairs.append((whole.at[pl.ds(pl.multiple_of((1 - c) * half + 96 * k, 96), 96), :], far))
+    stores = copies(pairs, sems)
     for s in range(NN):
         vectors[(n + NN - s) % NN] = packs[s, SUMS:LAST, :].astype(f32)[0:8, :]
     total = vectors[0] + vectors[1] + vectors[2] + vectors[3]
     row = lax.broadcasted_iota(jnp.int32, (8, D), 0)
     sums[...] = jnp.where(row == 6, column_sum(pre.astype(f32)), total)
+    stores += copies([(sums, sums_far)], sems.at[5:])
     for store in stores:
         store.wait()
 
 
-def weights_add_kernel(keep_far, got0, got1, got2, got3, slots_far, keep, got, slots, sems):
-    pairs = [(far, got.at[96 * k : 96 * (k + 1), :]) for k, far in enumerate((got0, got1, got2, got3))]
-    for load in copies([(keep_far, keep), *pairs], sems):
-        load.wait()
-    both = (keep[...] + got[...].astype(f32)).astype(bf16)
-    stores = []
-    for w in range(NW):
-        slots[w] = both[w * G : (w + 1) * G, :]
-        stores.append(pltpu.make_async_copy(slots.at[w], slots_far.at[w, :, 0 : 2 * F], sems.at[w]))
-        stores[w].start()
-    for store in stores:
-        store.wait()
-
-
-def input_back_kernel(
-    x_far, wq, wk, wv, got, out_whole, vec, part0_far, part1_far, part2_far, part3_far, send_far, keep_far, sums,
-    part0, part1, part2, part3, whole, send, wide_part, x, near, sems,
-):
-    n = lax.axis_index("narrow")
-    loads = copies([(x_far, x), (wq, near.at[0]), (wk, near.at[1]), (wv, near.at[2])], sems)
+def blocks_of(block):
+    return jnp.concatenate([block[:, k : k + T] for k in range(0, block.shape[1], T)], axis=0).astype(bf16)
+
+
+def input_weights_kernel(x_far, got, grad, send_far, keep_far, sums, whole, bias, x, sems):
+    c = lax.axis_index("dp")
+    load = copies([(x_far, x)], sems)[0]
     grads = []
     for j in range(3):
         grad_t = jnp.concatenate(
@@ -510,20 +504,8 @@
             axis=1,
         )
         grads.append(grad_t.astype(f32).T.astype(bf16))
-    grad = jnp.concatenate(grads, axis=1)
-    whole[:, 3 * E :] = out_whole[...]
-    loads[0].wait()
-    whole[:, 0 : 3 * E] = dot(x[...].reshape(TOK, D), grad, BOTH_FIRST)
-    for load in loads[1:]:
-        load.wait()
-    wide_part[...] = dot(grad, near[...].reshape(3 * E, D), NORMAL)
-    for r in range(R):
-        to = slice(r * C, (r + 1) * C)
-        part0[to, :] = wide_part[chunk_rows(n, r), :]
-        for s, part in ((1, part1), (2, part2), (3, part3)):
-            part[to, :] = wide_part[chunk_rows((n + s) % NN, r), :].astype(bf16)
-    pairs = [(part0, part0_far), (part1, part1_far), (part2, part2_far), (part3, part3_far)]
-    stores = copies(pairs, sems)
+    grads = jnp.concatenate(grads, axis=1)
+    grad[...] = grads
     heads = []
     for h in range(NH):
         block = got[h, 3 * HD :, :].astype(f32)
@@ -535,43 +517,102 @@
     third = jnp.concatenate([b[1:2, 0:HD] + b[3:4, 0:HD] for b in heads], axis=1)
     row = jnp.concatenate([first, second, third], axis=1)
     sums[...] = row
-    hi, mid, lo = split3(jnp.concatenate([row, jnp.zeros((1, E), f32)], axis=1))
-    send[D // 2 :, :] = jnp.concatenate([vec[...], hi, mid, lo, jnp.zeros((5, D), f32)], axis=0).astype(bf16)
-    for store in stores + halves(whole, send, send_far, keep_far, sems.at[4:]):
+    hi, mid, lo = split3(row)
+    bias[:, 0 : 3 * E] = jnp.concatenate([hi, mid, lo, jnp.zeros((13, 3 * E), f32)], axis=0).astype(bf16)
+    load.wait()
+    whole[:, 0 : 3 * E] = dot(x[...].reshape(TOK, D), grads, BOTH_FIRST).astype(bf16)
+    half = D // 2
+    pairs = [(bias, send_far.at[half:, :])]
+    pairs.append((whole.at[pl.ds(pl.multiple_of((1 - c) * half, half), half), :], send_far.at[0:half, :]))
+    pairs.append((whole.at[pl.ds(pl.multiple_of(c * half, half), half), :], keep_far))
+    for store in copies(pairs, sems):
         store.wait()
 
 
-def input_add_kernel(keep_far, got_far, slots_in, sums, vec, slots_far, b_q, b_k, b_v, keep, got, slots, sems):
-    for load in copies([(keep_far, keep), (got_far, got)], sems):
+def input_back_kernel(
+    wq, wk, wv, grad, part0_far, part1_far, part2_far, part3_far, part0, part1, part2, part3, wide_part, near, sems
+):
+    n = lax.axis_index("narrow")
+    for load in copies([(wq, near.at[0]), (wk, near.at[1]), (wv, near.at[2])], sems):
         load.wait()
-    both = (keep[...] + got[0 : D // 2, :].astype(f32)).astype(bf16)
-    more = got[D // 2 :, :].astype(f32)
-    rows = vec[...].astype(bf16).astype(f32) + more[0:8, :]
+    wide_part[...] = dot(grad[...], near[...].reshape(3 * E, D), NORMAL)
+    for r in range(R):
+        to = slice(r * C, (r + 1) * C)
+        part0[to, :] = wide_part[chunk_rows(n, r), :]
+        for s, part in ((1, part1), (2, part2), (3, part3)):
+            part[to, :] = wide_part[chunk_rows((n + s) % NN, r), :].astype(bf16)
+    pairs = [(part0, part0_far), (part1, part1_far), (part2, part2_far), (part3, part3_far)]
+    for store in copies(pairs, sems):
+        store.wait()
+
+
+def blocks_of(block):
+    return jnp.concatenate([block[:, k : k + T] for k in range(0, block.shape[1], T)], axis=0).astype(bf16)
+
+
+def slot_sums(vec, vec_got):
+    rows = vec[...] + vec_got[...]
     lanes = D // 3
-    rows = jnp.concatenate([rows[:, lanes * k : lanes * (k + 1)] for k in range(3)], axis=0).astype(bf16)
+    return jnp.concatenate([rows[:, lanes * k : lanes * (k + 1)] for k in range(3)], axis=0)
+
+
+def first_add_kernel(
+    keep_far, vec_far, got0, got1, got2, got3, vec_got_far, slots_far, tail, keep, got, vec, vec_got, slots, sems
+):
+    pairs = [(far, got.at[96 * k : 96 * (k + 1), :]) for k, far in enumerate((got0, got1, got2, got3))]
+    pairs += [(vec_far, vec), (vec_got_far, vec_got), (keep_far, keep)]
+    for load in copies(pairs, sems):
+        load.wait()
+    rows = slot_sums(vec, vec_got)
+    lanes = 2 * F + T
     stores = []
     for w in range(NW):
-        slots[w] = jnp.concatenate([both[w * G : (w + 1) * G, :], rows], axis=1)
-        stores.append(pltpu.make_async_copy(slots.at[w], slots_far.at[w, :, 2 * F :], sems.at[w]))
-        stores[w].start()
+        at = slice(w * G, (w + 1) * G)
+        both = keep[at, :].astype(f32) + got[at, :].astype(f32)
+        slots[w] = blocks_of(jnp.concatenate([both[:, 0:lanes], rows[:, 0:T]], axis=1))
+        tail[at, :] = jnp.concatenate([both[:, lanes : lanes + HD], rows[:, T : T + HD]], axis=1)
+        tail[D // 2 + w * G : D // 2 + (w + 1) * G, :] = jnp.concatenate([rows[:, T + HD :], rows[:, T + HD :]], axis=1)
+        stores += copies([(slots.at[w], slots_far.at[w, 0:FIRST_ROWS, :])], sems.at[w:])
+    for store in stores:
+        store.wait()
+
+
+def last_add_kernel(
+    qkv_far, slots_in, qkv_got_far, tail, sums, slots_far, b_q, b_k, b_v, qkv, qkv_got, slots, sems
+):
+    for load in copies([(qkv_far, qkv), (qkv_got_far, qkv_got)], sems):
+        load.wait()
+    stores = []
+    for w in range(NW):
+        at = slice(w * G, (w + 1) * G)
+        other = slice(D // 2 + w * G, D // 2 + (w + 1) * G)
+        both = qkv[at, 0 : 3 * E].astype(f32) + qkv_got[at, 0 : 3 * E].astype(f32)
+        parts = [tail[at, 0:HD], both, tail[at, HD:], tail[other, 0:HD]]
+        slots[w] = blocks_of(jnp.concatenate(parts, axis=1))
+        stores += copies([(slots.at[w], slots_far.at[w, FIRST_ROWS:, :])], sems.at[w:])
+    bias = qkv_got[D // 2 :, 0 : 3 * E].astype(f32)
     hi, mid, lo = split3(sums[...])
-    bias = more[:, 0 : 3 * E]
-    total = (hi + bias[8:9, :]) + ((mid + bias[9:10, :]) + (lo + bias[10:11, :]))
+    total = (hi + bias[0:1, :]) + ((mid + bias[1:2, :]) + (lo + bias[2:3, :]))
     for k, ref in enumerate((b_q, b_k, b_v)):
         ref[...] = total[:, k * E : (k + 1) * E].reshape(E)
     for store in stores:
         store.wait()
 
 
-def input_sum_kernel(got, g_up, g_down, g_q, g_k, g_v, g_out, g_two, s_two, b_down, g_one, s_one, b_out, b_up):
+def last_sum_kernel(got, g_q, g_k, g_v, up, down, out, g_two, s_two, b_down, g_one, s_one, b_out, b_up):
     total = got[0].astype(f32)
     for w in range(1, NW):
         total = total + got[w].astype(f32)
-    g_up[...] = total[:, 0:F]
-    g_down[...] = total[:, F : 2 * F]
-    for k, ref in enumerate((g_q, g_k, g_v, g_out)):
-        ref[...] = total[:, 2 * F + k * E : 2 * F + (k + 1) * E]
-    vec = jnp.concatenate([total[8 * k : 8 * (k + 1), 2 * F + D :] for k in range(3)], axis=1)
+    total = jnp.concatenate([total[k : k + G, :] for k in range(0, FIRST_ROWS + LAST_ROWS, G)], axis=1)
+    up[...] = total[:, 0:F]
+    down[...] = total[:, F : 2 * F]
+    lanes = 2 * F + T
+    out[...] = jnp.concatenate([total[:, 2 * F : lanes], total[:, lanes + T : lanes + T + HD]], axis=1)
+    begin = lanes + T + HD
+    for k, ref in enumerate((g_q, g_k, g_v)):
+        ref[...] = total[:, begin + k * E : begin + (k + 1) * E]
+    rows = jnp.concatenate([total[:, lanes : lanes + T], total[:, begin + 3 * E :]], axis=1)
+    vec = jnp.concatenate([rows[8 * k : 8 * (k + 1), :] for k in range(3)], axis=1)
     for k, ref in enumerate((g_two, s_two, b_down, g_one, s_one, b_out, b_up)):
         ref[...] = vec[k : k + 1, :].reshape(D)
 
@@ -713,21 +754,25 @@
         "middle",
         middle_kernel,
         [(slot_shape, bf16), chunk_f32, ((LAST, D), bf16), chunk_low],
-        (every, state, cotangent, w_out, gain_one, shift_one, *biases_up, bias_down, gain_two, shift_two),
+        (
+            every, state, cotangent, w_out, gain_one, shift_one, biases_up[0], bias_down, gain_two, shift_two,
+            *biases_up[1:],
+        ),
         scratch=[
             pltpu.VMEM((CH, D + T), f32),
             pltpu.VMEM((R, T, D), bf16),
             pltpu.VMEM((D, D), bf16),
+            *[pltpu.VMEM((D,), f32)] * 6,
             pltpu.VMEM((2, NN, NW, D // NW, F), bf16),
             pltpu.VMEM((NN, CH, F), f32),
             pltpu.VMEM((CH, D), f32),
             pltpu.VMEM(slot_shape, bf16),
             pltpu.VMEM((LAST, D), bf16),
             pltpu.VMEM((CH, D), bf16),
-            pltpu.SemaphoreType.DMA((11,)),
+            pltpu.SemaphoreType.DMA((17,)),
         ],
         mib=32,
-        far_in=range(4),
+        far_in=range(10),
         far=range(4),
     )
     got = exchange_all(later(slots, *firsts[1:]))
@@ -771,17 +816,16 @@
             pltpu.VMEM((HD, L), f32),
             pltpu.SemaphoreType.DMA((NW,)),
         ],
-        far_in=range(7),
+        any_in=(0,),
+        far_in=range(1, 7),
         far=(0,),
         after=(token, *packs[1:]),
         token=True,
     )
-    layers = gather_narrow(later(layer, token))
-    whole_out = ((R, T, D), f32)
-    *sends, up_keep, out_whole, vec = call(
+    *sends, up_keep, vec = call(
         "weights",
         weights_kernel,
-        [((96, 2 * F), bf16)] * 4 + [((D // 2, 2 * F), f32), ((D, E), f32), ((8, D), f32)],
+        [((96, WG), bf16)] * 4 + [((D // 2, WG), bf16), ((8, D), f32)],
         (*firsts, *packs, every, hidden, slope),
         scratch=[
             pltpu.VMEM((NN, FIRST, D), bf16),
@@ -789,81 +833,99 @@
             pltpu.VMEM((NW, D // NW, F), bf16),
             pltpu.VMEM((TOK, F), bf16),
             pltpu.VMEM((TOK, F), f32),
-            pltpu.VMEM((D, 2 * F), f32),
-            pltpu.VMEM((D // 2, 2 * F), bf16),
+            pltpu.VMEM((D, WG), bf16),
+            pltpu.VMEM((8, D), f32),
             pltpu.VMEM((NN, 8, D), f32),
             pltpu.SemaphoreType.DMA((11,)),
         ],
         mib=32,
         far_in=range(11),
-        far=range(5),
+        far=range(6),
         after=(token,),
     )
-    slots_shape = ((NW, G, 2 * F + D + D // 3), bf16)
-    last_slots, added = call(
-        "weights_add",
-        weights_add_kernel,
-        [slots_shape],
-        (up_keep, *(other_core(send) for send in sends)),
-        scratch=[
-            pltpu.VMEM((D // 2, 2 * F), f32),
-            pltpu.VMEM((D // 2, 2 * F), bf16),
-            pltpu.VMEM((NW, G, 2 * F), bf16),
+    got = exchange(slots)
+    last_shape = (NW, FIRST_ROWS + LAST_ROWS, T)
+    slots, tail, added = call(
+        "first_add",
+        first_add_kernel,
+        [(last_shape, bf16), ((D, T), f32)],
+        (up_keep, vec, *(other_core(send) for send in sends), other_core(vec)),
+        scratch=[
+            pltpu.VMEM((D // 2, WG), bf16),
+            pltpu.VMEM((D // 2, WG), bf16),
+            pltpu.VMEM((8, D), f32),
+            pltpu.VMEM((8, D), f32),
+            pltpu.VMEM((NW, FIRST_ROWS, T), bf16),
             pltpu.SemaphoreType.DMA((NW,)),
         ],
-        far_in=range(5),
+        far_in=range(2),
+        any_in=range(2, 7),
         far=(0,),
         token=True,
     )
-
-    got = exchange(slots)
-    *parts, send, keep, sums = call(
+    grad, send, keep, sums = call(
+        "input_weights",
+        input_weights_kernel,
+        [((TOK, 3 * E), bf16), ((D // 2 + 16, QKV), bf16), ((D // 2, QKV), bf16), ((1, 3 * E), f32)],
+        (hidden_in, got),
+        scratch=[
+            pltpu.VMEM((D, QKV), bf16),
+            pltpu.VMEM((16, QKV), bf16),
+            pltpu.VMEM((R, T, D), bf16),
+            pltpu.SemaphoreType.DMA((3,)),
+        ],
+        far_in=(0,),
+        far=(1, 2),
+        after=(added,),
+    )
+    parts = call(
         "input_back",
         input_back_kernel,
-        [*parts4, ((D // 2 + 16, D), bf16), ((D // 2, D), f32), ((1, 3 * E), f32)],
-        (hidden_in, query_t, key_t, value_t, got, out_whole, vec),
+        parts4,
+        (query_t, key_t, value_t, grad),
         scratch=[
             pltpu.VMEM((CH, D), f32),
             pltpu.VMEM((CH, D), bf16),
             pltpu.VMEM((CH, D), bf16),
             pltpu.VMEM((CH, D), bf16),
-            pltpu.VMEM((D, D), f32),
-            pltpu.VMEM((D // 2 + 16, D), bf16),
             pltpu.VMEM((TOK, D), f32),
-            pltpu.VMEM((R, T, D), bf16),
             pltpu.VMEM((3, E, D), bf16),
-            pltpu.SemaphoreType.DMA((6,)),
-        ],
-        far_in=range(4),
-        far=range(6),
-        after=(added, *layers[1:]),
+            pltpu.SemaphoreType.DMA((4,)),
+        ],
+        far_in=range(3),
+        far=range(4),
     )
     parts = scatter_narrow(parts)
     slots, b_query, b_key, b_value = call(
-        "input_add",
-        input_add_kernel,
-        [slots_shape, ((E,), f32), ((E,), f32), ((E,), f32)],
-        (keep, other_core(send), last_slots, sums, vec),
-        scratch=[
-            pltpu.VMEM((D // 2, D), f32),
-            pltpu.VMEM((D // 2 + 16, D), bf16),
-            pltpu.VMEM((NW, G, D + D // 3), bf16),
+        "last_add",
+        last_add_kernel,
+        [(last_shape, bf16), ((E,), f32), ((E,), f32), ((E,), f32)],
+        (keep, slots, other_core(send), tail, sums),
+        scratch=[
+            pltpu.VMEM((D // 2, QKV), bf16),
+            pltpu.VMEM((D // 2 + 16, QKV), bf16),
+            pltpu.VMEM((NW, LAST_ROWS, T), bf16),
             pltpu.SemaphoreType.DMA((NW,)),
         ],
-        any_in=(1,),
-        far_in=(0, 2),
+        far_in=range(2),
+        any_in=(2,),
         far=(0,),
-        aliases={2: 0},
+        aliases={1: 0},
     )
     (input_low,) = call("input_chunk", input_chunk_kernel, [chunk_low], (parts[0], grad_one, *parts[1:]),
         scratch=[pltpu.VMEM((CH, D), f32), pltpu.VMEM((CH, D), f32), pltpu.SemaphoreType.DMA((2,))],
         cost=COST, far_in=(0, 1),
     )
+    layers = gather_narrow(later(layer, parts[2]))
+    whole_out = ((R, T, D), f32)
     (layer_out,) = call("layer_out", spread_kernel, [whole_out], layers)
     (grad_input,) = call("grad_input", spread_kernel, [whole_out], gather_narrow(input_low))
     flat = ((D,), f32)
-    grad_up, grad_down, g_query, g_key, g_value, g_out, g_two, s_two, b_down, g_one, s_one, b_out, b_up = call(
-        "input_sum", input_sum_kernel, [((G, F), f32)] * 2 + [((G, E), f32)] * 4 + [flat] * 7, (exchange(slots),)
+    g_query, g_key, g_value, grad_up, grad_down, g_out, g_two, s_two, b_down, g_one, s_one, b_out, b_up = call(
+        "last_sum",
+        last_sum_kernel,
+        [((G, E), f32)] * 3 + [((G, F), f32)] * 2 + [((G, E), f32)] + [flat] * 7,
+        (exchange(slots),),
     )
     return (
         layer_out, grad_input, g_query, b_query, g_key, b_key, g_value, b_value, g_out.T, b_out,

time: 211 us -> 204 us (0.967)
  waiting for transfers between devices: 54.6 us -> 50 us
    all_to_all x3, waiting for transfers between devices: 21.9 us -> 16.9 us  [exchange(): return lax.all_to_all(slots, 'wide', 0, 0, tiled=True)]
    ppermute x8 -> x9, waiting for transfers between devices: 0.02 us -> 2.28 us  [other_core(): return lax.ppermute(x, 'dp', [(0, 1), (1, 0)])]
    pallas_call x15 -> x16, Pallas kernels: 71.8 us -> 71.7 us  [call(): pl.pallas_call(run, out_shape=[shape(k, s, t) for k, (s, t) in enumerate(...]
  transfers between devices with their start and end apart: 38 -> 39, of which waited for: 18 -> 19; matrix products, arithmetic and copies ran while one was open for 0% -> 0% of each run, Pallas kernels for 24% -> 26%
where the time goes in v3:
time: 204 us
  Pallas kernels  71.7 us (35%)
  starting transfers between devices  63.7 us (31%)
  waiting for transfers between devices  50 us (25%)
  between operations  14.5 us (7%)
  local copies, waits for them, and re-layouts  2.75 us (1%)
    pallas_call x16, Pallas kernels, call(): pl.pallas_call(run, out_shape=[shape(k, s, t) for k, (s, t) in enumerate(...  71.7 us
    ppermute x24, starting transfers between devices, shifted(): return lax.ppermute(x, 'narrow', [(i, (i + s) % NN) for i in range(NN)])  31.9 us
    ppermute x24, waiting for transfers between devices, shifted(): return lax.ppermute(x, 'narrow', [(i, (i + s) % NN) for i in range(NN)])  21.3 us
    all_to_all x3, waiting for transfers between devices, exchange(): return lax.all_to_all(slots, 'wide', 0, 0, tiled=True)  16.9 us
    all_to_all x3, starting transfers between devices, exchange(): return lax.all_to_all(slots, 'wide', 0, 0, tiled=True)  16.3 us
    all_to_all x2, starting transfers between devices, exchange_all(): return lax.all_to_all(slots, ('wide', 'narrow'), 0, 0, tiled=True)  13.5 us
    all_to_all x2, waiting for transfers between devices, exchange_all(): return lax.all_to_all(slots, ('wide', 'narrow'), 0, 0, tiled=True)  9.49 us
  transfers between devices with their start and end apart: 39, of which 19 were waited for; matrix products, arithmetic and copies ran while one was open for 0% of the time, Pallas kernels for 26%

profile of v3, /device:TPU:0, one launch (start us, length us, event | category | flops | bytes accessed | tf_op | source)
XLA Modules:
  0.0 203.6 jit_solution(989326782828521024)
XLA Ops:
  7.2 0.9 bitcast_select_fusion.refs_0_
  8.2 4.2 %collective-permute-start.2 = (bf16[48,768]{1,0:T(8,128)(2,1)S(1)}, bf16[48,768]{1,0:T(8,128)(2,1)S(1)}, u32[]{:S(2)}, u32[]{:S(2)}) collective-permute-start(bf16[48,768]{1,0:T(8,128)(2,1)S(1)} %bitcast_select_fusion.refs_0_), channel_id=1, source_target_pairs={{0,3},{1,0},{2,1},{3,2},{4,7},{5,4},{6,5},{7,6},{8,11},{9,8},{10,9... | collective-permute-start | bytes 221192 | tf_op jit(solution)/shard_map/ppermute | solution.py:636
  12.4 1.3 collective-permute-start
  13.6 3.1 %project.1 = (bf16[16,208,128]{2,1,0:T(8,128)(2,1)}, f32[8,128]{1,0:T(8,128)S(1)}) custom-call(bf16[3,128,768]{2,1,0:T(8,128)(2,1)} %refs_0_.5, s32[3,128]{1,0:T(4,128)} %refs_1_.2, bf16[192,768]{1,0:T(8,128)(2,1)} %bitcast.9, f32[192]{0:T(256)} %refs_3_.1, bf16[192,768]{1,0:T(8,128)(2,1)} %bitcast.11, f32[192]{0:T(256)} %refs_5_.3, ...), custom_call_target="tpu_custom_call" | custom-call | flops 1024 | bytes 1024 | tf_op jit(solution)/shard_map/project/pallas_call | solution.py:71
  16.8 1.6 collective-permute-done.1.refs_2_
  18.9 0.7 stack.1
  19.7 7.2 %all-to-all-start = ((bf16[16,208,128]{2,1,0:T(8,128)(2,1)}), bf16[16,208,128]{2,1,0:T(8,128)(2,1)S(1)}, u32[]{:S(2)}, u32[]{:S(2)}) async-start(bf16[16,208,128]{2,1,0:T(8,128)(2,1)} %get-tuple-element.78), calls=%async_computation | async-start | bytes 1703936 | tf_op jit(solution)/shard_map/all_to_all | solution.py:652
  26.9 0.9 collective-permute-start.5
  27.8 1.4 collective-permute-start.4
  29.2 0.6 collective-permute-start.3
  29.8 2.8 %collective-permute-done.5.refs_4_.refs_3_ = bf16[96,768]{1,0:T(8,128)(2,1)S(1)} collective-permute-done((bf16[96,768]{1,0:T(8,128)(2,1)S(1)}, bf16[96,768]{1,0:T(8,128)(2,1)S(1)}, u32[]{:S(2)}, u32[]{:S(2)}) %collective-permute-start.5) | collective-permute-done | bytes 147488 | tf_op jit(solution)/shard_map/ppermute | solution.py:636
  32.6 2.2 %collective-permute-done.4.refs_3_.refs_2_ = bf16[96,768]{1,0:T(8,128)(2,1)S(1)} collective-permute-done((bf16[96,768]{1,0:T(8,128)(2,1)S(1)}, bf16[96,768]{1,0:T(8,128)(2,1)S(1)}, u32[]{:S(2)}, u32[]{:S(2)}) %collective-permute-start.4) | collective-permute-done | bytes 147488 | tf_op jit(solution)/shard_map/ppermute | solution.py:636
  34.8 1.5 collective-permute-done.3.refs_2_.refs_1_
  36.3 6.1 %all-to-all-done.refs_0_ = bf16[16,208,128]{2,1,0:T(8,128)(2,1)S(1)} async-done(((bf16[16,208,128]{2,1,0:T(8,128)(2,1)}), bf16[16,208,128]{2,1,0:T(8,128)(2,1)S(1)}, u32[]{:S(2)}, u32[]{:S(2)}) %all-to-all-start) | async-done | bytes 852000 | tf_op jit(solution)/shard_map/all_to_all | solution.py:652
  42.5 13.4 %attend.1 = (bf16[64,16,128]{2,1,0:T(8,128)(2,1)}, bf16[80,2048]{1,0:T(8,128)(2,1)}, bf16[80,2048]{1,0:T(8,128)(2,1)}, bf16[80,2048]{1,0:T(8,128)(2,1)}, f32[64,...) custom-call(bf16[16,208,128]{2,1,0:T(8,128)(2,1)S(1)} %all-to-all-done.refs_0_, ...), custom_call_target="tpu_custom_call" | custom-call | flops 1024 | bytes 1024 | tf_op jit(solution)/shard_map/attend/pallas_call | solution.py:71
  55.9 5.2 %all-to-all-start.1 = ((bf16[64,16,128]{2,1,0:T(8,128)(2,1)}), bf16[64,16,128]{2,1,0:T(8,128)(2,1)S(1)}, u32[]{:S(2)}, u32[]{:S(2)}) async-start(bf16[64,16,128]{2,1,0:T(8,128)(2,1)} %get-tuple-element.79), calls=%async_computation.1 | async-start | bytes 524288 | tf_op jit(solution)/shard_map/all_to_all | solution.py:656
  61.2 0.5 collective-permute-start.7
  61.8 2.8 %collective-permute-start.11 = (f32[768]{0:T(1024)S(1)}, f32[768]{0:T(1024)S(1)}, u32[]{:S(2)}, u32[]{:S(2)}) collective-permute-start(f32[768]{0:T(1024)S(1)} %copy-done.5), channel_id=1, source_target_pairs={{0,3},{1,0},{2,1},{3,2},{4,7},{5,4},{6,5},{7,6},{8,11},{9,8},{10,9... | collective-permute-start | bytes 9224 | tf_op jit(solution)/shard_map/ppermute | solution.py:636
  64.6 0.9 collective-permute-start.10
  65.9 1.1 collective-permute-start.9
  67.0 2.7 %collective-permute-done.10.refs_13_.refs_11_ = f32[768]{0:T(1024)S(1)} collective-permute-done((f32[768]{0:T(1024)S(1)}, f32[768]{0:T(1024)S(1)}, u32[]{:S(2)}, u32[]{:S(2)}) %collective-permute-start.10) | collective-permute-done | bytes 3104 | tf_op jit(solution)/shard_map/ppermute | solution.py:636
  69.7 1.3 collective-permute-done.9.refs_12_.refs_10_
  71.1 2.9 %all-to-all-done.1.refs_8_ = bf16[64,16,128]{2,1,0:T(8,128)(2,1)S(1)} async-done(((bf16[64,16,128]{2,1,0:T(8,128)(2,1)}), bf16[64,16,128]{2,1,0:T(8,128)(2,1)S(1)}, u32[]{:S(2)}, u32[]{:S(2)}) %all-to-all-start.1) | async-done | bytes 262176 | tf_op jit(solution)/shard_map/all_to_all | solution.py:656
  74.0 3.0 %first.1 = (bf16[768,768]{1,0:T(8,128)(2,1)}, f32[96,896]{1,0:T(8,128)}, bf16[128,768]{1,0:T(8,128)(2,1)}, bf16[128,768]{1,0:T(8,128)(2,1)}, bf16[128,768]{1,0:T...) custom-call(bf16[192,768]{1,0:T(8,128)(2,1)} %refs_0_.4, bf16[96,768]{1,0:T(8,128)(2,1)} %copy-done.18, ...), custom_call_target="tpu_custom_call" | custom-call | flops 1024 | bytes 1024 | tf_op jit(solution)/shard_map/first/pallas_call | solution.py:71
  77.4 2.3 %collective-permute-start.13 = (bf16[128,768]{1,0:T(8,128)(2,1)}, bf16[128,768]{1,0:T(8,128)(2,1)S(1)}, u32[]{:S(2)}, u32[]{:S(2)}) collective-permute-start(bf16[128,768]{1,0:T(8,128)(2,1)} %get-tuple-element.86), channel_id=1, source_target_pairs={{0,2},{1,3},{2,0},{3,1},{4,6},{5,7},{6,4},{7,5},{8,10},{9,11},{10,... | collective-permute-start | bytes 589832 | tf_op jit(solution)/shard_map/ppermute | solution.py:636
  80.2 11.1 %middle.1 = (bf16[64,16,128]{2,1,0:T(8,128)(2,1)}, f32[96,768]{1,0:T(8,128)}, bf16[208,768]{1,0:T(8,128)(2,1)}, bf16[96,768]{1,0:T(8,128)(2,1)}) custom-call(bf16[2,16,4,48,768]{4,3,2,1,0:T(8,128)(2,1)} %later.3.refs_0_.refs_4_.refs_8_, f32[96,896]{1,0:T(8,128)} %get-tuple-element.81.refs_1_, bf16[3,128,768]{2,1,0:T(8,128)(2,1)} %refs_2_.1, ...), custom_call_target="tpu_custom_call" | custom-call | flops 1024 | bytes 1024 | tf_op jit(solution)/shard_map/middle/pallas_call | solution.py:71
  91.3 3.0 %collective-permute-start.17 = (bf16[208,768]{1,0:T(8,128)(2,1)}, bf16[208,768]{1,0:T(8,128)(2,1)S(1)}, u32[]{:S(2)}, u32[]{:S(2)}) collective-permute-start(bf16[208,768]{1,0:T(8,128)(2,1)} %get-tuple-element.96.refs_4_), channel_id=1, source_target_pairs={{0,3},{1,0},{2,1},{3,2},{4,7},{5,4},{6,5},{7,6},{8,11},{9,8},{10,9... | collective-permute-start | bytes 958472 | tf_op jit(solution)/shard_map/ppermute | solution.py:636
  94.3 0.7 collective-permute-start.16
  95.0 0.9 collective-permute-start.15
  96.0 0.6 copy-done.10
  96.7 8.3 %all-to-all-start.2 = ((bf16[64,16,128]{2,1,0:T(8,128)(2,1)}), bf16[64,16,128]{2,1,0:T(8,128)(2,1)S(1)}, u32[]{:S(2)}, u32[]{:S(2)}) async-start(bf16[64,16,128]{2,1,0:T(8,128)(2,1)} %later.4), calls=%async_computation.2 | async-start | bytes 524288 | tf_op jit(solution)/shard_map/all_to_all | solution.py:656
  105.0 3.8 %hidden.1 = (bf16[384,768]{1,0:T(8,128)(2,1)}, f32[384,768]{1,0:T(8,128)}, f32[8,128]{1,0:T(8,128)S(1)}) custom-call(bf16[128,768]{1,0:T(8,128)(2,1)} %get-tuple-element.94.refs_0_, bf16[128,768]{1,0:T(8,128)(2,1)} %copy-done.11, bf16[128,768]{1,0:T(8,128)(2,1)} %copy-done.10, bf16[128,768]{1,0:T(8,128)(2,1)} %copy-done.9, ...), custom_call_target="tpu_custom_call" | custom-call | flops 1024 | bytes 1024 | tf_op jit(solution)/shard_map/hidden/pallas_call | solution.py:71
  108.8 6.6 %all-to-all-done.2.refs_0_ = bf16[64,16,128]{2,1,0:T(8,128)(2,1)S(1)} async-done(((bf16[64,16,128]{2,1,0:T(8,128)(2,1)}), bf16[64,16,128]{2,1,0:T(8,128)(2,1)S(1)}, u32[]{:S(2)}, u32[]{:S(2)}) %all-to-all-start.2) | async-done | bytes 262176 | tf_op jit(solution)/shard_map/all_to_all | solution.py:656
  115.5 0.7 copy-done.12
  116.4 14.5 %attend_back.1 = (bf16[16,208,128]{2,1,0:T(8,128)(2,1)}, f32[8,128]{1,0:T(8,128)S(1)}) custom-call(bf16[64,16,128]{2,1,0:T(8,128)(2,1)S(1)} %all-to-all-done.2.refs_0_, f32[64,2048]{1,0:T(8,128)} %get-tuple-element.88.refs_1_, bf16[80,2048]{1,0:T(8,128)(2,1)} %get-tuple-element.89.refs_2_, bf16[80,2048]{1,0:T(8,128)(2,1)} %get-tuple-element.90.refs_3_, ...), custom_call_target="tpu_custom_call" | custom-call | flops 1024 | bytes 1024 | tf_op jit(solution)/shard_map/attend_back/pallas_call | solution.py:71
  131.0 4.1 %all-to-all-start.3 = ((bf16[16,208,128]{2,1,0:T(8,128)(2,1)}), bf16[16,208,128]{2,1,0:T(8,128)(2,1)S(1)}, u32[]{:S(2)}, u32[]{:S(2)}) async-start(bf16[16,208,128]{2,1,0:T(8,128)(2,1)} %get-tuple-element.97), calls=%async_computation.3 | async-start | bytes 1703936 | tf_op jit(solution)/shard_map/all_to_all | solution.py:652
  135.0 6.3 %weights.1 = (bf16[96,1792]{1,0:T(8,128)(2,1)}, bf16[96,1792]{1,0:T(8,128)(2,1)}, bf16[96,1792]{1,0:T(8,128)(2,1)}, bf16[96,1792]{1,0:T(8,128)(2,1)}, bf16[384,1792]{1,0:T(8,128)(2,1)}, /*index=5*/f32[8,768]{1,0:T(8,128)}) custom-call(bf16[128,768]{1,0:T(8,128)(2,1)} %get-tuple-element.94.refs_0_, bf16[128,768]{1,0:T(8,128)(2,1)} %copy-done.11, ...), custom_call_target="tpu_custom_call" | custom-call | flops 1024 | bytes 1024 | tf_op jit(solution)/shard_map/weights/pallas_call | solution.py:71
  141.5 0.5 collective-permute-start.19
  142.6 2.3 %collective-permute-done.22.refs_6_ = f32[8,768]{1,0:T(8,128)S(1)} collective-permute-done((f32[8,768]{1,0:T(8,128)}, f32[8,768]{1,0:T(8,128)S(1)}, u32[]{:S(2)}, u32[]{:S(2)}) %collective-permute-start.22) | collective-permute-done | bytes 24608 | tf_op jit(solution)/shard_map/ppermute | solution.py:648
  144.8 3.1 %first_add.1 = (bf16[16,480,128]{2,1,0:T(8,128)(2,1)}, f32[768,128]{1,0:T(8,128)S(1)}, f32[8,128]{1,0:T(8,128)S(1)}) custom-call(bf16[384,1792]{1,0:T(8,128)(2,1)} %get-tuple-element.101.refs_0_, f32[8,768]{1,0:T(8,128)} %get-tuple-element.102.refs_1_, bf16[96,1792]{1,0:T(8,128)(2,1)S(1)} %collective-permute-done.18.refs_2_, ...), custom_call_target="tpu_custom_call" | custom-call | flops 1024 | bytes 1024 | tf_op jit(solution)/shard_map/first_add/pallas_call | solution.py:71
  148.0 2.5 %all-to-all-done.3.refs_1_ = bf16[16,208,128]{2,1,0:T(8,128)(2,1)S(1)} async-done(((bf16[16,208,128]{2,1,0:T(8,128)(2,1)}), bf16[16,208,128]{2,1,0:T(8,128)(2,1)S(1)}, u32[]{:S(2)}, u32[]{:S(2)}) %all-to-all-start.3) | async-done | bytes 852000 | tf_op jit(solution)/shard_map/all_to_all | solution.py:652
  150.4 2.8 %input_weights.1 = (bf16[384,576]{1,0:T(8,128)(2,1)S(1)}, bf16[400,640]{1,0:T(8,128)(2,1)}, bf16[384,640]{1,0:T(8,128)(2,1)}, f32[1,576]{1,0:T(1,128)S(1)}) custom-call(bf16[3,128,768]{2,1,0:T(8,128)(2,1)} %refs_0_.5, bf16[16,208,128]{2,1,0:T(8,128)(2,1)S(1)} %all-to-all-done.3.refs_1_, f32[8,128]{1,0:T(8,128)S(1)} %get-tuple-element.107.refs_2_), custom_call_target="tpu_custom_call" | custom-call | flops 1024 | bytes 1024 | tf_op jit(solution)/shard_map/input_weights/pallas_call | solution.py:71
  153.3 2.7 %input_back.1 = (f32[96,768]{1,0:T(8,128)}, bf16[96,768]{1,0:T(8,128)(2,1)}, bf16[96,768]{1,0:T(8,128)(2,1)}, bf16[96,768]{1,0:T(8,128)(2,1)}) custom-call(bf16[192,768]{1,0:T(8,128)(2,1)} %bitcast.10, bf16[192,768]{1,0:T(8,128)(2,1)} %bitcast.12, bf16[192,768]{1,0:T(8,128)(2,1)} %bitcast.14, bf16[384,576]{1,0:T(8,128)(2,1)S(1)} %get-tuple-element.108.refs_3_), custom_call_target="tpu_custom_call" | custom-call | flops 1024 | bytes 1024 | tf_op jit(solution)/shard_map/input_back/pallas_call | solution.py:71
  156.1 0.7 collective-permute-start.23
  156.8 3.2 %collective-permute-start.28 = (bf16[96,768]{1,0:T(8,128)(2,1)}, bf16[96,768]{1,0:T(8,128)(2,1)S(1)}, u32[]{:S(2)}, u32[]{:S(2)}) collective-permute-start(bf16[96,768]{1,0:T(8,128)(2,1)} %get-tuple-element.113), channel_id=1, source_target_pairs={{0,3},{1,0},{2,1},{3,2},{4,7},{5,4},{6,5},{7,6},{8,11},{9,8},{10,9... | collective-permute-start | bytes 442376 | tf_op jit(solution)/shard_map/ppermute | solution.py:636
  160.0 2.7 %last_add.1 = (bf16[16,480,128]{2,1,0:T(8,128)(2,1)}, f32[192]{0:T(256)}, f32[192]{0:T(256)}, f32[192]{0:T(256)}) custom-call(bf16[384,640]{1,0:T(8,128)(2,1)} %get-tuple-element.114.refs_0_, bf16[16,480,128]{2,1,0:T(8,128)(2,1)} %get-tuple-element.115.refs_1_, ...), custom_call_target="tpu_custom_call", output_to_operand_aliasing={{0}: (1, {})} | custom-call | flops 1024 | bytes 1024 | tf_op jit(solution)/shard_map/last_add/pallas_call | solution.py:71
  162.7 5.1 %all-to-all-start.4 = ((bf16[16,480,128]{2,1,0:T(8,128)(2,1)}), bf16[16,480,128]{2,1,0:T(8,128)(2,1)S(1)}, u32[]{:S(2)}, u32[]{:S(2)}) async-start(bf16[16,480,128]{2,1,0:T(8,128)(2,1)} %get-tuple-element.119), calls=%async_computation.4 | async-start | bytes 3932160 | tf_op jit(solution)/shard_map/all_to_all | solution.py:652
  167.8 1.2 input_chunk.1.refs_0_
  169.0 0.8 collective-permute-start.31
  169.9 0.9 collective-permute-start.30
  170.7 1.3 collective-permute-start.29
  172.1 1.9 collective-permute-start.26
  174.0 1.5 collective-permute-start.25
  175.4 0.5 collective-permute-done.31.refs_3_
  175.9 0.8 collective-permute-start.24
  176.7 1.4 collective-permute-done.30.refs_2_
  178.1 3.8 %collective-permute-done.29.refs_1_ = bf16[96,768]{1,0:T(8,128)(2,1)S(1)} collective-permute-done((bf16[96,768]{1,0:T(8,128)(2,1)S(1)}, bf16[96,768]{1,0:T(8,128)(2,1)S(1)}, u32[]{:S(2)}, u32[]{:S(2)}) %collective-permute-start.29) | collective-permute-done | bytes 147488 | tf_op jit(solution)/shard_map/ppermute | solution.py:636
  181.9 1.1 grad_input.1
  183.0 1.2 collective-permute-done.25.refs_2_
  184.2 1.3 collective-permute-done.24.refs_1_
  185.6 0.9 copy-done.1
  186.5 1.1 layer_out.1
  187.6 8.3 %all-to-all-done.4.refs_0_ = bf16[16,480,128]{2,1,0:T(8,128)(2,1)S(1)} async-done(((bf16[16,480,128]{2,1,0:T(8,128)(2,1)}), bf16[16,480,128]{2,1,0:T(8,128)(2,1)S(1)}, u32[]{:S(2)}, u32[]{:S(2)}) %all-to-all-start.4) | async-done | bytes 1966112 | tf_op jit(solution)/shard_map/all_to_all | solution.py:652
  195.9 0.9 last_sum.1
  (83 shorter events, 3.4 us)
Async XLA Ops:
  7.2 73.0 %all-gather.3.cloned.1.call-start = ((), (), s32[]{:S(2)}) async-start(), calls=%async_computation.5 | async-start | bytes 9732096 | tf_op jit(solution)/shard_map/all_gather | solution.py:701
  8.2 8.6 %collective-permute-start.2 = (bf16[48,768]{1,0:T(8,128)(2,1)S(1)}, bf16[48,768]{1,0:T(8,128)(2,1)S(1)}, u32[]{:S(2)}, u32[]{:S(2)}) collective-permute-start(bf16[48,768]{1,0:T(8,128)(2,1)S(1)} %bitcast_select_fusion.refs_0_), channel_id=1, source_target_pairs={{0,3},{1,0},{2,1},{3,2},{4,7},{5,4},{6,5},{7,6},{8,11},{9,8},{10,9... | collective-permute-start | bytes 221192 | tf_op jit(solution)/shard_map/ppermute | solution.py:636
  12.4 6.0 %collective-permute-start.1 = (bf16[48,768]{1,0:T(8,128)(2,1)S(1)}, bf16[48,768]{1,0:T(8,128)(2,1)S(1)}, u32[]{:S(2)}, u32[]{:S(2)}) collective-permute-start(bf16[48,768]{1,0:T(8,128)(2,1)S(1)} %bitcast_select_fusion.refs_0_), channel_id=1, source_target_pairs={{0,2},{1,3},{2,0},{3,1},{4,6},{5,7},{6,4},{7,5},{8,10},{9,11},{10,... | collective-permute-start | bytes 221192 | tf_op jit(solution)/shard_map/ppermute | solution.py:636
  12.4 6.5 %collective-permute-start = (bf16[48,768]{1,0:T(8,128)(2,1)S(1)}, bf16[48,768]{1,0:T(8,128)(2,1)S(1)}, u32[]{:S(2)}, u32[]{:S(2)}) collective-permute-start(bf16[48,768]{1,0:T(8,128)(2,1)S(1)} %bitcast_select_fusion.refs_0_), channel_id=1, source_target_pairs={{0,1},{1,2},{2,3},{3,0},{4,5},{5,6},{6,7},{7,4},{8,9},{9,10},{10,1... | collective-permute-start | bytes 221192 | tf_op jit(solution)/shard_map/ppermute | solution.py:636
  13.6 13.3 %copy-start.15 = (bf16[192,768]{1,0:T(8,128)(2,1)S(1)}, bf16[192,768]{1,0:T(8,128)(2,1)}, u32[]{:S(2)}) copy-start(bf16[192,768]{1,0:T(8,128)(2,1)} %refs_0_.4) | copy-start | bytes 884740
  13.6 28.8 %copy-start.22 = (f32[64]{0:T(128)S(1)}, f32[64]{0:T(128)}, u32[]{:S(2)}) copy-start(f32[64]{0:T(128)} %constant.14.clone) | copy-start | bytes 772
  19.6 42.1 %copy-start.5 = (f32[768]{0:T(1024)S(1)}, f32[768]{0:T(1024)}, u32[]{:S(2)}) copy-start(f32[768]{0:T(1024)} %refs_5_.5) | copy-start | bytes 9220
  19.6 54.3 %copy-start = (bf16[3,128,768]{2,1,0:T(8,128)(2,1)S(1)}, bf16[3,128,768]{2,1,0:T(8,128)(2,1)}, u32[]{:S(2)}) copy-start(bf16[3,128,768]{2,1,0:T(8,128)(2,1)} %refs_0_.5) | copy-start | bytes 1769476
  19.7 54.3 %copy-start.3 = (f32[768]{0:T(1024)S(1)}, f32[768]{0:T(1024)}, u32[]{:S(2)}) copy-start(f32[768]{0:T(1024)} %refs_4_.1) | copy-start | bytes 9220
  19.7 54.3 %copy-start.4 = (f32[768]{0:T(1024)S(1)}, f32[768]{0:T(1024)}, u32[]{:S(2)}) copy-start(f32[768]{0:T(1024)} %refs_5_.4) | copy-start | bytes 9220
  19.7 54.3 %copy-start.7 = (f32[768]{0:T(1024)S(1)}, f32[768]{0:T(1024)}, u32[]{:S(2)}) copy-start(f32[768]{0:T(1024)} %refs_9_.2) | copy-start | bytes 9220
  19.7 22.7 %all-to-all-start = ((bf16[16,208,128]{2,1,0:T(8,128)(2,1)}), bf16[16,208,128]{2,1,0:T(8,128)(2,1)S(1)}, u32[]{:S(2)}, u32[]{:S(2)}) async-start(bf16[16,208,128]{2,1,0:T(8,128)(2,1)} %get-tuple-element.78), calls=%async_computation | async-start | bytes 1703936 | tf_op jit(solution)/shard_map/all_to_all | solution.py:652
  26.9 5.7 %collective-permute-start.5 = (bf16[96,768]{1,0:T(8,128)(2,1)S(1)}, bf16[96,768]{1,0:T(8,128)(2,1)S(1)}, u32[]{:S(2)}, u32[]{:S(2)}) collective-permute-start(bf16[96,768]{1,0:T(8,128)(2,1)S(1)} %constant_dynamic-slice_fusion), channel_id=1, source_target_pairs={{0,3},{1,0},{2,1},{3,2},{4,7},{5,4},{6,5},{7,6},{8,11},{9,8},{10,9... | collective-permute-start | bytes 442376 | tf_op jit(solution)/shard_map/ppermute | solution.py:636
  27.8 7.0 %collective-permute-start.4 = (bf16[96,768]{1,0:T(8,128)(2,1)S(1)}, bf16[96,768]{1,0:T(8,128)(2,1)S(1)}, u32[]{:S(2)}, u32[]{:S(2)}) collective-permute-start(bf16[96,768]{1,0:T(8,128)(2,1)S(1)} %constant_dynamic-slice_fusion), channel_id=1, source_target_pairs={{0,2},{1,3},{2,0},{3,1},{4,6},{5,7},{6,4},{7,5},{8,10},{9,11},{10,... | collective-permute-start | bytes 442376 | tf_op jit(solution)/shard_map/ppermute | solution.py:636
  29.2 7.1 %collective-permute-start.3 = (bf16[96,768]{1,0:T(8,128)(2,1)S(1)}, bf16[96,768]{1,0:T(8,128)(2,1)S(1)}, u32[]{:S(2)}, u32[]{:S(2)}) collective-permute-start(bf16[96,768]{1,0:T(8,128)(2,1)S(1)} %constant_dynamic-slice_fusion), channel_id=1, source_target_pairs={{0,1},{1,2},{2,3},{3,0},{4,5},{5,6},{6,7},{7,4},{8,9},{9,10},{10,1... | collective-permute-start | bytes 442376 | tf_op jit(solution)/shard_map/ppermute | solution.py:636
  32.6 9.9 %copy-start.16 = (bf16[96,768]{1,0:T(8,128)(2,1)}, bf16[96,768]{1,0:T(8,128)(2,1)S(1)}, u32[]{:S(2)}) copy-start(bf16[96,768]{1,0:T(8,128)(2,1)S(1)} %collective-permute-done.5.refs_4_.refs_3_) | copy-start | bytes 442372
  34.8 7.7 %copy-start.17 = (bf16[96,768]{1,0:T(8,128)(2,1)}, bf16[96,768]{1,0:T(8,128)(2,1)S(1)}, u32[]{:S(2)}) copy-start(bf16[96,768]{1,0:T(8,128)(2,1)S(1)} %collective-permute-done.4.refs_3_.refs_2_) | copy-start | bytes 442372
  36.3 6.2 %copy-start.18 = (bf16[96,768]{1,0:T(8,128)(2,1)}, bf16[96,768]{1,0:T(8,128)(2,1)S(1)}, u32[]{:S(2)}) copy-start(bf16[96,768]{1,0:T(8,128)(2,1)S(1)} %collective-permute-done.3.refs_2_.refs_1_) | copy-start | bytes 442372
  55.9 18.0 %all-to-all-start.1 = ((bf16[64,16,128]{2,1,0:T(8,128)(2,1)}), bf16[64,16,128]{2,1,0:T(8,128)(2,1)S(1)}, u32[]{:S(2)}, u32[]{:S(2)}) async-start(bf16[64,16,128]{2,1,0:T(8,128)(2,1)} %get-tuple-element.79), calls=%async_computation.1 | async-start | bytes 524288 | tf_op jit(solution)/shard_map/all_to_all | solution.py:656
  61.1 9.9 %collective-permute-start.8 = (bf16[96,768]{1,0:T(8,128)(2,1)}, bf16[96,768]{1,0:T(8,128)(2,1)S(1)}, u32[]{:S(2)}, u32[]{:S(2)}) collective-permute-start(bf16[96,768]{1,0:T(8,128)(2,1)} %copy-done.16), channel_id=1, source_target_pairs={{0,64},{64,0},{1,65},{65,1},{2,66},{66,2},{3,67},{67,3},{4,68},{68... | collective-permute-start | bytes 442376 | tf_op jit(solution)/shard_map/ppermute | solution.py:648
  61.2 9.8 %collective-permute-start.7 = (bf16[96,768]{1,0:T(8,128)(2,1)}, bf16[96,768]{1,0:T(8,128)(2,1)S(1)}, u32[]{:S(2)}, u32[]{:S(2)}) collective-permute-start(bf16[96,768]{1,0:T(8,128)(2,1)} %copy-done.17), channel_id=1, source_target_pairs={{0,64},{64,0},{1,65},{65,1},{2,66},{66,2},{3,67},{67,3},{4,68},{68... | collective-permute-start | bytes 442376 | tf_op jit(solution)/shard_map/ppermute | solution.py:648
  61.7 9.4 %collective-permute-start.6 = (bf16[96,768]{1,0:T(8,128)(2,1)}, bf16[96,768]{1,0:T(8,128)(2,1)S(1)}, u32[]{:S(2)}, u32[]{:S(2)}) collective-permute-start(bf16[96,768]{1,0:T(8,128)(2,1)} %copy-done.18), channel_id=1, source_target_pairs={{0,64},{64,0},{1,65},{65,1},{2,66},{66,2},{3,67},{67,3},{4,68},{68... | collective-permute-start | bytes 442376 | tf_op jit(solution)/shard_map/ppermute | solution.py:648
  61.8 4.1 %collective-permute-start.11 = (f32[768]{0:T(1024)S(1)}, f32[768]{0:T(1024)S(1)}, u32[]{:S(2)}, u32[]{:S(2)}) collective-permute-start(f32[768]{0:T(1024)S(1)} %copy-done.5), channel_id=1, source_target_pairs={{0,3},{1,0},{2,1},{3,2},{4,7},{5,4},{6,5},{7,6},{8,11},{9,8},{10,9... | collective-permute-start | bytes 9224 | tf_op jit(solution)/shard_map/ppermute | solution.py:636
  64.6 5.1 %collective-permute-start.10 = (f32[768]{0:T(1024)S(1)}, f32[768]{0:T(1024)S(1)}, u32[]{:S(2)}, u32[]{:S(2)}) collective-permute-start(f32[768]{0:T(1024)S(1)} %copy-done.5), channel_id=1, source_target_pairs={{0,2},{1,3},{2,0},{3,1},{4,6},{5,7},{6,4},{7,5},{8,10},{9,11},{10,... | collective-permute-start | bytes 9224 | tf_op jit(solution)/shard_map/ppermute | solution.py:636
  65.9 5.1 %collective-permute-start.9 = (f32[768]{0:T(1024)S(1)}, f32[768]{0:T(1024)S(1)}, u32[]{:S(2)}, u32[]{:S(2)}) collective-permute-start(f32[768]{0:T(1024)S(1)} %copy-done.5), channel_id=1, source_target_pairs={{0,1},{1,2},{2,3},{3,0},{4,5},{5,6},{6,7},{7,4},{8,9},{9,10},{10,1... | collective-permute-start | bytes 9224 | tf_op jit(solution)/shard_map/ppermute | solution.py:636
  71.0 2.9 %copy-start.19 = (bf16[96,768]{1,0:T(8,128)(2,1)}, bf16[96,768]{1,0:T(8,128)(2,1)S(1)}, u32[]{:S(2)}) copy-start(bf16[96,768]{1,0:T(8,128)(2,1)S(1)} %collective-permute-done.8.refs_6_) | copy-start | bytes 442372
  71.0 2.9 %copy-start.20 = (bf16[96,768]{1,0:T(8,128)(2,1)}, bf16[96,768]{1,0:T(8,128)(2,1)S(1)}, u32[]{:S(2)}) copy-start(bf16[96,768]{1,0:T(8,128)(2,1)S(1)} %collective-permute-done.7.refs_5_) | copy-start | bytes 442372
  71.0 2.9 %copy-start.21 = (bf16[96,768]{1,0:T(8,128)(2,1)}, bf16[96,768]{1,0:T(8,128)(2,1)S(1)}, u32[]{:S(2)}) copy-start(bf16[96,768]{1,0:T(8,128)(2,1)S(1)} %collective-permute-done.6.refs_4_) | copy-start | bytes 442372
  77.0 3.2 %copy-start.8 = (f32[8,128]{1,0:T(8,128)}, f32[8,128]{1,0:T(8,128)S(1)}, u32[]{:S(2)}) copy-start(f32[8,128]{1,0:T(8,128)S(1)} %get-tuple-element.80.refs_1_) | copy-start | bytes 12292
  77.0 18.0 %collective-permute-start.12 = (bf16[128,768]{1,0:T(8,128)(2,1)}, bf16[128,768]{1,0:T(8,128)(2,1)S(1)}, u32[]{:S(2)}, u32[]{:S(2)}) collective-permute-start(bf16[128,768]{1,0:T(8,128)(2,1)} %get-tuple-element.85), channel_id=1, source_target_pairs={{0,3},{1,0},{2,1},{3,2},{4,7},{5,4},{6,5},{7,6},{8,11},{9,8},{10,9... | collective-permute-start | bytes 589832 | tf_op jit(solution)/shard_map/ppermute | solution.py:636
  77.4 18.6 %collective-permute-start.13 = (bf16[128,768]{1,0:T(8,128)(2,1)}, bf16[128,768]{1,0:T(8,128)(2,1)S(1)}, u32[]{:S(2)}, u32[]{:S(2)}) collective-permute-start(bf16[128,768]{1,0:T(8,128)(2,1)} %get-tuple-element.86), channel_id=1, source_target_pairs={{0,2},{1,3},{2,0},{3,1},{4,6},{5,7},{6,4},{7,5},{8,10},{9,11},{10,... | collective-permute-start | bytes 589832 | tf_op jit(solution)/shard_map/ppermute | solution.py:636
  79.7 16.3 %collective-permute-start.14 = (bf16[128,768]{1,0:T(8,128)(2,1)}, bf16[128,768]{1,0:T(8,128)(2,1)S(1)}, u32[]{:S(2)}, u32[]{:S(2)}) collective-permute-start(bf16[128,768]{1,0:T(8,128)(2,1)} %get-tuple-element.87), channel_id=1, source_target_pairs={{0,1},{1,2},{2,3},{3,0},{4,5},{5,6},{6,7},{7,4},{8,9},{9,10},{10,1... | collective-permute-start | bytes 589832 | tf_op jit(solution)/shard_map/ppermute | solution.py:636
  80.2 24.9 %copy-start.6 = (f32[768]{0:T(1024)S(1)}, f32[768]{0:T(1024)}, u32[]{:S(2)}) copy-start(f32[768]{0:T(1024)} %refs_5_.5) | copy-start | bytes 9220
  91.3 24.1 %collective-permute-start.17 = (bf16[208,768]{1,0:T(8,128)(2,1)}, bf16[208,768]{1,0:T(8,128)(2,1)S(1)}, u32[]{:S(2)}, u32[]{:S(2)}) collective-permute-start(bf16[208,768]{1,0:T(8,128)(2,1)} %get-tuple-element.96.refs_4_), channel_id=1, source_target_pairs={{0,3},{1,0},{2,1},{3,2},{4,7},{5,4},{6,5},{7,6},{8,11},{9,8},{10,9... | collective-permute-start | bytes 958472 | tf_op jit(solution)/shard_map/ppermute | solution.py:636
  94.3 21.1 %collective-permute-start.16 = (bf16[208,768]{1,0:T(8,128)(2,1)}, bf16[208,768]{1,0:T(8,128)(2,1)S(1)}, u32[]{:S(2)}, u32[]{:S(2)}) collective-permute-start(bf16[208,768]{1,0:T(8,128)(2,1)} %get-tuple-element.96.refs_4_), channel_id=1, source_target_pairs={{0,2},{1,3},{2,0},{3,1},{4,6},{5,7},{6,4},{7,5},{8,10},{9,11},{10,... | collective-permute-start | bytes 958472 | tf_op jit(solution)/shard_map/ppermute | solution.py:636
  95.0 1.0 copy-start.9
  95.0 20.5 %collective-permute-start.15 = (bf16[208,768]{1,0:T(8,128)(2,1)}, bf16[208,768]{1,0:T(8,128)(2,1)S(1)}, u32[]{:S(2)}, u32[]{:S(2)}) collective-permute-start(bf16[208,768]{1,0:T(8,128)(2,1)} %get-tuple-element.96.refs_4_), channel_id=1, source_target_pairs={{0,1},{1,2},{2,3},{3,0},{4,5},{5,6},{6,7},{7,4},{8,9},{9,10},{10,1... | collective-permute-start | bytes 958472 | tf_op jit(solution)/shard_map/ppermute | solution.py:636
  96.0 0.7 copy-start.10
  96.0 0.8 copy-start.11
  96.7 18.7 %all-to-all-start.2 = ((bf16[64,16,128]{2,1,0:T(8,128)(2,1)}), bf16[64,16,128]{2,1,0:T(8,128)(2,1)S(1)}, u32[]{:S(2)}, u32[]{:S(2)}) async-start(bf16[64,16,128]{2,1,0:T(8,128)(2,1)} %later.4), calls=%async_computation.2 | async-start | bytes 524288 | tf_op jit(solution)/shard_map/all_to_all | solution.py:656
  115.5 0.7 copy-start.12
  115.5 0.9 copy-start.13
  115.5 0.9 copy-start.14
  131.0 19.5 %all-to-all-start.3 = ((bf16[16,208,128]{2,1,0:T(8,128)(2,1)}), bf16[16,208,128]{2,1,0:T(8,128)(2,1)S(1)}, u32[]{:S(2)}, u32[]{:S(2)}) async-start(bf16[16,208,128]{2,1,0:T(8,128)(2,1)} %get-tuple-element.97), calls=%async_computation.3 | async-start | bytes 1703936 | tf_op jit(solution)/shard_map/all_to_all | solution.py:652
  141.4 3.5 %collective-permute-start.18 = (bf16[96,1792]{1,0:T(8,128)(2,1)}, bf16[96,1792]{1,0:T(8,128)(2,1)S(1)}, u32[]{:S(2)}, u32[]{:S(2)}) collective-permute-start(bf16[96,1792]{1,0:T(8,128)(2,1)} %get-tuple-element.103), channel_id=1, source_target_pairs={{0,64},{64,0},{1,65},{65,1},{2,66},{66,2},{3,67},{67,3},{4,68},{68... | collective-permute-start | bytes 1032200 | tf_op jit(solution)/shard_map/ppermute | solution.py:648
  141.5 3.4 %collective-permute-start.19 = (bf16[96,1792]{1,0:T(8,128)(2,1)}, bf16[96,1792]{1,0:T(8,128)(2,1)S(1)}, u32[]{:S(2)}, u32[]{:S(2)}) collective-permute-start(bf16[96,1792]{1,0:T(8,128)(2,1)} %get-tuple-element.104), channel_id=1, source_target_pairs={{0,64},{64,0},{1,65},{65,1},{2,66},{66,2},{3,67},{67,3},{4,68},{68... | collective-permute-start | bytes 1032200 | tf_op jit(solution)/shard_map/ppermute | solution.py:648
  141.9 2.9 %collective-permute-start.20 = (bf16[96,1792]{1,0:T(8,128)(2,1)}, bf16[96,1792]{1,0:T(8,128)(2,1)S(1)}, u32[]{:S(2)}, u32[]{:S(2)}) collective-permute-start(bf16[96,1792]{1,0:T(8,128)(2,1)} %get-tuple-element.105), channel_id=1, source_target_pairs={{0,64},{64,0},{1,65},{65,1},{2,66},{66,2},{3,67},{67,3},{4,68},{68... | collective-permute-start | bytes 1032200 | tf_op jit(solution)/shard_map/ppermute | solution.py:648
  142.0 2.8 %collective-permute-start.21 = (bf16[96,1792]{1,0:T(8,128)(2,1)}, bf16[96,1792]{1,0:T(8,128)(2,1)S(1)}, u32[]{:S(2)}, u32[]{:S(2)}) collective-permute-start(bf16[96,1792]{1,0:T(8,128)(2,1)} %get-tuple-element.106), channel_id=1, source_target_pairs={{0,64},{64,0},{1,65},{65,1},{2,66},{66,2},{3,67},{67,3},{4,68},{68... | collective-permute-start | bytes 1032200 | tf_op jit(solution)/shard_map/ppermute | solution.py:648
  142.5 2.4 %collective-permute-start.22 = (f32[8,768]{1,0:T(8,128)}, f32[8,768]{1,0:T(8,128)S(1)}, u32[]{:S(2)}, u32[]{:S(2)}) collective-permute-start(f32[8,768]{1,0:T(8,128)} %get-tuple-element.102.refs_1_), channel_id=1, source_target_pairs={{0,64},{64,0},{1,65},{65,1},{2,66},{66,2},{3,67},{67,3},{4,68},{68... | collective-permute-start | bytes 73736 | tf_op jit(solution)/shard_map/ppermute | solution.py:648
  153.2 6.8 %collective-permute-start.32 = (bf16[400,640]{1,0:T(8,128)(2,1)}, bf16[400,640]{1,0:T(8,128)(2,1)S(1)}, u32[]{:S(2)}, u32[]{:S(2)}) collective-permute-start(bf16[400,640]{1,0:T(8,128)(2,1)} %get-tuple-element.116), channel_id=1, source_target_pairs={{0,64},{64,0},{1,65},{65,1},{2,66},{66,2},{3,67},{67,3},{4,68},{68... | collective-permute-start | bytes 1536008 | tf_op jit(solution)/shard_map/ppermute | solution.py:648
  156.1 11.7 %collective-permute-start.23 = (bf16[96,768]{1,0:T(8,128)(2,1)}, bf16[96,768]{1,0:T(8,128)(2,1)S(1)}, u32[]{:S(2)}, u32[]{:S(2)}) collective-permute-start(bf16[96,768]{1,0:T(8,128)(2,1)} %get-tuple-element.109), channel_id=1, source_target_pairs={{0,2},{1,3},{2,0},{3,1},{4,6},{5,7},{6,4},{7,5},{8,10},{9,11},{10,... | collective-permute-start | bytes 442376 | tf_op jit(solution)/shard_map/ppermute | solution.py:636
  156.8 11.0 %collective-permute-start.27 = (bf16[96,768]{1,0:T(8,128)(2,1)}, bf16[96,768]{1,0:T(8,128)(2,1)S(1)}, u32[]{:S(2)}, u32[]{:S(2)}) collective-permute-start(bf16[96,768]{1,0:T(8,128)(2,1)} %get-tuple-element.112), channel_id=1, source_target_pairs={{0,1},{1,2},{2,3},{3,0},{4,5},{5,6},{6,7},{7,4},{8,9},{9,10},{10,1... | collective-permute-start | bytes 442376 | tf_op jit(solution)/shard_map/ppermute | solution.py:636
  156.8 11.0 %collective-permute-start.28 = (bf16[96,768]{1,0:T(8,128)(2,1)}, bf16[96,768]{1,0:T(8,128)(2,1)S(1)}, u32[]{:S(2)}, u32[]{:S(2)}) collective-permute-start(bf16[96,768]{1,0:T(8,128)(2,1)} %get-tuple-element.113), channel_id=1, source_target_pairs={{0,3},{1,0},{2,1},{3,2},{4,7},{5,4},{6,5},{7,6},{8,11},{9,8},{10,9... | collective-permute-start | bytes 442376 | tf_op jit(solution)/shard_map/ppermute | solution.py:636
  162.7 33.2 %all-to-all-start.4 = ((bf16[16,480,128]{2,1,0:T(8,128)(2,1)}), bf16[16,480,128]{2,1,0:T(8,128)(2,1)S(1)}, u32[]{:S(2)}, u32[]{:S(2)}) async-start(bf16[16,480,128]{2,1,0:T(8,128)(2,1)} %get-tuple-element.119), calls=%async_computation.4 | async-start | bytes 3932160 | tf_op jit(solution)/shard_map/all_to_all | solution.py:652
  167.8 1.2 copy-start.2
  169.0 6.9 %collective-permute-start.31 = (bf16[96,768]{1,0:T(8,128)(2,1)S(1)}, bf16[96,768]{1,0:T(8,128)(2,1)S(1)}, u32[]{:S(2)}, u32[]{:S(2)}) collective-permute-start(bf16[96,768]{1,0:T(8,128)(2,1)S(1)} %input_chunk.1.refs_0_), channel_id=1, source_target_pairs={{0,3},{1,0},{2,1},{3,2},{4,7},{5,4},{6,5},{7,6},{8,11},{9,8},{10,9... | collective-permute-start | bytes 442376 | tf_op jit(solution)/shard_map/ppermute | solution.py:636
  169.9 8.3 %collective-permute-start.30 = (bf16[96,768]{1,0:T(8,128)(2,1)S(1)}, bf16[96,768]{1,0:T(8,128)(2,1)S(1)}, u32[]{:S(2)}, u32[]{:S(2)}) collective-permute-start(bf16[96,768]{1,0:T(8,128)(2,1)S(1)} %input_chunk.1.refs_0_), channel_id=1, source_target_pairs={{0,2},{1,3},{2,0},{3,1},{4,6},{5,7},{6,4},{7,5},{8,10},{9,11},{10,... | collective-permute-start | bytes 442376 | tf_op jit(solution)/shard_map/ppermute | solution.py:636
  170.7 11.2 %collective-permute-start.29 = (bf16[96,768]{1,0:T(8,128)(2,1)S(1)}, bf16[96,768]{1,0:T(8,128)(2,1)S(1)}, u32[]{:S(2)}, u32[]{:S(2)}) collective-permute-start(bf16[96,768]{1,0:T(8,128)(2,1)S(1)} %input_chunk.1.refs_0_), channel_id=1, source_target_pairs={{0,1},{1,2},{2,3},{3,0},{4,5},{5,6},{6,7},{7,4},{8,9},{9,10},{10,1... | collective-permute-start | bytes 442376 | tf_op jit(solution)/shard_map/ppermute | solution.py:636
  172.1 11.0 %collective-permute-start.26 = (bf16[96,768]{1,0:T(8,128)(2,1)}, bf16[96,768]{1,0:T(8,128)(2,1)S(1)}, u32[]{:S(2)}, u32[]{:S(2)}) collective-permute-start(bf16[96,768]{1,0:T(8,128)(2,1)} %later.5.refs_0_), channel_id=1, source_target_pairs={{0,3},{1,0},{2,1},{3,2},{4,7},{5,4},{6,5},{7,6},{8,11},{9,8},{10,9... | collective-permute-start | bytes 442376 | tf_op jit(solution)/shard_map/ppermute | solution.py:636
  174.0 10.3 %collective-permute-start.25 = (bf16[96,768]{1,0:T(8,128)(2,1)}, bf16[96,768]{1,0:T(8,128)(2,1)S(1)}, u32[]{:S(2)}, u32[]{:S(2)}) collective-permute-start(bf16[96,768]{1,0:T(8,128)(2,1)} %later.5.refs_0_), channel_id=1, source_target_pairs={{0,2},{1,3},{2,0},{3,1},{4,6},{5,7},{6,4},{7,5},{8,10},{9,11},{10,... | collective-permute-start | bytes 442376 | tf_op jit(solution)/shard_map/ppermute | solution.py:636
  175.9 9.7 %collective-permute-start.24 = (bf16[96,768]{1,0:T(8,128)(2,1)}, bf16[96,768]{1,0:T(8,128)(2,1)S(1)}, u32[]{:S(2)}, u32[]{:S(2)}) collective-permute-start(bf16[96,768]{1,0:T(8,128)(2,1)} %later.5.refs_0_), channel_id=1, source_target_pairs={{0,1},{1,2},{2,3},{3,0},{4,5},{5,6},{6,7},{7,4},{8,9},{9,10},{10,1... | collective-permute-start | bytes 442376 | tf_op jit(solution)/shard_map/ppermute | solution.py:636
  185.6 0.9 copy-start.1
Sparse Core Ops, SparseCore 0:
  19.8 60.3 all-gather.2

commit v4 on v3

--- a/solution.py
+++ b/solution.py
@@ -24,10 +24,9 @@
 CH = R * C
 PAIRS = R * NH
 G = D // (2 * NW)
-WG = 1792
-QKV = 640
-FIRST_ROWS, LAST_ROWS = 14 * G, 6 * G
+FIRST_ROWS, LAST_ROWS, BIAS_ROWS = 12 * G, 6 * G, 16
 SLOT = 3 * HD + 16
+VECTORS = 8 * D // T
 AUG = HD + 16
 EPSILON = 1e-12
 BIG = 1e30
@@ -85,7 +84,8 @@
     )(*args, *after)
 
 
-def later(x, *after):
+def later(x, *after, anywhere=()):
+    after = [*in_far_memory(after), *anywhere]
     return pl.pallas_call(
         lambda *refs: None,
         out_shape=jax.ShapeDtypeStruct(x.shape, x.dtype),
@@ -94,7 +94,7 @@
         input_output_aliases={0: 0},
         cost_estimate=pl.CostEstimate(flops=1024, bytes_accessed=1024, transcendentals=0),
         name="later",
-    )(x, *in_far_memory(after))
+    )(x, *after)
 
 
 def copies(pairs, sems):
@@ -159,8 +159,8 @@
 
 
 def attend_kernel(
-    got, freq, out_far, q_far, k_far, v_far, o_far, cos_far, sin_far,
-    out, q_t, k_t, v_t, o_t, cos_t, sin_t, k_nat, sems,
+    got, freq, out_far, q_far, k_far, qn_far, kn_far, vn_far, o_far, cos_far, sin_far,
+    out, q_t, k_t, v_t, q_nat, k_nat, v_nat, o_t, cos_t, sin_t, s_even, s_odd, lse_t, sems,
 ):
     @pl.when(lax.axis_index("wide") < PAIRS)
     def _():
@@ -195,14 +195,22 @@
             k_t[0:HD, at] = key.astype(bf16)
             k_t[HD:AUG, at] = key_ext.astype(bf16)
             k_nat[at, :] = jnp.concatenate([key, key_ext], axis=0).T.astype(bf16)
-            v_t[0:HD, at] = got[w, 2 * HD : 3 * HD, :]
-            v_t[HD:AUG, at] = jnp.where(ext < 3, 1.0, 0.0).astype(bf16)
-
-        stores = copies([(k_t, k_far), (v_t, v_far), (cos_t, cos_far), (sin_t, sin_far)], sems)
-
-        def tile(i, carry):
+            value = got[w, 2 * HD : 3 * HD, :].astype(f32)
+            value = jnp.concatenate([value, jnp.where(ext < 3, 1.0, 0.0)], axis=0)
+            v_t[:, at] = value.astype(bf16)
+            v_nat[at, :] = value.T.astype(bf16)
+            q_nat[at, :] = query.T.astype(bf16)
+
+        pairs = [(k_t, k_far), (cos_t, cos_far), (sin_t, sin_far), (q_nat, qn_far), (k_nat, kn_far), (v_nat, vn_far)]
+        stores = copies(pairs, sems)
+
+        def scores(i, s_ref):
             at = pl.ds(pl.multiple_of(i * 256, 256), 256)
-            s = dot(k_nat[...], q_t[:, at], NORMAL)
+            s_ref[...] = dot(k_nat[...], q_t[:, at], NORMAL)
+
+        def tile(i, s_ref):
+            at = pl.ds(pl.multiple_of(i * 256, 256), 256)
+            s = s_ref[...]
             top = jnp.max(s, axis=0, keepdims=True)
             p = jnp.exp2(s - top).astype(bf16)
             o = dot(v_t[...], p, NORMAL)
@@ -216,11 +224,19 @@
             hi, mid, lo = split3(-(top + jnp.log(total) * LOG2E))
             rows = lax.broadcasted_iota(jnp.int32, (16, 256), 0)
             more = jnp.where(rows == 5, hi, jnp.where(rows == 6, mid, jnp.where(rows == 7, lo, 0.0)))
-            q_t[HD:AUG, at] = (q_t[HD:AUG, at].astype(f32) + more).astype(bf16)
+            lse_t[:, at] = more
+
+        def two_tiles(k, carry):
+            scores(2 * k + 1, s_odd)
+            tile(2 * k, s_even)
+            scores(jnp.minimum(2 * k + 2, L // 256 - 1), s_even)
+            tile(2 * k + 1, s_odd)
             return carry
 
-        lax.fori_loop(0, L // 256, tile, 0)
-        last = [(out, out_far, 4), (q_t, q_far, 5), (o_t, o_far, 6)]
+        scores(0, s_even)
+        lax.fori_loop(0, L // 512, two_tiles, 0)
+        q_t[HD:AUG, :] = (q_t[HD:AUG, :].astype(f32) + lse_t[...]).astype(bf16)
+        last = [(out, out_far, 6), (q_t, q_far, 7), (o_t, o_far, 8)]
         last = [pltpu.make_async_copy(a, b, sems.at[k]) for a, b, k in last]
         for store in last:
             store.start()
@@ -229,22 +245,32 @@
 
 
 def attend_back_kernel(
-    got_far, o_far, q_far, k_far, v_far, cos_far, sin_far, out_far,
-    out, got, o_t, q_t, k_t, v_t, cos_t, sin_t, do_t, do_nat, q_nat, k_nat, v_nat, dq_t, sems,
+    got_far, q_far, k_far, qn_far, kn_far, vn_far, o_far, cos_far, sin_far, v0, v1, v2, v3, out_far,
+    out, near, vectors, got, o_t, q_t, k_t, cos_t, sin_t, do_t, do_nat, q_nat, k_nat, v_nat, dq_t, sems,
 ):
-    @pl.when(lax.axis_index("wide") < PAIRS)
+    n, attends = lax.axis_index("narrow"), lax.axis_index("wide") < PAIRS
+    pairs = [(got_far, got), (o_far, o_t), (qn_far, q_nat), (kn_far, k_nat), (vn_far, v_nat), (q_far, q_t)]
+    pairs += [(k_far, k_t), (cos_far, cos_t), (sin_far, sin_t)]
+    loads = [pltpu.make_async_copy(a, b, sems.at[k]) for k, (a, b) in enumerate(pairs)]
+
+    @pl.when(attends)
     def _():
-        pairs = [(q_far, q_t), (k_far, k_t), (v_far, v_t), (got_far, got), (o_far, o_t), (cos_far, cos_t), (sin_far, sin_t)]
-        loads = copies(pairs, sems)
-        for load in loads[:3]:
-            load.wait()
+        for load in loads:
+            load.start()
+
+    for s, load in enumerate(copies([(v, near.at[s]) for s, v in enumerate((v0, v1, v2, v3))], sems.at[len(loads) :])):
+        load.wait()
+        vectors[(n + NN - s) % NN] = near[s].astype(f32)
+    total = (vectors[0] + vectors[1] + vectors[2] + vectors[3])[0:8, :]
+    block = jnp.concatenate([total[:, k : k + T] for k in range(0, D, T)], axis=0).astype(bf16)
+    for w in range(NW):
+        out[w, SLOT:, :] = block
+    store = copies([(out.at[:, SLOT:, :], out_far.at[:, SLOT:, :])], sems.at[NW:])[0]
+
+    @pl.when(attends)
+    def _():
         ext = lax.broadcasted_iota(jnp.int32, (16, T), 0)
-        for w in range(NW):
-            at = slice(w * T, (w + 1) * T)
-            q_nat[at, :] = q_t[0:HD, at].astype(f32).T.astype(bf16)
-            k_nat[at, :] = k_t[:, at].astype(f32).T.astype(bf16)
-            v_nat[at, :] = v_t[:, at].astype(f32).T.astype(bf16)
-        for load in loads[3:]:
+        for load in loads[:2]:
             load.wait()
         for w in range(NW):
             at = slice(w * T, (w + 1) * T)
@@ -262,6 +288,8 @@
                 ext == 0, hi, jnp.where(ext == 1, mid, jnp.where(ext == 2, lo, 0.0))
             ).astype(bf16)
         dq_t[...] = jnp.zeros((HD, L), f32)
+        for load in loads[2:]:
+            load.wait()
 
         def folded(t):
             total = t[:, 0:T]
@@ -306,11 +334,13 @@
         )
         block = jnp.where(ext < 4, block, 0.0).astype(bf16)
         for w in range(NW):
-            out[w, 3 * HD :, :] = block
+            out[w, 3 * HD : SLOT, :] = block
         for store in stores:
             store.wait()
-        stores = copies([(out.at[:, 3 * HD :, :], out_far.at[:, 3 * HD :, :])], sems)
+        stores = copies([(out.at[:, 3 * HD : SLOT, :], out_far.at[:, 3 * HD : SLOT, :])], sems)
         stores[0].wait()
+
+    store.wait()
 
 
 def chunk_rows(c, r):
@@ -331,7 +361,7 @@
 
 
 ATTN, NORMED, FIRST = 0, 32, 128
-FFN, OUT, SUMS, LAST = 0, 96, 192, 208
+FFN, OUT, LAST = 0, 96, 192
 
 
 def first_kernel(
@@ -376,9 +406,9 @@
 
 def middle_kernel(
     every_far, state_far, cot_far, w_out_far, g_one_far, s_one_far, b0_far, b_down_far, g_two_far, s_two_far, b1, b2, b3,
-    slots_far, one_far, pack_far, layer_far,
+    slots_far, one_far, pack_far, layer_far, sums_far,
     state, cot, w_out, g_one, s_one, b0, b_down, g_two, s_two,
-    weights, slope, grad_one, slots, pack, layer, sems,
+    weights, slope, grad_one, slots, pack, layer, totals, sems,
 ):
     n = lax.axis_index("narrow")
     pairs = [(state_far, state), (cot_far, cot), (w_out_far, w_out), (g_one_far, g_one), (s_one_far, s_one)]
@@ -431,10 +461,11 @@
                 slot = jnp.concatenate([block[0 : C // 2], block[C // 2 :]], axis=1).astype(bf16)
                 slots[(r * NH + h) * NN + (n + NN - s) % NN] = slot
     stores = copies([(slots, slots_far), (grad_one, one_far), (layer, layer_far)], sems)
-    pack[OUT:SUMS, :] = low_one
+    pack[OUT:LAST, :] = low_one
+    stores += copies([(pack, pack_far)], sems.at[3:])
     sums = [ct * unit_two, ct, low_two.astype(f32), grad * unit, grad, low_one.astype(f32)]
-    pack[SUMS:LAST, :] = jnp.concatenate([column_sum(t) for t in sums] + [jnp.zeros((10, D), f32)], axis=0).astype(bf16)
-    stores += copies([(pack, pack_far)], sems.at[3:])
+    totals[...] = jnp.concatenate([column_sum(t) for t in sums] + [jnp.zeros((10, D), f32)], axis=0).astype(bf16)
+    stores += copies([(totals, sums_far)], sems.at[4:])
     for store in stores:
         store.wait()
 
@@ -453,10 +484,10 @@
 
 def weights_kernel(
     a0, a1, a2, a3, p0, p1, p2, p3, every_far, hidden_far, slope_far,
-    send0_far, send1_far, send2_far, send3_far, keep_far, sums_far,
-    firsts, packs, weights, hidden, slope, whole, sums, vectors, sems,
+    send0_far, send1_far, send2_far, send3_far, keep_far, out_whole, bias,
+    firsts, packs, weights, hidden, slope, whole, sems,
 ):
-    n, c = lax.axis_index("narrow"), lax.axis_index("dp")
+    c = lax.axis_index("dp")
     pairs = [(every_far.at[1, :, 0], weights), (slope_far, slope)]
     pairs += [(p, packs.at[s]) for s, p in enumerate((p0, p1, p2, p3))]
     pairs += [(p, firsts.at[s]) for s, p in enumerate((a0, a1, a2, a3))] + [(hidden_far, hidden)]
@@ -469,20 +500,15 @@
         load.wait()
     whole[:, 0:F] = dot(firsts[:, NORMED:FIRST, :].reshape(TOK, D), pre, BOTH_FIRST).astype(bf16)
     whole[:, F : 2 * F] = dot(grad_ffn, hidden[...], BOTH_FIRST).astype(bf16)
-    heads = [firsts[s, ATTN:NORMED, 256 * r : 256 * r + E] for s in range(NN) for r in range(R)]
-    heads = jnp.concatenate(heads, axis=0)
-    whole[:, 2 * F : 2 * F + E] = dot(packs[:, OUT:SUMS, :].reshape(TOK, D), heads, BOTH_FIRST).astype(bf16)
     half = D // 2
     pairs = [(whole.at[pl.ds(pl.multiple_of(c * half, half), half), :], keep_far)]
     for k, far in enumerate((send0_far, send1_far, send2_far, send3_far)):
         pairs.append((whole.at[pl.ds(pl.multiple_of((1 - c) * half + 96 * k, 96), 96), :], far))
     stores = copies(pairs, sems)
-    for s in range(NN):
-        vectors[(n + NN - s) % NN] = packs[s, SUMS:LAST, :].astype(f32)[0:8, :]
-    total = vectors[0] + vectors[1] + vectors[2] + vectors[3]
-    row = lax.broadcasted_iota(jnp.int32, (8, D), 0)
-    sums[...] = jnp.where(row == 6, column_sum(pre.astype(f32)), total)
-    stores += copies([(sums, sums_far)], sems.at[5:])
+    heads = [firsts[s, ATTN:NORMED, 256 * r : 256 * r + E] for s in range(NN) for r in range(R)]
+    heads = jnp.concatenate(heads, axis=0)
+    out_whole[...] = dot(packs[:, OUT:LAST, :].reshape(TOK, D), heads, BOTH_FIRST).astype(bf16)
+    bias[...] = jnp.broadcast_to(column_sum(pre.astype(f32)), (8, F))
     for store in stores:
         store.wait()
 
@@ -491,9 +517,12 @@
     return jnp.concatenate([block[:, k : k + T] for k in range(0, block.shape[1], T)], axis=0).astype(bf16)
 
 
-def input_weights_kernel(x_far, got, grad, send_far, keep_far, sums, whole, bias, x, sems):
-    c = lax.axis_index("dp")
-    load = copies([(x_far, x)], sems)[0]
+def input_back_kernel(
+    wq, wk, wv, got, part0_far, part1_far, part2_far, part3_far, grad,
+    part0, part1, part2, part3, wide_part, near, sems,
+):
+    n = lax.axis_index("narrow")
+    loads = copies([(wq, near.at[0]), (wk, near.at[1]), (wv, near.at[2])], sems)
     grads = []
     for j in range(3):
         grad_t = jnp.concatenate(
@@ -506,36 +535,9 @@
         grads.append(grad_t.astype(f32).T.astype(bf16))
     grads = jnp.concatenate(grads, axis=1)
     grad[...] = grads
-    heads = []
-    for h in range(NH):
-        block = got[h, 3 * HD :, :].astype(f32)
-        for r in range(1, R):
-            block = block + got[r * NH + h, 3 * HD :, :].astype(f32)
-        heads.append(block)
-    first = jnp.concatenate([b[0:1, 0:HD] + b[2:3, 0:HD] for b in heads], axis=1)
-    second = jnp.concatenate([b[0:1, HD:] + b[2:3, HD:] for b in heads], axis=1)
-    third = jnp.concatenate([b[1:2, 0:HD] + b[3:4, 0:HD] for b in heads], axis=1)
-    row = jnp.concatenate([first, second, third], axis=1)
-    sums[...] = row
-    hi, mid, lo = split3(row)
-    bias[:, 0 : 3 * E] = jnp.concatenate([hi, mid, lo, jnp.zeros((13, 3 * E), f32)], axis=0).astype(bf16)
-    load.wait()
-    whole[:, 0 : 3 * E] = dot(x[...].reshape(TOK, D), grads, BOTH_FIRST).astype(bf16)
-    half = D // 2
-    pairs = [(bias, send_far.at[half:, :])]
-    pairs.append((whole.at[pl.ds(pl.multiple_of((1 - c) * half, half), half), :], send_far.at[0:half, :]))
-    pairs.append((whole.at[pl.ds(pl.multiple_of(c * half, half), half), :], keep_far))
-    for store in copies(pairs, sems):
-        store.wait()
-
-
-def input_back_kernel(
-    wq, wk, wv, grad, part0_far, part1_far, part2_far, part3_far, part0, part1, part2, part3, wide_part, near, sems
-):
-    n = lax.axis_index("narrow")
-    for load in copies([(wq, near.at[0]), (wk, near.at[1]), (wv, near.at[2])], sems):
-        load.wait()
-    wide_part[...] = dot(grad[...], near[...].reshape(3 * E, D), NORMAL)
+    for load in loads:
+        load.wait()
+    wide_part[...] = dot(grads, near[...].reshape(3 * E, D), NORMAL)
     for r in range(R):
         to = slice(r * C, (r + 1) * C)
         part0[to, :] = wide_part[chunk_rows(n, r), :]
@@ -546,75 +548,89 @@
         store.wait()
 
 
-def blocks_of(block):
-    return jnp.concatenate([block[:, k : k + T] for k in range(0, block.shape[1], T)], axis=0).astype(bf16)
-
-
-def slot_sums(vec, vec_got):
-    rows = vec[...] + vec_got[...]
-    lanes = D // 3
-    return jnp.concatenate([rows[:, lanes * k : lanes * (k + 1)] for k in range(3)], axis=0)
-
-
-def first_add_kernel(
-    keep_far, vec_far, got0, got1, got2, got3, vec_got_far, slots_far, tail, keep, got, vec, vec_got, slots, sems
+def input_weights_kernel(x_far, got, out_whole, grad, send_far, keep_far, sums, whole, bias, x, sems):
+    c = lax.axis_index("dp")
+    load = copies([(x_far, x)], sems)[0]
+    heads = []
+    for h in range(NH):
+        block = got[h, 3 * HD : SLOT, :].astype(f32)
+        for r in range(1, R):
+            block = block + got[r * NH + h, 3 * HD : SLOT, :].astype(f32)
+        heads.append(block)
+    first = jnp.concatenate([b[0:1, 0:HD] + b[2:3, 0:HD] for b in heads], axis=1)
+    second = jnp.concatenate([b[0:1, HD:] + b[2:3, HD:] for b in heads], axis=1)
+    third = jnp.concatenate([b[1:2, 0:HD] + b[3:4, 0:HD] for b in heads], axis=1)
+    total = got[0, SLOT:, :].astype(f32)
+    for w in range(1, NW):
+        total = total + got[w, SLOT:, :].astype(f32)
+    total = jnp.concatenate([total[k : k + 8, :] for k in range(0, VECTORS, 8)], axis=1)
+    row = jnp.concatenate([first, second, third, jnp.zeros((1, E), f32)], axis=1)
+    sums[...] = jnp.concatenate([total[0:6, :], row, row], axis=0)
+    hi, mid, lo = split3(sums[...])
+    bias[...] = jnp.concatenate([hi[0:7, :], mid[0:7, :], lo[6:7, :], lo[6:7, :]], axis=0).astype(bf16)
+    whole[:, 3 * E :] = out_whole[...]
+    load.wait()
+    whole[:, 0 : 3 * E] = dot(x[...].reshape(TOK, D), grad[...], BOTH_FIRST).astype(bf16)
+    half = D // 2
+    pairs = [(bias, send_far.at[half:, :])]
+    pairs.append((whole.at[pl.ds(pl.multiple_of((1 - c) * half, half), half), :], send_far.at[0:half, :]))
+    pairs.append((whole.at[pl.ds(pl.multiple_of(c * half, half), half), :], keep_far))
+    for store in copies(pairs, sems):
+        store.wait()
+
+
+def first_add_kernel(keep_far, got0, got1, got2, got3, bias, bias_got, slots_far, keep, got, slots, more, sems):
+    pairs = [(far, got.at[96 * k : 96 * (k + 1), :]) for k, far in enumerate((got0, got1, got2, got3))]
+    loads = copies([*pairs, (keep_far, keep)], sems)
+    row = bias[...] + bias_got[...]
+    row = jnp.concatenate([row[0:1, k : k + T] for k in range(0, F, T)] + [jnp.zeros((10, T), f32)], axis=0)
+    for w in range(NW):
+        more[w] = row.astype(bf16)
+    for load in loads:
+        load.wait()
+    stores = copies([(more, slots_far.at[:, FIRST_ROWS + LAST_ROWS :, :])], sems.at[NW:])
+    for w in range(NW):
+        at = slice(w * G, (w + 1) * G)
+        slots[w] = blocks_of(keep[at, :].astype(f32) + got[at, :].astype(f32))
+        stores += copies([(slots.at[w], slots_far.at[w, 0:FIRST_ROWS, :])], sems.at[w:])
+    for store in stores:
+        store.wait()
+
+
+def last_add_kernel(
+    keep_far, slots_in, got_far, sums, slots_far, b_q, b_k, b_v, g_two, s_two, b_down, g_one, s_one, b_out,
+    keep, got, slots, sems,
 ):
-    pairs = [(far, got.at[96 * k : 96 * (k + 1), :]) for k, far in enumerate((got0, got1, got2, got3))]
-    pairs += [(vec_far, vec), (vec_got_far, vec_got), (keep_far, keep)]
-    for load in copies(pairs, sems):
-        load.wait()
-    rows = slot_sums(vec, vec_got)
-    lanes = 2 * F + T
+    for load in copies([(keep_far, keep), (got_far, got)], sems):
+        load.wait()
     stores = []
     for w in range(NW):
         at = slice(w * G, (w + 1) * G)
-        both = keep[at, :].astype(f32) + got[at, :].astype(f32)
-        slots[w] = blocks_of(jnp.concatenate([both[:, 0:lanes], rows[:, 0:T]], axis=1))
-        tail[at, :] = jnp.concatenate([both[:, lanes : lanes + HD], rows[:, T : T + HD]], axis=1)
-        tail[D // 2 + w * G : D // 2 + (w + 1) * G, :] = jnp.concatenate([rows[:, T + HD :], rows[:, T + HD :]], axis=1)
-        stores += copies([(slots.at[w], slots_far.at[w, 0:FIRST_ROWS, :])], sems.at[w:])
+        slots[w] = blocks_of(keep[at, :].astype(f32) + got[at, :].astype(f32))
+        stores += copies([(slots.at[w], slots_far.at[w, FIRST_ROWS : FIRST_ROWS + LAST_ROWS, :])], sems.at[w:])
+    other = got[D // 2 :, :].astype(f32)
+    hi, mid, lo = split3(sums[...])
+    total = (hi[0:7, :] + other[0:7, :]) + (mid[0:7, :] + other[7:14, :])
+    bias = total[6:7, :] + (lo[6:7, :] + other[14:15, :])
+    for k, ref in enumerate((b_q, b_k, b_v)):
+        ref[...] = bias[:, k * E : (k + 1) * E].reshape(E)
+    for k, ref in enumerate((g_two, s_two, b_down, g_one, s_one, b_out)):
+        ref[...] = total[k : k + 1, :].reshape(D)
     for store in stores:
         store.wait()
 
 
-def last_add_kernel(
-    qkv_far, slots_in, qkv_got_far, tail, sums, slots_far, b_q, b_k, b_v, qkv, qkv_got, slots, sems
-):
-    for load in copies([(qkv_far, qkv), (qkv_got_far, qkv_got)], sems):
-        load.wait()
-    stores = []
-    for w in range(NW):
-        at = slice(w * G, (w + 1) * G)
-        other = slice(D // 2 + w * G, D // 2 + (w + 1) * G)
-        both = qkv[at, 0 : 3 * E].astype(f32) + qkv_got[at, 0 : 3 * E].astype(f32)
-        parts = [tail[at, 0:HD], both, tail[at, HD:], tail[other, 0:HD]]
-        slots[w] = blocks_of(jnp.concatenate(parts, axis=1))
-        stores += copies([(slots.at[w], slots_far.at[w, FIRST_ROWS:, :])], sems.at[w:])
-    bias = qkv_got[D // 2 :, 0 : 3 * E].astype(f32)
-    hi, mid, lo = split3(sums[...])
-    total = (hi + bias[0:1, :]) + ((mid + bias[1:2, :]) + (lo + bias[2:3, :]))
-    for k, ref in enumerate((b_q, b_k, b_v)):
-        ref[...] = total[:, k * E : (k + 1) * E].reshape(E)
-    for store in stores:
-        store.wait()
-
-
-def last_sum_kernel(got, g_q, g_k, g_v, up, down, out, g_two, s_two, b_down, g_one, s_one, b_out, b_up):
+def last_sum_kernel(got, g_q, g_k, g_v, out, up, down, b_up):
     total = got[0].astype(f32)
     for w in range(1, NW):
         total = total + got[w].astype(f32)
-    total = jnp.concatenate([total[k : k + G, :] for k in range(0, FIRST_ROWS + LAST_ROWS, G)], axis=1)
+    end = FIRST_ROWS + LAST_ROWS
+    b_up[...] = jnp.concatenate([total[end + k : end + k + 1, :] for k in range(F // T)], axis=1).reshape(F)
+    total = jnp.concatenate([total[k : k + G, :] for k in range(0, end, G)], axis=1)
     up[...] = total[:, 0:F]
     down[...] = total[:, F : 2 * F]
-    lanes = 2 * F + T
-    out[...] = jnp.concatenate([total[:, 2 * F : lanes], total[:, lanes + T : lanes + T + HD]], axis=1)
-    begin = lanes + T + HD
-    for k, ref in enumerate((g_q, g_k, g_v)):
-        ref[...] = total[:, begin + k * E : begin + (k + 1) * E]
-    rows = jnp.concatenate([total[:, lanes : lanes + T], total[:, begin + 3 * E :]], axis=1)
-    vec = jnp.concatenate([rows[8 * k : 8 * (k + 1), :] for k in range(3)], axis=1)
-    for k, ref in enumerate((g_two, s_two, b_down, g_one, s_one, b_out, b_up)):
-        ref[...] = vec[k : k + 1, :].reshape(D)
+    for k, ref in enumerate((g_q, g_k, g_v, out)):
+        ref[...] = total[:, 2 * F + k * E : 2 * F + (k + 1) * E]
 
 
 def input_chunk_kernel(part_far, one_far, part1, part2, part3, low, part0, grad_one, sems):
@@ -700,14 +716,16 @@
     )
     every = lax.all_gather(shards, ("dp", "wide")).reshape(2, NW, NN, D // NW, F)
     got = exchange(slots)
-    out_slots, q_t, k_t, v_t, o_t, cos_t, sin_t = call(
+    out_slots, *saved = call(
         "attend",
         attend_kernel,
         [
             ((NW * NN, C // 2, 2 * HD), bf16),
             ((AUG, L), bf16),
             ((AUG, L), bf16),
-            ((AUG, L), bf16),
+            ((L, HD), bf16),
+            ((L, AUG), bf16),
+            ((L, AUG), bf16),
             ((HD, L), f32),
             ((HD, L), f32),
             ((HD, L), f32),
@@ -718,14 +736,20 @@
             pltpu.VMEM((AUG, L), bf16),
             pltpu.VMEM((AUG, L), bf16),
             pltpu.VMEM((AUG, L), bf16),
+            pltpu.VMEM((L, HD), bf16),
+            pltpu.VMEM((L, AUG), bf16),
+            pltpu.VMEM((L, AUG), bf16),
             pltpu.VMEM((HD, L), f32),
             pltpu.VMEM((HD, L), f32),
             pltpu.VMEM((HD, L), f32),
-            pltpu.VMEM((L, AUG), bf16),
-            pltpu.SemaphoreType.DMA((7,)),
-        ],
+            pltpu.VMEM((L, 256), f32),
+            pltpu.VMEM((L, 256), f32),
+            pltpu.VMEM((16, L), f32),
+            pltpu.SemaphoreType.DMA((9,)),
+        ],
+        mib=24,
         after=weights_got,
-        far=range(7),
+        far=range(9),
     )
     attn = exchange_all(out_slots)
     chunk_f32, chunk_low = ((CH, D), f32), ((CH, D), bf16)
@@ -750,10 +774,10 @@
     )
     firsts = (firsts[0], *(shifted(firsts[s], NN - s) for s in range(1, NN)))
     every = later(every, token)
-    slots, grad_one, pack, layer = call(
+    slots, grad_one, pack, layer, totals = call(
         "middle",
         middle_kernel,
-        [(slot_shape, bf16), chunk_f32, ((LAST, D), bf16), chunk_low],
+        [(slot_shape, bf16), chunk_f32, ((LAST, D), bf16), chunk_low, ((16, D), bf16)],
         (
             every, state, cotangent, w_out, gain_one, shift_one, biases_up[0], bias_down, gain_two, shift_two,
             *biases_up[1:],
@@ -769,16 +793,16 @@
             pltpu.VMEM(slot_shape, bf16),
             pltpu.VMEM((LAST, D), bf16),
             pltpu.VMEM((CH, D), bf16),
+            pltpu.VMEM((16, D), bf16),
             pltpu.SemaphoreType.DMA((17,)),
         ],
         mib=32,
         far_in=range(10),
-        far=range(4),
+        far=range(5),
     )
     got = exchange_all(later(slots, *firsts[1:]))
-    packs = gather_narrow(pack)
     firsts = (firsts[0], firsts[3], firsts[2], firsts[1])
-    hidden, slope, token = call(
+    hidden, slope = call(
         "hidden",
         hidden_kernel,
         [((TOK, F), bf16), ((TOK, F), f32)],
@@ -792,18 +816,20 @@
         ],
         far_in=range(5),
         far=(0, 1),
-        token=True,
-    )
+    )
+    totals = gather_narrow(totals)
+    packs = gather_narrow(later(pack, hidden, got, *totals[1:]))
     slots, token = call(
         "attend_back",
         attend_back_kernel,
-        [((NW, SLOT, T), bf16)],
-        (got, o_t, q_t, k_t, v_t, cos_t, sin_t),
-        scratch=[
-            pltpu.VMEM((NW, SLOT, T), bf16),
+        [((NW, SLOT + VECTORS, T), bf16)],
+        (got, *saved, *totals),
+        scratch=[
+            pltpu.VMEM((NW, SLOT + VECTORS, T), bf16),
+            pltpu.VMEM((NN, 16, D), bf16),
+            pltpu.VMEM((NN, 16, D), f32),
             pltpu.VMEM((NW * NN, C // 2, 2 * HD), bf16),
             pltpu.VMEM((HD, L), f32),
-            pltpu.VMEM((AUG, L), bf16),
             pltpu.VMEM((AUG, L), bf16),
             pltpu.VMEM((AUG, L), bf16),
             pltpu.VMEM((HD, L), f32),
@@ -814,18 +840,16 @@
             pltpu.VMEM((L, AUG), bf16),
             pltpu.VMEM((L, AUG), bf16),
             pltpu.VMEM((HD, L), f32),
-            pltpu.SemaphoreType.DMA((NW,)),
-        ],
-        any_in=(0,),
-        far_in=range(1, 7),
+            pltpu.SemaphoreType.DMA((NW + 1,)),
+        ],
+        far_in=range(13),
         far=(0,),
-        after=(token, *packs[1:]),
         token=True,
     )
-    *sends, up_keep, vec = call(
+    *sends, up_keep, out_whole, bias = call(
         "weights",
         weights_kernel,
-        [((96, WG), bf16)] * 4 + [((D // 2, WG), bf16), ((8, D), f32)],
+        [((96, 2 * F), bf16)] * 4 + [((D // 2, 2 * F), bf16), ((D, E), bf16), ((8, D), f32)],
         (*firsts, *packs, every, hidden, slope),
         scratch=[
             pltpu.VMEM((NN, FIRST, D), bf16),
@@ -833,56 +857,39 @@
             pltpu.VMEM((NW, D // NW, F), bf16),
             pltpu.VMEM((TOK, F), bf16),
             pltpu.VMEM((TOK, F), f32),
-            pltpu.VMEM((D, WG), bf16),
-            pltpu.VMEM((8, D), f32),
-            pltpu.VMEM((NN, 8, D), f32),
+            pltpu.VMEM((D, 2 * F), bf16),
             pltpu.SemaphoreType.DMA((11,)),
         ],
         mib=32,
         far_in=range(11),
-        far=range(6),
+        far=range(5),
+        cost=COST,
         after=(token,),
     )
     got = exchange(slots)
-    last_shape = (NW, FIRST_ROWS + LAST_ROWS, T)
-    slots, tail, added = call(
+    last_shape = (NW, FIRST_ROWS + LAST_ROWS + BIAS_ROWS, T)
+    slots, added = call(
         "first_add",
         first_add_kernel,
-        [(last_shape, bf16), ((D, T), f32)],
-        (up_keep, vec, *(other_core(send) for send in sends), other_core(vec)),
-        scratch=[
-            pltpu.VMEM((D // 2, WG), bf16),
-            pltpu.VMEM((D // 2, WG), bf16),
-            pltpu.VMEM((8, D), f32),
-            pltpu.VMEM((8, D), f32),
+        [(last_shape, bf16)],
+        (up_keep, *(other_core(send) for send in sends), bias, other_core(bias)),
+        scratch=[
+            pltpu.VMEM((D // 2, 2 * F), bf16),
+            pltpu.VMEM((D // 2, 2 * F), bf16),
             pltpu.VMEM((NW, FIRST_ROWS, T), bf16),
-            pltpu.SemaphoreType.DMA((NW,)),
-        ],
-        far_in=range(2),
-        any_in=range(2, 7),
+            pltpu.VMEM((NW, BIAS_ROWS, T), bf16),
+            pltpu.SemaphoreType.DMA((NW + 1,)),
+        ],
+        far_in=(0,),
+        any_in=range(1, 5),
         far=(0,),
         token=True,
     )
-    grad, send, keep, sums = call(
-        "input_weights",
-        input_weights_kernel,
-        [((TOK, 3 * E), bf16), ((D // 2 + 16, QKV), bf16), ((D // 2, QKV), bf16), ((1, 3 * E), f32)],
-        (hidden_in, got),
-        scratch=[
-            pltpu.VMEM((D, QKV), bf16),
-            pltpu.VMEM((16, QKV), bf16),
-            pltpu.VMEM((R, T, D), bf16),
-            pltpu.SemaphoreType.DMA((3,)),
-        ],
-        far_in=(0,),
-        far=(1, 2),
-        after=(added,),
-    )
-    parts = call(
+    *parts, grad = call(
         "input_back",
         input_back_kernel,
-        parts4,
-        (query_t, key_t, value_t, grad),
+        [*parts4, ((TOK, 3 * E), bf16)],
+        (query_t, key_t, value_t, got),
         scratch=[
             pltpu.VMEM((CH, D), f32),
             pltpu.VMEM((CH, D), bf16),
@@ -894,16 +901,31 @@
         ],
         far_in=range(3),
         far=range(4),
+        after=(added,),
+    )
+    send, keep, sums = call(
+        "input_weights",
+        input_weights_kernel,
+        [((D // 2 + 16, D), bf16), ((D // 2, D), bf16), ((8, D), f32)],
+        (hidden_in, got, out_whole, grad),
+        scratch=[
+            pltpu.VMEM((D, D), bf16),
+            pltpu.VMEM((16, D), bf16),
+            pltpu.VMEM((R, T, D), bf16),
+            pltpu.SemaphoreType.DMA((3,)),
+        ],
+        far_in=(0,),
+        far=(0, 1),
     )
     parts = scatter_narrow(parts)
-    slots, b_query, b_key, b_value = call(
+    slots, b_query, b_key, b_value, g_two, s_two, b_down, g_one, s_one, b_out = call(
         "last_add",
         last_add_kernel,
-        [(last_shape, bf16), ((E,), f32), ((E,), f32), ((E,), f32)],
-        (keep, slots, other_core(send), tail, sums),
-        scratch=[
-            pltpu.VMEM((D // 2, QKV), bf16),
-            pltpu.VMEM((D // 2 + 16, QKV), bf16),
+        [(last_shape, bf16)] + [((E,), f32)] * 3 + [((D,), f32)] * 6,
+        (keep, slots, other_core(send), sums),
+        scratch=[
+            pltpu.VMEM((D // 2, D), bf16),
+            pltpu.VMEM((D // 2 + 16, D), bf16),
             pltpu.VMEM((NW, LAST_ROWS, T), bf16),
             pltpu.SemaphoreType.DMA((NW,)),
         ],
@@ -920,12 +942,8 @@
     whole_out = ((R, T, D), f32)
     (layer_out,) = call("layer_out", spread_kernel, [whole_out], layers)
     (grad_input,) = call("grad_input", spread_kernel, [whole_out], gather_narrow(input_low))
-    flat = ((D,), f32)
-    g_query, g_key, g_value, grad_up, grad_down, g_out, g_two, s_two, b_down, g_one, s_one, b_out, b_up = call(
-        "last_sum",
-        last_sum_kernel,
-        [((G, E), f32)] * 3 + [((G, F), f32)] * 2 + [((G, E), f32)] + [flat] * 7,
-        (exchange(slots),),
+    g_query, g_key, g_value, g_out, grad_up, grad_down, b_up = call(
+        "last_sum", last_sum_kernel, [((G, E), f32)] * 4 + [((G, F), f32)] * 2 + [((F,), f32)], (exchange(slots),)
     )
     return (
         layer_out, grad_input, g_query, b_query, g_key, b_key, g_value, b_value, g_out.T, b_out,

time: 204 us -> 204 us (level)
  starting transfers between devices: 63.7 us -> 68.1 us
  Pallas kernels: 71.7 us -> 67.9 us
    all_to_all x2, waiting for transfers between devices: 9.49 us -> 4.43 us  [exchange_all(): return lax.all_to_all(slots, ('wide', 'narrow'), 0, 0, tiled=True)]
    ppermute x24 -> x27, starting transfers between devices: 31.9 us -> 36.9 us  [shifted(): return lax.ppermute(x, 'narrow', [(i, (i + s) % NN) for i in range(NN)])]
    pallas_call x16, Pallas kernels: 71.7 us -> 67.9 us  [call(): pl.pallas_call(run, out_shape=[shape(k, s, t) for k, (s, t) in enumerate(...]
    all_gather x1, waiting for transfers between devices: 0.02 us -> 3.36 us  [body(): lax.all_gather(shards, ('dp', 'wide')).reshape(2, NW, NN, D // NW, F)]
    ppermute x24 -> x27, waiting for transfers between devices: 21.3 us -> 22.2 us  [shifted(): return lax.ppermute(x, 'narrow', [(i, (i + s) % NN) for i in range(NN)])]
  transfers between devices with their start and end apart: 39 -> 42, of which waited for: 19 -> 24; matrix products, arithmetic and copies ran while one was open for 0% -> 0% of each run, Pallas kernels for 26% -> 30%
where the time goes in v4:
time: 204 us; the launch traced here: 203 us
  starting transfers between devices  68.1 us (33%)
  Pallas kernels  67.9 us (33%)
  waiting for transfers between devices  48.9 us (24%)
  between operations  14.6 us (7%)
  local copies, waits for them, and re-layouts  2.6 us (1%)
    pallas_call x16, Pallas kernels, call(): pl.pallas_call(run, out_shape=[shape(k, s, t) for k, (s, t) in enumerate(...  67.9 us
    ppermute x27, starting transfers between devices, shifted(): return lax.ppermute(x, 'narrow', [(i, (i + s) % NN) for i in range(NN)])  36.9 us
    ppermute x27, waiting for transfers between devices, shifted(): return lax.ppermute(x, 'narrow', [(i, (i + s) % NN) for i in range(NN)])  22.2 us
    all_to_all x3, waiting for transfers between devices, exchange(): return lax.all_to_all(slots, 'wide', 0, 0, tiled=True)  16.9 us
    all_to_all x3, starting transfers between devices, exchange(): return lax.all_to_all(slots, 'wide', 0, 0, tiled=True)  15.5 us
    all_to_all x2, starting transfers between devices, exchange_all(): return lax.all_to_all(slots, ('wide', 'narrow'), 0, 0, tiled=True)  13.6 us
    all_to_all x2, waiting for transfers between devices, exchange_all(): return lax.all_to_all(slots, ('wide', 'narrow'), 0, 0, tiled=True)  4.43 us
  transfers between devices with their start and end apart: 42, of which 24 were waited for; matrix products, arithmetic and copies ran while one was open for 0% of the time, Pallas kernels for 30%

profile of v4, /device:TPU:0, one launch (start us, length us, event | category | flops | bytes accessed | tf_op | source)
XLA Modules:
  0.0 203.0 jit_solution(1224782928544876821)
XLA Ops:
  7.2 0.9 bitcast_select_fusion.refs_0_
  8.2 4.2 %collective-permute-start.2 = (bf16[48,768]{1,0:T(8,128)(2,1)S(1)}, bf16[48,768]{1,0:T(8,128)(2,1)S(1)}, u32[]{:S(2)}, u32[]{:S(2)}) collective-permute-start(bf16[48,768]{1,0:T(8,128)(2,1)S(1)} %bitcast_select_fusion.refs_0_), channel_id=1, source_target_pairs={{0,3},{1,0},{2,1},{3,2},{4,7},{5,4},{6,5},{7,6},{8,11},{9,8},{10,9... | collective-permute-start | bytes 221192 | tf_op jit(solution)/shard_map/ppermute | solution.py:652
  12.4 1.3 collective-permute-start
  13.6 3.1 %project.1 = (bf16[16,208,128]{2,1,0:T(8,128)(2,1)}, f32[8,128]{1,0:T(8,128)S(1)}) custom-call(bf16[3,128,768]{2,1,0:T(8,128)(2,1)} %refs_0_.5, s32[3,128]{1,0:T(4,128)} %refs_1_.2, bf16[192,768]{1,0:T(8,128)(2,1)} %bitcast.9, f32[192]{0:T(256)} %refs_3_.1, bf16[192,768]{1,0:T(8,128)(2,1)} %bitcast.11, f32[192]{0:T(256)} %refs_5_.3, ...), custom_call_target="tpu_custom_call" | custom-call | flops 1024 | bytes 1024 | tf_op jit(solution)/shard_map/project/pallas_call | solution.py:70
  16.8 1.6 collective-permute-done.1.refs_2_
  18.9 0.7 stack.1
  19.7 7.2 %all-to-all-start = ((bf16[16,208,128]{2,1,0:T(8,128)(2,1)}), bf16[16,208,128]{2,1,0:T(8,128)(2,1)S(1)}, u32[]{:S(2)}, u32[]{:S(2)}) async-start(bf16[16,208,128]{2,1,0:T(8,128)(2,1)} %get-tuple-element.80), calls=%async_computation | async-start | bytes 1703936 | tf_op jit(solution)/shard_map/all_to_all | solution.py:668
  26.9 0.9 collective-permute-start.5
  27.8 1.4 collective-permute-start.4
  29.2 0.6 collective-permute-start.3
  29.8 2.8 %collective-permute-done.5.refs_4_.refs_3_ = bf16[96,768]{1,0:T(8,128)(2,1)S(1)} collective-permute-done((bf16[96,768]{1,0:T(8,128)(2,1)S(1)}, bf16[96,768]{1,0:T(8,128)(2,1)S(1)}, u32[]{:S(2)}, u32[]{:S(2)}) %collective-permute-start.5) | collective-permute-done | bytes 147488 | tf_op jit(solution)/shard_map/ppermute | solution.py:652
  32.6 2.2 %collective-permute-done.4.refs_3_.refs_2_ = bf16[96,768]{1,0:T(8,128)(2,1)S(1)} collective-permute-done((bf16[96,768]{1,0:T(8,128)(2,1)S(1)}, bf16[96,768]{1,0:T(8,128)(2,1)S(1)}, u32[]{:S(2)}, u32[]{:S(2)}) %collective-permute-start.4) | collective-permute-done | bytes 147488 | tf_op jit(solution)/shard_map/ppermute | solution.py:652
  34.8 1.5 collective-permute-done.3.refs_2_.refs_1_
  36.3 6.1 %all-to-all-done.refs_0_ = bf16[16,208,128]{2,1,0:T(8,128)(2,1)S(1)} async-done(((bf16[16,208,128]{2,1,0:T(8,128)(2,1)}), bf16[16,208,128]{2,1,0:T(8,128)(2,1)S(1)}, u32[]{:S(2)}, u32[]{:S(2)}) %all-to-all-start) | async-done | bytes 852000 | tf_op jit(solution)/shard_map/all_to_all | solution.py:668
  42.5 9.9 %attend.1 = (bf16[64,16,128]{2,1,0:T(8,128)(2,1)}, bf16[80,2048]{1,0:T(8,128)(2,1)}, bf16[80,2048]{1,0:T(8,128)(2,1)}, bf16[2048,64]{1,0:T(8,128)(2,1)}, bf16[20...) custom-call(bf16[16,208,128]{2,1,0:T(8,128)(2,1)S(1)} %all-to-all-do, ...), custom_call_target="tpu_custom_call" | custom-call | flops 1024 | bytes 1024 | tf_op jit(solution)/shard_map/attend/pallas_call | solution.py:70
  52.5 5.2 %all-to-all-start.1 = ((bf16[64,16,128]{2,1,0:T(8,128)(2,1)}), bf16[64,16,128]{2,1,0:T(8,128)(2,1)S(1)}, u32[]{:S(2)}, u32[]{:S(2)}) async-start(bf16[64,16,128]{2,1,0:T(8,128)(2,1)} %get-tuple-element.81), calls=%async_computation.1 | async-start | bytes 524288 | tf_op jit(solution)/shard_map/all_to_all | solution.py:672
  58.3 2.8 %collective-permute-start.11 = (f32[768]{0:T(1024)S(1)}, f32[768]{0:T(1024)S(1)}, u32[]{:S(2)}, u32[]{:S(2)}) collective-permute-start(f32[768]{0:T(1024)S(1)} %copy-done.5), channel_id=1, source_target_pairs={{0,3},{1,0},{2,1},{3,2},{4,7},{5,4},{6,5},{7,6},{8,11},{9,8},{10,9... | collective-permute-start | bytes 9224 | tf_op jit(solution)/shard_map/ppermute | solution.py:652
  61.1 0.9 collective-permute-start.10
  62.4 1.1 collective-permute-start.9
  63.5 2.7 %collective-permute-done.10.refs_13_.refs_11_ = f32[768]{0:T(1024)S(1)} collective-permute-done((f32[768]{0:T(1024)S(1)}, f32[768]{0:T(1024)S(1)}, u32[]{:S(2)}, u32[]{:S(2)}) %collective-permute-start.10) | collective-permute-done | bytes 3104 | tf_op jit(solution)/shard_map/ppermute | solution.py:652
  66.2 1.3 collective-permute-done.9.refs_12_.refs_10_
  67.6 2.9 %all-to-all-done.1.refs_8_ = bf16[64,16,128]{2,1,0:T(8,128)(2,1)S(1)} async-done(((bf16[64,16,128]{2,1,0:T(8,128)(2,1)}), bf16[64,16,128]{2,1,0:T(8,128)(2,1)S(1)}, u32[]{:S(2)}, u32[]{:S(2)}) %all-to-all-start.1) | async-done | bytes 262176 | tf_op jit(solution)/shard_map/all_to_all | solution.py:672
  70.5 3.1 %first.1 = (bf16[768,768]{1,0:T(8,128)(2,1)}, f32[96,896]{1,0:T(8,128)}, bf16[128,768]{1,0:T(8,128)(2,1)}, bf16[128,768]{1,0:T(8,128)(2,1)}, bf16[128,768]{1,0:T...) custom-call(bf16[192,768]{1,0:T(8,128)(2,1)} %refs_0_.4, bf16[96,768]{1,0:T(8,128)(2,1)} %copy-done.16, ...), custom_call_target="tpu_custom_call" | custom-call | flops 1024 | bytes 1024 | tf_op jit(solution)/shard_map/first/pallas_call | solution.py:70
  73.9 2.3 %collective-permute-start.13 = (bf16[128,768]{1,0:T(8,128)(2,1)}, bf16[128,768]{1,0:T(8,128)(2,1)S(1)}, u32[]{:S(2)}, u32[]{:S(2)}) collective-permute-start(bf16[128,768]{1,0:T(8,128)(2,1)} %get-tuple-element.88), channel_id=1, source_target_pairs={{0,2},{1,3},{2,0},{3,1},{4,6},{5,7},{6,4},{7,5},{8,10},{9,11},{10,... | collective-permute-start | bytes 589832 | tf_op jit(solution)/shard_map/ppermute | solution.py:652
  76.7 3.4 %all-gather.3.cloned.1.call-done = bf16[128,48,768]{2,1,0:T(8,128)(2,1)} async-done(((bf16[4,48,768]{2,1,0:T(8,128)(2,1)}), bf16[128,48,768]{2,1,0:T(8,128)(2,1)}) %all-gather.3.cloned.1.call-update) | async-done | bytes 9437200 | tf_op jit(solution)/shard_map/all_gather | solution.py:717
  80.0 11.1 %middle.1 = (bf16[64,16,128]{2,1,0:T(8,128)(2,1)}, f32[96,768]{1,0:T(8,128)}, bf16[192,768]{1,0:T(8,128)(2,1)}, bf16[96,768]{1,0:T(8,128)(2,1)}, bf16[16,768]{1,0:T(8,128)(2,1)}) custom-call(bf16[2,16,4,48,768]{4,3,2,1,0:T(8,128)(2,1)} %later.4.refs_0_.refs_4_.refs_8_, f32[96,896]{1,0:T(8,128)} %get-tuple-element.83.refs_1_, bf16[3,128,768]{2,1,0:T(8,128)(2,1)} %refs_2_.1, ...), custom_call_target="tpu_custom_call" | custom-call | flops 1024 | bytes 1024 | tf_op jit(solution)/shard_map/middle/pallas_call | solution.py:70
  91.2 0.6 copy-done.10
  92.0 8.5 %all-to-all-start.2 = ((bf16[64,16,128]{2,1,0:T(8,128)(2,1)}), bf16[64,16,128]{2,1,0:T(8,128)(2,1)S(1)}, u32[]{:S(2)}, u32[]{:S(2)}) async-start(bf16[64,16,128]{2,1,0:T(8,128)(2,1)} %later.5), calls=%async_computation.2 | async-start | bytes 524288 | tf_op jit(solution)/shard_map/all_to_all | solution.py:672
  100.5 2.9 %collective-permute-start.17 = (bf16[16,768]{1,0:T(8,128)(2,1)}, bf16[16,768]{1,0:T(8,128)(2,1)S(1)}, u32[]{:S(2)}, u32[]{:S(2)}) collective-permute-start(bf16[16,768]{1,0:T(8,128)(2,1)} %get-tuple-element.98.refs_9_), channel_id=1, source_target_pairs={{0,3},{1,0},{2,1},{3,2},{4,7},{5,4},{6,5},{7,6},{8,11},{9,8},{10,9... | collective-permute-start | bytes 73736 | tf_op jit(solution)/shard_map/ppermute | solution.py:652
  103.4 0.9 collective-permute-start.16
  104.2 0.9 collective-permute-start.15
  105.1 3.8 %hidden.1 = (bf16[384,768]{1,0:T(8,128)(2,1)}, f32[384,768]{1,0:T(8,128)}) custom-call(bf16[128,768]{1,0:T(8,128)(2,1)} %get-tuple-element.100.refs_0_, bf16[128,768]{1,0:T(8,128)(2,1)} %copy-done.12, bf16[128,768]{1,0:T(8,128)(2,1)} %copy-done.11, bf16[128,768]{1,0:T(8,128)(2,1)} %copy-done.10, bf16[2,16,4,48,768]{4,3,2,1,0:T(8,128)(2,1)} %later.4.refs_0_.refs_4_.refs_8_, ...), custom_call_target="tpu_custom_call" | custom-call | flops 1024 | bytes 1024 | tf_op jit(solution)/shard_map/hidden/pallas_call | solution.py:70
  109.8 1.6 all-to-all-done.2.refs_0_.refs_2_
  111.4 0.7 copy-done.9
  112.0 1.0 collective-permute-start.20
  113.1 1.6 collective-permute-start.19
  114.7 15.0 %attend_back.1 = (bf16[16,256,128]{2,1,0:T(8,128)(2,1)}, f32[8,128]{1,0:T(8,128)S(1)}) custom-call(bf16[64,16,128]{2,1,0:T(8,128)(2,1)} %copy-done.9, bf16[80,2048]{1,0:T(8,128)(2,1)} %get-tuple-element.90.refs_1_, bf16[80,2048]{1,0:T(8,128)(2,1)} %get-tuple-element.91.refs_2_, bf16[2048,64]{1,0:T(8,128)(2,1)} %get-tuple-element.92.refs_3_, ...), custom_call_target="tpu_custom_call" | custom-call | flops 1024 | bytes 1024 | tf_op jit(solution)/shard_map/attend_back/pallas_call | solution.py:70
  129.8 4.1 %all-to-all-start.3 = ((bf16[16,256,128]{2,1,0:T(8,128)(2,1)}), bf16[16,256,128]{2,1,0:T(8,128)(2,1)S(1)}, u32[]{:S(2)}, u32[]{:S(2)}) async-start(bf16[16,256,128]{2,1,0:T(8,128)(2,1)} %get-tuple-element.99), calls=%async_computation.3 | async-start | bytes 2097152 | tf_op jit(solution)/shard_map/all_to_all | solution.py:668
  133.9 0.7 copy-done.24
  134.9 5.7 %weights.1 = (bf16[96,1536]{1,0:T(8,128)(2,1)}, bf16[96,1536]{1,0:T(8,128)(2,1)}, bf16[96,1536]{1,0:T(8,128)(2,1)}, bf16[96,1536]{1,0:T(8,128)(2,1)}, bf16[384,1...) custom-call(bf16[128,768]{1,0:T(8,128)(2,1)} %get-tuple-element.100.refs_0_, ...), custom_call_target="tpu_custom_call" | custom-call | flops 99999997952 | bytes 1024 | tf_op jit(solution)/shard_map/weights/pallas_call | solution.py:70
  141.7 1.4 collective-permute-done.25.refs_6_
  143.7 2.7 %first_add.1 = (bf16[16,448,128]{2,1,0:T(8,128)(2,1)}, f32[8,128]{1,0:T(8,128)S(1)}) custom-call(bf16[384,1536]{1,0:T(8,128)(2,1)} %get-tuple-element.105.refs_0_, bf16[96,1536]{1,0:T(8,128)(2,1)S(1)} %collective-permute-done.21.refs_1_, bf16[96,1536]{1,0:T(8,128)(2,1)S(1)} %collective-permute-done.22.refs_2_, ...), custom_call_target="tpu_custom_call" | custom-call | flops 1024 | bytes 1024 | tf_op jit(solution)/shard_map/first_add/pallas_call | solution.py:70
  146.4 3.0 %all-to-all-done.3.refs_3_.refs_1_ = bf16[16,256,128]{2,1,0:T(8,128)(2,1)S(1)} async-done(((bf16[16,256,128]{2,1,0:T(8,128)(2,1)}), bf16[16,256,128]{2,1,0:T(8,128)(2,1)S(1)}, u32[]{:S(2)}, u32[]{:S(2)}) %all-to-all-start.3) | async-done | bytes 1048608 | tf_op jit(solution)/shard_map/all_to_all | solution.py:668
  149.5 2.8 %input_back.1 = (f32[96,768]{1,0:T(8,128)}, bf16[96,768]{1,0:T(8,128)(2,1)}, bf16[96,768]{1,0:T(8,128)(2,1)}, bf16[96,768]{1,0:T(8,128)(2,1)}, bf16[384,576]{1,0:T(8,128)(2,1)S(1)}) custom-call(bf16[192,768]{1,0:T(8,128)(2,1)} %bitcast.10, bf16[192,768]{1,0:T(8,128)(2,1)} %bitcast.12, bf16[192,768]{1,0:T(8,128)(2,1)} %bitcast.14, ...), custom_call_target="tpu_custom_call" | custom-call | flops 1024 | bytes 1024 | tf_op jit(solution)/shard_map/input_back/pallas_call | solution.py:70
  152.3 2.9 %input_weights.1 = (bf16[400,768]{1,0:T(8,128)(2,1)}, bf16[384,768]{1,0:T(8,128)(2,1)}, f32[8,768]{1,0:T(8,128)S(1)}) custom-call(bf16[3,128,768]{2,1,0:T(8,128)(2,1)} %refs_0_.5, bf16[16,256,128]{2,1,0:T(8,128)(2,1)S(1)} %all-to-all-done.3.refs_3_.refs_1_, bf16[768,192]{1,0:T(8,128)(2,1)S(1)} %get-tuple-element.117.refs_2_, ...), custom_call_target="tpu_custom_call" | custom-call | flops 1024 | bytes 1024 | tf_op jit(solution)/shard_map/input_weights/pallas_call | solution.py:70
  155.3 3.3 %collective-permute-start.26 = (bf16[96,768]{1,0:T(8,128)(2,1)S(1)}, bf16[96,768]{1,0:T(8,128)(2,1)S(1)}, u32[]{:S(2)}, u32[]{:S(2)}) collective-permute-start(bf16[96,768]{1,0:T(8,128)(2,1)S(1)} %copy-done.29), channel_id=1, source_target_pairs={{0,2},{1,3},{2,0},{3,1},{4,6},{5,7},{6,4},{7,5},{8,10},{9,11},{10,... | collective-permute-start | bytes 442376 | tf_op jit(solution)/shard_map/ppermute | solution.py:652
  158.6 0.6 collective-permute-start.30
  159.2 2.6 %collective-permute-start.31 = (bf16[96,768]{1,0:T(8,128)(2,1)S(1)}, bf16[96,768]{1,0:T(8,128)(2,1)S(1)}, u32[]{:S(2)}, u32[]{:S(2)}) collective-permute-start(bf16[96,768]{1,0:T(8,128)(2,1)S(1)} %copy-done.27), channel_id=1, source_target_pairs={{0,3},{1,0},{2,1},{3,2},{4,7},{5,4},{6,5},{7,6},{8,11},{9,8},{10,9... | collective-permute-start | bytes 442376 | tf_op jit(solution)/shard_map/ppermute | solution.py:652
  161.9 2.7 %last_add.1 = (bf16[16,448,128]{2,1,0:T(8,128)(2,1)}, f32[192]{0:T(256)}, f32[192]{0:T(256)}, f32[192]{0:T(256)}, f32[768]{0:T(1024)}, /*index=5*/f32[768]{0:T(1...) custom-call(bf16[384,768]{1,0:T(8,128)(2,1)} %get-tuple-element.119.refs_0_, ...), custom_call_target="tpu_custom_call", output_to_operand_aliasing={{0}: (1, {})} | custom-call | flops 1024 | bytes 1024 | tf_op jit(solution)/shard_map/last_add/pallas_call | solution.py:70
  164.6 4.3 %all-to-all-start.4 = ((bf16[16,448,128]{2,1,0:T(8,128)(2,1)}), bf16[16,448,128]{2,1,0:T(8,128)(2,1)S(1)}, u32[]{:S(2)}, u32[]{:S(2)}) async-start(bf16[16,448,128]{2,1,0:T(8,128)(2,1)} %get-tuple-element.123), calls=%async_computation.4 | async-start | bytes 3670016 | tf_op jit(solution)/shard_map/all_to_all | solution.py:668
  168.9 1.2 input_chunk.1.refs_0_
  170.4 1.5 collective-permute-start.33
  172.2 2.9 %collective-permute-start.29 = (bf16[96,768]{1,0:T(8,128)(2,1)}, bf16[96,768]{1,0:T(8,128)(2,1)S(1)}, u32[]{:S(2)}, u32[]{:S(2)}) collective-permute-start(bf16[96,768]{1,0:T(8,128)(2,1)} %later.7.refs_0_), channel_id=1, source_target_pairs={{0,3},{1,0},{2,1},{3,2},{4,7},{5,4},{6,5},{7,6},{8,11},{9,8},{10,9... | collective-permute-start | bytes 442376 | tf_op jit(solution)/shard_map/ppermute | solution.py:652
  175.1 1.2 collective-permute-start.28
  176.4 0.6 collective-permute-done.34.refs_3_
  177.0 0.8 collective-permute-start.27
  177.8 0.8 collective-permute-done.33.refs_2_
  178.6 4.5 %collective-permute-done.32.refs_1_ = bf16[96,768]{1,0:T(8,128)(2,1)S(1)} collective-permute-done((bf16[96,768]{1,0:T(8,128)(2,1)S(1)}, bf16[96,768]{1,0:T(8,128)(2,1)S(1)}, u32[]{:S(2)}, u32[]{:S(2)}) %collective-permute-start.32) | collective-permute-done | bytes 147488 | tf_op jit(solution)/shard_map/ppermute | solution.py:652
  183.1 1.1 grad_input.1
  184.2 0.7 collective-permute-done.28.refs_2_
  184.9 1.5 collective-permute-done.27.refs_1_
  186.4 1.1 layer_out.1
  187.5 7.8 %all-to-all-done.4.refs_0_ = bf16[16,448,128]{2,1,0:T(8,128)(2,1)S(1)} async-done(((bf16[16,448,128]{2,1,0:T(8,128)(2,1)}), bf16[16,448,128]{2,1,0:T(8,128)(2,1)S(1)}, u32[]{:S(2)}, u32[]{:S(2)}) %all-to-all-start.4) | async-done | bytes 1835040 | tf_op jit(solution)/shard_map/all_to_all | solution.py:668
  195.3 0.9 last_sum.1
  (104 shorter events, 6.5 us)
Async XLA Ops:
  7.2 72.8 %all-gather.3.cloned.1.call-start = ((), (), s32[]{:S(2)}) async-start(), calls=%async_computation.5 | async-start | bytes 9732096 | tf_op jit(solution)/shard_map/all_gather | solution.py:717
  8.2 8.6 %collective-permute-start.2 = (bf16[48,768]{1,0:T(8,128)(2,1)S(1)}, bf16[48,768]{1,0:T(8,128)(2,1)S(1)}, u32[]{:S(2)}, u32[]{:S(2)}) collective-permute-start(bf16[48,768]{1,0:T(8,128)(2,1)S(1)} %bitcast_select_fusion.refs_0_), channel_id=1, source_target_pairs={{0,3},{1,0},{2,1},{3,2},{4,7},{5,4},{6,5},{7,6},{8,11},{9,8},{10,9... | collective-permute-start | bytes 221192 | tf_op jit(solution)/shard_map/ppermute | solution.py:652
  12.4 6.0 %collective-permute-start.1 = (bf16[48,768]{1,0:T(8,128)(2,1)S(1)}, bf16[48,768]{1,0:T(8,128)(2,1)S(1)}, u32[]{:S(2)}, u32[]{:S(2)}) collective-permute-start(bf16[48,768]{1,0:T(8,128)(2,1)S(1)} %bitcast_select_fusion.refs_0_), channel_id=1, source_target_pairs={{0,2},{1,3},{2,0},{3,1},{4,6},{5,7},{6,4},{7,5},{8,10},{9,11},{10,... | collective-permute-start | bytes 221192 | tf_op jit(solution)/shard_map/ppermute | solution.py:652
  12.4 6.5 %collective-permute-start = (bf16[48,768]{1,0:T(8,128)(2,1)S(1)}, bf16[48,768]{1,0:T(8,128)(2,1)S(1)}, u32[]{:S(2)}, u32[]{:S(2)}) collective-permute-start(bf16[48,768]{1,0:T(8,128)(2,1)S(1)} %bitcast_select_fusion.refs_0_), channel_id=1, source_target_pairs={{0,1},{1,2},{2,3},{3,0},{4,5},{5,6},{6,7},{7,4},{8,9},{9,10},{10,1... | collective-permute-start | bytes 221192 | tf_op jit(solution)/shard_map/ppermute | solution.py:652
  13.6 13.3 %copy-start.13 = (bf16[192,768]{1,0:T(8,128)(2,1)S(1)}, bf16[192,768]{1,0:T(8,128)(2,1)}, u32[]{:S(2)}) copy-start(bf16[192,768]{1,0:T(8,128)(2,1)} %refs_0_.4) | copy-start | bytes 884740
  13.6 28.8 %copy-start.23 = (f32[64]{0:T(128)S(1)}, f32[64]{0:T(128)}, u32[]{:S(2)}) copy-start(f32[64]{0:T(128)} %constant.14.clone) | copy-start | bytes 772
  19.6 38.7 %copy-start.5 = (f32[768]{0:T(1024)S(1)}, f32[768]{0:T(1024)}, u32[]{:S(2)}) copy-start(f32[768]{0:T(1024)} %refs_5_.5) | copy-start | bytes 9220
  19.6 50.8 %copy-start = (bf16[3,128,768]{2,1,0:T(8,128)(2,1)S(1)}, bf16[3,128,768]{2,1,0:T(8,128)(2,1)}, u32[]{:S(2)}) copy-start(bf16[3,128,768]{2,1,0:T(8,128)(2,1)} %refs_0_.5) | copy-start | bytes 1769476
  19.7 50.8 %copy-start.3 = (f32[768]{0:T(1024)S(1)}, f32[768]{0:T(1024)}, u32[]{:S(2)}) copy-start(f32[768]{0:T(1024)} %refs_4_.1) | copy-start | bytes 9220
  19.7 50.8 %copy-start.4 = (f32[768]{0:T(1024)S(1)}, f32[768]{0:T(1024)}, u32[]{:S(2)}) copy-start(f32[768]{0:T(1024)} %refs_5_.4) | copy-start | bytes 9220
  19.7 50.8 %copy-start.7 = (f32[768]{0:T(1024)S(1)}, f32[768]{0:T(1024)}, u32[]{:S(2)}) copy-start(f32[768]{0:T(1024)} %refs_9_.2) | copy-start | bytes 9220
  19.7 22.7 %all-to-all-start = ((bf16[16,208,128]{2,1,0:T(8,128)(2,1)}), bf16[16,208,128]{2,1,0:T(8,128)(2,1)S(1)}, u32[]{:S(2)}, u32[]{:S(2)}) async-start(bf16[16,208,128]{2,1,0:T(8,128)(2,1)} %get-tuple-element.80), calls=%async_computation | async-start | bytes 1703936 | tf_op jit(solution)/shard_map/all_to_all | solution.py:668
  26.9 5.7 %collective-permute-start.5 = (bf16[96,768]{1,0:T(8,128)(2,1)S(1)}, bf16[96,768]{1,0:T(8,128)(2,1)S(1)}, u32[]{:S(2)}, u32[]{:S(2)}) collective-permute-start(bf16[96,768]{1,0:T(8,128)(2,1)S(1)} %constant_dynamic-slice_fusion), channel_id=1, source_target_pairs={{0,3},{1,0},{2,1},{3,2},{4,7},{5,4},{6,5},{7,6},{8,11},{9,8},{10,9... | collective-permute-start | bytes 442376 | tf_op jit(solution)/shard_map/ppermute | solution.py:652
  27.8 7.0 %collective-permute-start.4 = (bf16[96,768]{1,0:T(8,128)(2,1)S(1)}, bf16[96,768]{1,0:T(8,128)(2,1)S(1)}, u32[]{:S(2)}, u32[]{:S(2)}) collective-permute-start(bf16[96,768]{1,0:T(8,128)(2,1)S(1)} %constant_dynamic-slice_fusion), channel_id=1, source_target_pairs={{0,2},{1,3},{2,0},{3,1},{4,6},{5,7},{6,4},{7,5},{8,10},{9,11},{10,... | collective-permute-start | bytes 442376 | tf_op jit(solution)/shard_map/ppermute | solution.py:652
  29.2 7.1 %collective-permute-start.3 = (bf16[96,768]{1,0:T(8,128)(2,1)S(1)}, bf16[96,768]{1,0:T(8,128)(2,1)S(1)}, u32[]{:S(2)}, u32[]{:S(2)}) collective-permute-start(bf16[96,768]{1,0:T(8,128)(2,1)S(1)} %constant_dynamic-slice_fusion), channel_id=1, source_target_pairs={{0,1},{1,2},{2,3},{3,0},{4,5},{5,6},{6,7},{7,4},{8,9},{9,10},{10,1... | collective-permute-start | bytes 442376 | tf_op jit(solution)/shard_map/ppermute | solution.py:652
  32.6 9.9 %copy-start.14 = (bf16[96,768]{1,0:T(8,128)(2,1)}, bf16[96,768]{1,0:T(8,128)(2,1)S(1)}, u32[]{:S(2)}) copy-start(bf16[96,768]{1,0:T(8,128)(2,1)S(1)} %collective-permute-done.5.refs_4_.refs_3_) | copy-start | bytes 442372
  34.8 7.7 %copy-start.15 = (bf16[96,768]{1,0:T(8,128)(2,1)}, bf16[96,768]{1,0:T(8,128)(2,1)S(1)}, u32[]{:S(2)}) copy-start(bf16[96,768]{1,0:T(8,128)(2,1)S(1)} %collective-permute-done.4.refs_3_.refs_2_) | copy-start | bytes 442372
  36.3 6.2 %copy-start.16 = (bf16[96,768]{1,0:T(8,128)(2,1)}, bf16[96,768]{1,0:T(8,128)(2,1)S(1)}, u32[]{:S(2)}) copy-start(bf16[96,768]{1,0:T(8,128)(2,1)S(1)} %collective-permute-done.3.refs_2_.refs_1_) | copy-start | bytes 442372
  52.5 18.0 %all-to-all-start.1 = ((bf16[64,16,128]{2,1,0:T(8,128)(2,1)}), bf16[64,16,128]{2,1,0:T(8,128)(2,1)S(1)}, u32[]{:S(2)}, u32[]{:S(2)}) async-start(bf16[64,16,128]{2,1,0:T(8,128)(2,1)} %get-tuple-element.81), calls=%async_computation.1 | async-start | bytes 524288 | tf_op jit(solution)/shard_map/all_to_all | solution.py:672
  57.6 9.9 %collective-permute-start.8 = (bf16[96,768]{1,0:T(8,128)(2,1)}, bf16[96,768]{1,0:T(8,128)(2,1)S(1)}, u32[]{:S(2)}, u32[]{:S(2)}) collective-permute-start(bf16[96,768]{1,0:T(8,128)(2,1)} %copy-done.14), channel_id=1, source_target_pairs={{0,64},{64,0},{1,65},{65,1},{2,66},{66,2},{3,67},{67,3},{4,68},{68... | collective-permute-start | bytes 442376 | tf_op jit(solution)/shard_map/ppermute | solution.py:664
  57.7 9.8 %collective-permute-start.7 = (bf16[96,768]{1,0:T(8,128)(2,1)}, bf16[96,768]{1,0:T(8,128)(2,1)S(1)}, u32[]{:S(2)}, u32[]{:S(2)}) collective-permute-start(bf16[96,768]{1,0:T(8,128)(2,1)} %copy-done.15), channel_id=1, source_target_pairs={{0,64},{64,0},{1,65},{65,1},{2,66},{66,2},{3,67},{67,3},{4,68},{68... | collective-permute-start | bytes 442376 | tf_op jit(solution)/shard_map/ppermute | solution.py:664
  58.2 9.4 %collective-permute-start.6 = (bf16[96,768]{1,0:T(8,128)(2,1)}, bf16[96,768]{1,0:T(8,128)(2,1)S(1)}, u32[]{:S(2)}, u32[]{:S(2)}) collective-permute-start(bf16[96,768]{1,0:T(8,128)(2,1)} %copy-done.16), channel_id=1, source_target_pairs={{0,64},{64,0},{1,65},{65,1},{2,66},{66,2},{3,67},{67,3},{4,68},{68... | collective-permute-start | bytes 442376 | tf_op jit(solution)/shard_map/ppermute | solution.py:664
  58.3 4.1 %collective-permute-start.11 = (f32[768]{0:T(1024)S(1)}, f32[768]{0:T(1024)S(1)}, u32[]{:S(2)}, u32[]{:S(2)}) collective-permute-start(f32[768]{0:T(1024)S(1)} %copy-done.5), channel_id=1, source_target_pairs={{0,3},{1,0},{2,1},{3,2},{4,7},{5,4},{6,5},{7,6},{8,11},{9,8},{10,9... | collective-permute-start | bytes 9224 | tf_op jit(solution)/shard_map/ppermute | solution.py:652
  61.1 5.1 %collective-permute-start.10 = (f32[768]{0:T(1024)S(1)}, f32[768]{0:T(1024)S(1)}, u32[]{:S(2)}, u32[]{:S(2)}) collective-permute-start(f32[768]{0:T(1024)S(1)} %copy-done.5), channel_id=1, source_target_pairs={{0,2},{1,3},{2,0},{3,1},{4,6},{5,7},{6,4},{7,5},{8,10},{9,11},{10,... | collective-permute-start | bytes 9224 | tf_op jit(solution)/shard_map/ppermute | solution.py:652
  62.4 5.1 %collective-permute-start.9 = (f32[768]{0:T(1024)S(1)}, f32[768]{0:T(1024)S(1)}, u32[]{:S(2)}, u32[]{:S(2)}) collective-permute-start(f32[768]{0:T(1024)S(1)} %copy-done.5), channel_id=1, source_target_pairs={{0,1},{1,2},{2,3},{3,0},{4,5},{5,6},{6,7},{7,4},{8,9},{9,10},{10,1... | collective-permute-start | bytes 9224 | tf_op jit(solution)/shard_map/ppermute | solution.py:652
  67.5 2.9 %copy-start.17 = (bf16[96,768]{1,0:T(8,128)(2,1)}, bf16[96,768]{1,0:T(8,128)(2,1)S(1)}, u32[]{:S(2)}) copy-start(bf16[96,768]{1,0:T(8,128)(2,1)S(1)} %collective-permute-done.8.refs_6_) | copy-start | bytes 442372
  67.6 2.9 %copy-start.18 = (bf16[96,768]{1,0:T(8,128)(2,1)}, bf16[96,768]{1,0:T(8,128)(2,1)S(1)}, u32[]{:S(2)}) copy-start(bf16[96,768]{1,0:T(8,128)(2,1)S(1)} %collective-permute-done.7.refs_5_) | copy-start | bytes 442372
  67.6 2.9 %copy-start.19 = (bf16[96,768]{1,0:T(8,128)(2,1)}, bf16[96,768]{1,0:T(8,128)(2,1)S(1)}, u32[]{:S(2)}) copy-start(bf16[96,768]{1,0:T(8,128)(2,1)S(1)} %collective-permute-done.6.refs_4_) | copy-start | bytes 442372
  73.6 6.4 %copy-start.8 = (f32[8,128]{1,0:T(8,128)}, f32[8,128]{1,0:T(8,128)S(1)}, u32[]{:S(2)}) copy-start(f32[8,128]{1,0:T(8,128)S(1)} %get-tuple-element.82.refs_1_) | copy-start | bytes 12292
  73.6 17.6 %collective-permute-start.12 = (bf16[128,768]{1,0:T(8,128)(2,1)}, bf16[128,768]{1,0:T(8,128)(2,1)S(1)}, u32[]{:S(2)}, u32[]{:S(2)}) collective-permute-start(bf16[128,768]{1,0:T(8,128)(2,1)} %get-tuple-element.87), channel_id=1, source_target_pairs={{0,3},{1,0},{2,1},{3,2},{4,7},{5,4},{6,5},{7,6},{8,11},{9,8},{10,9... | collective-permute-start | bytes 589832 | tf_op jit(solution)/shard_map/ppermute | solution.py:652
  73.9 17.3 %collective-permute-start.13 = (bf16[128,768]{1,0:T(8,128)(2,1)}, bf16[128,768]{1,0:T(8,128)(2,1)S(1)}, u32[]{:S(2)}, u32[]{:S(2)}) collective-permute-start(bf16[128,768]{1,0:T(8,128)(2,1)} %get-tuple-element.88), channel_id=1, source_target_pairs={{0,2},{1,3},{2,0},{3,1},{4,6},{5,7},{6,4},{7,5},{8,10},{9,11},{10,... | collective-permute-start | bytes 589832 | tf_op jit(solution)/shard_map/ppermute | solution.py:652
  76.2 15.0 %collective-permute-start.14 = (bf16[128,768]{1,0:T(8,128)(2,1)}, bf16[128,768]{1,0:T(8,128)(2,1)S(1)}, u32[]{:S(2)}, u32[]{:S(2)}) collective-permute-start(bf16[128,768]{1,0:T(8,128)(2,1)} %get-tuple-element.89), channel_id=1, source_target_pairs={{0,1},{1,2},{2,3},{3,0},{4,5},{5,6},{6,7},{7,4},{8,9},{9,10},{10,1... | collective-permute-start | bytes 589832 | tf_op jit(solution)/shard_map/ppermute | solution.py:652
  80.0 25.0 %copy-start.6 = (f32[768]{0:T(1024)S(1)}, f32[768]{0:T(1024)}, u32[]{:S(2)}) copy-start(f32[768]{0:T(1024)} %refs_5_.5) | copy-start | bytes 9220
  92.0 19.3 %all-to-all-start.2 = ((bf16[64,16,128]{2,1,0:T(8,128)(2,1)}), bf16[64,16,128]{2,1,0:T(8,128)(2,1)S(1)}, u32[]{:S(2)}, u32[]{:S(2)}) async-start(bf16[64,16,128]{2,1,0:T(8,128)(2,1)} %later.5), calls=%async_computation.2 | async-start | bytes 524288 | tf_op jit(solution)/shard_map/all_to_all | solution.py:672
  100.5 8.3 %collective-permute-start.17 = (bf16[16,768]{1,0:T(8,128)(2,1)}, bf16[16,768]{1,0:T(8,128)(2,1)S(1)}, u32[]{:S(2)}, u32[]{:S(2)}) collective-permute-start(bf16[16,768]{1,0:T(8,128)(2,1)} %get-tuple-element.98.refs_9_), channel_id=1, source_target_pairs={{0,3},{1,0},{2,1},{3,2},{4,7},{5,4},{6,5},{7,6},{8,11},{9,8},{10,9... | collective-permute-start | bytes 73736 | tf_op jit(solution)/shard_map/ppermute | solution.py:652
  103.4 6.0 %collective-permute-start.16 = (bf16[16,768]{1,0:T(8,128)(2,1)}, bf16[16,768]{1,0:T(8,128)(2,1)S(1)}, u32[]{:S(2)}, u32[]{:S(2)}) collective-permute-start(bf16[16,768]{1,0:T(8,128)(2,1)} %get-tuple-element.98.refs_9_), channel_id=1, source_target_pairs={{0,2},{1,3},{2,0},{3,1},{4,6},{5,7},{6,4},{7,5},{8,10},{9,11},{10,... | collective-permute-start | bytes 73736 | tf_op jit(solution)/shard_map/ppermute | solution.py:652
  104.2 5.6 %collective-permute-start.15 = (bf16[16,768]{1,0:T(8,128)(2,1)}, bf16[16,768]{1,0:T(8,128)(2,1)S(1)}, u32[]{:S(2)}, u32[]{:S(2)}) collective-permute-start(bf16[16,768]{1,0:T(8,128)(2,1)} %get-tuple-element.98.refs_9_), channel_id=1, source_target_pairs={{0,1},{1,2},{2,3},{3,0},{4,5},{5,6},{6,7},{7,4},{8,9},{9,10},{10,1... | collective-permute-start | bytes 73736 | tf_op jit(solution)/shard_map/ppermute | solution.py:652
  108.9 2.5 %copy-start.20 = (bf16[16,768]{1,0:T(8,128)(2,1)}, bf16[16,768]{1,0:T(8,128)(2,1)S(1)}, u32[]{:S(2)}) copy-start(bf16[16,768]{1,0:T(8,128)(2,1)S(1)} %collective-permute-done.17.refs_12_.refs_5_) | copy-start | bytes 73732
  109.3 2.0 copy-start.21
  109.8 1.6 copy-start.22
  112.0 21.8 %collective-permute-start.20 = (bf16[192,768]{1,0:T(8,128)(2,1)}, bf16[192,768]{1,0:T(8,128)(2,1)S(1)}, u32[]{:S(2)}, u32[]{:S(2)}) collective-permute-start(bf16[192,768]{1,0:T(8,128)(2,1)} %later.6.refs_4_), channel_id=1, source_target_pairs={{0,3},{1,0},{2,1},{3,2},{4,7},{5,4},{6,5},{7,6},{8,11},{9,8},{10,9... | collective-permute-start | bytes 884744 | tf_op jit(solution)/shard_map/ppermute | solution.py:652
  113.1 20.8 %collective-permute-start.19 = (bf16[192,768]{1,0:T(8,128)(2,1)}, bf16[192,768]{1,0:T(8,128)(2,1)S(1)}, u32[]{:S(2)}, u32[]{:S(2)}) collective-permute-start(bf16[192,768]{1,0:T(8,128)(2,1)} %later.6.refs_4_), channel_id=1, source_target_pairs={{0,2},{1,3},{2,0},{3,1},{4,6},{5,7},{6,4},{7,5},{8,10},{9,11},{10,... | collective-permute-start | bytes 884744 | tf_op jit(solution)/shard_map/ppermute | solution.py:652
  114.7 19.2 %collective-permute-start.18 = (bf16[192,768]{1,0:T(8,128)(2,1)}, bf16[192,768]{1,0:T(8,128)(2,1)S(1)}, u32[]{:S(2)}, u32[]{:S(2)}) collective-permute-start(bf16[192,768]{1,0:T(8,128)(2,1)} %later.6.refs_4_), channel_id=1, source_target_pairs={{0,1},{1,2},{2,3},{3,0},{4,5},{5,6},{6,7},{7,4},{8,9},{9,10},{10,1... | collective-permute-start | bytes 884744 | tf_op jit(solution)/shard_map/ppermute | solution.py:652
  129.8 19.7 %all-to-all-start.3 = ((bf16[16,256,128]{2,1,0:T(8,128)(2,1)}), bf16[16,256,128]{2,1,0:T(8,128)(2,1)S(1)}, u32[]{:S(2)}, u32[]{:S(2)}) async-start(bf16[16,256,128]{2,1,0:T(8,128)(2,1)} %get-tuple-element.99), calls=%async_computation.3 | async-start | bytes 2097152 | tf_op jit(solution)/shard_map/all_to_all | solution.py:668
  140.6 2.6 %collective-permute-start.21 = (bf16[96,1536]{1,0:T(8,128)(2,1)}, bf16[96,1536]{1,0:T(8,128)(2,1)S(1)}, u32[]{:S(2)}, u32[]{:S(2)}) collective-permute-start(bf16[96,1536]{1,0:T(8,128)(2,1)} %get-tuple-element.106), channel_id=1, source_target_pairs={{0,64},{64,0},{1,65},{65,1},{2,66},{66,2},{3,67},{67,3},{4,68},{68... | collective-permute-start | bytes 884744 | tf_op jit(solution)/shard_map/ppermute | solution.py:664
  140.6 2.5 %collective-permute-start.22 = (bf16[96,1536]{1,0:T(8,128)(2,1)}, bf16[96,1536]{1,0:T(8,128)(2,1)S(1)}, u32[]{:S(2)}, u32[]{:S(2)}) collective-permute-start(bf16[96,1536]{1,0:T(8,128)(2,1)} %get-tuple-element.107), channel_id=1, source_target_pairs={{0,64},{64,0},{1,65},{65,1},{2,66},{66,2},{3,67},{67,3},{4,68},{68... | collective-permute-start | bytes 884744 | tf_op jit(solution)/shard_map/ppermute | solution.py:664
  141.1 2.1 %collective-permute-start.23 = (bf16[96,1536]{1,0:T(8,128)(2,1)}, bf16[96,1536]{1,0:T(8,128)(2,1)S(1)}, u32[]{:S(2)}, u32[]{:S(2)}) collective-permute-start(bf16[96,1536]{1,0:T(8,128)(2,1)} %get-tuple-element.108), channel_id=1, source_target_pairs={{0,64},{64,0},{1,65},{65,1},{2,66},{66,2},{3,67},{67,3},{4,68},{68... | collective-permute-start | bytes 884744 | tf_op jit(solution)/shard_map/ppermute | solution.py:664
  141.2 2.5 %collective-permute-start.24 = (bf16[96,1536]{1,0:T(8,128)(2,1)}, bf16[96,1536]{1,0:T(8,128)(2,1)S(1)}, u32[]{:S(2)}, u32[]{:S(2)}) collective-permute-start(bf16[96,1536]{1,0:T(8,128)(2,1)} %get-tuple-element.109), channel_id=1, source_target_pairs={{0,64},{64,0},{1,65},{65,1},{2,66},{66,2},{3,67},{67,3},{4,68},{68... | collective-permute-start | bytes 884744 | tf_op jit(solution)/shard_map/ppermute | solution.py:664
  141.7 1.5 collective-permute-start.25
  152.3 3.0 %copy-start.29 = (bf16[96,768]{1,0:T(8,128)(2,1)S(1)}, bf16[96,768]{1,0:T(8,128)(2,1)}, u32[]{:S(2)}) copy-start(bf16[96,768]{1,0:T(8,128)(2,1)} %get-tuple-element.112) | copy-start | bytes 442372
  152.3 6.3 %copy-start.28 = (bf16[96,768]{1,0:T(8,128)(2,1)S(1)}, bf16[96,768]{1,0:T(8,128)(2,1)}, u32[]{:S(2)}) copy-start(bf16[96,768]{1,0:T(8,128)(2,1)} %get-tuple-element.115) | copy-start | bytes 442372
  152.3 6.9 %copy-start.27 = (bf16[96,768]{1,0:T(8,128)(2,1)S(1)}, bf16[96,768]{1,0:T(8,128)(2,1)}, u32[]{:S(2)}) copy-start(bf16[96,768]{1,0:T(8,128)(2,1)} %get-tuple-element.116) | copy-start | bytes 442372
  155.2 6.6 %collective-permute-start.35 = (bf16[400,768]{1,0:T(8,128)(2,1)}, bf16[400,768]{1,0:T(8,128)(2,1)S(1)}, u32[]{:S(2)}, u32[]{:S(2)}) collective-permute-start(bf16[400,768]{1,0:T(8,128)(2,1)} %get-tuple-element.121), channel_id=1, source_target_pairs={{0,64},{64,0},{1,65},{65,1},{2,66},{66,2},{3,67},{67,3},{4,68},{68... | collective-permute-start | bytes 1843208 | tf_op jit(solution)/shard_map/ppermute | solution.py:664
  155.3 13.5 %collective-permute-start.26 = (bf16[96,768]{1,0:T(8,128)(2,1)S(1)}, bf16[96,768]{1,0:T(8,128)(2,1)S(1)}, u32[]{:S(2)}, u32[]{:S(2)}) collective-permute-start(bf16[96,768]{1,0:T(8,128)(2,1)S(1)} %copy-done.29), channel_id=1, source_target_pairs={{0,2},{1,3},{2,0},{3,1},{4,6},{5,7},{6,4},{7,5},{8,10},{9,11},{10,... | collective-permute-start | bytes 442376 | tf_op jit(solution)/shard_map/ppermute | solution.py:652
  158.6 10.3 %collective-permute-start.30 = (bf16[96,768]{1,0:T(8,128)(2,1)S(1)}, bf16[96,768]{1,0:T(8,128)(2,1)S(1)}, u32[]{:S(2)}, u32[]{:S(2)}) collective-permute-start(bf16[96,768]{1,0:T(8,128)(2,1)S(1)} %copy-done.28), channel_id=1, source_target_pairs={{0,1},{1,2},{2,3},{3,0},{4,5},{5,6},{6,7},{7,4},{8,9},{9,10},{10,1... | collective-permute-start | bytes 442376 | tf_op jit(solution)/shard_map/ppermute | solution.py:652
  159.2 9.7 %collective-permute-start.31 = (bf16[96,768]{1,0:T(8,128)(2,1)S(1)}, bf16[96,768]{1,0:T(8,128)(2,1)S(1)}, u32[]{:S(2)}, u32[]{:S(2)}) collective-permute-start(bf16[96,768]{1,0:T(8,128)(2,1)S(1)} %copy-done.27), channel_id=1, source_target_pairs={{0,3},{1,0},{2,1},{3,2},{4,7},{5,4},{6,5},{7,6},{8,11},{9,8},{10,9... | collective-permute-start | bytes 442376 | tf_op jit(solution)/shard_map/ppermute | solution.py:652
  164.6 30.8 %all-to-all-start.4 = ((bf16[16,448,128]{2,1,0:T(8,128)(2,1)}), bf16[16,448,128]{2,1,0:T(8,128)(2,1)S(1)}, u32[]{:S(2)}, u32[]{:S(2)}) async-start(bf16[16,448,128]{2,1,0:T(8,128)(2,1)} %get-tuple-element.123), calls=%async_computation.4 | async-start | bytes 3670016 | tf_op jit(solution)/shard_map/all_to_all | solution.py:668
  170.1 6.9 %collective-permute-start.34 = (bf16[96,768]{1,0:T(8,128)(2,1)S(1)}, bf16[96,768]{1,0:T(8,128)(2,1)S(1)}, u32[]{:S(2)}, u32[]{:S(2)}) collective-permute-start(bf16[96,768]{1,0:T(8,128)(2,1)S(1)} %input_chunk.1.refs_0_), channel_id=1, source_target_pairs={{0,3},{1,0},{2,1},{3,2},{4,7},{5,4},{6,5},{7,6},{8,11},{9,8},{10,9... | collective-permute-start | bytes 442376 | tf_op jit(solution)/shard_map/ppermute | solution.py:652
  170.4 8.1 %collective-permute-start.33 = (bf16[96,768]{1,0:T(8,128)(2,1)S(1)}, bf16[96,768]{1,0:T(8,128)(2,1)S(1)}, u32[]{:S(2)}, u32[]{:S(2)}) collective-permute-start(bf16[96,768]{1,0:T(8,128)(2,1)S(1)} %input_chunk.1.refs_0_), channel_id=1, source_target_pairs={{0,2},{1,3},{2,0},{3,1},{4,6},{5,7},{6,4},{7,5},{8,10},{9,11},{10,... | collective-permute-start | bytes 442376 | tf_op jit(solution)/shard_map/ppermute | solution.py:652
  171.9 11.2 %collective-permute-start.32 = (bf16[96,768]{1,0:T(8,128)(2,1)S(1)}, bf16[96,768]{1,0:T(8,128)(2,1)S(1)}, u32[]{:S(2)}, u32[]{:S(2)}) collective-permute-start(bf16[96,768]{1,0:T(8,128)(2,1)S(1)} %input_chunk.1.refs_0_), channel_id=1, source_target_pairs={{0,1},{1,2},{2,3},{3,0},{4,5},{5,6},{6,7},{7,4},{8,9},{9,10},{10,1... | collective-permute-start | bytes 442376 | tf_op jit(solution)/shard_map/ppermute | solution.py:652
  172.2 14.2 %copy-start.1 = (bf16[96,768]{1,0:T(8,128)(2,1)S(1)}, bf16[96,768]{1,0:T(8,128)(2,1)}, u32[]{:S(2)}) copy-start(bf16[96,768]{1,0:T(8,128)(2,1)} %later.7.refs_0_) | copy-start | bytes 442372
  172.2 12.0 %collective-permute-start.29 = (bf16[96,768]{1,0:T(8,128)(2,1)}, bf16[96,768]{1,0:T(8,128)(2,1)S(1)}, u32[]{:S(2)}, u32[]{:S(2)}) collective-permute-start(bf16[96,768]{1,0:T(8,128)(2,1)} %later.7.refs_0_), channel_id=1, source_target_pairs={{0,3},{1,0},{2,1},{3,2},{4,7},{5,4},{6,5},{7,6},{8,11},{9,8},{10,9... | collective-permute-start | bytes 442376 | tf_op jit(solution)/shard_map/ppermute | solution.py:652
  175.1 9.8 %collective-permute-start.28 = (bf16[96,768]{1,0:T(8,128)(2,1)}, bf16[96,768]{1,0:T(8,128)(2,1)S(1)}, u32[]{:S(2)}, u32[]{:S(2)}) collective-permute-start(bf16[96,768]{1,0:T(8,128)(2,1)} %later.7.refs_0_), channel_id=1, source_target_pairs={{0,2},{1,3},{2,0},{3,1},{4,6},{5,7},{6,4},{7,5},{8,10},{9,11},{10,... | collective-permute-start | bytes 442376 | tf_op jit(solution)/shard_map/ppermute | solution.py:652
  177.0 9.4 %collective-permute-start.27 = (bf16[96,768]{1,0:T(8,128)(2,1)}, bf16[96,768]{1,0:T(8,128)(2,1)S(1)}, u32[]{:S(2)}, u32[]{:S(2)}) collective-permute-start(bf16[96,768]{1,0:T(8,128)(2,1)} %later.7.refs_0_), channel_id=1, source_target_pairs={{0,1},{1,2},{2,3},{3,0},{4,5},{5,6},{6,7},{7,4},{8,9},{9,10},{10,1... | collective-permute-start | bytes 442376 | tf_op jit(solution)/shard_map/ppermute | solution.py:652
  (8 other events, 6.6 us)
Sparse Core Ops, SparseCore 0:
  19.8 60.2 all-gather.2

commit v5 on v4

--- a/solution.py
+++ b/solution.py
@@ -414,7 +414,7 @@
     pairs = [(state_far, state), (cot_far, cot), (w_out_far, w_out), (g_one_far, g_one), (s_one_far, s_one)]
     pairs += [(b0_far, b0), (b_down_far, b_down), (g_two_far, g_two), (s_two_far, s_two)]
     first = copies(pairs, sems.at[8:])
-    pairs = [(every_far.at[which, :, s], weights.at[which, s]) for which in range(2) for s in range(NN)]
+    pairs = [(every_far.at[which, :, s], weights.at[which, s]) for s in range(NN) for which in range(2)]
     loads = copies(pairs, sems)
     for load in first:
         load.wait()
@@ -429,9 +429,9 @@
 
     total = None
     for s, b in enumerate((b0, b1, b2, b3)):
-        loads[s].wait()
+        loads[2 * s].wait()
         hidden, slope[s] = gelu_and_slope(dot(low, weight(0, s), NORMAL) + row_of(b))
-        loads[NN + s].wait()
+        loads[2 * s + 1].wait()
         term = dot(hidden, weight(1, s), BOTH_LAST)
         total = term if s == 0 else total + term
     residual = normed + (total + row_of(b_down))
@@ -517,12 +517,9 @@
     return jnp.concatenate([block[:, k : k + T] for k in range(0, block.shape[1], T)], axis=0).astype(bf16)
 
 
-def input_back_kernel(
-    wq, wk, wv, got, part0_far, part1_far, part2_far, part3_far, grad,
-    part0, part1, part2, part3, wide_part, near, sems,
-):
-    n = lax.axis_index("narrow")
-    loads = copies([(wq, near.at[0]), (wk, near.at[1]), (wv, near.at[2])], sems)
+def input_weights_kernel(x_far, got, out_whole, grad, send_far, keep_far, sums, whole, bias, x, sems):
+    c = lax.axis_index("dp")
+    load = copies([(x_far, x)], sems)[0]
     grads = []
     for j in range(3):
         grad_t = jnp.concatenate(
@@ -535,22 +532,6 @@
         grads.append(grad_t.astype(f32).T.astype(bf16))
     grads = jnp.concatenate(grads, axis=1)
     grad[...] = grads
-    for load in loads:
-        load.wait()
-    wide_part[...] = dot(grads, near[...].reshape(3 * E, D), NORMAL)
-    for r in range(R):
-        to = slice(r * C, (r + 1) * C)
-        part0[to, :] = wide_part[chunk_rows(n, r), :]
-        for s, part in ((1, part1), (2, part2), (3, part3)):
-            part[to, :] = wide_part[chunk_rows((n + s) % NN, r), :].astype(bf16)
-    pairs = [(part0, part0_far), (part1, part1_far), (part2, part2_far), (part3, part3_far)]
-    for store in copies(pairs, sems):
-        store.wait()
-
-
-def input_weights_kernel(x_far, got, out_whole, grad, send_far, keep_far, sums, whole, bias, x, sems):
-    c = lax.axis_index("dp")
-    load = copies([(x_far, x)], sems)[0]
     heads = []
     for h in range(NH):
         block = got[h, 3 * HD : SLOT, :].astype(f32)
@@ -560,21 +541,39 @@
     first = jnp.concatenate([b[0:1, 0:HD] + b[2:3, 0:HD] for b in heads], axis=1)
     second = jnp.concatenate([b[0:1, HD:] + b[2:3, HD:] for b in heads], axis=1)
     third = jnp.concatenate([b[1:2, 0:HD] + b[3:4, 0:HD] for b in heads], axis=1)
+    row = jnp.concatenate([first, second, third], axis=1)
     total = got[0, SLOT:, :].astype(f32)
     for w in range(1, NW):
         total = total + got[w, SLOT:, :].astype(f32)
     total = jnp.concatenate([total[k : k + 8, :] for k in range(0, VECTORS, 8)], axis=1)
-    row = jnp.concatenate([first, second, third, jnp.zeros((1, E), f32)], axis=1)
+    row = jnp.concatenate([row, jnp.zeros((1, E), f32)], axis=1)
     sums[...] = jnp.concatenate([total[0:6, :], row, row], axis=0)
     hi, mid, lo = split3(sums[...])
     bias[...] = jnp.concatenate([hi[0:7, :], mid[0:7, :], lo[6:7, :], lo[6:7, :]], axis=0).astype(bf16)
     whole[:, 3 * E :] = out_whole[...]
     load.wait()
-    whole[:, 0 : 3 * E] = dot(x[...].reshape(TOK, D), grad[...], BOTH_FIRST).astype(bf16)
+    whole[:, 0 : 3 * E] = dot(x[...].reshape(TOK, D), grads, BOTH_FIRST).astype(bf16)
     half = D // 2
     pairs = [(bias, send_far.at[half:, :])]
     pairs.append((whole.at[pl.ds(pl.multiple_of((1 - c) * half, half), half), :], send_far.at[0:half, :]))
     pairs.append((whole.at[pl.ds(pl.multiple_of(c * half, half), half), :], keep_far))
+    for store in copies(pairs, sems):
+        store.wait()
+
+
+def input_back_kernel(
+    wq, wk, wv, grad, part0_far, part1_far, part2_far, part3_far, part0, part1, part2, part3, wide_part, near, sems
+):
+    n = lax.axis_index("narrow")
+    for load in copies([(wq, near.at[0]), (wk, near.at[1]), (wv, near.at[2])], sems):
+        load.wait()
+    wide_part[...] = dot(grad[...], near[...].reshape(3 * E, D), NORMAL)
+    for r in range(R):
+        to = slice(r * C, (r + 1) * C)
+        part0[to, :] = wide_part[chunk_rows(n, r), :]
+        for s, part in ((1, part1), (2, part2), (3, part3)):
+            part[to, :] = wide_part[chunk_rows((n + s) % NN, r), :].astype(bf16)
+    pairs = [(part0, part0_far), (part1, part1_far), (part2, part2_far), (part3, part3_far)]
     for store in copies(pairs, sems):
         store.wait()
 
@@ -885,11 +884,26 @@
         far=(0,),
         token=True,
     )
-    *parts, grad = call(
+    grad, send, keep, sums = call(
+        "input_weights",
+        input_weights_kernel,
+        [((TOK, 3 * E), bf16), ((D // 2 + 16, D), bf16), ((D // 2, D), bf16), ((8, D), f32)],
+        (hidden_in, got, out_whole),
+        scratch=[
+            pltpu.VMEM((D, D), bf16),
+            pltpu.VMEM((16, D), bf16),
+            pltpu.VMEM((R, T, D), bf16),
+            pltpu.SemaphoreType.DMA((3,)),
+        ],
+        far_in=(0,),
+        far=(1, 2),
+        after=(added,),
+    )
+    *parts, done = call(
         "input_back",
         input_back_kernel,
-        [*parts4, ((TOK, 3 * E), bf16)],
-        (query_t, key_t, value_t, got),
+        parts4,
+        (query_t, key_t, value_t, grad),
         scratch=[
             pltpu.VMEM((CH, D), f32),
             pltpu.VMEM((CH, D), bf16),
@@ -901,24 +915,9 @@
         ],
         far_in=range(3),
         far=range(4),
-        after=(added,),
-    )
-    send, keep, sums = call(
-        "input_weights",
-        input_weights_kernel,
-        [((D // 2 + 16, D), bf16), ((D // 2, D), bf16), ((8, D), f32)],
-        (hidden_in, got, out_whole, grad),
-        scratch=[
-            pltpu.VMEM((D, D), bf16),
-            pltpu.VMEM((16, D), bf16),
-            pltpu.VMEM((R, T, D), bf16),
-            pltpu.SemaphoreType.DMA((3,)),
-        ],
-        far_in=(0,),
-        far=(0, 1),
-    )
-    parts = scatter_narrow(parts)
-    slots, b_query, b_key, b_value, g_two, s_two, b_down, g_one, s_one, b_out = call(
+        token=True,
+    )
+    slots, b_query, b_key, b_value, g_two, s_two, b_down, g_one, s_one, b_out, token = call(
         "last_add",
         last_add_kernel,
         [(last_shape, bf16)] + [((E,), f32)] * 3 + [((D,), f32)] * 6,
@@ -933,12 +932,15 @@
         any_in=(2,),
         far=(0,),
         aliases={1: 0},
-    )
+        after=(done,),
+        token=True,
+    )
+    parts = scatter_narrow([parts[0], *(later(part, anywhere=(token,)) for part in parts[1:])])
     (input_low,) = call("input_chunk", input_chunk_kernel, [chunk_low], (parts[0], grad_one, *parts[1:]),
         scratch=[pltpu.VMEM((CH, D), f32), pltpu.VMEM((CH, D), f32), pltpu.SemaphoreType.DMA((2,))],
-        cost=COST, far_in=(0, 1),
-    )
-    layers = gather_narrow(later(layer, parts[2]))
+        far_in=(0, 1),
+    )
+    layers = gather_narrow(later(layer, anywhere=(token,)))
     whole_out = ((R, T, D), f32)
     (layer_out,) = call("layer_out", spread_kernel, [whole_out], layers)
     (grad_input,) = call("grad_input", spread_kernel, [whole_out], gather_narrow(input_low))

time: 204 us -> 199 us (0.975)
  waiting for transfers between devices: 48.9 us -> 44 us
    all_to_all x3, waiting for transfers between devices: 16.9 us -> 11.1 us  [exchange(): return lax.all_to_all(slots, 'wide', 0, 0, tiled=True)]
where the time goes in v5:
time: 199 us; the launch traced here: 198 us
  starting transfers between devices  67.5 us (34%)
  Pallas kernels  67 us (34%)
  waiting for transfers between devices  44 us (22%)
  between operations  14.6 us (7%)
  local copies, waits for them, and re-layouts  4.04 us (2%)
    pallas_call x16, Pallas kernels, call(): pl.pallas_call(run, out_shape=[shape(k, s, t) for k, (s, t) in enumerate(...  67 us
    ppermute x27, starting transfers between devices, shifted(): return lax.ppermute(x, 'narrow', [(i, (i + s) % NN) for i in range(NN)])  36.3 us
    ppermute x27, waiting for transfers between devices, shifted(): return lax.ppermute(x, 'narrow', [(i, (i + s) % NN) for i in range(NN)])  23.1 us
    all_to_all x3, starting transfers between devices, exchange(): return lax.all_to_all(slots, 'wide', 0, 0, tiled=True)  15.6 us
    all_to_all x2, starting transfers between devices, exchange_all(): return lax.all_to_all(slots, ('wide', 'narrow'), 0, 0, tiled=True)  13.7 us
    all_to_all x3, waiting for transfers between devices, exchange(): return lax.all_to_all(slots, 'wide', 0, 0, tiled=True)  11.1 us
    all_to_all x2, waiting for transfers between devices, exchange_all(): return lax.all_to_all(slots, ('wide', 'narrow'), 0, 0, tiled=True)  4.43 us
  transfers between devices with their start and end apart: 42, of which 24 were waited for; matrix products, arithmetic and copies ran while one was open for 0% of the time, Pallas kernels for 30%

profile of v5, /device:TPU:0, one launch (start us, length us, event | category | flops | bytes accessed | tf_op | source)
XLA Modules:
  0.0 198.1 jit_solution(18000344321386188145)
XLA Ops:
  7.2 0.9 bitcast_select_fusion.refs_0_
  8.2 4.2 %collective-permute-start.2 = (bf16[48,768]{1,0:T(8,128)(2,1)S(1)}, bf16[48,768]{1,0:T(8,128)(2,1)S(1)}, u32[]{:S(2)}, u32[]{:S(2)}) collective-permute-start(bf16[48,768]{1,0:T(8,128)(2,1)S(1)} %bitcast_select_fusion.refs_0_), channel_id=1, source_target_pairs={{0,3},{1,0},{2,1},{3,2},{4,7},{5,4},{6,5},{7,6},{8,11},{9,8},{10,9... | collective-permute-start | bytes 221192 | tf_op jit(solution)/shard_map/ppermute | solution.py:651
  12.4 1.3 collective-permute-start
  13.6 3.1 %project.1 = (bf16[16,208,128]{2,1,0:T(8,128)(2,1)}, f32[8,128]{1,0:T(8,128)S(1)}) custom-call(bf16[3,128,768]{2,1,0:T(8,128)(2,1)} %refs_0_.5, s32[3,128]{1,0:T(4,128)} %refs_1_.2, bf16[192,768]{1,0:T(8,128)(2,1)} %bitcast.9, f32[192]{0:T(256)} %refs_3_.1, bf16[192,768]{1,0:T(8,128)(2,1)} %bitcast.11, f32[192]{0:T(256)} %refs_5_.3, ...), custom_call_target="tpu_custom_call" | custom-call | flops 1024 | bytes 1024 | tf_op jit(solution)/shard_map/project/pallas_call | solution.py:70
  16.8 1.6 collective-permute-done.1.refs_2_
  18.9 0.8 stack.1
  19.7 7.2 %all-to-all-start = ((bf16[16,208,128]{2,1,0:T(8,128)(2,1)}), bf16[16,208,128]{2,1,0:T(8,128)(2,1)S(1)}, u32[]{:S(2)}, u32[]{:S(2)}) async-start(bf16[16,208,128]{2,1,0:T(8,128)(2,1)} %get-tuple-element.82), calls=%async_computation | async-start | bytes 1703936 | tf_op jit(solution)/shard_map/all_to_all | solution.py:667
  26.9 0.9 collective-permute-start.5
  27.9 1.4 collective-permute-start.4
  29.2 0.6 collective-permute-start.3
  29.8 2.8 %collective-permute-done.5.refs_4_.refs_3_ = bf16[96,768]{1,0:T(8,128)(2,1)S(1)} collective-permute-done((bf16[96,768]{1,0:T(8,128)(2,1)S(1)}, bf16[96,768]{1,0:T(8,128)(2,1)S(1)}, u32[]{:S(2)}, u32[]{:S(2)}) %collective-permute-start.5) | collective-permute-done | bytes 147488 | tf_op jit(solution)/shard_map/ppermute | solution.py:651
  32.7 2.2 %collective-permute-done.4.refs_3_.refs_2_ = bf16[96,768]{1,0:T(8,128)(2,1)S(1)} collective-permute-done((bf16[96,768]{1,0:T(8,128)(2,1)S(1)}, bf16[96,768]{1,0:T(8,128)(2,1)S(1)}, u32[]{:S(2)}, u32[]{:S(2)}) %collective-permute-start.4) | collective-permute-done | bytes 147488 | tf_op jit(solution)/shard_map/ppermute | solution.py:651
  34.8 1.5 collective-permute-done.3.refs_2_.refs_1_
  36.3 6.1 %all-to-all-done.refs_0_ = bf16[16,208,128]{2,1,0:T(8,128)(2,1)S(1)} async-done(((bf16[16,208,128]{2,1,0:T(8,128)(2,1)}), bf16[16,208,128]{2,1,0:T(8,128)(2,1)S(1)}, u32[]{:S(2)}, u32[]{:S(2)}) %all-to-all-start) | async-done | bytes 852000 | tf_op jit(solution)/shard_map/all_to_all | solution.py:667
  42.5 9.9 %attend.1 = (bf16[64,16,128]{2,1,0:T(8,128)(2,1)}, bf16[80,2048]{1,0:T(8,128)(2,1)}, bf16[80,2048]{1,0:T(8,128)(2,1)}, bf16[2048,64]{1,0:T(8,128)(2,1)}, bf16[20...) custom-call(bf16[16,208,128]{2,1,0:T(8,128)(2,1)S(1)} %all-to-all-do, ...), custom_call_target="tpu_custom_call" | custom-call | flops 1024 | bytes 1024 | tf_op jit(solution)/shard_map/attend/pallas_call | solution.py:70
  52.5 5.2 %all-to-all-start.1 = ((bf16[64,16,128]{2,1,0:T(8,128)(2,1)}), bf16[64,16,128]{2,1,0:T(8,128)(2,1)S(1)}, u32[]{:S(2)}, u32[]{:S(2)}) async-start(bf16[64,16,128]{2,1,0:T(8,128)(2,1)} %get-tuple-element.83), calls=%async_computation.1 | async-start | bytes 524288 | tf_op jit(solution)/shard_map/all_to_all | solution.py:671
  58.3 2.8 %collective-permute-start.11 = (f32[768]{0:T(1024)S(1)}, f32[768]{0:T(1024)S(1)}, u32[]{:S(2)}, u32[]{:S(2)}) collective-permute-start(f32[768]{0:T(1024)S(1)} %copy-done.5), channel_id=1, source_target_pairs={{0,3},{1,0},{2,1},{3,2},{4,7},{5,4},{6,5},{7,6},{8,11},{9,8},{10,9... | collective-permute-start | bytes 9224 | tf_op jit(solution)/shard_map/ppermute | solution.py:651
  61.1 0.9 collective-permute-start.10
  62.5 1.1 collective-permute-start.9
  63.5 2.7 %collective-permute-done.10.refs_13_.refs_11_ = f32[768]{0:T(1024)S(1)} collective-permute-done((f32[768]{0:T(1024)S(1)}, f32[768]{0:T(1024)S(1)}, u32[]{:S(2)}, u32[]{:S(2)}) %collective-permute-start.10) | collective-permute-done | bytes 3104 | tf_op jit(solution)/shard_map/ppermute | solution.py:651
  66.2 1.3 collective-permute-done.9.refs_12_.refs_10_
  67.6 2.9 %all-to-all-done.1.refs_8_ = bf16[64,16,128]{2,1,0:T(8,128)(2,1)S(1)} async-done(((bf16[64,16,128]{2,1,0:T(8,128)(2,1)}), bf16[64,16,128]{2,1,0:T(8,128)(2,1)S(1)}, u32[]{:S(2)}, u32[]{:S(2)}) %all-to-all-start.1) | async-done | bytes 262176 | tf_op jit(solution)/shard_map/all_to_all | solution.py:671
  70.5 3.1 %first.1 = (bf16[768,768]{1,0:T(8,128)(2,1)}, f32[96,896]{1,0:T(8,128)}, bf16[128,768]{1,0:T(8,128)(2,1)}, bf16[128,768]{1,0:T(8,128)(2,1)}, bf16[128,768]{1,0:T...) custom-call(bf16[192,768]{1,0:T(8,128)(2,1)} %refs_0_.4, bf16[96,768]{1,0:T(8,128)(2,1)} %copy-done.16, ...), custom_call_target="tpu_custom_call" | custom-call | flops 1024 | bytes 1024 | tf_op jit(solution)/shard_map/first/pallas_call | solution.py:70
  73.9 2.3 %collective-permute-start.13 = (bf16[128,768]{1,0:T(8,128)(2,1)}, bf16[128,768]{1,0:T(8,128)(2,1)S(1)}, u32[]{:S(2)}, u32[]{:S(2)}) collective-permute-start(bf16[128,768]{1,0:T(8,128)(2,1)} %get-tuple-element.90), channel_id=1, source_target_pairs={{0,2},{1,3},{2,0},{3,1},{4,6},{5,7},{6,4},{7,5},{8,10},{9,11},{10,... | collective-permute-start | bytes 589832 | tf_op jit(solution)/shard_map/ppermute | solution.py:651
  76.7 3.3 %all-gather.3.cloned.1.call-done = bf16[128,48,768]{2,1,0:T(8,128)(2,1)} async-done(((bf16[4,48,768]{2,1,0:T(8,128)(2,1)}), bf16[128,48,768]{2,1,0:T(8,128)(2,1)}) %all-gather.3.cloned.1.call-update) | async-done | bytes 9437200 | tf_op jit(solution)/shard_map/all_gather | solution.py:716
  80.1 10.4 %middle.1 = (bf16[64,16,128]{2,1,0:T(8,128)(2,1)}, f32[96,768]{1,0:T(8,128)}, bf16[192,768]{1,0:T(8,128)(2,1)}, bf16[96,768]{1,0:T(8,128)(2,1)}, bf16[16,768]{1,0:T(8,128)(2,1)}) custom-call(bf16[2,16,4,48,768]{4,3,2,1,0:T(8,128)(2,1)} %later.7.refs_0_.refs_4_.refs_8_, f32[96,896]{1,0:T(8,128)} %get-tuple-element.85.refs_1_, bf16[3,128,768]{2,1,0:T(8,128)(2,1)} %refs_2_.1, ...), custom_call_target="tpu_custom_call" | custom-call | flops 1024 | bytes 1024 | tf_op jit(solution)/shard_map/middle/pallas_call | solution.py:70
  90.5 0.6 copy-done.10
  91.3 8.5 %all-to-all-start.2 = ((bf16[64,16,128]{2,1,0:T(8,128)(2,1)}), bf16[64,16,128]{2,1,0:T(8,128)(2,1)S(1)}, u32[]{:S(2)}, u32[]{:S(2)}) async-start(bf16[64,16,128]{2,1,0:T(8,128)(2,1)} %later.8), calls=%async_computation.2 | async-start | bytes 524288 | tf_op jit(solution)/shard_map/all_to_all | solution.py:671
  99.8 2.9 %collective-permute-start.17 = (bf16[16,768]{1,0:T(8,128)(2,1)}, bf16[16,768]{1,0:T(8,128)(2,1)S(1)}, u32[]{:S(2)}, u32[]{:S(2)}) collective-permute-start(bf16[16,768]{1,0:T(8,128)(2,1)} %get-tuple-element.100.refs_9_), channel_id=1, source_target_pairs={{0,3},{1,0},{2,1},{3,2},{4,7},{5,4},{6,5},{7,6},{8,11},{9,8},{10,9... | collective-permute-start | bytes 73736 | tf_op jit(solution)/shard_map/ppermute | solution.py:651
  102.6 0.9 collective-permute-start.16
  103.5 0.9 collective-permute-start.15
  104.3 3.8 %hidden.1 = (bf16[384,768]{1,0:T(8,128)(2,1)}, f32[384,768]{1,0:T(8,128)}) custom-call(bf16[128,768]{1,0:T(8,128)(2,1)} %get-tuple-element.102.refs_0_, bf16[128,768]{1,0:T(8,128)(2,1)} %copy-done.12, bf16[128,768]{1,0:T(8,128)(2,1)} %copy-done.11, bf16[128,768]{1,0:T(8,128)(2,1)} %copy-done.10, bf16[2,16,4,48,768]{4,3,2,1,0:T(8,128)(2,1)} %later.7.refs_0_.refs_4_.refs_8_, ...), custom_call_target="tpu_custom_call" | custom-call | flops 1024 | bytes 1024 | tf_op jit(solution)/shard_map/hidden/pallas_call | solution.py:70
  109.0 1.6 all-to-all-done.2.refs_0_.refs_2_
  110.6 0.7 copy-done.9
  111.3 1.0 collective-permute-start.20
  112.4 1.6 collective-permute-start.19
  114.0 15.0 %attend_back.1 = (bf16[16,256,128]{2,1,0:T(8,128)(2,1)}, f32[8,128]{1,0:T(8,128)S(1)}) custom-call(bf16[64,16,128]{2,1,0:T(8,128)(2,1)} %copy-done.9, bf16[80,2048]{1,0:T(8,128)(2,1)} %get-tuple-element.92.refs_1_, bf16[80,2048]{1,0:T(8,128)(2,1)} %get-tuple-element.93.refs_2_, bf16[2048,64]{1,0:T(8,128)(2,1)} %get-tuple-element.94.refs_3_, ...), custom_call_target="tpu_custom_call" | custom-call | flops 1024 | bytes 1024 | tf_op jit(solution)/shard_map/attend_back/pallas_call | solution.py:70
  129.0 4.1 %all-to-all-start.3 = ((bf16[16,256,128]{2,1,0:T(8,128)(2,1)}), bf16[16,256,128]{2,1,0:T(8,128)(2,1)S(1)}, u32[]{:S(2)}, u32[]{:S(2)}) async-start(bf16[16,256,128]{2,1,0:T(8,128)(2,1)} %get-tuple-element.101), calls=%async_computation.3 | async-start | bytes 2097152 | tf_op jit(solution)/shard_map/all_to_all | solution.py:667
  133.2 0.7 copy-done.24
  134.1 5.7 %weights.1 = (bf16[96,1536]{1,0:T(8,128)(2,1)}, bf16[96,1536]{1,0:T(8,128)(2,1)}, bf16[96,1536]{1,0:T(8,128)(2,1)}, bf16[96,1536]{1,0:T(8,128)(2,1)}, bf16[384,1...) custom-call(bf16[128,768]{1,0:T(8,128)(2,1)} %get-tuple-element.102.refs_0_, ...), custom_call_target="tpu_custom_call" | custom-call | flops 99999997952 | bytes 1024 | tf_op jit(solution)/shard_map/weights/pallas_call | solution.py:70
  141.0 1.4 collective-permute-done.25.refs_6_
  142.9 2.7 %first_add.1 = (bf16[16,448,128]{2,1,0:T(8,128)(2,1)}, f32[8,128]{1,0:T(8,128)S(1)}) custom-call(bf16[384,1536]{1,0:T(8,128)(2,1)} %get-tuple-element.108.refs_0_, bf16[96,1536]{1,0:T(8,128)(2,1)S(1)} %collective-permute-done.21.refs_1_, bf16[96,1536]{1,0:T(8,128)(2,1)S(1)} %collective-permute-done.22.refs_2_, ...), custom_call_target="tpu_custom_call" | custom-call | flops 1024 | bytes 1024 | tf_op jit(solution)/shard_map/first_add/pallas_call | solution.py:70
  145.7 3.0 %all-to-all-done.3.refs_1_ = bf16[16,256,128]{2,1,0:T(8,128)(2,1)S(1)} async-done(((bf16[16,256,128]{2,1,0:T(8,128)(2,1)}), bf16[16,256,128]{2,1,0:T(8,128)(2,1)S(1)}, u32[]{:S(2)}, u32[]{:S(2)}) %all-to-all-start.3) | async-done | bytes 1048608 | tf_op jit(solution)/shard_map/all_to_all | solution.py:667
  148.7 2.9 %input_weights.1 = (bf16[384,576]{1,0:T(8,128)(2,1)S(1)}, bf16[400,768]{1,0:T(8,128)(2,1)}, bf16[384,768]{1,0:T(8,128)(2,1)}, f32[8,768]{1,0:T(8,128)S(1)}) custom-call(bf16[3,128,768]{2,1,0:T(8,128)(2,1)} %refs_0_.5, bf16[16,256,128]{2,1,0:T(8,128)(2,1)S(1)} %all-to-all-done.3.refs_1_, bf16[768,192]{1,0:T(8,128)(2,1)S(1)} %get-tuple-element.107.refs_2_, ...), custom_call_target="tpu_custom_call" | custom-call | flops 1024 | bytes 1024 | tf_op jit(solution)/shard_map/input_weights/pallas_call | solution.py:70
  151.6 2.7 %input_back.1 = (f32[96,768]{1,0:T(8,128)}, bf16[96,768]{1,0:T(8,128)(2,1)}, bf16[96,768]{1,0:T(8,128)(2,1)}, bf16[96,768]{1,0:T(8,128)(2,1)}, f32[8,128]{1,0:T(8,128)S(1)}) custom-call(bf16[192,768]{1,0:T(8,128)(2,1)} %bitcast.10, bf16[192,768]{1,0:T(8,128)(2,1)} %bitcast.12, bf16[192,768]{1,0:T(8,128)(2,1)} %bitcast.14, ...), custom_call_target="tpu_custom_call" | custom-call | flops 1024 | bytes 1024 | tf_op jit(solution)/shard_map/input_back/pallas_call | solution.py:70
  154.4 2.7 %last_add.1 = (bf16[16,448,128]{2,1,0:T(8,128)(2,1)}, f32[192]{0:T(256)}, f32[192]{0:T(256)}, f32[192]{0:T(256)}, f32[768]{0:T(1024)}, /*index=5*/f32[768]{0:T(1...) custom-call(bf16[384,768]{1,0:T(8,128)(2,1)} %get-tuple-element.115., ...), custom_call_target="tpu_custom_call", output_to_operand_aliasing={{0}: (1, {})} | custom-call | flops 1024 | bytes 1024 | tf_op jit(solution)/shard_map/last_add/pallas_call | solution.py:70
  157.7 4.4 %all-to-all-start.4 = ((bf16[16,448,128]{2,1,0:T(8,128)(2,1)}), bf16[16,448,128]{2,1,0:T(8,128)(2,1)S(1)}, u32[]{:S(2)}, u32[]{:S(2)}) async-start(bf16[16,448,128]{2,1,0:T(8,128)(2,1)} %get-tuple-element.127), calls=%async_computation.4 | async-start | bytes 3670016 | tf_op jit(solution)/shard_map/all_to_all | solution.py:667
  162.1 2.1 %collective-permute-start.30 = (bf16[96,768]{1,0:T(8,128)(2,1)}, bf16[96,768]{1,0:T(8,128)(2,1)S(1)}, u32[]{:S(2)}, u32[]{:S(2)}) collective-permute-start(bf16[96,768]{1,0:T(8,128)(2,1)} %later.11), channel_id=1, source_target_pairs={{0,1},{1,2},{2,3},{3,0},{4,5},{5,6},{6,7},{7,4},{8,9},{9,10},{10,1... | collective-permute-start | bytes 442376 | tf_op jit(solution)/shard_map/ppermute | solution.py:651
  164.2 2.7 %collective-permute-start.31 = (bf16[96,768]{1,0:T(8,128)(2,1)}, bf16[96,768]{1,0:T(8,128)(2,1)S(1)}, u32[]{:S(2)}, u32[]{:S(2)}) collective-permute-start(bf16[96,768]{1,0:T(8,128)(2,1)} %later.12), channel_id=1, source_target_pairs={{0,2},{1,3},{2,0},{3,1},{4,6},{5,7},{6,4},{7,5},{8,10},{9,11},{10,... | collective-permute-start | bytes 442376 | tf_op jit(solution)/shard_map/ppermute | solution.py:651
  166.8 1.1 collective-permute-start.32
  168.3 2.7 %collective-permute-start.28 = (bf16[96,768]{1,0:T(8,128)(2,1)}, bf16[96,768]{1,0:T(8,128)(2,1)S(1)}, u32[]{:S(2)}, u32[]{:S(2)}) collective-permute-start(bf16[96,768]{1,0:T(8,128)(2,1)} %later.10.refs_0_), channel_id=1, source_target_pairs={{0,2},{1,3},{2,0},{3,1},{4,6},{5,7},{6,4},{7,5},{8,10},{9,11},{10,... | collective-permute-start | bytes 442376 | tf_op jit(solution)/shard_map/ppermute | solution.py:651
  171.0 4.0 %collective-permute-done.31.refs_3_ = bf16[96,768]{1,0:T(8,128)(2,1)S(1)} collective-permute-done((bf16[96,768]{1,0:T(8,128)(2,1)}, bf16[96,768]{1,0:T(8,128)(2,1)S(1)}, u32[]{:S(2)}, u32[]{:S(2)}) %collective-permute-start.31) | collective-permute-done | bytes 147488 | tf_op jit(solution)/shard_map/ppermute | solution.py:651
  175.0 1.1 input_chunk.1.refs_0_
  176.1 1.7 collective-permute-start.35
  177.9 1.3 collective-permute-start.34
  179.1 1.0 collective-permute-start.33
  180.3 0.9 copy-done.1
  181.3 1.1 layer_out.1
  182.4 1.5 collective-permute-done.35.refs_3_
  183.9 1.8 collective-permute-done.34.refs_2_
  185.7 1.5 collective-permute-done.33.refs_1_
  187.2 1.1 grad_input.1
  188.3 2.0 %all-to-all-done.4.refs_0_ = bf16[16,448,128]{2,1,0:T(8,128)(2,1)S(1)} async-done(((bf16[16,448,128]{2,1,0:T(8,128)(2,1)}), bf16[16,448,128]{2,1,0:T(8,128)(2,1)S(1)}, u32[]{:S(2)}, u32[]{:S(2)}) %all-to-all-start.4) | async-done | bytes 1835040 | tf_op jit(solution)/shard_map/all_to_all | solution.py:667
  190.3 0.9 last_sum.1
  (101 shorter events, 6.9 us)
Async XLA Ops:
  7.2 72.9 %all-gather.3.cloned.1.call-start = ((), (), s32[]{:S(2)}) async-start(), calls=%async_computation.5 | async-start | bytes 9732096 | tf_op jit(solution)/shard_map/all_gather | solution.py:716
  8.2 8.6 %collective-permute-start.2 = (bf16[48,768]{1,0:T(8,128)(2,1)S(1)}, bf16[48,768]{1,0:T(8,128)(2,1)S(1)}, u32[]{:S(2)}, u32[]{:S(2)}) collective-permute-start(bf16[48,768]{1,0:T(8,128)(2,1)S(1)} %bitcast_select_fusion.refs_0_), channel_id=1, source_target_pairs={{0,3},{1,0},{2,1},{3,2},{4,7},{5,4},{6,5},{7,6},{8,11},{9,8},{10,9... | collective-permute-start | bytes 221192 | tf_op jit(solution)/shard_map/ppermute | solution.py:651
  12.4 6.0 %collective-permute-start.1 = (bf16[48,768]{1,0:T(8,128)(2,1)S(1)}, bf16[48,768]{1,0:T(8,128)(2,1)S(1)}, u32[]{:S(2)}, u32[]{:S(2)}) collective-permute-start(bf16[48,768]{1,0:T(8,128)(2,1)S(1)} %bitcast_select_fusion.refs_0_), channel_id=1, source_target_pairs={{0,2},{1,3},{2,0},{3,1},{4,6},{5,7},{6,4},{7,5},{8,10},{9,11},{10,... | collective-permute-start | bytes 221192 | tf_op jit(solution)/shard_map/ppermute | solution.py:651
  12.4 6.5 %collective-permute-start = (bf16[48,768]{1,0:T(8,128)(2,1)S(1)}, bf16[48,768]{1,0:T(8,128)(2,1)S(1)}, u32[]{:S(2)}, u32[]{:S(2)}) collective-permute-start(bf16[48,768]{1,0:T(8,128)(2,1)S(1)} %bitcast_select_fusion.refs_0_), channel_id=1, source_target_pairs={{0,1},{1,2},{2,3},{3,0},{4,5},{5,6},{6,7},{7,4},{8,9},{9,10},{10,1... | collective-permute-start | bytes 221192 | tf_op jit(solution)/shard_map/ppermute | solution.py:651
  13.6 13.3 %copy-start.13 = (bf16[192,768]{1,0:T(8,128)(2,1)S(1)}, bf16[192,768]{1,0:T(8,128)(2,1)}, u32[]{:S(2)}) copy-start(bf16[192,768]{1,0:T(8,128)(2,1)} %refs_0_.4) | copy-start | bytes 884740
  13.6 28.8 %copy-start.23 = (f32[64]{0:T(128)S(1)}, f32[64]{0:T(128)}, u32[]{:S(2)}) copy-start(f32[64]{0:T(128)} %constant.14.clone) | copy-start | bytes 772
  19.6 38.7 %copy-start.5 = (f32[768]{0:T(1024)S(1)}, f32[768]{0:T(1024)}, u32[]{:S(2)}) copy-start(f32[768]{0:T(1024)} %refs_5_.5) | copy-start | bytes 9220
  19.7 50.8 %copy-start = (bf16[3,128,768]{2,1,0:T(8,128)(2,1)S(1)}, bf16[3,128,768]{2,1,0:T(8,128)(2,1)}, u32[]{:S(2)}) copy-start(bf16[3,128,768]{2,1,0:T(8,128)(2,1)} %refs_0_.5) | copy-start | bytes 1769476
  19.7 50.8 %copy-start.3 = (f32[768]{0:T(1024)S(1)}, f32[768]{0:T(1024)}, u32[]{:S(2)}) copy-start(f32[768]{0:T(1024)} %refs_4_.1) | copy-start | bytes 9220
  19.7 50.8 %copy-start.4 = (f32[768]{0:T(1024)S(1)}, f32[768]{0:T(1024)}, u32[]{:S(2)}) copy-start(f32[768]{0:T(1024)} %refs_5_.4) | copy-start | bytes 9220
  19.7 50.8 %copy-start.7 = (f32[768]{0:T(1024)S(1)}, f32[768]{0:T(1024)}, u32[]{:S(2)}) copy-start(f32[768]{0:T(1024)} %refs_9_.2) | copy-start | bytes 9220
  19.7 22.7 %all-to-all-start = ((bf16[16,208,128]{2,1,0:T(8,128)(2,1)}), bf16[16,208,128]{2,1,0:T(8,128)(2,1)S(1)}, u32[]{:S(2)}, u32[]{:S(2)}) async-start(bf16[16,208,128]{2,1,0:T(8,128)(2,1)} %get-tuple-element.82), calls=%async_computation | async-start | bytes 1703936 | tf_op jit(solution)/shard_map/all_to_all | solution.py:667
  26.9 5.7 %collective-permute-start.5 = (bf16[96,768]{1,0:T(8,128)(2,1)S(1)}, bf16[96,768]{1,0:T(8,128)(2,1)S(1)}, u32[]{:S(2)}, u32[]{:S(2)}) collective-permute-start(bf16[96,768]{1,0:T(8,128)(2,1)S(1)} %constant_dynamic-slice_fusion), channel_id=1, source_target_pairs={{0,3},{1,0},{2,1},{3,2},{4,7},{5,4},{6,5},{7,6},{8,11},{9,8},{10,9... | collective-permute-start | bytes 442376 | tf_op jit(solution)/shard_map/ppermute | solution.py:651
  27.9 7.0 %collective-permute-start.4 = (bf16[96,768]{1,0:T(8,128)(2,1)S(1)}, bf16[96,768]{1,0:T(8,128)(2,1)S(1)}, u32[]{:S(2)}, u32[]{:S(2)}) collective-permute-start(bf16[96,768]{1,0:T(8,128)(2,1)S(1)} %constant_dynamic-slice_fusion), channel_id=1, source_target_pairs={{0,2},{1,3},{2,0},{3,1},{4,6},{5,7},{6,4},{7,5},{8,10},{9,11},{10,... | collective-permute-start | bytes 442376 | tf_op jit(solution)/shard_map/ppermute | solution.py:651
  29.2 7.1 %collective-permute-start.3 = (bf16[96,768]{1,0:T(8,128)(2,1)S(1)}, bf16[96,768]{1,0:T(8,128)(2,1)S(1)}, u32[]{:S(2)}, u32[]{:S(2)}) collective-permute-start(bf16[96,768]{1,0:T(8,128)(2,1)S(1)} %constant_dynamic-slice_fusion), channel_id=1, source_target_pairs={{0,1},{1,2},{2,3},{3,0},{4,5},{5,6},{6,7},{7,4},{8,9},{9,10},{10,1... | collective-permute-start | bytes 442376 | tf_op jit(solution)/shard_map/ppermute | solution.py:651
  32.7 9.9 %copy-start.14 = (bf16[96,768]{1,0:T(8,128)(2,1)}, bf16[96,768]{1,0:T(8,128)(2,1)S(1)}, u32[]{:S(2)}) copy-start(bf16[96,768]{1,0:T(8,128)(2,1)S(1)} %collective-permute-done.5.refs_4_.refs_3_) | copy-start | bytes 442372
  34.8 7.7 %copy-start.15 = (bf16[96,768]{1,0:T(8,128)(2,1)}, bf16[96,768]{1,0:T(8,128)(2,1)S(1)}, u32[]{:S(2)}) copy-start(bf16[96,768]{1,0:T(8,128)(2,1)S(1)} %collective-permute-done.4.refs_3_.refs_2_) | copy-start | bytes 442372
  36.3 6.2 %copy-start.16 = (bf16[96,768]{1,0:T(8,128)(2,1)}, bf16[96,768]{1,0:T(8,128)(2,1)S(1)}, u32[]{:S(2)}) copy-start(bf16[96,768]{1,0:T(8,128)(2,1)S(1)} %collective-permute-done.3.refs_2_.refs_1_) | copy-start | bytes 442372
  52.5 18.0 %all-to-all-start.1 = ((bf16[64,16,128]{2,1,0:T(8,128)(2,1)}), bf16[64,16,128]{2,1,0:T(8,128)(2,1)S(1)}, u32[]{:S(2)}, u32[]{:S(2)}) async-start(bf16[64,16,128]{2,1,0:T(8,128)(2,1)} %get-tuple-element.83), calls=%async_computation.1 | async-start | bytes 524288 | tf_op jit(solution)/shard_map/all_to_all | solution.py:671
  57.7 9.9 %collective-permute-start.8 = (bf16[96,768]{1,0:T(8,128)(2,1)}, bf16[96,768]{1,0:T(8,128)(2,1)S(1)}, u32[]{:S(2)}, u32[]{:S(2)}) collective-permute-start(bf16[96,768]{1,0:T(8,128)(2,1)} %copy-done.14), channel_id=1, source_target_pairs={{0,64},{64,0},{1,65},{65,1},{2,66},{66,2},{3,67},{67,3},{4,68},{68... | collective-permute-start | bytes 442376 | tf_op jit(solution)/shard_map/ppermute | solution.py:663
  57.8 9.8 %collective-permute-start.7 = (bf16[96,768]{1,0:T(8,128)(2,1)}, bf16[96,768]{1,0:T(8,128)(2,1)S(1)}, u32[]{:S(2)}, u32[]{:S(2)}) collective-permute-start(bf16[96,768]{1,0:T(8,128)(2,1)} %copy-done.15), channel_id=1, source_target_pairs={{0,64},{64,0},{1,65},{65,1},{2,66},{66,2},{3,67},{67,3},{4,68},{68... | collective-permute-start | bytes 442376 | tf_op jit(solution)/shard_map/ppermute | solution.py:663
  58.2 9.4 %collective-permute-start.6 = (bf16[96,768]{1,0:T(8,128)(2,1)}, bf16[96,768]{1,0:T(8,128)(2,1)S(1)}, u32[]{:S(2)}, u32[]{:S(2)}) collective-permute-start(bf16[96,768]{1,0:T(8,128)(2,1)} %copy-done.16), channel_id=1, source_target_pairs={{0,64},{64,0},{1,65},{65,1},{2,66},{66,2},{3,67},{67,3},{4,68},{68... | collective-permute-start | bytes 442376 | tf_op jit(solution)/shard_map/ppermute | solution.py:663
  58.3 4.1 %collective-permute-start.11 = (f32[768]{0:T(1024)S(1)}, f32[768]{0:T(1024)S(1)}, u32[]{:S(2)}, u32[]{:S(2)}) collective-permute-start(f32[768]{0:T(1024)S(1)} %copy-done.5), channel_id=1, source_target_pairs={{0,3},{1,0},{2,1},{3,2},{4,7},{5,4},{6,5},{7,6},{8,11},{9,8},{10,9... | collective-permute-start | bytes 9224 | tf_op jit(solution)/shard_map/ppermute | solution.py:651
  61.1 5.1 %collective-permute-start.10 = (f32[768]{0:T(1024)S(1)}, f32[768]{0:T(1024)S(1)}, u32[]{:S(2)}, u32[]{:S(2)}) collective-permute-start(f32[768]{0:T(1024)S(1)} %copy-done.5), channel_id=1, source_target_pairs={{0,2},{1,3},{2,0},{3,1},{4,6},{5,7},{6,4},{7,5},{8,10},{9,11},{10,... | collective-permute-start | bytes 9224 | tf_op jit(solution)/shard_map/ppermute | solution.py:651
  62.5 5.1 %collective-permute-start.9 = (f32[768]{0:T(1024)S(1)}, f32[768]{0:T(1024)S(1)}, u32[]{:S(2)}, u32[]{:S(2)}) collective-permute-start(f32[768]{0:T(1024)S(1)} %copy-done.5), channel_id=1, source_target_pairs={{0,1},{1,2},{2,3},{3,0},{4,5},{5,6},{6,7},{7,4},{8,9},{9,10},{10,1... | collective-permute-start | bytes 9224 | tf_op jit(solution)/shard_map/ppermute | solution.py:651
  67.6 2.9 %copy-start.17 = (bf16[96,768]{1,0:T(8,128)(2,1)}, bf16[96,768]{1,0:T(8,128)(2,1)S(1)}, u32[]{:S(2)}) copy-start(bf16[96,768]{1,0:T(8,128)(2,1)S(1)} %collective-permute-done.8.refs_6_) | copy-start | bytes 442372
  67.6 2.9 %copy-start.18 = (bf16[96,768]{1,0:T(8,128)(2,1)}, bf16[96,768]{1,0:T(8,128)(2,1)S(1)}, u32[]{:S(2)}) copy-start(bf16[96,768]{1,0:T(8,128)(2,1)S(1)} %collective-permute-done.7.refs_5_) | copy-start | bytes 442372
  67.6 2.9 %copy-start.19 = (bf16[96,768]{1,0:T(8,128)(2,1)}, bf16[96,768]{1,0:T(8,128)(2,1)S(1)}, u32[]{:S(2)}) copy-start(bf16[96,768]{1,0:T(8,128)(2,1)S(1)} %collective-permute-done.6.refs_4_) | copy-start | bytes 442372
  73.6 6.4 %copy-start.8 = (f32[8,128]{1,0:T(8,128)}, f32[8,128]{1,0:T(8,128)S(1)}, u32[]{:S(2)}) copy-start(f32[8,128]{1,0:T(8,128)S(1)} %get-tuple-element.84.refs_1_) | copy-start | bytes 12292
  73.6 16.8 %collective-permute-start.12 = (bf16[128,768]{1,0:T(8,128)(2,1)}, bf16[128,768]{1,0:T(8,128)(2,1)S(1)}, u32[]{:S(2)}, u32[]{:S(2)}) collective-permute-start(bf16[128,768]{1,0:T(8,128)(2,1)} %get-tuple-element.89), channel_id=1, source_target_pairs={{0,3},{1,0},{2,1},{3,2},{4,7},{5,4},{6,5},{7,6},{8,11},{9,8},{10,9... | collective-permute-start | bytes 589832 | tf_op jit(solution)/shard_map/ppermute | solution.py:651
  73.9 16.5 %collective-permute-start.13 = (bf16[128,768]{1,0:T(8,128)(2,1)}, bf16[128,768]{1,0:T(8,128)(2,1)S(1)}, u32[]{:S(2)}, u32[]{:S(2)}) collective-permute-start(bf16[128,768]{1,0:T(8,128)(2,1)} %get-tuple-element.90), channel_id=1, source_target_pairs={{0,2},{1,3},{2,0},{3,1},{4,6},{5,7},{6,4},{7,5},{8,10},{9,11},{10,... | collective-permute-start | bytes 589832 | tf_op jit(solution)/shard_map/ppermute | solution.py:651
  76.2 14.2 %collective-permute-start.14 = (bf16[128,768]{1,0:T(8,128)(2,1)}, bf16[128,768]{1,0:T(8,128)(2,1)S(1)}, u32[]{:S(2)}, u32[]{:S(2)}) collective-permute-start(bf16[128,768]{1,0:T(8,128)(2,1)} %get-tuple-element.91), channel_id=1, source_target_pairs={{0,1},{1,2},{2,3},{3,0},{4,5},{5,6},{6,7},{7,4},{8,9},{9,10},{10,1... | collective-permute-start | bytes 589832 | tf_op jit(solution)/shard_map/ppermute | solution.py:651
  80.1 24.3 %copy-start.6 = (f32[768]{0:T(1024)S(1)}, f32[768]{0:T(1024)}, u32[]{:S(2)}) copy-start(f32[768]{0:T(1024)} %refs_5_.5) | copy-start | bytes 9220
  90.5 0.8 copy-start.12
  91.3 19.3 %all-to-all-start.2 = ((bf16[64,16,128]{2,1,0:T(8,128)(2,1)}), bf16[64,16,128]{2,1,0:T(8,128)(2,1)S(1)}, u32[]{:S(2)}, u32[]{:S(2)}) async-start(bf16[64,16,128]{2,1,0:T(8,128)(2,1)} %later.8), calls=%async_computation.2 | async-start | bytes 524288 | tf_op jit(solution)/shard_map/all_to_all | solution.py:671
  99.8 8.3 %collective-permute-start.17 = (bf16[16,768]{1,0:T(8,128)(2,1)}, bf16[16,768]{1,0:T(8,128)(2,1)S(1)}, u32[]{:S(2)}, u32[]{:S(2)}) collective-permute-start(bf16[16,768]{1,0:T(8,128)(2,1)} %get-tuple-element.100.refs_9_), channel_id=1, source_target_pairs={{0,3},{1,0},{2,1},{3,2},{4,7},{5,4},{6,5},{7,6},{8,11},{9,8},{10,9... | collective-permute-start | bytes 73736 | tf_op jit(solution)/shard_map/ppermute | solution.py:651
  102.6 6.0 %collective-permute-start.16 = (bf16[16,768]{1,0:T(8,128)(2,1)}, bf16[16,768]{1,0:T(8,128)(2,1)S(1)}, u32[]{:S(2)}, u32[]{:S(2)}) collective-permute-start(bf16[16,768]{1,0:T(8,128)(2,1)} %get-tuple-element.100.refs_9_), channel_id=1, source_target_pairs={{0,2},{1,3},{2,0},{3,1},{4,6},{5,7},{6,4},{7,5},{8,10},{9,11},{10,... | collective-permute-start | bytes 73736 | tf_op jit(solution)/shard_map/ppermute | solution.py:651
  103.5 5.6 %collective-permute-start.15 = (bf16[16,768]{1,0:T(8,128)(2,1)}, bf16[16,768]{1,0:T(8,128)(2,1)S(1)}, u32[]{:S(2)}, u32[]{:S(2)}) collective-permute-start(bf16[16,768]{1,0:T(8,128)(2,1)} %get-tuple-element.100.refs_9_), channel_id=1, source_target_pairs={{0,1},{1,2},{2,3},{3,0},{4,5},{5,6},{6,7},{7,4},{8,9},{9,10},{10,1... | collective-permute-start | bytes 73736 | tf_op jit(solution)/shard_map/ppermute | solution.py:651
  108.1 2.5 %copy-start.20 = (bf16[16,768]{1,0:T(8,128)(2,1)}, bf16[16,768]{1,0:T(8,128)(2,1)S(1)}, u32[]{:S(2)}) copy-start(bf16[16,768]{1,0:T(8,128)(2,1)S(1)} %collective-permute-done.17.refs_12_.refs_5_) | copy-start | bytes 73732
  108.6 2.0 %copy-start.21 = (bf16[16,768]{1,0:T(8,128)(2,1)}, bf16[16,768]{1,0:T(8,128)(2,1)S(1)}, u32[]{:S(2)}) copy-start(bf16[16,768]{1,0:T(8,128)(2,1)S(1)} %collective-permute-done.16.refs_11_.refs_4_) | copy-start | bytes 73732
  109.0 1.6 copy-start.22
  111.3 21.8 %collective-permute-start.20 = (bf16[192,768]{1,0:T(8,128)(2,1)}, bf16[192,768]{1,0:T(8,128)(2,1)S(1)}, u32[]{:S(2)}, u32[]{:S(2)}) collective-permute-start(bf16[192,768]{1,0:T(8,128)(2,1)} %later.9.refs_4_), channel_id=1, source_target_pairs={{0,3},{1,0},{2,1},{3,2},{4,7},{5,4},{6,5},{7,6},{8,11},{9,8},{10,9... | collective-permute-start | bytes 884744 | tf_op jit(solution)/shard_map/ppermute | solution.py:651
  112.4 20.8 %collective-permute-start.19 = (bf16[192,768]{1,0:T(8,128)(2,1)}, bf16[192,768]{1,0:T(8,128)(2,1)S(1)}, u32[]{:S(2)}, u32[]{:S(2)}) collective-permute-start(bf16[192,768]{1,0:T(8,128)(2,1)} %later.9.refs_4_), channel_id=1, source_target_pairs={{0,2},{1,3},{2,0},{3,1},{4,6},{5,7},{6,4},{7,5},{8,10},{9,11},{10,... | collective-permute-start | bytes 884744 | tf_op jit(solution)/shard_map/ppermute | solution.py:651
  113.9 19.2 %collective-permute-start.18 = (bf16[192,768]{1,0:T(8,128)(2,1)}, bf16[192,768]{1,0:T(8,128)(2,1)S(1)}, u32[]{:S(2)}, u32[]{:S(2)}) collective-permute-start(bf16[192,768]{1,0:T(8,128)(2,1)} %later.9.refs_4_), channel_id=1, source_target_pairs={{0,1},{1,2},{2,3},{3,0},{4,5},{5,6},{6,7},{7,4},{8,9},{9,10},{10,1... | collective-permute-start | bytes 884744 | tf_op jit(solution)/shard_map/ppermute | solution.py:651
  129.0 19.6 %all-to-all-start.3 = ((bf16[16,256,128]{2,1,0:T(8,128)(2,1)}), bf16[16,256,128]{2,1,0:T(8,128)(2,1)S(1)}, u32[]{:S(2)}, u32[]{:S(2)}) async-start(bf16[16,256,128]{2,1,0:T(8,128)(2,1)} %get-tuple-element.101), calls=%async_computation.3 | async-start | bytes 2097152 | tf_op jit(solution)/shard_map/all_to_all | solution.py:667
  133.2 0.8 copy-start.25
  133.2 0.9 copy-start.26
  139.8 2.6 %collective-permute-start.21 = (bf16[96,1536]{1,0:T(8,128)(2,1)}, bf16[96,1536]{1,0:T(8,128)(2,1)S(1)}, u32[]{:S(2)}, u32[]{:S(2)}) collective-permute-start(bf16[96,1536]{1,0:T(8,128)(2,1)} %get-tuple-element.109), channel_id=1, source_target_pairs={{0,64},{64,0},{1,65},{65,1},{2,66},{66,2},{3,67},{67,3},{4,68},{68... | collective-permute-start | bytes 884744 | tf_op jit(solution)/shard_map/ppermute | solution.py:663
  139.9 2.5 %collective-permute-start.22 = (bf16[96,1536]{1,0:T(8,128)(2,1)}, bf16[96,1536]{1,0:T(8,128)(2,1)S(1)}, u32[]{:S(2)}, u32[]{:S(2)}) collective-permute-start(bf16[96,1536]{1,0:T(8,128)(2,1)} %get-tuple-element.110), channel_id=1, source_target_pairs={{0,64},{64,0},{1,65},{65,1},{2,66},{66,2},{3,67},{67,3},{4,68},{68... | collective-permute-start | bytes 884744 | tf_op jit(solution)/shard_map/ppermute | solution.py:663
  140.4 2.1 %collective-permute-start.23 = (bf16[96,1536]{1,0:T(8,128)(2,1)}, bf16[96,1536]{1,0:T(8,128)(2,1)S(1)}, u32[]{:S(2)}, u32[]{:S(2)}) collective-permute-start(bf16[96,1536]{1,0:T(8,128)(2,1)} %get-tuple-element.111), channel_id=1, source_target_pairs={{0,64},{64,0},{1,65},{65,1},{2,66},{66,2},{3,67},{67,3},{4,68},{68... | collective-permute-start | bytes 884744 | tf_op jit(solution)/shard_map/ppermute | solution.py:663
  140.5 2.5 %collective-permute-start.24 = (bf16[96,1536]{1,0:T(8,128)(2,1)}, bf16[96,1536]{1,0:T(8,128)(2,1)S(1)}, u32[]{:S(2)}, u32[]{:S(2)}) collective-permute-start(bf16[96,1536]{1,0:T(8,128)(2,1)} %get-tuple-element.112), channel_id=1, source_target_pairs={{0,64},{64,0},{1,65},{65,1},{2,66},{66,2},{3,67},{67,3},{4,68},{68... | collective-permute-start | bytes 884744 | tf_op jit(solution)/shard_map/ppermute | solution.py:663
  140.9 1.5 collective-permute-start.25
  151.5 2.8 %collective-permute-start.26 = (bf16[400,768]{1,0:T(8,128)(2,1)}, bf16[400,768]{1,0:T(8,128)(2,1)S(1)}, u32[]{:S(2)}, u32[]{:S(2)}) collective-permute-start(bf16[400,768]{1,0:T(8,128)(2,1)} %get-tuple-element.117), channel_id=1, source_target_pairs={{0,64},{64,0},{1,65},{65,1},{2,66},{66,2},{3,67},{67,3},{4,68},{68... | collective-permute-start | bytes 1843208 | tf_op jit(solution)/shard_map/ppermute | solution.py:663
  157.7 32.7 %all-to-all-start.4 = ((bf16[16,448,128]{2,1,0:T(8,128)(2,1)}), bf16[16,448,128]{2,1,0:T(8,128)(2,1)S(1)}, u32[]{:S(2)}, u32[]{:S(2)}) async-start(bf16[16,448,128]{2,1,0:T(8,128)(2,1)} %get-tuple-element.127), calls=%async_computation.4 | async-start | bytes 3670016 | tf_op jit(solution)/shard_map/all_to_all | solution.py:667
  162.1 8.9 %collective-permute-start.30 = (bf16[96,768]{1,0:T(8,128)(2,1)}, bf16[96,768]{1,0:T(8,128)(2,1)S(1)}, u32[]{:S(2)}, u32[]{:S(2)}) collective-permute-start(bf16[96,768]{1,0:T(8,128)(2,1)} %later.11), channel_id=1, source_target_pairs={{0,1},{1,2},{2,3},{3,0},{4,5},{5,6},{6,7},{7,4},{8,9},{9,10},{10,1... | collective-permute-start | bytes 442376 | tf_op jit(solution)/shard_map/ppermute | solution.py:651
  164.2 10.8 %collective-permute-start.31 = (bf16[96,768]{1,0:T(8,128)(2,1)}, bf16[96,768]{1,0:T(8,128)(2,1)S(1)}, u32[]{:S(2)}, u32[]{:S(2)}) collective-permute-start(bf16[96,768]{1,0:T(8,128)(2,1)} %later.12), channel_id=1, source_target_pairs={{0,2},{1,3},{2,0},{3,1},{4,6},{5,7},{6,4},{7,5},{8,10},{9,11},{10,... | collective-permute-start | bytes 442376 | tf_op jit(solution)/shard_map/ppermute | solution.py:651
  166.8 8.1 %collective-permute-start.32 = (bf16[96,768]{1,0:T(8,128)(2,1)}, bf16[96,768]{1,0:T(8,128)(2,1)S(1)}, u32[]{:S(2)}, u32[]{:S(2)}) collective-permute-start(bf16[96,768]{1,0:T(8,128)(2,1)} %later.13), channel_id=1, source_target_pairs={{0,3},{1,0},{2,1},{3,2},{4,7},{5,4},{6,5},{7,6},{8,11},{9,8},{10,9... | collective-permute-start | bytes 442376 | tf_op jit(solution)/shard_map/ppermute | solution.py:651
  168.0 11.2 %collective-permute-start.29 = (bf16[96,768]{1,0:T(8,128)(2,1)}, bf16[96,768]{1,0:T(8,128)(2,1)S(1)}, u32[]{:S(2)}, u32[]{:S(2)}) collective-permute-start(bf16[96,768]{1,0:T(8,128)(2,1)} %later.10.refs_0_), channel_id=1, source_target_pairs={{0,3},{1,0},{2,1},{3,2},{4,7},{5,4},{6,5},{7,6},{8,11},{9,8},{10,9... | collective-permute-start | bytes 442376 | tf_op jit(solution)/shard_map/ppermute | solution.py:651
  168.3 11.9 %collective-permute-start.28 = (bf16[96,768]{1,0:T(8,128)(2,1)}, bf16[96,768]{1,0:T(8,128)(2,1)S(1)}, u32[]{:S(2)}, u32[]{:S(2)}) collective-permute-start(bf16[96,768]{1,0:T(8,128)(2,1)} %later.10.refs_0_), channel_id=1, source_target_pairs={{0,2},{1,3},{2,0},{3,1},{4,6},{5,7},{6,4},{7,5},{8,10},{9,11},{10,... | collective-permute-start | bytes 442376 | tf_op jit(solution)/shard_map/ppermute | solution.py:651
  171.0 9.4 %collective-permute-start.27 = (bf16[96,768]{1,0:T(8,128)(2,1)}, bf16[96,768]{1,0:T(8,128)(2,1)S(1)}, u32[]{:S(2)}, u32[]{:S(2)}) collective-permute-start(bf16[96,768]{1,0:T(8,128)(2,1)} %later.10.refs_0_), channel_id=1, source_target_pairs={{0,1},{1,2},{2,3},{3,0},{4,5},{5,6},{6,7},{7,4},{8,9},{9,10},{10,1... | collective-permute-start | bytes 442376 | tf_op jit(solution)/shard_map/ppermute | solution.py:651
  176.1 7.7 %collective-permute-start.35 = (bf16[96,768]{1,0:T(8,128)(2,1)S(1)}, bf16[96,768]{1,0:T(8,128)(2,1)S(1)}, u32[]{:S(2)}, u32[]{:S(2)}) collective-permute-start(bf16[96,768]{1,0:T(8,128)(2,1)S(1)} %input_chunk.1.refs_0_), channel_id=1, source_target_pairs={{0,3},{1,0},{2,1},{3,2},{4,7},{5,4},{6,5},{7,6},{8,11},{9,8},{10,9... | collective-permute-start | bytes 442376 | tf_op jit(solution)/shard_map/ppermute | solution.py:651
  177.9 7.8 %collective-permute-start.34 = (bf16[96,768]{1,0:T(8,128)(2,1)S(1)}, bf16[96,768]{1,0:T(8,128)(2,1)S(1)}, u32[]{:S(2)}, u32[]{:S(2)}) collective-permute-start(bf16[96,768]{1,0:T(8,128)(2,1)S(1)} %input_chunk.1.refs_0_), channel_id=1, source_target_pairs={{0,2},{1,3},{2,0},{3,1},{4,6},{5,7},{6,4},{7,5},{8,10},{9,11},{10,... | collective-permute-start | bytes 442376 | tf_op jit(solution)/shard_map/ppermute | solution.py:651
  179.1 8.0 %collective-permute-start.33 = (bf16[96,768]{1,0:T(8,128)(2,1)S(1)}, bf16[96,768]{1,0:T(8,128)(2,1)S(1)}, u32[]{:S(2)}, u32[]{:S(2)}) collective-permute-start(bf16[96,768]{1,0:T(8,128)(2,1)S(1)} %input_chunk.1.refs_0_), channel_id=1, source_target_pairs={{0,1},{1,2},{2,3},{3,0},{4,5},{5,6},{6,7},{7,4},{8,9},{9,10},{10,1... | collective-permute-start | bytes 442376 | tf_op jit(solution)/shard_map/ppermute | solution.py:651
  180.3 0.9 copy-start.1
  (5 other events, 3.4 us)
Sparse Core Ops, SparseCore 0:
  19.8 60.2 all-gather.2

commit v6 on v5

--- a/solution.py
+++ b/solution.py
@@ -335,10 +335,9 @@
         block = jnp.where(ext < 4, block, 0.0).astype(bf16)
         for w in range(NW):
             out[w, 3 * HD : SLOT, :] = block
+        stores += copies([(out.at[:, 3 * HD : SLOT, :], out_far.at[:, 3 * HD : SLOT, :])], sems.at[NW + 1 :])
         for store in stores:
             store.wait()
-        stores = copies([(out.at[:, 3 * HD : SLOT, :], out_far.at[:, 3 * HD : SLOT, :])], sems)
-        stores[0].wait()
 
     store.wait()
 
@@ -839,7 +838,7 @@
             pltpu.VMEM((L, AUG), bf16),
             pltpu.VMEM((L, AUG), bf16),
             pltpu.VMEM((HD, L), f32),
-            pltpu.SemaphoreType.DMA((NW + 1,)),
+            pltpu.SemaphoreType.DMA((NW + 2,)),
         ],
         far_in=range(13),
         far=(0,),
@@ -917,7 +916,7 @@
         far=range(4),
         token=True,
     )
-    slots, b_query, b_key, b_value, g_two, s_two, b_down, g_one, s_one, b_out, token = call(
+    slots, b_query, b_key, b_value, g_two, s_two, b_down, g_one, s_one, b_out = call(
         "last_add",
         last_add_kernel,
         [(last_shape, bf16)] + [((E,), f32)] * 3 + [((D,), f32)] * 6,
@@ -933,14 +932,13 @@
         far=(0,),
         aliases={1: 0},
         after=(done,),
-        token=True,
-    )
-    parts = scatter_narrow([parts[0], *(later(part, anywhere=(token,)) for part in parts[1:])])
+    )
+    parts = scatter_narrow([parts[0], *(later(part, slots) for part in parts[1:])])
     (input_low,) = call("input_chunk", input_chunk_kernel, [chunk_low], (parts[0], grad_one, *parts[1:]),
         scratch=[pltpu.VMEM((CH, D), f32), pltpu.VMEM((CH, D), f32), pltpu.SemaphoreType.DMA((2,))],
         far_in=(0, 1),
     )
-    layers = gather_narrow(later(layer, anywhere=(token,)))
+    layers = gather_narrow(later(layer, slots))
     whole_out = ((R, T, D), f32)
     (layer_out,) = call("layer_out", spread_kernel, [whole_out], layers)
     (grad_input,) = call("grad_input", spread_kernel, [whole_out], gather_narrow(input_low))

time: 199 us -> 198 us (level)
  no operation moved by 1% of the time
where the time goes in v6:
time: 198 us; the launch traced here: 197 us
  starting transfers between devices  67.5 us (34%)
  Pallas kernels  66.4 us (34%)
  waiting for transfers between devices  44 us (22%)
  between operations  14.6 us (7%)
  local copies, waits for them, and re-layouts  3.46 us (2%)
    pallas_call x16, Pallas kernels, call(): pl.pallas_call(run, out_shape=[shape(k, s, t) for k, (s, t) in enumerate(...  66.4 us
    ppermute x27, starting transfers between devices, shifted(): return lax.ppermute(x, 'narrow', [(i, (i + s) % NN) for i in range(NN)])  36.2 us
    ppermute x27, waiting for transfers between devices, shifted(): return lax.ppermute(x, 'narrow', [(i, (i + s) % NN) for i in range(NN)])  24 us
    all_to_all x3, starting transfers between devices, exchange(): return lax.all_to_all(slots, 'wide', 0, 0, tiled=True)  15.6 us
    all_to_all x2, starting transfers between devices, exchange_all(): return lax.all_to_all(slots, ('wide', 'narrow'), 0, 0, tiled=True)  13.7 us
    all_to_all x3, waiting for transfers between devices, exchange(): return lax.all_to_all(slots, 'wide', 0, 0, tiled=True)  10.3 us
    all_to_all x2, waiting for transfers between devices, exchange_all(): return lax.all_to_all(slots, ('wide', 'narrow'), 0, 0, tiled=True)  4.43 us
  transfers between devices with their start and end apart: 42, of which 24 were waited for; matrix products, arithmetic and copies ran while one was open for 0% of the time, Pallas kernels for 30%

profile of v6, /device:TPU:0, one launch (start us, length us, event | category | flops | bytes accessed | tf_op | source)
XLA Modules:
  0.0 196.8 jit_solution(8463971731698179673)
XLA Ops:
  7.2 0.9 bitcast_select_fusion.refs_0_
  8.2 4.2 %collective-permute-start.2 = (bf16[48,768]{1,0:T(8,128)(2,1)S(1)}, bf16[48,768]{1,0:T(8,128)(2,1)S(1)}, u32[]{:S(2)}, u32[]{:S(2)}) collective-permute-start(bf16[48,768]{1,0:T(8,128)(2,1)S(1)} %bitcast_select_fusion.refs_0_), channel_id=1, source_target_pairs={{0,3},{1,0},{2,1},{3,2},{4,7},{5,4},{6,5},{7,6},{8,11},{9,8},{10,9... | collective-permute-start | bytes 221192 | tf_op jit(solution)/shard_map/ppermute | solution.py:650
  12.4 1.3 collective-permute-start
  13.6 3.1 %project.1 = (bf16[16,208,128]{2,1,0:T(8,128)(2,1)}, f32[8,128]{1,0:T(8,128)S(1)}) custom-call(bf16[3,128,768]{2,1,0:T(8,128)(2,1)} %refs_0_.5, s32[3,128]{1,0:T(4,128)} %refs_1_.2, bf16[192,768]{1,0:T(8,128)(2,1)} %bitcast.9, f32[192]{0:T(256)} %refs_3_.1, bf16[192,768]{1,0:T(8,128)(2,1)} %bitcast.11, f32[192]{0:T(256)} %refs_5_.3, ...), custom_call_target="tpu_custom_call" | custom-call | flops 1024 | bytes 1024 | tf_op jit(solution)/shard_map/project/pallas_call | solution.py:70
  16.8 1.6 collective-permute-done.1.refs_2_
  18.9 0.8 stack.1
  19.7 7.2 %all-to-all-start = ((bf16[16,208,128]{2,1,0:T(8,128)(2,1)}), bf16[16,208,128]{2,1,0:T(8,128)(2,1)S(1)}, u32[]{:S(2)}, u32[]{:S(2)}) async-start(bf16[16,208,128]{2,1,0:T(8,128)(2,1)} %get-tuple-element.81), calls=%async_computation | async-start | bytes 1703936 | tf_op jit(solution)/shard_map/all_to_all | solution.py:666
  26.9 0.9 collective-permute-start.5
  27.9 1.4 collective-permute-start.4
  29.2 0.6 collective-permute-start.3
  29.8 2.8 %collective-permute-done.5.refs_4_.refs_3_ = bf16[96,768]{1,0:T(8,128)(2,1)S(1)} collective-permute-done((bf16[96,768]{1,0:T(8,128)(2,1)S(1)}, bf16[96,768]{1,0:T(8,128)(2,1)S(1)}, u32[]{:S(2)}, u32[]{:S(2)}) %collective-permute-start.5) | collective-permute-done | bytes 147488 | tf_op jit(solution)/shard_map/ppermute | solution.py:650
  32.7 2.2 %collective-permute-done.4.refs_3_.refs_2_ = bf16[96,768]{1,0:T(8,128)(2,1)S(1)} collective-permute-done((bf16[96,768]{1,0:T(8,128)(2,1)S(1)}, bf16[96,768]{1,0:T(8,128)(2,1)S(1)}, u32[]{:S(2)}, u32[]{:S(2)}) %collective-permute-start.4) | collective-permute-done | bytes 147488 | tf_op jit(solution)/shard_map/ppermute | solution.py:650
  34.8 1.5 collective-permute-done.3.refs_2_.refs_1_
  36.3 6.1 %all-to-all-done.refs_0_ = bf16[16,208,128]{2,1,0:T(8,128)(2,1)S(1)} async-done(((bf16[16,208,128]{2,1,0:T(8,128)(2,1)}), bf16[16,208,128]{2,1,0:T(8,128)(2,1)S(1)}, u32[]{:S(2)}, u32[]{:S(2)}) %all-to-all-start) | async-done | bytes 852000 | tf_op jit(solution)/shard_map/all_to_all | solution.py:666
  42.5 9.9 %attend.1 = (bf16[64,16,128]{2,1,0:T(8,128)(2,1)}, bf16[80,2048]{1,0:T(8,128)(2,1)}, bf16[80,2048]{1,0:T(8,128)(2,1)}, bf16[2048,64]{1,0:T(8,128)(2,1)}, bf16[20...) custom-call(bf16[16,208,128]{2,1,0:T(8,128)(2,1)S(1)} %all-to-all-do, ...), custom_call_target="tpu_custom_call" | custom-call | flops 1024 | bytes 1024 | tf_op jit(solution)/shard_map/attend/pallas_call | solution.py:70
  52.5 5.2 %all-to-all-start.1 = ((bf16[64,16,128]{2,1,0:T(8,128)(2,1)}), bf16[64,16,128]{2,1,0:T(8,128)(2,1)S(1)}, u32[]{:S(2)}, u32[]{:S(2)}) async-start(bf16[64,16,128]{2,1,0:T(8,128)(2,1)} %get-tuple-element.82), calls=%async_computation.1 | async-start | bytes 524288 | tf_op jit(solution)/shard_map/all_to_all | solution.py:670
  58.3 2.8 %collective-permute-start.11 = (f32[768]{0:T(1024)S(1)}, f32[768]{0:T(1024)S(1)}, u32[]{:S(2)}, u32[]{:S(2)}) collective-permute-start(f32[768]{0:T(1024)S(1)} %copy-done.4), channel_id=1, source_target_pairs={{0,3},{1,0},{2,1},{3,2},{4,7},{5,4},{6,5},{7,6},{8,11},{9,8},{10,9... | collective-permute-start | bytes 9224 | tf_op jit(solution)/shard_map/ppermute | solution.py:650
  61.1 0.9 collective-permute-start.10
  62.5 1.1 collective-permute-start.9
  63.5 2.7 %collective-permute-done.10.refs_13_.refs_11_ = f32[768]{0:T(1024)S(1)} collective-permute-done((f32[768]{0:T(1024)S(1)}, f32[768]{0:T(1024)S(1)}, u32[]{:S(2)}, u32[]{:S(2)}) %collective-permute-start.10) | collective-permute-done | bytes 3104 | tf_op jit(solution)/shard_map/ppermute | solution.py:650
  66.2 1.3 collective-permute-done.9.refs_12_.refs_10_
  67.6 2.9 %all-to-all-done.1.refs_8_ = bf16[64,16,128]{2,1,0:T(8,128)(2,1)S(1)} async-done(((bf16[64,16,128]{2,1,0:T(8,128)(2,1)}), bf16[64,16,128]{2,1,0:T(8,128)(2,1)S(1)}, u32[]{:S(2)}, u32[]{:S(2)}) %all-to-all-start.1) | async-done | bytes 262176 | tf_op jit(solution)/shard_map/all_to_all | solution.py:670
  70.5 3.1 %first.1 = (bf16[768,768]{1,0:T(8,128)(2,1)}, f32[96,896]{1,0:T(8,128)}, bf16[128,768]{1,0:T(8,128)(2,1)}, bf16[128,768]{1,0:T(8,128)(2,1)}, bf16[128,768]{1,0:T...) custom-call(bf16[192,768]{1,0:T(8,128)(2,1)} %refs_0_.4, bf16[96,768]{1,0:T(8,128)(2,1)} %copy-done.15, ...), custom_call_target="tpu_custom_call" | custom-call | flops 1024 | bytes 1024 | tf_op jit(solution)/shard_map/first/pallas_call | solution.py:70
  73.9 2.3 %collective-permute-start.13 = (bf16[128,768]{1,0:T(8,128)(2,1)}, bf16[128,768]{1,0:T(8,128)(2,1)S(1)}, u32[]{:S(2)}, u32[]{:S(2)}) collective-permute-start(bf16[128,768]{1,0:T(8,128)(2,1)} %get-tuple-element.89), channel_id=1, source_target_pairs={{0,2},{1,3},{2,0},{3,1},{4,6},{5,7},{6,4},{7,5},{8,10},{9,11},{10,... | collective-permute-start | bytes 589832 | tf_op jit(solution)/shard_map/ppermute | solution.py:650
  76.7 3.3 %all-gather.3.cloned.1.call-done = bf16[128,48,768]{2,1,0:T(8,128)(2,1)} async-done(((bf16[4,48,768]{2,1,0:T(8,128)(2,1)}), bf16[128,48,768]{2,1,0:T(8,128)(2,1)}) %all-gather.3.cloned.1.call-update) | async-done | bytes 9437200 | tf_op jit(solution)/shard_map/all_gather | solution.py:715
  80.1 10.4 %middle.1 = (bf16[64,16,128]{2,1,0:T(8,128)(2,1)}, f32[96,768]{1,0:T(8,128)}, bf16[192,768]{1,0:T(8,128)(2,1)}, bf16[96,768]{1,0:T(8,128)(2,1)}, bf16[16,768]{1,0:T(8,128)(2,1)}) custom-call(bf16[2,16,4,48,768]{4,3,2,1,0:T(8,128)(2,1)} %later.7.refs_0_.refs_4_.refs_8_, f32[96,896]{1,0:T(8,128)} %get-tuple-element.84.refs_1_, bf16[3,128,768]{2,1,0:T(8,128)(2,1)} %refs_2_.1, ...), custom_call_target="tpu_custom_call" | custom-call | flops 1024 | bytes 1024 | tf_op jit(solution)/shard_map/middle/pallas_call | solution.py:70
  90.5 0.6 copy-done.9
  91.3 8.5 %all-to-all-start.2 = ((bf16[64,16,128]{2,1,0:T(8,128)(2,1)}), bf16[64,16,128]{2,1,0:T(8,128)(2,1)S(1)}, u32[]{:S(2)}, u32[]{:S(2)}) async-start(bf16[64,16,128]{2,1,0:T(8,128)(2,1)} %later.8), calls=%async_computation.2 | async-start | bytes 524288 | tf_op jit(solution)/shard_map/all_to_all | solution.py:670
  99.8 2.9 %collective-permute-start.17 = (bf16[16,768]{1,0:T(8,128)(2,1)}, bf16[16,768]{1,0:T(8,128)(2,1)S(1)}, u32[]{:S(2)}, u32[]{:S(2)}) collective-permute-start(bf16[16,768]{1,0:T(8,128)(2,1)} %get-tuple-element.99.refs_9_), channel_id=1, source_target_pairs={{0,3},{1,0},{2,1},{3,2},{4,7},{5,4},{6,5},{7,6},{8,11},{9,8},{10,9... | collective-permute-start | bytes 73736 | tf_op jit(solution)/shard_map/ppermute | solution.py:650
  102.6 0.9 collective-permute-start.16
  103.5 0.9 collective-permute-start.15
  104.3 3.8 %hidden.1 = (bf16[384,768]{1,0:T(8,128)(2,1)}, f32[384,768]{1,0:T(8,128)}) custom-call(bf16[128,768]{1,0:T(8,128)(2,1)} %get-tuple-element.101.refs_0_, bf16[128,768]{1,0:T(8,128)(2,1)} %copy-done.11, bf16[128,768]{1,0:T(8,128)(2,1)} %copy-done.10, bf16[128,768]{1,0:T(8,128)(2,1)} %copy-done.9, bf16[2,16,4,48,768]{4,3,2,1,0:T(8,128)(2,1)} %later.7.refs_0_.refs_4_.refs_8_, ...), custom_call_target="tpu_custom_call" | custom-call | flops 1024 | bytes 1024 | tf_op jit(solution)/shard_map/hidden/pallas_call | solution.py:70
  109.0 1.6 all-to-all-done.2.refs_0_.refs_2_
  110.6 0.7 copy-done.8
  111.3 1.0 collective-permute-start.20
  112.4 1.6 collective-permute-start.19
  114.0 14.4 %attend_back.1 = (bf16[16,256,128]{2,1,0:T(8,128)(2,1)}, f32[8,128]{1,0:T(8,128)S(1)}) custom-call(bf16[64,16,128]{2,1,0:T(8,128)(2,1)} %copy-done.8, bf16[80,2048]{1,0:T(8,128)(2,1)} %get-tuple-element.91.refs_1_, bf16[80,2048]{1,0:T(8,128)(2,1)} %get-tuple-element.92.refs_2_, bf16[2048,64]{1,0:T(8,128)(2,1)} %get-tuple-element.93.refs_3_, ...), custom_call_target="tpu_custom_call" | custom-call | flops 1024 | bytes 1024 | tf_op jit(solution)/shard_map/attend_back/pallas_call | solution.py:70
  128.4 4.1 %all-to-all-start.3 = ((bf16[16,256,128]{2,1,0:T(8,128)(2,1)}), bf16[16,256,128]{2,1,0:T(8,128)(2,1)S(1)}, u32[]{:S(2)}, u32[]{:S(2)}) async-start(bf16[16,256,128]{2,1,0:T(8,128)(2,1)} %get-tuple-element.100), calls=%async_computation.3 | async-start | bytes 2097152 | tf_op jit(solution)/shard_map/all_to_all | solution.py:666
  132.6 0.7 copy-done.24
  133.5 5.7 %weights.1 = (bf16[96,1536]{1,0:T(8,128)(2,1)}, bf16[96,1536]{1,0:T(8,128)(2,1)}, bf16[96,1536]{1,0:T(8,128)(2,1)}, bf16[96,1536]{1,0:T(8,128)(2,1)}, bf16[384,1...) custom-call(bf16[128,768]{1,0:T(8,128)(2,1)} %get-tuple-element.101.refs_0_, ...), custom_call_target="tpu_custom_call" | custom-call | flops 99999997952 | bytes 1024 | tf_op jit(solution)/shard_map/weights/pallas_call | solution.py:70
  140.3 1.4 collective-permute-done.25.refs_6_
  142.3 2.7 %first_add.1 = (bf16[16,448,128]{2,1,0:T(8,128)(2,1)}, f32[8,128]{1,0:T(8,128)S(1)}) custom-call(bf16[384,1536]{1,0:T(8,128)(2,1)} %get-tuple-element.107.refs_0_, bf16[96,1536]{1,0:T(8,128)(2,1)S(1)} %collective-permute-done.21.refs_1_, bf16[96,1536]{1,0:T(8,128)(2,1)S(1)} %collective-permute-done.22.refs_2_, ...), custom_call_target="tpu_custom_call" | custom-call | flops 1024 | bytes 1024 | tf_op jit(solution)/shard_map/first_add/pallas_call | solution.py:70
  145.1 3.0 %all-to-all-done.3.refs_1_ = bf16[16,256,128]{2,1,0:T(8,128)(2,1)S(1)} async-done(((bf16[16,256,128]{2,1,0:T(8,128)(2,1)}), bf16[16,256,128]{2,1,0:T(8,128)(2,1)S(1)}, u32[]{:S(2)}, u32[]{:S(2)}) %all-to-all-start.3) | async-done | bytes 1048608 | tf_op jit(solution)/shard_map/all_to_all | solution.py:666
  148.0 2.9 %input_weights.1 = (bf16[384,576]{1,0:T(8,128)(2,1)S(1)}, bf16[400,768]{1,0:T(8,128)(2,1)}, bf16[384,768]{1,0:T(8,128)(2,1)}, f32[8,768]{1,0:T(8,128)S(1)}) custom-call(bf16[3,128,768]{2,1,0:T(8,128)(2,1)} %refs_0_.5, bf16[16,256,128]{2,1,0:T(8,128)(2,1)S(1)} %all-to-all-done.3.refs_1_, bf16[768,192]{1,0:T(8,128)(2,1)S(1)} %get-tuple-element.106.refs_2_, ...), custom_call_target="tpu_custom_call" | custom-call | flops 1024 | bytes 1024 | tf_op jit(solution)/shard_map/input_weights/pallas_call | solution.py:70
  151.0 2.7 %input_back.1 = (f32[96,768]{1,0:T(8,128)}, bf16[96,768]{1,0:T(8,128)(2,1)}, bf16[96,768]{1,0:T(8,128)(2,1)}, bf16[96,768]{1,0:T(8,128)(2,1)}, f32[8,128]{1,0:T(8,128)S(1)}) custom-call(bf16[192,768]{1,0:T(8,128)(2,1)} %bitcast.10, bf16[192,768]{1,0:T(8,128)(2,1)} %bitcast.12, bf16[192,768]{1,0:T(8,128)(2,1)} %bitcast.14, ...), custom_call_target="tpu_custom_call" | custom-call | flops 1024 | bytes 1024 | tf_op jit(solution)/shard_map/input_back/pallas_call | solution.py:70
  153.8 2.7 %last_add.1 = (bf16[16,448,128]{2,1,0:T(8,128)(2,1)}, f32[192]{0:T(256)}, f32[192]{0:T(256)}, f32[192]{0:T(256)}, f32[768]{0:T(1024)}, /*index=5*/f32[768]{0:T(1...) custom-call(bf16[384,768]{1,0:T(8,128)(2,1)} %get-tuple-element.114.refs_0_, ...), custom_call_target="tpu_custom_call", output_to_operand_aliasing={{0}: (1, {})} | custom-call | flops 1024 | bytes 1024 | tf_op jit(solution)/shard_map/last_add/pallas_call | solution.py:70
  156.4 4.4 %all-to-all-start.4 = ((bf16[16,448,128]{2,1,0:T(8,128)(2,1)}), bf16[16,448,128]{2,1,0:T(8,128)(2,1)S(1)}, u32[]{:S(2)}, u32[]{:S(2)}) async-start(bf16[16,448,128]{2,1,0:T(8,128)(2,1)} %get-tuple-element.120.refs_1_), calls=%async_computation.4 | async-start | bytes 3670016 | tf_op jit(solution)/shard_map/all_to_all | solution.py:666
  160.9 2.1 %collective-permute-start.30 = (bf16[96,768]{1,0:T(8,128)(2,1)}, bf16[96,768]{1,0:T(8,128)(2,1)S(1)}, u32[]{:S(2)}, u32[]{:S(2)}) collective-permute-start(bf16[96,768]{1,0:T(8,128)(2,1)} %later.11), channel_id=1, source_target_pairs={{0,1},{1,2},{2,3},{3,0},{4,5},{5,6},{6,7},{7,4},{8,9},{9,10},{10,1... | collective-permute-start | bytes 442376 | tf_op jit(solution)/shard_map/ppermute | solution.py:650
  162.9 2.7 %collective-permute-start.31 = (bf16[96,768]{1,0:T(8,128)(2,1)S(1)}, bf16[96,768]{1,0:T(8,128)(2,1)S(1)}, u32[]{:S(2)}, u32[]{:S(2)}) collective-permute-start(bf16[96,768]{1,0:T(8,128)(2,1)S(1)} %copy-done.19), channel_id=1, source_target_pairs={{0,2},{1,3},{2,0},{3,1},{4,6},{5,7},{6,4},{7,5},{8,10},{9,11},{10,... | collective-permute-start | bytes 442376 | tf_op jit(solution)/shard_map/ppermute | solution.py:650
  165.6 1.1 collective-permute-start.32
  167.0 2.7 %collective-permute-start.28 = (bf16[96,768]{1,0:T(8,128)(2,1)}, bf16[96,768]{1,0:T(8,128)(2,1)S(1)}, u32[]{:S(2)}, u32[]{:S(2)}) collective-permute-start(bf16[96,768]{1,0:T(8,128)(2,1)} %later.10.refs_0_), channel_id=1, source_target_pairs={{0,2},{1,3},{2,0},{3,1},{4,6},{5,7},{6,4},{7,5},{8,10},{9,11},{10,... | collective-permute-start | bytes 442376 | tf_op jit(solution)/shard_map/ppermute | solution.py:650
  169.9 3.9 %collective-permute-done.31.refs_3_ = bf16[96,768]{1,0:T(8,128)(2,1)S(1)} collective-permute-done((bf16[96,768]{1,0:T(8,128)(2,1)S(1)}, bf16[96,768]{1,0:T(8,128)(2,1)S(1)}, u32[]{:S(2)}, u32[]{:S(2)}) %collective-permute-start.31) | collective-permute-done | bytes 147488 | tf_op jit(solution)/shard_map/ppermute | solution.py:650
  173.8 1.1 input_chunk.1.refs_0_
  174.9 1.9 collective-permute-start.35
  176.9 0.8 collective-permute-start.34
  177.7 1.1 collective-permute-start.33
  179.1 0.9 copy-done.1
  180.0 1.1 layer_out.1
  181.1 2.0 %collective-permute-done.35.refs_3_ = bf16[96,768]{1,0:T(8,128)(2,1)S(1)} collective-permute-done((bf16[96,768]{1,0:T(8,128)(2,1)S(1)}, bf16[96,768]{1,0:T(8,128)(2,1)S(1)}, u32[]{:S(2)}, u32[]{:S(2)}) %collective-permute-start.35) | collective-permute-done | bytes 147488 | tf_op jit(solution)/shard_map/ppermute | solution.py:650
  183.2 2.0 collective-permute-done.34.refs_2_
  185.1 1.7 collective-permute-done.33.refs_1_
  186.8 1.1 grad_input.1
  187.9 1.2 all-to-all-done.4.refs_0_
  189.1 0.9 last_sum.1
  (101 shorter events, 6.6 us)
Async XLA Ops:
  7.2 72.9 %all-gather.3.cloned.1.call-start = ((), (), s32[]{:S(2)}) async-start(), calls=%async_computation.5 | async-start | bytes 9732096 | tf_op jit(solution)/shard_map/all_gather | solution.py:715
  8.2 8.6 %collective-permute-start.2 = (bf16[48,768]{1,0:T(8,128)(2,1)S(1)}, bf16[48,768]{1,0:T(8,128)(2,1)S(1)}, u32[]{:S(2)}, u32[]{:S(2)}) collective-permute-start(bf16[48,768]{1,0:T(8,128)(2,1)S(1)} %bitcast_select_fusion.refs_0_), channel_id=1, source_target_pairs={{0,3},{1,0},{2,1},{3,2},{4,7},{5,4},{6,5},{7,6},{8,11},{9,8},{10,9... | collective-permute-start | bytes 221192 | tf_op jit(solution)/shard_map/ppermute | solution.py:650
  12.4 6.0 %collective-permute-start.1 = (bf16[48,768]{1,0:T(8,128)(2,1)S(1)}, bf16[48,768]{1,0:T(8,128)(2,1)S(1)}, u32[]{:S(2)}, u32[]{:S(2)}) collective-permute-start(bf16[48,768]{1,0:T(8,128)(2,1)S(1)} %bitcast_select_fusion.refs_0_), channel_id=1, source_target_pairs={{0,2},{1,3},{2,0},{3,1},{4,6},{5,7},{6,4},{7,5},{8,10},{9,11},{10,... | collective-permute-start | bytes 221192 | tf_op jit(solution)/shard_map/ppermute | solution.py:650
  12.4 6.5 %collective-permute-start = (bf16[48,768]{1,0:T(8,128)(2,1)S(1)}, bf16[48,768]{1,0:T(8,128)(2,1)S(1)}, u32[]{:S(2)}, u32[]{:S(2)}) collective-permute-start(bf16[48,768]{1,0:T(8,128)(2,1)S(1)} %bitcast_select_fusion.refs_0_), channel_id=1, source_target_pairs={{0,1},{1,2},{2,3},{3,0},{4,5},{5,6},{6,7},{7,4},{8,9},{9,10},{10,1... | collective-permute-start | bytes 221192 | tf_op jit(solution)/shard_map/ppermute | solution.py:650
  13.6 13.3 %copy-start.12 = (bf16[192,768]{1,0:T(8,128)(2,1)S(1)}, bf16[192,768]{1,0:T(8,128)(2,1)}, u32[]{:S(2)}) copy-start(bf16[192,768]{1,0:T(8,128)(2,1)} %refs_0_.4) | copy-start | bytes 884740
  13.6 28.8 %copy-start.23 = (f32[64]{0:T(128)S(1)}, f32[64]{0:T(128)}, u32[]{:S(2)}) copy-start(f32[64]{0:T(128)} %constant.14.clone) | copy-start | bytes 772
  19.6 38.7 %copy-start.4 = (f32[768]{0:T(1024)S(1)}, f32[768]{0:T(1024)}, u32[]{:S(2)}) copy-start(f32[768]{0:T(1024)} %refs_5_.5) | copy-start | bytes 9220
  19.7 50.8 %copy-start = (bf16[3,128,768]{2,1,0:T(8,128)(2,1)S(1)}, bf16[3,128,768]{2,1,0:T(8,128)(2,1)}, u32[]{:S(2)}) copy-start(bf16[3,128,768]{2,1,0:T(8,128)(2,1)} %refs_0_.5) | copy-start | bytes 1769476
  19.7 50.8 %copy-start.2 = (f32[768]{0:T(1024)S(1)}, f32[768]{0:T(1024)}, u32[]{:S(2)}) copy-start(f32[768]{0:T(1024)} %refs_4_.1) | copy-start | bytes 9220
  19.7 50.8 %copy-start.3 = (f32[768]{0:T(1024)S(1)}, f32[768]{0:T(1024)}, u32[]{:S(2)}) copy-start(f32[768]{0:T(1024)} %refs_5_.4) | copy-start | bytes 9220
  19.7 50.8 %copy-start.6 = (f32[768]{0:T(1024)S(1)}, f32[768]{0:T(1024)}, u32[]{:S(2)}) copy-start(f32[768]{0:T(1024)} %refs_9_.2) | copy-start | bytes 9220
  19.7 22.7 %all-to-all-start = ((bf16[16,208,128]{2,1,0:T(8,128)(2,1)}), bf16[16,208,128]{2,1,0:T(8,128)(2,1)S(1)}, u32[]{:S(2)}, u32[]{:S(2)}) async-start(bf16[16,208,128]{2,1,0:T(8,128)(2,1)} %get-tuple-element.81), calls=%async_computation | async-start | bytes 1703936 | tf_op jit(solution)/shard_map/all_to_all | solution.py:666
  26.9 5.7 %collective-permute-start.5 = (bf16[96,768]{1,0:T(8,128)(2,1)S(1)}, bf16[96,768]{1,0:T(8,128)(2,1)S(1)}, u32[]{:S(2)}, u32[]{:S(2)}) collective-permute-start(bf16[96,768]{1,0:T(8,128)(2,1)S(1)} %constant_dynamic-slice_fusion), channel_id=1, source_target_pairs={{0,3},{1,0},{2,1},{3,2},{4,7},{5,4},{6,5},{7,6},{8,11},{9,8},{10,9... | collective-permute-start | bytes 442376 | tf_op jit(solution)/shard_map/ppermute | solution.py:650
  27.9 7.0 %collective-permute-start.4 = (bf16[96,768]{1,0:T(8,128)(2,1)S(1)}, bf16[96,768]{1,0:T(8,128)(2,1)S(1)}, u32[]{:S(2)}, u32[]{:S(2)}) collective-permute-start(bf16[96,768]{1,0:T(8,128)(2,1)S(1)} %constant_dynamic-slice_fusion), channel_id=1, source_target_pairs={{0,2},{1,3},{2,0},{3,1},{4,6},{5,7},{6,4},{7,5},{8,10},{9,11},{10,... | collective-permute-start | bytes 442376 | tf_op jit(solution)/shard_map/ppermute | solution.py:650
  29.2 7.1 %collective-permute-start.3 = (bf16[96,768]{1,0:T(8,128)(2,1)S(1)}, bf16[96,768]{1,0:T(8,128)(2,1)S(1)}, u32[]{:S(2)}, u32[]{:S(2)}) collective-permute-start(bf16[96,768]{1,0:T(8,128)(2,1)S(1)} %constant_dynamic-slice_fusion), channel_id=1, source_target_pairs={{0,1},{1,2},{2,3},{3,0},{4,5},{5,6},{6,7},{7,4},{8,9},{9,10},{10,1... | collective-permute-start | bytes 442376 | tf_op jit(solution)/shard_map/ppermute | solution.py:650
  32.7 9.9 %copy-start.13 = (bf16[96,768]{1,0:T(8,128)(2,1)}, bf16[96,768]{1,0:T(8,128)(2,1)S(1)}, u32[]{:S(2)}) copy-start(bf16[96,768]{1,0:T(8,128)(2,1)S(1)} %collective-permute-done.5.refs_4_.refs_3_) | copy-start | bytes 442372
  34.8 7.7 %copy-start.14 = (bf16[96,768]{1,0:T(8,128)(2,1)}, bf16[96,768]{1,0:T(8,128)(2,1)S(1)}, u32[]{:S(2)}) copy-start(bf16[96,768]{1,0:T(8,128)(2,1)S(1)} %collective-permute-done.4.refs_3_.refs_2_) | copy-start | bytes 442372
  36.3 6.2 %copy-start.15 = (bf16[96,768]{1,0:T(8,128)(2,1)}, bf16[96,768]{1,0:T(8,128)(2,1)S(1)}, u32[]{:S(2)}) copy-start(bf16[96,768]{1,0:T(8,128)(2,1)S(1)} %collective-permute-done.3.refs_2_.refs_1_) | copy-start | bytes 442372
  52.5 18.0 %all-to-all-start.1 = ((bf16[64,16,128]{2,1,0:T(8,128)(2,1)}), bf16[64,16,128]{2,1,0:T(8,128)(2,1)S(1)}, u32[]{:S(2)}, u32[]{:S(2)}) async-start(bf16[64,16,128]{2,1,0:T(8,128)(2,1)} %get-tuple-element.82), calls=%async_computation.1 | async-start | bytes 524288 | tf_op jit(solution)/shard_map/all_to_all | solution.py:670
  57.7 9.9 %collective-permute-start.8 = (bf16[96,768]{1,0:T(8,128)(2,1)}, bf16[96,768]{1,0:T(8,128)(2,1)S(1)}, u32[]{:S(2)}, u32[]{:S(2)}) collective-permute-start(bf16[96,768]{1,0:T(8,128)(2,1)} %copy-done.13), channel_id=1, source_target_pairs={{0,64},{64,0},{1,65},{65,1},{2,66},{66,2},{3,67},{67,3},{4,68},{68... | collective-permute-start | bytes 442376 | tf_op jit(solution)/shard_map/ppermute | solution.py:662
  57.8 9.8 %collective-permute-start.7 = (bf16[96,768]{1,0:T(8,128)(2,1)}, bf16[96,768]{1,0:T(8,128)(2,1)S(1)}, u32[]{:S(2)}, u32[]{:S(2)}) collective-permute-start(bf16[96,768]{1,0:T(8,128)(2,1)} %copy-done.14), channel_id=1, source_target_pairs={{0,64},{64,0},{1,65},{65,1},{2,66},{66,2},{3,67},{67,3},{4,68},{68... | collective-permute-start | bytes 442376 | tf_op jit(solution)/shard_map/ppermute | solution.py:662
  58.2 9.4 %collective-permute-start.6 = (bf16[96,768]{1,0:T(8,128)(2,1)}, bf16[96,768]{1,0:T(8,128)(2,1)S(1)}, u32[]{:S(2)}, u32[]{:S(2)}) collective-permute-start(bf16[96,768]{1,0:T(8,128)(2,1)} %copy-done.15), channel_id=1, source_target_pairs={{0,64},{64,0},{1,65},{65,1},{2,66},{66,2},{3,67},{67,3},{4,68},{68... | collective-permute-start | bytes 442376 | tf_op jit(solution)/shard_map/ppermute | solution.py:662
  58.3 4.1 %collective-permute-start.11 = (f32[768]{0:T(1024)S(1)}, f32[768]{0:T(1024)S(1)}, u32[]{:S(2)}, u32[]{:S(2)}) collective-permute-start(f32[768]{0:T(1024)S(1)} %copy-done.4), channel_id=1, source_target_pairs={{0,3},{1,0},{2,1},{3,2},{4,7},{5,4},{6,5},{7,6},{8,11},{9,8},{10,9... | collective-permute-start | bytes 9224 | tf_op jit(solution)/shard_map/ppermute | solution.py:650
  61.1 5.1 %collective-permute-start.10 = (f32[768]{0:T(1024)S(1)}, f32[768]{0:T(1024)S(1)}, u32[]{:S(2)}, u32[]{:S(2)}) collective-permute-start(f32[768]{0:T(1024)S(1)} %copy-done.4), channel_id=1, source_target_pairs={{0,2},{1,3},{2,0},{3,1},{4,6},{5,7},{6,4},{7,5},{8,10},{9,11},{10,... | collective-permute-start | bytes 9224 | tf_op jit(solution)/shard_map/ppermute | solution.py:650
  62.5 5.1 %collective-permute-start.9 = (f32[768]{0:T(1024)S(1)}, f32[768]{0:T(1024)S(1)}, u32[]{:S(2)}, u32[]{:S(2)}) collective-permute-start(f32[768]{0:T(1024)S(1)} %copy-done.4), channel_id=1, source_target_pairs={{0,1},{1,2},{2,3},{3,0},{4,5},{5,6},{6,7},{7,4},{8,9},{9,10},{10,1... | collective-permute-start | bytes 9224 | tf_op jit(solution)/shard_map/ppermute | solution.py:650
  67.6 2.9 %copy-start.16 = (bf16[96,768]{1,0:T(8,128)(2,1)}, bf16[96,768]{1,0:T(8,128)(2,1)S(1)}, u32[]{:S(2)}) copy-start(bf16[96,768]{1,0:T(8,128)(2,1)S(1)} %collective-permute-done.8.refs_6_) | copy-start | bytes 442372
  67.6 2.9 %copy-start.17 = (bf16[96,768]{1,0:T(8,128)(2,1)}, bf16[96,768]{1,0:T(8,128)(2,1)S(1)}, u32[]{:S(2)}) copy-start(bf16[96,768]{1,0:T(8,128)(2,1)S(1)} %collective-permute-done.7.refs_5_) | copy-start | bytes 442372
  67.6 2.9 %copy-start.18 = (bf16[96,768]{1,0:T(8,128)(2,1)}, bf16[96,768]{1,0:T(8,128)(2,1)S(1)}, u32[]{:S(2)}) copy-start(bf16[96,768]{1,0:T(8,128)(2,1)S(1)} %collective-permute-done.6.refs_4_) | copy-start | bytes 442372
  73.6 6.4 %copy-start.7 = (f32[8,128]{1,0:T(8,128)}, f32[8,128]{1,0:T(8,128)S(1)}, u32[]{:S(2)}) copy-start(f32[8,128]{1,0:T(8,128)S(1)} %get-tuple-element.83.refs_1_) | copy-start | bytes 12292
  73.6 16.8 %collective-permute-start.12 = (bf16[128,768]{1,0:T(8,128)(2,1)}, bf16[128,768]{1,0:T(8,128)(2,1)S(1)}, u32[]{:S(2)}, u32[]{:S(2)}) collective-permute-start(bf16[128,768]{1,0:T(8,128)(2,1)} %get-tuple-element.88), channel_id=1, source_target_pairs={{0,3},{1,0},{2,1},{3,2},{4,7},{5,4},{6,5},{7,6},{8,11},{9,8},{10,9... | collective-permute-start | bytes 589832 | tf_op jit(solution)/shard_map/ppermute | solution.py:650
  73.9 16.5 %collective-permute-start.13 = (bf16[128,768]{1,0:T(8,128)(2,1)}, bf16[128,768]{1,0:T(8,128)(2,1)S(1)}, u32[]{:S(2)}, u32[]{:S(2)}) collective-permute-start(bf16[128,768]{1,0:T(8,128)(2,1)} %get-tuple-element.89), channel_id=1, source_target_pairs={{0,2},{1,3},{2,0},{3,1},{4,6},{5,7},{6,4},{7,5},{8,10},{9,11},{10,... | collective-permute-start | bytes 589832 | tf_op jit(solution)/shard_map/ppermute | solution.py:650
  76.2 14.2 %collective-permute-start.14 = (bf16[128,768]{1,0:T(8,128)(2,1)}, bf16[128,768]{1,0:T(8,128)(2,1)S(1)}, u32[]{:S(2)}, u32[]{:S(2)}) collective-permute-start(bf16[128,768]{1,0:T(8,128)(2,1)} %get-tuple-element.90), channel_id=1, source_target_pairs={{0,1},{1,2},{2,3},{3,0},{4,5},{5,6},{6,7},{7,4},{8,9},{9,10},{10,1... | collective-permute-start | bytes 589832 | tf_op jit(solution)/shard_map/ppermute | solution.py:650
  80.1 24.3 %copy-start.5 = (f32[768]{0:T(1024)S(1)}, f32[768]{0:T(1024)}, u32[]{:S(2)}) copy-start(f32[768]{0:T(1024)} %refs_5_.5) | copy-start | bytes 9220
  91.3 19.3 %all-to-all-start.2 = ((bf16[64,16,128]{2,1,0:T(8,128)(2,1)}), bf16[64,16,128]{2,1,0:T(8,128)(2,1)S(1)}, u32[]{:S(2)}, u32[]{:S(2)}) async-start(bf16[64,16,128]{2,1,0:T(8,128)(2,1)} %later.8), calls=%async_computation.2 | async-start | bytes 524288 | tf_op jit(solution)/shard_map/all_to_all | solution.py:670
  99.8 8.3 %collective-permute-start.17 = (bf16[16,768]{1,0:T(8,128)(2,1)}, bf16[16,768]{1,0:T(8,128)(2,1)S(1)}, u32[]{:S(2)}, u32[]{:S(2)}) collective-permute-start(bf16[16,768]{1,0:T(8,128)(2,1)} %get-tuple-element.99.refs_9_), channel_id=1, source_target_pairs={{0,3},{1,0},{2,1},{3,2},{4,7},{5,4},{6,5},{7,6},{8,11},{9,8},{10,9... | collective-permute-start | bytes 73736 | tf_op jit(solution)/shard_map/ppermute | solution.py:650
  102.6 6.0 %collective-permute-start.16 = (bf16[16,768]{1,0:T(8,128)(2,1)}, bf16[16,768]{1,0:T(8,128)(2,1)S(1)}, u32[]{:S(2)}, u32[]{:S(2)}) collective-permute-start(bf16[16,768]{1,0:T(8,128)(2,1)} %get-tuple-element.99.refs_9_), channel_id=1, source_target_pairs={{0,2},{1,3},{2,0},{3,1},{4,6},{5,7},{6,4},{7,5},{8,10},{9,11},{10,... | collective-permute-start | bytes 73736 | tf_op jit(solution)/shard_map/ppermute | solution.py:650
  103.5 5.6 %collective-permute-start.15 = (bf16[16,768]{1,0:T(8,128)(2,1)}, bf16[16,768]{1,0:T(8,128)(2,1)S(1)}, u32[]{:S(2)}, u32[]{:S(2)}) collective-permute-start(bf16[16,768]{1,0:T(8,128)(2,1)} %get-tuple-element.99.refs_9_), channel_id=1, source_target_pairs={{0,1},{1,2},{2,3},{3,0},{4,5},{5,6},{6,7},{7,4},{8,9},{9,10},{10,1... | collective-permute-start | bytes 73736 | tf_op jit(solution)/shard_map/ppermute | solution.py:650
  108.1 2.5 %copy-start.20 = (bf16[16,768]{1,0:T(8,128)(2,1)}, bf16[16,768]{1,0:T(8,128)(2,1)S(1)}, u32[]{:S(2)}) copy-start(bf16[16,768]{1,0:T(8,128)(2,1)S(1)} %collective-permute-done.17.refs_12_.refs_5_) | copy-start | bytes 73732
  108.6 2.0 %copy-start.21 = (bf16[16,768]{1,0:T(8,128)(2,1)}, bf16[16,768]{1,0:T(8,128)(2,1)S(1)}, u32[]{:S(2)}) copy-start(bf16[16,768]{1,0:T(8,128)(2,1)S(1)} %collective-permute-done.16.refs_11_.refs_4_) | copy-start | bytes 73732
  109.0 1.6 copy-start.22
  111.3 21.2 %collective-permute-start.20 = (bf16[192,768]{1,0:T(8,128)(2,1)}, bf16[192,768]{1,0:T(8,128)(2,1)S(1)}, u32[]{:S(2)}, u32[]{:S(2)}) collective-permute-start(bf16[192,768]{1,0:T(8,128)(2,1)} %later.9.refs_4_), channel_id=1, source_target_pairs={{0,3},{1,0},{2,1},{3,2},{4,7},{5,4},{6,5},{7,6},{8,11},{9,8},{10,9... | collective-permute-start | bytes 884744 | tf_op jit(solution)/shard_map/ppermute | solution.py:650
  112.4 20.2 %collective-permute-start.19 = (bf16[192,768]{1,0:T(8,128)(2,1)}, bf16[192,768]{1,0:T(8,128)(2,1)S(1)}, u32[]{:S(2)}, u32[]{:S(2)}) collective-permute-start(bf16[192,768]{1,0:T(8,128)(2,1)} %later.9.refs_4_), channel_id=1, source_target_pairs={{0,2},{1,3},{2,0},{3,1},{4,6},{5,7},{6,4},{7,5},{8,10},{9,11},{10,... | collective-permute-start | bytes 884744 | tf_op jit(solution)/shard_map/ppermute | solution.py:650
  113.9 18.6 %collective-permute-start.18 = (bf16[192,768]{1,0:T(8,128)(2,1)}, bf16[192,768]{1,0:T(8,128)(2,1)S(1)}, u32[]{:S(2)}, u32[]{:S(2)}) collective-permute-start(bf16[192,768]{1,0:T(8,128)(2,1)} %later.9.refs_4_), channel_id=1, source_target_pairs={{0,1},{1,2},{2,3},{3,0},{4,5},{5,6},{6,7},{7,4},{8,9},{9,10},{10,1... | collective-permute-start | bytes 884744 | tf_op jit(solution)/shard_map/ppermute | solution.py:650
  128.4 19.6 %all-to-all-start.3 = ((bf16[16,256,128]{2,1,0:T(8,128)(2,1)}), bf16[16,256,128]{2,1,0:T(8,128)(2,1)S(1)}, u32[]{:S(2)}, u32[]{:S(2)}) async-start(bf16[16,256,128]{2,1,0:T(8,128)(2,1)} %get-tuple-element.100), calls=%async_computation.3 | async-start | bytes 2097152 | tf_op jit(solution)/shard_map/all_to_all | solution.py:666
  132.5 0.8 copy-start.25
  132.5 0.9 copy-start.26
  139.1 2.6 %collective-permute-start.21 = (bf16[96,1536]{1,0:T(8,128)(2,1)}, bf16[96,1536]{1,0:T(8,128)(2,1)S(1)}, u32[]{:S(2)}, u32[]{:S(2)}) collective-permute-start(bf16[96,1536]{1,0:T(8,128)(2,1)} %get-tuple-element.108), channel_id=1, source_target_pairs={{0,64},{64,0},{1,65},{65,1},{2,66},{66,2},{3,67},{67,3},{4,68},{68... | collective-permute-start | bytes 884744 | tf_op jit(solution)/shard_map/ppermute | solution.py:662
  139.2 2.5 %collective-permute-start.22 = (bf16[96,1536]{1,0:T(8,128)(2,1)}, bf16[96,1536]{1,0:T(8,128)(2,1)S(1)}, u32[]{:S(2)}, u32[]{:S(2)}) collective-permute-start(bf16[96,1536]{1,0:T(8,128)(2,1)} %get-tuple-element.109), channel_id=1, source_target_pairs={{0,64},{64,0},{1,65},{65,1},{2,66},{66,2},{3,67},{67,3},{4,68},{68... | collective-permute-start | bytes 884744 | tf_op jit(solution)/shard_map/ppermute | solution.py:662
  139.7 2.1 %collective-permute-start.23 = (bf16[96,1536]{1,0:T(8,128)(2,1)}, bf16[96,1536]{1,0:T(8,128)(2,1)S(1)}, u32[]{:S(2)}, u32[]{:S(2)}) collective-permute-start(bf16[96,1536]{1,0:T(8,128)(2,1)} %get-tuple-element.110), channel_id=1, source_target_pairs={{0,64},{64,0},{1,65},{65,1},{2,66},{66,2},{3,67},{67,3},{4,68},{68... | collective-permute-start | bytes 884744 | tf_op jit(solution)/shard_map/ppermute | solution.py:662
  139.8 2.5 %collective-permute-start.24 = (bf16[96,1536]{1,0:T(8,128)(2,1)}, bf16[96,1536]{1,0:T(8,128)(2,1)S(1)}, u32[]{:S(2)}, u32[]{:S(2)}) collective-permute-start(bf16[96,1536]{1,0:T(8,128)(2,1)} %get-tuple-element.111), channel_id=1, source_target_pairs={{0,64},{64,0},{1,65},{65,1},{2,66},{66,2},{3,67},{67,3},{4,68},{68... | collective-permute-start | bytes 884744 | tf_op jit(solution)/shard_map/ppermute | solution.py:662
  140.2 1.5 collective-permute-start.25
  150.9 2.8 %collective-permute-start.26 = (bf16[400,768]{1,0:T(8,128)(2,1)}, bf16[400,768]{1,0:T(8,128)(2,1)S(1)}, u32[]{:S(2)}, u32[]{:S(2)}) collective-permute-start(bf16[400,768]{1,0:T(8,128)(2,1)} %get-tuple-element.116), channel_id=1, source_target_pairs={{0,64},{64,0},{1,65},{65,1},{2,66},{66,2},{3,67},{67,3},{4,68},{68... | collective-permute-start | bytes 1843208 | tf_op jit(solution)/shard_map/ppermute | solution.py:662
  156.4 32.7 %all-to-all-start.4 = ((bf16[16,448,128]{2,1,0:T(8,128)(2,1)}), bf16[16,448,128]{2,1,0:T(8,128)(2,1)S(1)}, u32[]{:S(2)}, u32[]{:S(2)}) async-start(bf16[16,448,128]{2,1,0:T(8,128)(2,1)} %get-tuple-element.120.refs_1_), calls=%async_computation.4 | async-start | bytes 3670016 | tf_op jit(solution)/shard_map/all_to_all | solution.py:666
  160.9 2.1 %copy-start.19 = (bf16[96,768]{1,0:T(8,128)(2,1)S(1)}, bf16[96,768]{1,0:T(8,128)(2,1)}, u32[]{:S(2)}) copy-start(bf16[96,768]{1,0:T(8,128)(2,1)} %later.12) | copy-start | bytes 442372
  160.9 8.9 %collective-permute-start.30 = (bf16[96,768]{1,0:T(8,128)(2,1)}, bf16[96,768]{1,0:T(8,128)(2,1)S(1)}, u32[]{:S(2)}, u32[]{:S(2)}) collective-permute-start(bf16[96,768]{1,0:T(8,128)(2,1)} %later.11), channel_id=1, source_target_pairs={{0,1},{1,2},{2,3},{3,0},{4,5},{5,6},{6,7},{7,4},{8,9},{9,10},{10,1... | collective-permute-start | bytes 442376 | tf_op jit(solution)/shard_map/ppermute | solution.py:650
  162.9 10.8 %collective-permute-start.31 = (bf16[96,768]{1,0:T(8,128)(2,1)S(1)}, bf16[96,768]{1,0:T(8,128)(2,1)S(1)}, u32[]{:S(2)}, u32[]{:S(2)}) collective-permute-start(bf16[96,768]{1,0:T(8,128)(2,1)S(1)} %copy-done.19), channel_id=1, source_target_pairs={{0,2},{1,3},{2,0},{3,1},{4,6},{5,7},{6,4},{7,5},{8,10},{9,11},{10,... | collective-permute-start | bytes 442376 | tf_op jit(solution)/shard_map/ppermute | solution.py:650
  165.6 8.1 %collective-permute-start.32 = (bf16[96,768]{1,0:T(8,128)(2,1)}, bf16[96,768]{1,0:T(8,128)(2,1)S(1)}, u32[]{:S(2)}, u32[]{:S(2)}) collective-permute-start(bf16[96,768]{1,0:T(8,128)(2,1)} %later.13), channel_id=1, source_target_pairs={{0,3},{1,0},{2,1},{3,2},{4,7},{5,4},{6,5},{7,6},{8,11},{9,8},{10,9... | collective-permute-start | bytes 442376 | tf_op jit(solution)/shard_map/ppermute | solution.py:650
  166.8 10.9 %collective-permute-start.29 = (bf16[96,768]{1,0:T(8,128)(2,1)}, bf16[96,768]{1,0:T(8,128)(2,1)S(1)}, u32[]{:S(2)}, u32[]{:S(2)}) collective-permute-start(bf16[96,768]{1,0:T(8,128)(2,1)} %later.10.refs_0_), channel_id=1, source_target_pairs={{0,3},{1,0},{2,1},{3,2},{4,7},{5,4},{6,5},{7,6},{8,11},{9,8},{10,9... | collective-permute-start | bytes 442376 | tf_op jit(solution)/shard_map/ppermute | solution.py:650
  167.0 11.7 %collective-permute-start.28 = (bf16[96,768]{1,0:T(8,128)(2,1)}, bf16[96,768]{1,0:T(8,128)(2,1)S(1)}, u32[]{:S(2)}, u32[]{:S(2)}) collective-permute-start(bf16[96,768]{1,0:T(8,128)(2,1)} %later.10.refs_0_), channel_id=1, source_target_pairs={{0,2},{1,3},{2,0},{3,1},{4,6},{5,7},{6,4},{7,5},{8,10},{9,11},{10,... | collective-permute-start | bytes 442376 | tf_op jit(solution)/shard_map/ppermute | solution.py:650
  169.8 9.4 %collective-permute-start.27 = (bf16[96,768]{1,0:T(8,128)(2,1)}, bf16[96,768]{1,0:T(8,128)(2,1)S(1)}, u32[]{:S(2)}, u32[]{:S(2)}) collective-permute-start(bf16[96,768]{1,0:T(8,128)(2,1)} %later.10.refs_0_), channel_id=1, source_target_pairs={{0,1},{1,2},{2,3},{3,0},{4,5},{5,6},{6,7},{7,4},{8,9},{9,10},{10,1... | collective-permute-start | bytes 442376 | tf_op jit(solution)/shard_map/ppermute | solution.py:650
  174.9 8.2 %collective-permute-start.35 = (bf16[96,768]{1,0:T(8,128)(2,1)S(1)}, bf16[96,768]{1,0:T(8,128)(2,1)S(1)}, u32[]{:S(2)}, u32[]{:S(2)}) collective-permute-start(bf16[96,768]{1,0:T(8,128)(2,1)S(1)} %input_chunk.1.refs_0_), channel_id=1, source_target_pairs={{0,3},{1,0},{2,1},{3,2},{4,7},{5,4},{6,5},{7,6},{8,11},{9,8},{10,9... | collective-permute-start | bytes 442376 | tf_op jit(solution)/shard_map/ppermute | solution.py:650
  176.9 8.3 %collective-permute-start.34 = (bf16[96,768]{1,0:T(8,128)(2,1)S(1)}, bf16[96,768]{1,0:T(8,128)(2,1)S(1)}, u32[]{:S(2)}, u32[]{:S(2)}) collective-permute-start(bf16[96,768]{1,0:T(8,128)(2,1)S(1)} %input_chunk.1.refs_0_), channel_id=1, source_target_pairs={{0,2},{1,3},{2,0},{3,1},{4,6},{5,7},{6,4},{7,5},{8,10},{9,11},{10,... | collective-permute-start | bytes 442376 | tf_op jit(solution)/shard_map/ppermute | solution.py:650
  177.7 9.1 %collective-permute-start.33 = (bf16[96,768]{1,0:T(8,128)(2,1)S(1)}, bf16[96,768]{1,0:T(8,128)(2,1)S(1)}, u32[]{:S(2)}, u32[]{:S(2)}) collective-permute-start(bf16[96,768]{1,0:T(8,128)(2,1)S(1)} %input_chunk.1.refs_0_), channel_id=1, source_target_pairs={{0,1},{1,2},{2,3},{3,0},{4,5},{5,6},{6,7},{7,4},{8,9},{9,10},{10,1... | collective-permute-start | bytes 442376 | tf_op jit(solution)/shard_map/ppermute | solution.py:650
  179.1 0.9 copy-start.1
  (5 other events, 3.6 us)
Sparse Core Ops, SparseCore 0:
  19.8 60.2 all-gather.2

commit v7 on v6

--- a/solution.py
+++ b/solution.py
@@ -516,7 +516,7 @@
     return jnp.concatenate([block[:, k : k + T] for k in range(0, block.shape[1], T)], axis=0).astype(bf16)
 
 
-def input_weights_kernel(x_far, got, out_whole, grad, send_far, keep_far, sums, whole, bias, x, sems):
+def input_weights_kernel(x_far, got, out_whole, grad, send_far, keep, sums, whole, bias, x, sems):
     c = lax.axis_index("dp")
     load = copies([(x_far, x)], sems)[0]
     grads = []
@@ -555,8 +555,9 @@
     half = D // 2
     pairs = [(bias, send_far.at[half:, :])]
     pairs.append((whole.at[pl.ds(pl.multiple_of((1 - c) * half, half), half), :], send_far.at[0:half, :]))
-    pairs.append((whole.at[pl.ds(pl.multiple_of(c * half, half), half), :], keep_far))
-    for store in copies(pairs, sems):
+    stores = copies(pairs, sems)
+    keep[...] = whole[pl.ds(pl.multiple_of(c * half, half), half), :]
+    for store in stores:
         store.wait()
 
 
@@ -596,10 +597,10 @@
 
 
 def last_add_kernel(
-    keep_far, slots_in, got_far, sums, slots_far, b_q, b_k, b_v, g_two, s_two, b_down, g_one, s_one, b_out,
-    keep, got, slots, sems,
+    keep, slots_in, got_far, sums, slots_far, b_q, b_k, b_v, g_two, s_two, b_down, g_one, s_one, b_out,
+    got, slots, sems,
 ):
-    for load in copies([(keep_far, keep), (got_far, got)], sems):
+    for load in copies([(got_far, got)], sems):
         load.wait()
     stores = []
     for w in range(NW):
@@ -895,7 +896,7 @@
             pltpu.SemaphoreType.DMA((3,)),
         ],
         far_in=(0,),
-        far=(1, 2),
+        far=(1,),
         after=(added,),
     )
     *parts, done = call(
@@ -922,12 +923,11 @@
         [(last_shape, bf16)] + [((E,), f32)] * 3 + [((D,), f32)] * 6,
         (keep, slots, other_core(send), sums),
         scratch=[
-            pltpu.VMEM((D // 2, D), bf16),
             pltpu.VMEM((D // 2 + 16, D), bf16),
             pltpu.VMEM((NW, LAST_ROWS, T), bf16),
             pltpu.SemaphoreType.DMA((NW,)),
         ],
-        far_in=range(2),
+        far_in=(1,),
         any_in=(2,),
         far=(0,),
         aliases={1: 0},

time: 198 us -> 197 us (level)
  no operation moved by 1% of the time
where the time goes in v7:
time: 197 us; the launch traced here: 196 us
  starting transfers between devices  67.5 us (34%)
  Pallas kernels  65.4 us (33%)
  waiting for transfers between devices  44 us (22%)
  between operations  14.6 us (7%)
  local copies, waits for them, and re-layouts  3.46 us (2%)
    pallas_call x16, Pallas kernels, call(): pl.pallas_call(run, out_shape=[shape(k, s, t) for k, (s, t) in enumerate(...  65.4 us
    ppermute x27, starting transfers between devices, shifted(): return lax.ppermute(x, 'narrow', [(i, (i + s) % NN) for i in range(NN)])  36.2 us
    ppermute x27, waiting for transfers between devices, shifted(): return lax.ppermute(x, 'narrow', [(i, (i + s) % NN) for i in range(NN)])  23.9 us
    all_to_all x3, starting transfers between devices, exchange(): return lax.all_to_all(slots, 'wide', 0, 0, tiled=True)  15.6 us
    all_to_all x2, starting transfers between devices, exchange_all(): return lax.all_to_all(slots, ('wide', 'narrow'), 0, 0, tiled=True)  13.7 us
    all_to_all x3, waiting for transfers between devices, exchange(): return lax.all_to_all(slots, 'wide', 0, 0, tiled=True)  10.3 us
    all_to_all x2, waiting for transfers between devices, exchange_all(): return lax.all_to_all(slots, ('wide', 'narrow'), 0, 0, tiled=True)  4.43 us
  transfers between devices with their start and end apart: 42, of which 24 were waited for; matrix products, arithmetic and copies ran while one was open for 0% of the time, Pallas kernels for 30%

profile of v7, /device:TPU:0, one launch (start us, length us, event | category | flops | bytes accessed | tf_op | source)
XLA Modules:
  0.0 195.8 jit_solution(5097056893033359565)
XLA Ops:
  7.2 0.9 bitcast_select_fusion.refs_0_
  8.2 4.2 %collective-permute-start.2 = (bf16[48,768]{1,0:T(8,128)(2,1)S(1)}, bf16[48,768]{1,0:T(8,128)(2,1)S(1)}, u32[]{:S(2)}, u32[]{:S(2)}) collective-permute-start(bf16[48,768]{1,0:T(8,128)(2,1)S(1)} %bitcast_select_fusion.refs_0_), channel_id=1, source_target_pairs={{0,3},{1,0},{2,1},{3,2},{4,7},{5,4},{6,5},{7,6},{8,11},{9,8},{10,9... | collective-permute-start | bytes 221192 | tf_op jit(solution)/shard_map/ppermute | solution.py:651
  12.4 1.3 collective-permute-start
  13.6 3.1 %project.1 = (bf16[16,208,128]{2,1,0:T(8,128)(2,1)}, f32[8,128]{1,0:T(8,128)S(1)}) custom-call(bf16[3,128,768]{2,1,0:T(8,128)(2,1)} %refs_0_.5, s32[3,128]{1,0:T(4,128)} %refs_1_.2, bf16[192,768]{1,0:T(8,128)(2,1)} %bitcast.9, f32[192]{0:T(256)} %refs_3_.1, bf16[192,768]{1,0:T(8,128)(2,1)} %bitcast.11, f32[192]{0:T(256)} %refs_5_.3, ...), custom_call_target="tpu_custom_call" | custom-call | flops 1024 | bytes 1024 | tf_op jit(solution)/shard_map/project/pallas_call | solution.py:70
  16.8 1.6 collective-permute-done.1.refs_2_
  18.9 0.8 stack.1
  19.7 7.2 %all-to-all-start = ((bf16[16,208,128]{2,1,0:T(8,128)(2,1)}), bf16[16,208,128]{2,1,0:T(8,128)(2,1)S(1)}, u32[]{:S(2)}, u32[]{:S(2)}) async-start(bf16[16,208,128]{2,1,0:T(8,128)(2,1)} %get-tuple-element.81), calls=%async_computation | async-start | bytes 1703936 | tf_op jit(solution)/shard_map/all_to_all | solution.py:667
  26.9 0.9 collective-permute-start.5
  27.9 1.4 collective-permute-start.4
  29.2 0.6 collective-permute-start.3
  29.8 2.8 %collective-permute-done.5.refs_4_.refs_3_ = bf16[96,768]{1,0:T(8,128)(2,1)S(1)} collective-permute-done((bf16[96,768]{1,0:T(8,128)(2,1)S(1)}, bf16[96,768]{1,0:T(8,128)(2,1)S(1)}, u32[]{:S(2)}, u32[]{:S(2)}) %collective-permute-start.5) | collective-permute-done | bytes 147488 | tf_op jit(solution)/shard_map/ppermute | solution.py:651
  32.7 2.2 %collective-permute-done.4.refs_3_.refs_2_ = bf16[96,768]{1,0:T(8,128)(2,1)S(1)} collective-permute-done((bf16[96,768]{1,0:T(8,128)(2,1)S(1)}, bf16[96,768]{1,0:T(8,128)(2,1)S(1)}, u32[]{:S(2)}, u32[]{:S(2)}) %collective-permute-start.4) | collective-permute-done | bytes 147488 | tf_op jit(solution)/shard_map/ppermute | solution.py:651
  34.8 1.5 collective-permute-done.3.refs_2_.refs_1_
  36.3 6.1 %all-to-all-done.refs_0_ = bf16[16,208,128]{2,1,0:T(8,128)(2,1)S(1)} async-done(((bf16[16,208,128]{2,1,0:T(8,128)(2,1)}), bf16[16,208,128]{2,1,0:T(8,128)(2,1)S(1)}, u32[]{:S(2)}, u32[]{:S(2)}) %all-to-all-start) | async-done | bytes 852000 | tf_op jit(solution)/shard_map/all_to_all | solution.py:667
  42.5 9.9 %attend.1 = (bf16[64,16,128]{2,1,0:T(8,128)(2,1)}, bf16[80,2048]{1,0:T(8,128)(2,1)}, bf16[80,2048]{1,0:T(8,128)(2,1)}, bf16[2048,64]{1,0:T(8,128)(2,1)}, bf16[20...) custom-call(bf16[16,208,128]{2,1,0:T(8,128)(2,1)S(1)} %all-to-all-do, ...), custom_call_target="tpu_custom_call" | custom-call | flops 1024 | bytes 1024 | tf_op jit(solution)/shard_map/attend/pallas_call | solution.py:70
  52.5 5.2 %all-to-all-start.1 = ((bf16[64,16,128]{2,1,0:T(8,128)(2,1)}), bf16[64,16,128]{2,1,0:T(8,128)(2,1)S(1)}, u32[]{:S(2)}, u32[]{:S(2)}) async-start(bf16[64,16,128]{2,1,0:T(8,128)(2,1)} %get-tuple-element.82), calls=%async_computation.1 | async-start | bytes 524288 | tf_op jit(solution)/shard_map/all_to_all | solution.py:671
  58.3 2.8 %collective-permute-start.11 = (f32[768]{0:T(1024)S(1)}, f32[768]{0:T(1024)S(1)}, u32[]{:S(2)}, u32[]{:S(2)}) collective-permute-start(f32[768]{0:T(1024)S(1)} %copy-done.4), channel_id=1, source_target_pairs={{0,3},{1,0},{2,1},{3,2},{4,7},{5,4},{6,5},{7,6},{8,11},{9,8},{10,9... | collective-permute-start | bytes 9224 | tf_op jit(solution)/shard_map/ppermute | solution.py:651
  61.1 0.9 collective-permute-start.10
  62.5 1.1 collective-permute-start.9
  63.5 2.7 %collective-permute-done.10.refs_13_.refs_11_ = f32[768]{0:T(1024)S(1)} collective-permute-done((f32[768]{0:T(1024)S(1)}, f32[768]{0:T(1024)S(1)}, u32[]{:S(2)}, u32[]{:S(2)}) %collective-permute-start.10) | collective-permute-done | bytes 3104 | tf_op jit(solution)/shard_map/ppermute | solution.py:651
  66.2 1.3 collective-permute-done.9.refs_12_.refs_10_
  67.6 2.9 %all-to-all-done.1.refs_8_ = bf16[64,16,128]{2,1,0:T(8,128)(2,1)S(1)} async-done(((bf16[64,16,128]{2,1,0:T(8,128)(2,1)}), bf16[64,16,128]{2,1,0:T(8,128)(2,1)S(1)}, u32[]{:S(2)}, u32[]{:S(2)}) %all-to-all-start.1) | async-done | bytes 262176 | tf_op jit(solution)/shard_map/all_to_all | solution.py:671
  70.5 3.1 %first.1 = (bf16[768,768]{1,0:T(8,128)(2,1)}, f32[96,896]{1,0:T(8,128)}, bf16[128,768]{1,0:T(8,128)(2,1)}, bf16[128,768]{1,0:T(8,128)(2,1)}, bf16[128,768]{1,0:T...) custom-call(bf16[192,768]{1,0:T(8,128)(2,1)} %refs_0_.4, bf16[96,768]{1,0:T(8,128)(2,1)} %copy-done.15, ...), custom_call_target="tpu_custom_call" | custom-call | flops 1024 | bytes 1024 | tf_op jit(solution)/shard_map/first/pallas_call | solution.py:70
  73.9 2.3 %collective-permute-start.13 = (bf16[128,768]{1,0:T(8,128)(2,1)}, bf16[128,768]{1,0:T(8,128)(2,1)S(1)}, u32[]{:S(2)}, u32[]{:S(2)}) collective-permute-start(bf16[128,768]{1,0:T(8,128)(2,1)} %get-tuple-element.89), channel_id=1, source_target_pairs={{0,2},{1,3},{2,0},{3,1},{4,6},{5,7},{6,4},{7,5},{8,10},{9,11},{10,... | collective-permute-start | bytes 589832 | tf_op jit(solution)/shard_map/ppermute | solution.py:651
  76.7 3.3 %all-gather.3.cloned.1.call-done = bf16[128,48,768]{2,1,0:T(8,128)(2,1)} async-done(((bf16[4,48,768]{2,1,0:T(8,128)(2,1)}), bf16[128,48,768]{2,1,0:T(8,128)(2,1)}) %all-gather.3.cloned.1.call-update) | async-done | bytes 9437200 | tf_op jit(solution)/shard_map/all_gather | solution.py:716
  80.1 10.4 %middle.1 = (bf16[64,16,128]{2,1,0:T(8,128)(2,1)}, f32[96,768]{1,0:T(8,128)}, bf16[192,768]{1,0:T(8,128)(2,1)}, bf16[96,768]{1,0:T(8,128)(2,1)}, bf16[16,768]{1,0:T(8,128)(2,1)}) custom-call(bf16[2,16,4,48,768]{4,3,2,1,0:T(8,128)(2,1)} %later.7.refs_0_.refs_4_.refs_8_, f32[96,896]{1,0:T(8,128)} %get-tuple-element.84.refs_1_, bf16[3,128,768]{2,1,0:T(8,128)(2,1)} %refs_2_.1, ...), custom_call_target="tpu_custom_call" | custom-call | flops 1024 | bytes 1024 | tf_op jit(solution)/shard_map/middle/pallas_call | solution.py:70
  90.5 0.6 copy-done.9
  91.3 8.5 %all-to-all-start.2 = ((bf16[64,16,128]{2,1,0:T(8,128)(2,1)}), bf16[64,16,128]{2,1,0:T(8,128)(2,1)S(1)}, u32[]{:S(2)}, u32[]{:S(2)}) async-start(bf16[64,16,128]{2,1,0:T(8,128)(2,1)} %later.8), calls=%async_computation.2 | async-start | bytes 524288 | tf_op jit(solution)/shard_map/all_to_all | solution.py:671
  99.8 2.9 %collective-permute-start.17 = (bf16[16,768]{1,0:T(8,128)(2,1)}, bf16[16,768]{1,0:T(8,128)(2,1)S(1)}, u32[]{:S(2)}, u32[]{:S(2)}) collective-permute-start(bf16[16,768]{1,0:T(8,128)(2,1)} %get-tuple-element.99.refs_9_), channel_id=1, source_target_pairs={{0,3},{1,0},{2,1},{3,2},{4,7},{5,4},{6,5},{7,6},{8,11},{9,8},{10,9... | collective-permute-start | bytes 73736 | tf_op jit(solution)/shard_map/ppermute | solution.py:651
  102.6 0.9 collective-permute-start.16
  103.5 0.9 collective-permute-start.15
  104.3 3.8 %hidden.1 = (bf16[384,768]{1,0:T(8,128)(2,1)}, f32[384,768]{1,0:T(8,128)}) custom-call(bf16[128,768]{1,0:T(8,128)(2,1)} %get-tuple-element.101.refs_0_, bf16[128,768]{1,0:T(8,128)(2,1)} %copy-done.11, bf16[128,768]{1,0:T(8,128)(2,1)} %copy-done.10, bf16[128,768]{1,0:T(8,128)(2,1)} %copy-done.9, bf16[2,16,4,48,768]{4,3,2,1,0:T(8,128)(2,1)} %later.7.refs_0_.refs_4_.refs_8_, ...), custom_call_target="tpu_custom_call" | custom-call | flops 1024 | bytes 1024 | tf_op jit(solution)/shard_map/hidden/pallas_call | solution.py:70
  109.0 1.6 all-to-all-done.2.refs_0_.refs_2_
  110.6 0.7 copy-done.8
  111.3 1.0 collective-permute-start.20
  112.4 1.6 collective-permute-start.19
  114.0 14.4 %attend_back.1 = (bf16[16,256,128]{2,1,0:T(8,128)(2,1)}, f32[8,128]{1,0:T(8,128)S(1)}) custom-call(bf16[64,16,128]{2,1,0:T(8,128)(2,1)} %copy-done.8, bf16[80,2048]{1,0:T(8,128)(2,1)} %get-tuple-element.91.refs_1_, bf16[80,2048]{1,0:T(8,128)(2,1)} %get-tuple-element.92.refs_2_, bf16[2048,64]{1,0:T(8,128)(2,1)} %get-tuple-element.93.refs_3_, ...), custom_call_target="tpu_custom_call" | custom-call | flops 1024 | bytes 1024 | tf_op jit(solution)/shard_map/attend_back/pallas_call | solution.py:70
  128.4 4.1 %all-to-all-start.3 = ((bf16[16,256,128]{2,1,0:T(8,128)(2,1)}), bf16[16,256,128]{2,1,0:T(8,128)(2,1)S(1)}, u32[]{:S(2)}, u32[]{:S(2)}) async-start(bf16[16,256,128]{2,1,0:T(8,128)(2,1)} %get-tuple-element.100), calls=%async_computation.3 | async-start | bytes 2097152 | tf_op jit(solution)/shard_map/all_to_all | solution.py:667
  132.6 0.7 copy-done.24
  133.5 5.7 %weights.1 = (bf16[96,1536]{1,0:T(8,128)(2,1)}, bf16[96,1536]{1,0:T(8,128)(2,1)}, bf16[96,1536]{1,0:T(8,128)(2,1)}, bf16[96,1536]{1,0:T(8,128)(2,1)}, bf16[384,1...) custom-call(bf16[128,768]{1,0:T(8,128)(2,1)} %get-tuple-element.101.refs_0_, ...), custom_call_target="tpu_custom_call" | custom-call | flops 99999997952 | bytes 1024 | tf_op jit(solution)/shard_map/weights/pallas_call | solution.py:70
  140.3 1.4 collective-permute-done.25.refs_6_
  142.3 2.7 %first_add.1 = (bf16[16,448,128]{2,1,0:T(8,128)(2,1)}, f32[8,128]{1,0:T(8,128)S(1)}) custom-call(bf16[384,1536]{1,0:T(8,128)(2,1)} %get-tuple-element.107.refs_0_, bf16[96,1536]{1,0:T(8,128)(2,1)S(1)} %collective-permute-done.21.refs_1_, bf16[96,1536]{1,0:T(8,128)(2,1)S(1)} %collective-permute-done.22.refs_2_, ...), custom_call_target="tpu_custom_call" | custom-call | flops 1024 | bytes 1024 | tf_op jit(solution)/shard_map/first_add/pallas_call | solution.py:70
  145.1 3.0 %all-to-all-done.3.refs_1_ = bf16[16,256,128]{2,1,0:T(8,128)(2,1)S(1)} async-done(((bf16[16,256,128]{2,1,0:T(8,128)(2,1)}), bf16[16,256,128]{2,1,0:T(8,128)(2,1)S(1)}, u32[]{:S(2)}, u32[]{:S(2)}) %all-to-all-start.3) | async-done | bytes 1048608 | tf_op jit(solution)/shard_map/all_to_all | solution.py:667
  148.0 2.8 %input_weights.1 = (bf16[384,576]{1,0:T(8,128)(2,1)S(1)}, bf16[400,768]{1,0:T(8,128)(2,1)}, bf16[384,768]{1,0:T(8,128)(2,1)S(1)}, f32[8,768]{1,0:T(8,128)S(1)}) custom-call(bf16[3,128,768]{2,1,0:T(8,128)(2,1)} %refs_0_.5, bf16[16,256,128]{2,1,0:T(8,128)(2,1)S(1)} %all-to-all-done.3.refs_1_, bf16[768,192]{1,0:T(8,128)(2,1)S(1)} %get-tuple-element.106.refs_2_, ...), custom_call_target="tpu_custom_call" | custom-call | flops 1024 | bytes 1024 | tf_op jit(solution)/shard_map/input_weights/pallas_call | solution.py:70
  151.0 2.7 %input_back.1 = (f32[96,768]{1,0:T(8,128)}, bf16[96,768]{1,0:T(8,128)(2,1)}, bf16[96,768]{1,0:T(8,128)(2,1)}, bf16[96,768]{1,0:T(8,128)(2,1)}, f32[8,128]{1,0:T(8,128)S(1)}) custom-call(bf16[192,768]{1,0:T(8,128)(2,1)} %bitcast.10, bf16[192,768]{1,0:T(8,128)(2,1)} %bitcast.12, bf16[192,768]{1,0:T(8,128)(2,1)} %bitcast.14, ...), custom_call_target="tpu_custom_call" | custom-call | flops 1024 | bytes 1024 | tf_op jit(solution)/shard_map/input_back/pallas_call | solution.py:70
  153.7 1.8 last_add.1
  155.4 4.4 %all-to-all-start.4 = ((bf16[16,448,128]{2,1,0:T(8,128)(2,1)}), bf16[16,448,128]{2,1,0:T(8,128)(2,1)S(1)}, u32[]{:S(2)}, u32[]{:S(2)}) async-start(bf16[16,448,128]{2,1,0:T(8,128)(2,1)} %get-tuple-element.120.refs_1_), calls=%async_computation.4 | async-start | bytes 3670016 | tf_op jit(solution)/shard_map/all_to_all | solution.py:667
  159.9 2.1 %collective-permute-start.30 = (bf16[96,768]{1,0:T(8,128)(2,1)}, bf16[96,768]{1,0:T(8,128)(2,1)S(1)}, u32[]{:S(2)}, u32[]{:S(2)}) collective-permute-start(bf16[96,768]{1,0:T(8,128)(2,1)} %later.11), channel_id=1, source_target_pairs={{0,1},{1,2},{2,3},{3,0},{4,5},{5,6},{6,7},{7,4},{8,9},{9,10},{10,1... | collective-permute-start | bytes 442376 | tf_op jit(solution)/shard_map/ppermute | solution.py:651
  161.9 2.7 %collective-permute-start.31 = (bf16[96,768]{1,0:T(8,128)(2,1)S(1)}, bf16[96,768]{1,0:T(8,128)(2,1)S(1)}, u32[]{:S(2)}, u32[]{:S(2)}) collective-permute-start(bf16[96,768]{1,0:T(8,128)(2,1)S(1)} %copy-done.19), channel_id=1, source_target_pairs={{0,2},{1,3},{2,0},{3,1},{4,6},{5,7},{6,4},{7,5},{8,10},{9,11},{10,... | collective-permute-start | bytes 442376 | tf_op jit(solution)/shard_map/ppermute | solution.py:651
  164.6 1.1 collective-permute-start.32
  166.0 2.7 %collective-permute-start.28 = (bf16[96,768]{1,0:T(8,128)(2,1)}, bf16[96,768]{1,0:T(8,128)(2,1)S(1)}, u32[]{:S(2)}, u32[]{:S(2)}) collective-permute-start(bf16[96,768]{1,0:T(8,128)(2,1)} %later.10.refs_0_), channel_id=1, source_target_pairs={{0,2},{1,3},{2,0},{3,1},{4,6},{5,7},{6,4},{7,5},{8,10},{9,11},{10,... | collective-permute-start | bytes 442376 | tf_op jit(solution)/shard_map/ppermute | solution.py:651
  168.9 3.9 %collective-permute-done.31.refs_3_ = bf16[96,768]{1,0:T(8,128)(2,1)S(1)} collective-permute-done((bf16[96,768]{1,0:T(8,128)(2,1)S(1)}, bf16[96,768]{1,0:T(8,128)(2,1)S(1)}, u32[]{:S(2)}, u32[]{:S(2)}) %collective-permute-start.31) | collective-permute-done | bytes 147488 | tf_op jit(solution)/shard_map/ppermute | solution.py:651
  172.8 1.1 input_chunk.1.refs_0_
  173.9 1.9 collective-permute-start.35
  175.9 0.8 collective-permute-start.34
  176.7 1.1 collective-permute-start.33
  178.1 0.9 copy-done.1
  179.0 1.1 layer_out.1
  180.1 2.0 %collective-permute-done.35.refs_3_ = bf16[96,768]{1,0:T(8,128)(2,1)S(1)} collective-permute-done((bf16[96,768]{1,0:T(8,128)(2,1)S(1)}, bf16[96,768]{1,0:T(8,128)(2,1)S(1)}, u32[]{:S(2)}, u32[]{:S(2)}) %collective-permute-start.35) | collective-permute-done | bytes 147488 | tf_op jit(solution)/shard_map/ppermute | solution.py:651
  182.2 2.0 %collective-permute-done.34.refs_2_ = bf16[96,768]{1,0:T(8,128)(2,1)S(1)} collective-permute-done((bf16[96,768]{1,0:T(8,128)(2,1)S(1)}, bf16[96,768]{1,0:T(8,128)(2,1)S(1)}, u32[]{:S(2)}, u32[]{:S(2)}) %collective-permute-start.34) | collective-permute-done | bytes 147488 | tf_op jit(solution)/shard_map/ppermute | solution.py:651
  184.1 1.6 collective-permute-done.33.refs_1_
  185.8 1.1 grad_input.1
  186.9 1.2 all-to-all-done.4.refs_0_
  188.1 0.9 last_sum.1
  (101 shorter events, 6.6 us)
Async XLA Ops:
  7.2 72.9 %all-gather.3.cloned.1.call-start = ((), (), s32[]{:S(2)}) async-start(), calls=%async_computation.5 | async-start | bytes 9732096 | tf_op jit(solution)/shard_map/all_gather | solution.py:716
  8.2 8.6 %collective-permute-start.2 = (bf16[48,768]{1,0:T(8,128)(2,1)S(1)}, bf16[48,768]{1,0:T(8,128)(2,1)S(1)}, u32[]{:S(2)}, u32[]{:S(2)}) collective-permute-start(bf16[48,768]{1,0:T(8,128)(2,1)S(1)} %bitcast_select_fusion.refs_0_), channel_id=1, source_target_pairs={{0,3},{1,0},{2,1},{3,2},{4,7},{5,4},{6,5},{7,6},{8,11},{9,8},{10,9... | collective-permute-start | bytes 221192 | tf_op jit(solution)/shard_map/ppermute | solution.py:651
  12.4 6.0 %collective-permute-start.1 = (bf16[48,768]{1,0:T(8,128)(2,1)S(1)}, bf16[48,768]{1,0:T(8,128)(2,1)S(1)}, u32[]{:S(2)}, u32[]{:S(2)}) collective-permute-start(bf16[48,768]{1,0:T(8,128)(2,1)S(1)} %bitcast_select_fusion.refs_0_), channel_id=1, source_target_pairs={{0,2},{1,3},{2,0},{3,1},{4,6},{5,7},{6,4},{7,5},{8,10},{9,11},{10,... | collective-permute-start | bytes 221192 | tf_op jit(solution)/shard_map/ppermute | solution.py:651
  12.4 6.5 %collective-permute-start = (bf16[48,768]{1,0:T(8,128)(2,1)S(1)}, bf16[48,768]{1,0:T(8,128)(2,1)S(1)}, u32[]{:S(2)}, u32[]{:S(2)}) collective-permute-start(bf16[48,768]{1,0:T(8,128)(2,1)S(1)} %bitcast_select_fusion.refs_0_), channel_id=1, source_target_pairs={{0,1},{1,2},{2,3},{3,0},{4,5},{5,6},{6,7},{7,4},{8,9},{9,10},{10,1... | collective-permute-start | bytes 221192 | tf_op jit(solution)/shard_map/ppermute | solution.py:651
  13.6 13.3 %copy-start.12 = (bf16[192,768]{1,0:T(8,128)(2,1)S(1)}, bf16[192,768]{1,0:T(8,128)(2,1)}, u32[]{:S(2)}) copy-start(bf16[192,768]{1,0:T(8,128)(2,1)} %refs_0_.4) | copy-start | bytes 884740
  13.6 28.8 %copy-start.23 = (f32[64]{0:T(128)S(1)}, f32[64]{0:T(128)}, u32[]{:S(2)}) copy-start(f32[64]{0:T(128)} %constant.14.clone) | copy-start | bytes 772
  19.6 38.7 %copy-start.4 = (f32[768]{0:T(1024)S(1)}, f32[768]{0:T(1024)}, u32[]{:S(2)}) copy-start(f32[768]{0:T(1024)} %refs_5_.5) | copy-start | bytes 9220
  19.7 50.8 %copy-start = (bf16[3,128,768]{2,1,0:T(8,128)(2,1)S(1)}, bf16[3,128,768]{2,1,0:T(8,128)(2,1)}, u32[]{:S(2)}) copy-start(bf16[3,128,768]{2,1,0:T(8,128)(2,1)} %refs_0_.5) | copy-start | bytes 1769476
  19.7 50.8 %copy-start.2 = (f32[768]{0:T(1024)S(1)}, f32[768]{0:T(1024)}, u32[]{:S(2)}) copy-start(f32[768]{0:T(1024)} %refs_4_.1) | copy-start | bytes 9220
  19.7 50.8 %copy-start.3 = (f32[768]{0:T(1024)S(1)}, f32[768]{0:T(1024)}, u32[]{:S(2)}) copy-start(f32[768]{0:T(1024)} %refs_5_.4) | copy-start | bytes 9220
  19.7 50.8 %copy-start.6 = (f32[768]{0:T(1024)S(1)}, f32[768]{0:T(1024)}, u32[]{:S(2)}) copy-start(f32[768]{0:T(1024)} %refs_9_.2) | copy-start | bytes 9220
  19.7 22.7 %all-to-all-start = ((bf16[16,208,128]{2,1,0:T(8,128)(2,1)}), bf16[16,208,128]{2,1,0:T(8,128)(2,1)S(1)}, u32[]{:S(2)}, u32[]{:S(2)}) async-start(bf16[16,208,128]{2,1,0:T(8,128)(2,1)} %get-tuple-element.81), calls=%async_computation | async-start | bytes 1703936 | tf_op jit(solution)/shard_map/all_to_all | solution.py:667
  26.9 5.7 %collective-permute-start.5 = (bf16[96,768]{1,0:T(8,128)(2,1)S(1)}, bf16[96,768]{1,0:T(8,128)(2,1)S(1)}, u32[]{:S(2)}, u32[]{:S(2)}) collective-permute-start(bf16[96,768]{1,0:T(8,128)(2,1)S(1)} %constant_dynamic-slice_fusion), channel_id=1, source_target_pairs={{0,3},{1,0},{2,1},{3,2},{4,7},{5,4},{6,5},{7,6},{8,11},{9,8},{10,9... | collective-permute-start | bytes 442376 | tf_op jit(solution)/shard_map/ppermute | solution.py:651
  27.9 7.0 %collective-permute-start.4 = (bf16[96,768]{1,0:T(8,128)(2,1)S(1)}, bf16[96,768]{1,0:T(8,128)(2,1)S(1)}, u32[]{:S(2)}, u32[]{:S(2)}) collective-permute-start(bf16[96,768]{1,0:T(8,128)(2,1)S(1)} %constant_dynamic-slice_fusion), channel_id=1, source_target_pairs={{0,2},{1,3},{2,0},{3,1},{4,6},{5,7},{6,4},{7,5},{8,10},{9,11},{10,... | collective-permute-start | bytes 442376 | tf_op jit(solution)/shard_map/ppermute | solution.py:651
  29.2 7.1 %collective-permute-start.3 = (bf16[96,768]{1,0:T(8,128)(2,1)S(1)}, bf16[96,768]{1,0:T(8,128)(2,1)S(1)}, u32[]{:S(2)}, u32[]{:S(2)}) collective-permute-start(bf16[96,768]{1,0:T(8,128)(2,1)S(1)} %constant_dynamic-slice_fusion), channel_id=1, source_target_pairs={{0,1},{1,2},{2,3},{3,0},{4,5},{5,6},{6,7},{7,4},{8,9},{9,10},{10,1... | collective-permute-start | bytes 442376 | tf_op jit(solution)/shard_map/ppermute | solution.py:651
  32.7 9.9 %copy-start.13 = (bf16[96,768]{1,0:T(8,128)(2,1)}, bf16[96,768]{1,0:T(8,128)(2,1)S(1)}, u32[]{:S(2)}) copy-start(bf16[96,768]{1,0:T(8,128)(2,1)S(1)} %collective-permute-done.5.refs_4_.refs_3_) | copy-start | bytes 442372
  34.8 7.7 %copy-start.14 = (bf16[96,768]{1,0:T(8,128)(2,1)}, bf16[96,768]{1,0:T(8,128)(2,1)S(1)}, u32[]{:S(2)}) copy-start(bf16[96,768]{1,0:T(8,128)(2,1)S(1)} %collective-permute-done.4.refs_3_.refs_2_) | copy-start | bytes 442372
  36.3 6.2 %copy-start.15 = (bf16[96,768]{1,0:T(8,128)(2,1)}, bf16[96,768]{1,0:T(8,128)(2,1)S(1)}, u32[]{:S(2)}) copy-start(bf16[96,768]{1,0:T(8,128)(2,1)S(1)} %collective-permute-done.3.refs_2_.refs_1_) | copy-start | bytes 442372
  52.5 18.0 %all-to-all-start.1 = ((bf16[64,16,128]{2,1,0:T(8,128)(2,1)}), bf16[64,16,128]{2,1,0:T(8,128)(2,1)S(1)}, u32[]{:S(2)}, u32[]{:S(2)}) async-start(bf16[64,16,128]{2,1,0:T(8,128)(2,1)} %get-tuple-element.82), calls=%async_computation.1 | async-start | bytes 524288 | tf_op jit(solution)/shard_map/all_to_all | solution.py:671
  57.7 9.9 %collective-permute-start.8 = (bf16[96,768]{1,0:T(8,128)(2,1)}, bf16[96,768]{1,0:T(8,128)(2,1)S(1)}, u32[]{:S(2)}, u32[]{:S(2)}) collective-permute-start(bf16[96,768]{1,0:T(8,128)(2,1)} %copy-done.13), channel_id=1, source_target_pairs={{0,64},{64,0},{1,65},{65,1},{2,66},{66,2},{3,67},{67,3},{4,68},{68... | collective-permute-start | bytes 442376 | tf_op jit(solution)/shard_map/ppermute | solution.py:663
  57.8 9.8 %collective-permute-start.7 = (bf16[96,768]{1,0:T(8,128)(2,1)}, bf16[96,768]{1,0:T(8,128)(2,1)S(1)}, u32[]{:S(2)}, u32[]{:S(2)}) collective-permute-start(bf16[96,768]{1,0:T(8,128)(2,1)} %copy-done.14), channel_id=1, source_target_pairs={{0,64},{64,0},{1,65},{65,1},{2,66},{66,2},{3,67},{67,3},{4,68},{68... | collective-permute-start | bytes 442376 | tf_op jit(solution)/shard_map/ppermute | solution.py:663
  58.2 9.4 %collective-permute-start.6 = (bf16[96,768]{1,0:T(8,128)(2,1)}, bf16[96,768]{1,0:T(8,128)(2,1)S(1)}, u32[]{:S(2)}, u32[]{:S(2)}) collective-permute-start(bf16[96,768]{1,0:T(8,128)(2,1)} %copy-done.15), channel_id=1, source_target_pairs={{0,64},{64,0},{1,65},{65,1},{2,66},{66,2},{3,67},{67,3},{4,68},{68... | collective-permute-start | bytes 442376 | tf_op jit(solution)/shard_map/ppermute | solution.py:663
  58.3 4.1 %collective-permute-start.11 = (f32[768]{0:T(1024)S(1)}, f32[768]{0:T(1024)S(1)}, u32[]{:S(2)}, u32[]{:S(2)}) collective-permute-start(f32[768]{0:T(1024)S(1)} %copy-done.4), channel_id=1, source_target_pairs={{0,3},{1,0},{2,1},{3,2},{4,7},{5,4},{6,5},{7,6},{8,11},{9,8},{10,9... | collective-permute-start | bytes 9224 | tf_op jit(solution)/shard_map/ppermute | solution.py:651
  61.1 5.1 %collective-permute-start.10 = (f32[768]{0:T(1024)S(1)}, f32[768]{0:T(1024)S(1)}, u32[]{:S(2)}, u32[]{:S(2)}) collective-permute-start(f32[768]{0:T(1024)S(1)} %copy-done.4), channel_id=1, source_target_pairs={{0,2},{1,3},{2,0},{3,1},{4,6},{5,7},{6,4},{7,5},{8,10},{9,11},{10,... | collective-permute-start | bytes 9224 | tf_op jit(solution)/shard_map/ppermute | solution.py:651
  62.5 5.1 %collective-permute-start.9 = (f32[768]{0:T(1024)S(1)}, f32[768]{0:T(1024)S(1)}, u32[]{:S(2)}, u32[]{:S(2)}) collective-permute-start(f32[768]{0:T(1024)S(1)} %copy-done.4), channel_id=1, source_target_pairs={{0,1},{1,2},{2,3},{3,0},{4,5},{5,6},{6,7},{7,4},{8,9},{9,10},{10,1... | collective-permute-start | bytes 9224 | tf_op jit(solution)/shard_map/ppermute | solution.py:651
  67.6 2.9 %copy-start.16 = (bf16[96,768]{1,0:T(8,128)(2,1)}, bf16[96,768]{1,0:T(8,128)(2,1)S(1)}, u32[]{:S(2)}) copy-start(bf16[96,768]{1,0:T(8,128)(2,1)S(1)} %collective-permute-done.8.refs_6_) | copy-start | bytes 442372
  67.6 2.9 %copy-start.17 = (bf16[96,768]{1,0:T(8,128)(2,1)}, bf16[96,768]{1,0:T(8,128)(2,1)S(1)}, u32[]{:S(2)}) copy-start(bf16[96,768]{1,0:T(8,128)(2,1)S(1)} %collective-permute-done.7.refs_5_) | copy-start | bytes 442372
  67.6 2.9 %copy-start.18 = (bf16[96,768]{1,0:T(8,128)(2,1)}, bf16[96,768]{1,0:T(8,128)(2,1)S(1)}, u32[]{:S(2)}) copy-start(bf16[96,768]{1,0:T(8,128)(2,1)S(1)} %collective-permute-done.6.refs_4_) | copy-start | bytes 442372
  73.6 6.4 %copy-start.7 = (f32[8,128]{1,0:T(8,128)}, f32[8,128]{1,0:T(8,128)S(1)}, u32[]{:S(2)}) copy-start(f32[8,128]{1,0:T(8,128)S(1)} %get-tuple-element.83.refs_1_) | copy-start | bytes 12292
  73.6 16.8 %collective-permute-start.12 = (bf16[128,768]{1,0:T(8,128)(2,1)}, bf16[128,768]{1,0:T(8,128)(2,1)S(1)}, u32[]{:S(2)}, u32[]{:S(2)}) collective-permute-start(bf16[128,768]{1,0:T(8,128)(2,1)} %get-tuple-element.88), channel_id=1, source_target_pairs={{0,3},{1,0},{2,1},{3,2},{4,7},{5,4},{6,5},{7,6},{8,11},{9,8},{10,9... | collective-permute-start | bytes 589832 | tf_op jit(solution)/shard_map/ppermute | solution.py:651
  73.9 16.5 %collective-permute-start.13 = (bf16[128,768]{1,0:T(8,128)(2,1)}, bf16[128,768]{1,0:T(8,128)(2,1)S(1)}, u32[]{:S(2)}, u32[]{:S(2)}) collective-permute-start(bf16[128,768]{1,0:T(8,128)(2,1)} %get-tuple-element.89), channel_id=1, source_target_pairs={{0,2},{1,3},{2,0},{3,1},{4,6},{5,7},{6,4},{7,5},{8,10},{9,11},{10,... | collective-permute-start | bytes 589832 | tf_op jit(solution)/shard_map/ppermute | solution.py:651
  76.2 14.2 %collective-permute-start.14 = (bf16[128,768]{1,0:T(8,128)(2,1)}, bf16[128,768]{1,0:T(8,128)(2,1)S(1)}, u32[]{:S(2)}, u32[]{:S(2)}) collective-permute-start(bf16[128,768]{1,0:T(8,128)(2,1)} %get-tuple-element.90), channel_id=1, source_target_pairs={{0,1},{1,2},{2,3},{3,0},{4,5},{5,6},{6,7},{7,4},{8,9},{9,10},{10,1... | collective-permute-start | bytes 589832 | tf_op jit(solution)/shard_map/ppermute | solution.py:651
  80.1 24.3 %copy-start.5 = (f32[768]{0:T(1024)S(1)}, f32[768]{0:T(1024)}, u32[]{:S(2)}) copy-start(f32[768]{0:T(1024)} %refs_5_.5) | copy-start | bytes 9220
  91.3 19.3 %all-to-all-start.2 = ((bf16[64,16,128]{2,1,0:T(8,128)(2,1)}), bf16[64,16,128]{2,1,0:T(8,128)(2,1)S(1)}, u32[]{:S(2)}, u32[]{:S(2)}) async-start(bf16[64,16,128]{2,1,0:T(8,128)(2,1)} %later.8), calls=%async_computation.2 | async-start | bytes 524288 | tf_op jit(solution)/shard_map/all_to_all | solution.py:671
  99.8 8.3 %collective-permute-start.17 = (bf16[16,768]{1,0:T(8,128)(2,1)}, bf16[16,768]{1,0:T(8,128)(2,1)S(1)}, u32[]{:S(2)}, u32[]{:S(2)}) collective-permute-start(bf16[16,768]{1,0:T(8,128)(2,1)} %get-tuple-element.99.refs_9_), channel_id=1, source_target_pairs={{0,3},{1,0},{2,1},{3,2},{4,7},{5,4},{6,5},{7,6},{8,11},{9,8},{10,9... | collective-permute-start | bytes 73736 | tf_op jit(solution)/shard_map/ppermute | solution.py:651
  102.6 6.0 %collective-permute-start.16 = (bf16[16,768]{1,0:T(8,128)(2,1)}, bf16[16,768]{1,0:T(8,128)(2,1)S(1)}, u32[]{:S(2)}, u32[]{:S(2)}) collective-permute-start(bf16[16,768]{1,0:T(8,128)(2,1)} %get-tuple-element.99.refs_9_), channel_id=1, source_target_pairs={{0,2},{1,3},{2,0},{3,1},{4,6},{5,7},{6,4},{7,5},{8,10},{9,11},{10,... | collective-permute-start | bytes 73736 | tf_op jit(solution)/shard_map/ppermute | solution.py:651
  103.5 5.6 %collective-permute-start.15 = (bf16[16,768]{1,0:T(8,128)(2,1)}, bf16[16,768]{1,0:T(8,128)(2,1)S(1)}, u32[]{:S(2)}, u32[]{:S(2)}) collective-permute-start(bf16[16,768]{1,0:T(8,128)(2,1)} %get-tuple-element.99.refs_9_), channel_id=1, source_target_pairs={{0,1},{1,2},{2,3},{3,0},{4,5},{5,6},{6,7},{7,4},{8,9},{9,10},{10,1... | collective-permute-start | bytes 73736 | tf_op jit(solution)/shard_map/ppermute | solution.py:651
  108.1 2.5 %copy-start.20 = (bf16[16,768]{1,0:T(8,128)(2,1)}, bf16[16,768]{1,0:T(8,128)(2,1)S(1)}, u32[]{:S(2)}) copy-start(bf16[16,768]{1,0:T(8,128)(2,1)S(1)} %collective-permute-done.17.refs_12_.refs_5_) | copy-start | bytes 73732
  108.6 2.0 %copy-start.21 = (bf16[16,768]{1,0:T(8,128)(2,1)}, bf16[16,768]{1,0:T(8,128)(2,1)S(1)}, u32[]{:S(2)}) copy-start(bf16[16,768]{1,0:T(8,128)(2,1)S(1)} %collective-permute-done.16.refs_11_.refs_4_) | copy-start | bytes 73732
  109.0 1.6 copy-start.22
  111.3 21.2 %collective-permute-start.20 = (bf16[192,768]{1,0:T(8,128)(2,1)}, bf16[192,768]{1,0:T(8,128)(2,1)S(1)}, u32[]{:S(2)}, u32[]{:S(2)}) collective-permute-start(bf16[192,768]{1,0:T(8,128)(2,1)} %later.9.refs_4_), channel_id=1, source_target_pairs={{0,3},{1,0},{2,1},{3,2},{4,7},{5,4},{6,5},{7,6},{8,11},{9,8},{10,9... | collective-permute-start | bytes 884744 | tf_op jit(solution)/shard_map/ppermute | solution.py:651
  112.4 20.2 %collective-permute-start.19 = (bf16[192,768]{1,0:T(8,128)(2,1)}, bf16[192,768]{1,0:T(8,128)(2,1)S(1)}, u32[]{:S(2)}, u32[]{:S(2)}) collective-permute-start(bf16[192,768]{1,0:T(8,128)(2,1)} %later.9.refs_4_), channel_id=1, source_target_pairs={{0,2},{1,3},{2,0},{3,1},{4,6},{5,7},{6,4},{7,5},{8,10},{9,11},{10,... | collective-permute-start | bytes 884744 | tf_op jit(solution)/shard_map/ppermute | solution.py:651
  113.9 18.6 %collective-permute-start.18 = (bf16[192,768]{1,0:T(8,128)(2,1)}, bf16[192,768]{1,0:T(8,128)(2,1)S(1)}, u32[]{:S(2)}, u32[]{:S(2)}) collective-permute-start(bf16[192,768]{1,0:T(8,128)(2,1)} %later.9.refs_4_), channel_id=1, source_target_pairs={{0,1},{1,2},{2,3},{3,0},{4,5},{5,6},{6,7},{7,4},{8,9},{9,10},{10,1... | collective-permute-start | bytes 884744 | tf_op jit(solution)/shard_map/ppermute | solution.py:651
  128.4 19.6 %all-to-all-start.3 = ((bf16[16,256,128]{2,1,0:T(8,128)(2,1)}), bf16[16,256,128]{2,1,0:T(8,128)(2,1)S(1)}, u32[]{:S(2)}, u32[]{:S(2)}) async-start(bf16[16,256,128]{2,1,0:T(8,128)(2,1)} %get-tuple-element.100), calls=%async_computation.3 | async-start | bytes 2097152 | tf_op jit(solution)/shard_map/all_to_all | solution.py:667
  132.5 0.8 copy-start.25
  132.5 0.9 copy-start.26
  139.1 2.6 %collective-permute-start.21 = (bf16[96,1536]{1,0:T(8,128)(2,1)}, bf16[96,1536]{1,0:T(8,128)(2,1)S(1)}, u32[]{:S(2)}, u32[]{:S(2)}) collective-permute-start(bf16[96,1536]{1,0:T(8,128)(2,1)} %get-tuple-element.108), channel_id=1, source_target_pairs={{0,64},{64,0},{1,65},{65,1},{2,66},{66,2},{3,67},{67,3},{4,68},{68... | collective-permute-start | bytes 884744 | tf_op jit(solution)/shard_map/ppermute | solution.py:663
  139.2 2.5 %collective-permute-start.22 = (bf16[96,1536]{1,0:T(8,128)(2,1)}, bf16[96,1536]{1,0:T(8,128)(2,1)S(1)}, u32[]{:S(2)}, u32[]{:S(2)}) collective-permute-start(bf16[96,1536]{1,0:T(8,128)(2,1)} %get-tuple-element.109), channel_id=1, source_target_pairs={{0,64},{64,0},{1,65},{65,1},{2,66},{66,2},{3,67},{67,3},{4,68},{68... | collective-permute-start | bytes 884744 | tf_op jit(solution)/shard_map/ppermute | solution.py:663
  139.7 2.1 %collective-permute-start.23 = (bf16[96,1536]{1,0:T(8,128)(2,1)}, bf16[96,1536]{1,0:T(8,128)(2,1)S(1)}, u32[]{:S(2)}, u32[]{:S(2)}) collective-permute-start(bf16[96,1536]{1,0:T(8,128)(2,1)} %get-tuple-element.110), channel_id=1, source_target_pairs={{0,64},{64,0},{1,65},{65,1},{2,66},{66,2},{3,67},{67,3},{4,68},{68... | collective-permute-start | bytes 884744 | tf_op jit(solution)/shard_map/ppermute | solution.py:663
  139.8 2.5 %collective-permute-start.24 = (bf16[96,1536]{1,0:T(8,128)(2,1)}, bf16[96,1536]{1,0:T(8,128)(2,1)S(1)}, u32[]{:S(2)}, u32[]{:S(2)}) collective-permute-start(bf16[96,1536]{1,0:T(8,128)(2,1)} %get-tuple-element.111), channel_id=1, source_target_pairs={{0,64},{64,0},{1,65},{65,1},{2,66},{66,2},{3,67},{67,3},{4,68},{68... | collective-permute-start | bytes 884744 | tf_op jit(solution)/shard_map/ppermute | solution.py:663
  140.2 1.5 collective-permute-start.25
  150.9 2.8 %collective-permute-start.26 = (bf16[400,768]{1,0:T(8,128)(2,1)}, bf16[400,768]{1,0:T(8,128)(2,1)S(1)}, u32[]{:S(2)}, u32[]{:S(2)}) collective-permute-start(bf16[400,768]{1,0:T(8,128)(2,1)} %get-tuple-element.116), channel_id=1, source_target_pairs={{0,64},{64,0},{1,65},{65,1},{2,66},{66,2},{3,67},{67,3},{4,68},{68... | collective-permute-start | bytes 1843208 | tf_op jit(solution)/shard_map/ppermute | solution.py:663
  155.4 32.7 %all-to-all-start.4 = ((bf16[16,448,128]{2,1,0:T(8,128)(2,1)}), bf16[16,448,128]{2,1,0:T(8,128)(2,1)S(1)}, u32[]{:S(2)}, u32[]{:S(2)}) async-start(bf16[16,448,128]{2,1,0:T(8,128)(2,1)} %get-tuple-element.120.refs_1_), calls=%async_computation.4 | async-start | bytes 3670016 | tf_op jit(solution)/shard_map/all_to_all | solution.py:667
  159.9 2.1 %copy-start.19 = (bf16[96,768]{1,0:T(8,128)(2,1)S(1)}, bf16[96,768]{1,0:T(8,128)(2,1)}, u32[]{:S(2)}) copy-start(bf16[96,768]{1,0:T(8,128)(2,1)} %later.12) | copy-start | bytes 442372
  159.9 8.9 %collective-permute-start.30 = (bf16[96,768]{1,0:T(8,128)(2,1)}, bf16[96,768]{1,0:T(8,128)(2,1)S(1)}, u32[]{:S(2)}, u32[]{:S(2)}) collective-permute-start(bf16[96,768]{1,0:T(8,128)(2,1)} %later.11), channel_id=1, source_target_pairs={{0,1},{1,2},{2,3},{3,0},{4,5},{5,6},{6,7},{7,4},{8,9},{9,10},{10,1... | collective-permute-start | bytes 442376 | tf_op jit(solution)/shard_map/ppermute | solution.py:651
  161.9 10.8 %collective-permute-start.31 = (bf16[96,768]{1,0:T(8,128)(2,1)S(1)}, bf16[96,768]{1,0:T(8,128)(2,1)S(1)}, u32[]{:S(2)}, u32[]{:S(2)}) collective-permute-start(bf16[96,768]{1,0:T(8,128)(2,1)S(1)} %copy-done.19), channel_id=1, source_target_pairs={{0,2},{1,3},{2,0},{3,1},{4,6},{5,7},{6,4},{7,5},{8,10},{9,11},{10,... | collective-permute-start | bytes 442376 | tf_op jit(solution)/shard_map/ppermute | solution.py:651
  164.6 8.1 %collective-permute-start.32 = (bf16[96,768]{1,0:T(8,128)(2,1)}, bf16[96,768]{1,0:T(8,128)(2,1)S(1)}, u32[]{:S(2)}, u32[]{:S(2)}) collective-permute-start(bf16[96,768]{1,0:T(8,128)(2,1)} %later.13), channel_id=1, source_target_pairs={{0,3},{1,0},{2,1},{3,2},{4,7},{5,4},{6,5},{7,6},{8,11},{9,8},{10,9... | collective-permute-start | bytes 442376 | tf_op jit(solution)/shard_map/ppermute | solution.py:651
  165.8 10.9 %collective-permute-start.29 = (bf16[96,768]{1,0:T(8,128)(2,1)}, bf16[96,768]{1,0:T(8,128)(2,1)S(1)}, u32[]{:S(2)}, u32[]{:S(2)}) collective-permute-start(bf16[96,768]{1,0:T(8,128)(2,1)} %later.10.refs_0_), channel_id=1, source_target_pairs={{0,3},{1,0},{2,1},{3,2},{4,7},{5,4},{6,5},{7,6},{8,11},{9,8},{10,9... | collective-permute-start | bytes 442376 | tf_op jit(solution)/shard_map/ppermute | solution.py:651
  166.0 11.7 %collective-permute-start.28 = (bf16[96,768]{1,0:T(8,128)(2,1)}, bf16[96,768]{1,0:T(8,128)(2,1)S(1)}, u32[]{:S(2)}, u32[]{:S(2)}) collective-permute-start(bf16[96,768]{1,0:T(8,128)(2,1)} %later.10.refs_0_), channel_id=1, source_target_pairs={{0,2},{1,3},{2,0},{3,1},{4,6},{5,7},{6,4},{7,5},{8,10},{9,11},{10,... | collective-permute-start | bytes 442376 | tf_op jit(solution)/shard_map/ppermute | solution.py:651
  168.8 9.4 %collective-permute-start.27 = (bf16[96,768]{1,0:T(8,128)(2,1)}, bf16[96,768]{1,0:T(8,128)(2,1)S(1)}, u32[]{:S(2)}, u32[]{:S(2)}) collective-permute-start(bf16[96,768]{1,0:T(8,128)(2,1)} %later.10.refs_0_), channel_id=1, source_target_pairs={{0,1},{1,2},{2,3},{3,0},{4,5},{5,6},{6,7},{7,4},{8,9},{9,10},{10,1... | collective-permute-start | bytes 442376 | tf_op jit(solution)/shard_map/ppermute | solution.py:651
  173.9 8.2 %collective-permute-start.35 = (bf16[96,768]{1,0:T(8,128)(2,1)S(1)}, bf16[96,768]{1,0:T(8,128)(2,1)S(1)}, u32[]{:S(2)}, u32[]{:S(2)}) collective-permute-start(bf16[96,768]{1,0:T(8,128)(2,1)S(1)} %input_chunk.1.refs_0_), channel_id=1, source_target_pairs={{0,3},{1,0},{2,1},{3,2},{4,7},{5,4},{6,5},{7,6},{8,11},{9,8},{10,9... | collective-permute-start | bytes 442376 | tf_op jit(solution)/shard_map/ppermute | solution.py:651
  175.9 8.3 %collective-permute-start.34 = (bf16[96,768]{1,0:T(8,128)(2,1)S(1)}, bf16[96,768]{1,0:T(8,128)(2,1)S(1)}, u32[]{:S(2)}, u32[]{:S(2)}) collective-permute-start(bf16[96,768]{1,0:T(8,128)(2,1)S(1)} %input_chunk.1.refs_0_), channel_id=1, source_target_pairs={{0,2},{1,3},{2,0},{3,1},{4,6},{5,7},{6,4},{7,5},{8,10},{9,11},{10,... | collective-permute-start | bytes 442376 | tf_op jit(solution)/shard_map/ppermute | solution.py:651
  176.7 9.1 %collective-permute-start.33 = (bf16[96,768]{1,0:T(8,128)(2,1)S(1)}, bf16[96,768]{1,0:T(8,128)(2,1)S(1)}, u32[]{:S(2)}, u32[]{:S(2)}) collective-permute-start(bf16[96,768]{1,0:T(8,128)(2,1)S(1)} %input_chunk.1.refs_0_), channel_id=1, source_target_pairs={{0,1},{1,2},{2,3},{3,0},{4,5},{5,6},{6,7},{7,4},{8,9},{9,10},{10,1... | collective-permute-start | bytes 442376 | tf_op jit(solution)/shard_map/ppermute | solution.py:651
  178.1 0.9 copy-start.1
  (5 other events, 3.6 us)
Sparse Core Ops, SparseCore 0:
  19.8 60.2 all-gather.2
